TPU v7x, 128 devices: a whole 4x4x4 slice. The times are simulated.
128 devices in a mesh: gr: 16 (over y, x_lo, core), gc: 8 (over x_hi, z).
Axes of the slice: x: 4 (x_hi: 2, x_lo: 2; x = x_hi * 2 + x_lo), y: 4, z: 4, core: 2. Of those that a mesh axis runs over, the one named last changes fastest.
Arguments:
- features: bfloat16 [131072, 256], P(('gr', 'gc')), may hold values from -6 to 6
- weight: bfloat16 [256, 256], replicated, may hold values from -0.375 to 0.375
- cotangent: bfloat16 [131072, 256], P(('gr', 'gc')), may hold values from -6 to 6
- blocks: bfloat16 [16, 8, 128, 128, 128], P('gr', 'gc'), may hold values from -0.21875 to 0.21875
- block_row: int32 [16, 8, 128], P('gr', 'gc'), may hold values from 0 to 63, as said below
- block_col: int32 [16, 8, 128], P('gr', 'gc'), may hold values from 0 to 127, as said below
- counts: int32 [16, 8], P('gr', 'gc'), may hold values from 16 to 128, as said below
Outputs:
- activations: bfloat16 [131072, 256], P(('gr', 'gc'))
- weight_grad: float32 [256, 256], replicated
- feature_grad: bfloat16 [131072, 256], P(('gr', 'gc'))
Inputs may be any that keep to these rules, and one draw needn't show every extreme that they name: `block_row`: within one grid cell the 128 slots name distinct pairs of tile row and tile column. `block_col`: within one grid cell the 128 slots name distinct pairs of tile row and tile column. `counts`: some grid cell fills all 128 slots in every draw.
All inputs are finite; a program needn't handle non-finite values.
Results may differ from a plain program's by a relative error of at most 0.024.
Values may be sent and summed in bfloat16 or wider, within the bound.
No kernel may reach another device: no remote copies, remote signals or barrier semaphores. Data moves between devices by JAX's collectives and lax.ppermute only.
A program may use at most 192 MiB of HBM per device.

v0:
```python
import math

import jax
import jax.numpy as jnp
from jax import lax
from jax.sharding import PartitionSpec as P


def block_pass(tile_stack, target_ids, source_ids, live_count, source_blocks, out_tiles, adjoint):
    slot_total = tile_stack.shape[0]
    source_total = source_blocks.shape[0]
    group_size = math.gcd(slot_total, 64)
    live_flags = jnp.arange(slot_total) < live_count
    einsum_form = "gij,gif->gjf" if adjoint else "gij,gjf->gif"
    source_range = jnp.arange(source_total, dtype=jnp.int32)
    target_range = jnp.arange(out_tiles, dtype=jnp.int32)

    def one_group(running, group_index):
        offset = group_index * group_size
        tile_group = lax.dynamic_slice_in_dim(tile_stack, offset, group_size, 0)
        target_group = lax.dynamic_slice_in_dim(target_ids, offset, group_size, 0)
        source_group = lax.dynamic_slice_in_dim(source_ids, offset, group_size, 0)
        flag_group = lax.dynamic_slice_in_dim(live_flags, offset, group_size, 0)
        source_hot = (source_group[:, None] == source_range[None, :]).astype(jnp.bfloat16)
        picked = jnp.einsum(
            "gs,stf->gtf", source_hot, source_blocks, preferred_element_type=jnp.float32
        ).astype(jnp.bfloat16)
        product = jnp.einsum(einsum_form, tile_group, picked, preferred_element_type=jnp.float32)
        target_hot = (
            (target_group[:, None] == target_range[None, :]) & flag_group[:, None]
        ).astype(jnp.bfloat16)
        high_part = product.astype(jnp.bfloat16)
        low_part = (product - high_part.astype(jnp.float32)).astype(jnp.bfloat16)
        placed = jnp.einsum(
            "go,gif->oif", target_hot, high_part, preferred_element_type=jnp.float32
        )
        placed = placed + jnp.einsum(
            "go,gif->oif", target_hot, low_part, preferred_element_type=jnp.float32
        )
        return (running + placed, None)

    running, unused = lax.scan(
        one_group,
        jnp.zeros((out_tiles, tile_stack.shape[-1], source_blocks.shape[-1]), jnp.float32),
        jnp.arange(slot_total // group_size),
    )
    return running


def silu_parts(pre_act):
    sigmoid_val = jax.nn.sigmoid(pre_act)
    return (pre_act * sigmoid_val, sigmoid_val * (1.0 + pre_act * (1.0 - sigmoid_val)))


def transpose_product(left_rows, right_rows):
    return lax.dot_general(
        left_rows, right_rows, (((1,), (1,)), ((), ())), preferred_element_type=jnp.float32
    )


def body(features, weight, cotangent, blocks, block_row, block_col, counts):
    tile_stack = blocks[0, 0]
    row_ids = block_row[0, 0]
    col_ids = block_col[0, 0]
    live_count = counts[0, 0]
    tile_side = tile_stack.shape[-1]
    feat_width = features.shape[1]
    local_rows = features.shape[0]
    column_feats = lax.all_gather(features, "gr", axis=0, tiled=True)
    column_blocks = column_feats.reshape(-1, tile_side, feat_width)
    row_tiles = local_rows * lax.axis_size("gc") // tile_side
    partial_value = block_pass(
        tile_stack, row_ids, col_ids, live_count, column_blocks, row_tiles, False
    ).reshape(-1, feat_width)
    own_summed = lax.psum_scatter(
        partial_value.astype(jnp.bfloat16), "gc", scatter_dimension=0, tiled=True
    )
    pre_act = jnp.dot(own_summed, weight, preferred_element_type=jnp.float32)
    activated, slope = silu_parts(pre_act)
    activations = activated.astype(jnp.bfloat16)
    own_grad = (cotangent.astype(jnp.float32) * slope).astype(jnp.bfloat16)
    grad_mixed = transpose_product(own_grad, weight).astype(jnp.bfloat16)
    row_grads = lax.all_gather(grad_mixed, "gc", axis=0, tiled=True)
    local_wgrad = lax.dot_general(
        own_summed, own_grad, (((0,), (0,)), ((), ())), preferred_element_type=jnp.float32
    )
    node_total = local_rows * lax.axis_size("gr") * lax.axis_size("gc")
    weight_grad = lax.psum(local_wgrad, ("gr", "gc")) * (1.0 / math.sqrt(node_total))
    grad_blocks = row_grads.reshape(-1, tile_side, feat_width)
    column_tiles = local_rows * lax.axis_size("gr") // tile_side
    adjoint_part = block_pass(
        tile_stack, col_ids, row_ids, live_count, grad_blocks, column_tiles, True
    ).reshape(-1, feat_width)
    feature_grad = lax.psum_scatter(
        adjoint_part.astype(jnp.bfloat16), "gr", scatter_dimension=0, tiled=True
    )
    return (activations, weight_grad, feature_grad)


def solution(mesh):
    return jax.shard_map(
        body,
        mesh=mesh,
        in_specs=(
            P(("gr", "gc"), None),
            P(),
            P(("gr", "gc"), None),
            P("gr", "gc", None, None, None),
            P("gr", "gc", None),
            P("gr", "gc", None),
            P("gr", "gc"),
        ),
        out_specs=(P(("gr", "gc"), None), P(), P(("gr", "gc"), None)),
        check_vma=False,
    )
```

profile of v0, /device:TPU:0, one launch (start us, length us, event | category | flops | bytes accessed | tf_op | source)
XLA Modules:
  0.0 549.1 jit_solution(14157882542608244131)
XLA Ops:
  7.2 0.0 copy-start
  7.2 0.0 all-gather.3.cloned.1.call-start
  7.2 0.7 all-gather.3.cloned.1.call-update
  7.9 0.0 reduce-scatter.3.cloned.1.call-start
  8.6 55.7 %all-gather.3.cloned.1.call-done = bf16[16384,256]{1,0:T(8,128)(2,1)} async-done(((bf16[1024,256]{1,0:T(8,128)(2,1)}), bf16[16384,256]{1,0:T(8,128)(2,1)}) %all-gather.3.cloned.1.call-update) | async-done | bytes 8388624 | tf_op jit(solution)/shard_map/all_gather | solution.py:69
  64.3 64.6 %while.22 = (s32[]{:T(128)}, f32[64,128,256]{2,0,1:T(8,128)}, s32[2]{0:T(128)S(1)}, s32[128]{0:T(128)}, pred[128]{0:T(512)(128)(4,1)S(1)}, /*index=5*/bf16[128,1...) while((s32[]{:T(128)}, f32[64,128,256]{2,0,1:T(8,128)}, ...), condition=%wide.region_1.2_spmd.clone, body=%wide.region_0.1_spmd.clone.sunk | while | flops 1625317376 | bytes 85985512 | solution.py:42
  64.3 0.6 dynamic_slice.60
  65.6 0.1 dynamic_slice.63
  65.6 0.7 dynamic_slice.62
  66.4 0.7 dynamic_slice.61
  67.1 9.0 %fusion.78 = bf16[64,128,256]{2,0,1:T(8,128)(2,1)S(1)} fusion(bf16[128,128,256]{2,1,0:T(8,128)(2,1)} %get-tuple-element.362, s32[64]{0:T(128)S(1)} %dynamic_slice.61), kind=kOutput, calls=%fused_computation.5.clone.1 | convolution fusion | flops 536879104 | bytes 12583168 | tf_op jit(solution)/shard_map/while/body/eval_jaxpr/gs,stf->gtf/dot_general | solution.py:25
  76.1 0.0 copy-done.2
  76.1 3.0 subtract_convert_fusion.4
  79.1 3.3 fusion.79
  82.3 6.7 %select_add_fusion.4 = f32[64,128,256]{2,0,1:T(8,128)} fusion(f32[64,128,256]{2,0,1:T(8,128)} %get-tuple-element.344, f32[64,128,256]{2,0,1:T(8,128)S(1)} %fusion.79, pred[]{:T(512)S(6)} %compare.6, bf16[64,128,256]{2,1,0:T(8,128)(2,1)S(1)} %get-tuple-element.320, s32[64]{0:T(128)S(1)} %dynamic_slice.62, pred[64]{0:T(512)(128)(4,1)S(1)} %dynamic_slice.63), kind=kOutput, calls=%fused_computation.7.clone.1 | convolution fusion | flops 274735104 | bytes 29360448 | tf_op jit(solution)/shard_map/while/body/eval_jaxpr/go,gif->oif/dot_general | solution.py:34
  89.0 0.6 dynamic_slice.60
  90.3 0.1 dynamic_slice.63
  90.4 0.7 dynamic_slice.62
  91.1 0.7 dynamic_slice.61
  91.8 9.0 %fusion.78 = bf16[64,128,256]{2,0,1:T(8,128)(2,1)S(1)} fusion(bf16[128,128,256]{2,1,0:T(8,128)(2,1)} %get-tuple-element.362, s32[64]{0:T(128)S(1)} %dynamic_slice.61), kind=kOutput, calls=%fused_computation.5.clone.1 | convolution fusion | flops 536879104 | bytes 12583168 | tf_op jit(solution)/shard_map/while/body/eval_jaxpr/gs,stf->gtf/dot_general | solution.py:25
  100.8 0.0 copy-done.2
  100.8 3.0 subtract_convert_fusion.4
  103.8 3.3 fusion.79
  107.1 8.9 %select_add_fusion.4 = f32[64,128,256]{2,0,1:T(8,128)} fusion(f32[64,128,256]{2,0,1:T(8,128)} %get-tuple-element.344, f32[64,128,256]{2,0,1:T(8,128)S(1)} %fusion.79, pred[]{:T(512)S(6)} %compare.6, bf16[64,128,256]{2,1,0:T(8,128)(2,1)S(1)} %get-tuple-element.320, s32[64]{0:T(128)S(1)} %dynamic_slice.62, pred[64]{0:T(512)(128)(4,1)S(1)} %dynamic_slice.63), kind=kOutput, calls=%fused_computation.7.clone.1 | convolution fusion | flops 274735104 | bytes 29360448 | tf_op jit(solution)/shard_map/while/body/eval_jaxpr/go,gif->oif/dot_general | solution.py:34
  128.9 9.8 %copy.49 = bf16[64,128,256]{2,1,0:T(8,128)(2,1)} copy(f32[64,128,256]{2,0,1:T(8,128)} %get-tuple-element.107) | data formatting | bytes 12582912 | tf_op jit(solution)/shard_map/while | solution.py:42
  138.7 0.0 reduce-scatter.3.cloned.1.call-update
  138.7 0.0 all-gather.5.cloned.1.call-start
  138.8 85.7 %reduce-scatter.3.cloned.1.call-done = bf16[1024,256]{1,0:T(8,128)(2,1)} async-done(((bf16[8192,256]{1,0:T(8,128)(2,1)}), bf16[1024,256]{1,0:T(8,128)(2,1)}) %reduce-scatter.3.cloned.1.call-update) | async-done | bytes 524304 | tf_op jit(solution)/shard_map/reduce_scatter | solution.py:75
  224.5 0.0 copy-done
  224.5 2.5 multiply_convert_fusion
  227.0 1.1 convolution_convert_fusion
  228.1 0.0 all-gather.5.cloned.1.call-update
  228.1 0.0 all-reduce.2.cloned.1.call-start
  228.2 0.0 copy-start.6
  228.2 0.0 copy-start.7
  228.2 6.5 %copy.21 = bf16[1,1,128,128,128]{3,4,2,1,0:T(8,128)(2,1)} copy(bf16[1,1,128,128,128]{4,3,2,1,0:T(8,128)(2,1)} %bitcast.51) | data formatting | bytes 8388608 | tf_op args[3]
  234.7 1.0 fusion.49
  235.7 0.0 all-reduce.2.cloned.1.call-update
  235.7 0.0 reduce-scatter.5.cloned.1.call-start
  235.8 62.9 %all-gather.5.cloned.1.call-done = bf16[8192,256]{1,0:T(8,128)(2,1)} async-done(((bf16[1024,256]{1,0:T(8,128)(2,1)}), bf16[8192,256]{1,0:T(8,128)(2,1)}) %all-gather.5.cloned.1.call-update) | async-done | bytes 4194320 | tf_op jit(solution)/shard_map/all_gather | solution.py:83
  298.7 0.0 copy-done.7
  298.7 83.2 %while.23 = (s32[]{:T(128)}, f32[128,128,256]{2,0,1:T(8,128)}, s32[2]{0:T(128)S(1)}, s32[128]{0:T(128)S(1)}, pred[128]{0:T(512)(128)(4,1)S(1)}, /*index=5*/bf16[...) while((s32[]{:T(128)}, f32[128,128,256]{2,0,1:T(8,128)}, ...), condition=%wide.region_5.6_spmd.clone, body=%wide.region_4.5_spmd.clone.sunk | while | flops 1900056576 | bytes 115345640 | solution.py:42
  298.7 0.6 dynamic_slice.65
  299.9 0.1 dynamic_slice.68
  300.0 0.1 dynamic_slice.67
  300.1 0.1 dynamic_slice.66
  300.2 5.6 %fusion.86 = bf16[64,128,256]{2,0,1:T(8,128)(2,1)S(1)} fusion(bf16[64,128,256]{2,1,0:T(8,128)(2,1)} %get-tuple-element.398, s32[64]{0:T(128)S(1)} %dynamic_slice.66), kind=kOutput, calls=%fused_computation.30.clone.1 | convolution fusion | flops 268439552 | bytes 8388864 | tf_op jit(solution)/shard_map/while/body/eval_jaxpr/gs,stf->gtf/dot_general | solution.py:25
  305.8 4.9 subtract_convert_fusion.5
  310.7 9.0 %fusion.87 = f32[128,128,256]{2,0,1:T(8,128)} fusion(bf16[64,128,256]{2,1,0:T(8,128)(2,1)S(1)} %get-tuple-element.329, s32[64]{0:T(128)S(1)} %dynamic_slice.67, pred[64]{0:T(512)(128)(4,1)S(1)} %dynamic_slice.68), kind=kOutput, calls=%fused_computation.33.clone.1 | convolution fusion | flops 536887296 | bytes 20971840 | tf_op jit(solution)/shard_map/while/body/eval_jaxpr/go,gif->oif/dot_general | solution.py:34
  319.7 18.2 %select_add_fusion.5 = f32[128,128,256]{2,0,1:T(8,128)} fusion(f32[128,128,256]{2,0,1:T(8,128)} %get-tuple-element.380, f32[128,128,256]{2,0,1:T(8,128)} %fusion.87, pred[]{:T(512)S(6)} %compare.7, bf16[64,128,256]{2,1,0:T(8,128)(2,1)} %get-tuple-element.330, s32[64]{0:T(128)S(1)} %dynamic_slice.67, pred[64]{0:T(512)(128)(4,1)S(1)} %dynamic_slice.68), kind=kOutput, calls=%fused_computation.26.clone.1 | convolution fusion | flops 549470208 | bytes 54526272 | tf_op jit(solution)/shard_map/while/body/eval_jaxpr/go,gif->oif/dot_general | solution.py:37
  337.9 0.6 dynamic_slice.65
  339.2 0.1 dynamic_slice.68
  339.2 0.1 dynamic_slice.67
  339.3 0.1 dynamic_slice.66
  339.4 5.6 %fusion.86 = bf16[64,128,256]{2,0,1:T(8,128)(2,1)S(1)} fusion(bf16[64,128,256]{2,1,0:T(8,128)(2,1)} %get-tuple-element.398, s32[64]{0:T(128)S(1)} %dynamic_slice.66), kind=kOutput, calls=%fused_computation.30.clone.1 | convolution fusion | flops 268439552 | bytes 8388864 | tf_op jit(solution)/shard_map/while/body/eval_jaxpr/gs,stf->gtf/dot_general | solution.py:25
  345.0 4.9 subtract_convert_fusion.5
  349.9 9.0 %fusion.87 = f32[128,128,256]{2,0,1:T(8,128)} fusion(bf16[64,128,256]{2,1,0:T(8,128)(2,1)S(1)} %get-tuple-element.329, s32[64]{0:T(128)S(1)} %dynamic_slice.67, pred[64]{0:T(512)(128)(4,1)S(1)} %dynamic_slice.68), kind=kOutput, calls=%fused_computation.33.clone.1 | convolution fusion | flops 536887296 | bytes 20971840 | tf_op jit(solution)/shard_map/while/body/eval_jaxpr/go,gif->oif/dot_general | solution.py:34
  359.0 22.9 %select_add_fusion.5 = f32[128,128,256]{2,0,1:T(8,128)} fusion(f32[128,128,256]{2,0,1:T(8,128)} %get-tuple-element.380, f32[128,128,256]{2,0,1:T(8,128)} %fusion.87, pred[]{:T(512)S(6)} %compare.7, bf16[64,128,256]{2,1,0:T(8,128)(2,1)} %get-tuple-element.330, s32[64]{0:T(128)S(1)} %dynamic_slice.67, pred[64]{0:T(512)(128)(4,1)S(1)} %dynamic_slice.68), kind=kOutput, calls=%fused_computation.26.clone.1 | convolution fusion | flops 549470208 | bytes 54526272 | tf_op jit(solution)/shard_map/while/body/eval_jaxpr/go,gif->oif/dot_general | solution.py:37
  381.9 9.0 %convert_element_type.58 = bf16[128,128,256]{2,0,1:T(8,128)(2,1)} convert(f32[128,128,256]{2,0,1:T(8,128)} %get-tuple-element.108) | non-fusion elementwise | flops 4194304 | bytes 25165824 | tf_op jit(solution)/shard_map/convert_element_type | solution.py:95
  390.9 11.4 %copy.24 = bf16[128,128,256]{2,1,0:T(8,128)(2,1)} copy(bf16[128,128,256]{2,0,1:T(8,128)(2,1)} %convert_element_type.58) | data formatting | bytes 16777216 | tf_op jit(solution)/shard_map/convert_element_type | solution.py:95
  402.3 0.0 reduce-scatter.5.cloned.1.call-update
  402.4 42.0 %all-reduce.2.cloned.1.call-done = f32[256,256]{1,0:T(8,128)} async-done(((f32[256,256]{1,0:T(8,128)}), f32[256,256]{1,0:T(8,128)}) %all-reduce.2.cloned.1.call-update) | async-done | bytes 262160 | tf_op jit(solution)/shard_map/psum | solution.py:88
  444.4 1.7 broadcast_multiply_fusion
  446.0 96.1 %reduce-scatter.5.cloned.1.call-done = bf16[1024,256]{1,0:T(8,128)(2,1)} async-done(((bf16[16384,256]{1,0:T(8,128)(2,1)}), bf16[1024,256]{1,0:T(8,128)(2,1)}) %reduce-scatter.5.cloned.1.call-update) | async-done | bytes 524304 | tf_op jit(solution)/shard_map/reduce_scatter | solution.py:94
  (18 shorter events, 0.0 us)
Async XLA Ops:
  7.2 217.3 %copy-start = (bf16[256,256]{1,0:T(8,128)(2,1)S(1)}, bf16[256,256]{1,0:T(8,128)(2,1)}, u32[]{:S(2)}) copy-start(bf16[256,256]{1,0:T(8,128)(2,1)} %param.12) | copy-start | bytes 393220
  7.2 57.1 %all-gather.3.cloned.1.call-start = ((), (), s32[]{:S(2)}) async-start(), calls=%async_computation.2 | async-start | bytes 8912896 | tf_op jit(solution)/shard_map/all_gather | solution.py:69
  7.9 216.6 %reduce-scatter.3.cloned.1.call-start = ((), (), s32[]{:S(2)}) async-start(), calls=%async_computation.3 | async-start | bytes 4718592 | tf_op jit(solution)/shard_map/reduce_scatter | solution.py:75
  67.1 9.0 %copy-start.2 = (bf16[128,128,128]{2,1,0:T(8,128)(2,1)S(1)}, bf16[128,128,128]{2,1,0:T(8,128)(2,1)}, u32[]{:S(2)}) copy-start(bf16[128,128,128]{2,1,0:T(8,128)(2,1)} %get-tuple-element.360) | copy-start | bytes 12582916 | tf_op jit(solution)/shard_map/while
  91.8 9.0 %copy-start.2 = (bf16[128,128,128]{2,1,0:T(8,128)(2,1)S(1)}, bf16[128,128,128]{2,1,0:T(8,128)(2,1)}, u32[]{:S(2)}) copy-start(bf16[128,128,128]{2,1,0:T(8,128)(2,1)} %get-tuple-element.360) | copy-start | bytes 12582916 | tf_op jit(solution)/shard_map/while
  138.7 85.8 %copy-start.5 = (bf16[1024,256]{1,0:T(8,128)(2,1)S(1)}, bf16[1024,256]{1,0:T(8,128)(2,1)}, u32[]{:S(2)}) copy-start(bf16[1024,256]{1,0:T(8,128)(2,1)} %param.13) | copy-start | bytes 1572868
  138.7 160.0 %all-gather.5.cloned.1.call-start = ((), (), s32[]{:S(2)}) async-start(), calls=%async_computation.5 | async-start | bytes 4718592 | tf_op jit(solution)/shard_map/all_gather | solution.py:83
  228.1 216.2 %all-reduce.2.cloned.1.call-start = ((), (), s32[]{:S(2)}) async-start(), calls=%async_computation.4 | async-start | bytes 524288 | tf_op jit(solution)/shard_map/psum | solution.py:88
  228.2 6.5 %copy-start.4 = (bf16[1024,256]{1,0:T(8,128)(2,1)S(1)}, bf16[1024,256]{1,0:T(8,128)(2,1)}, u32[]{:S(2)}) copy-start(bf16[1024,256]{1,0:T(8,128)(2,1)} %reduce-scatter.3.cloned.1.call-done) | copy-start | bytes 1572868
  228.2 70.5 %copy-start.6 = (s32[128]{0:T(128)S(1)}, s32[128]{0:T(128)}, u32[]{:S(2)}) copy-start(s32[128]{0:T(128)} %get-tuple-element.424) | copy-start | bytes 1540
  228.2 70.5 %copy-start.7 = (s32[128]{0:T(128)S(1)}, s32[128]{0:T(128)}, u32[]{:S(2)}) copy-start(s32[128]{0:T(128)} %get-tuple-element.425) | copy-start | bytes 1540
  235.7 306.4 %reduce-scatter.5.cloned.1.call-start = ((), (), s32[]{:S(2)}) async-start(), calls=%async_computation.6 | async-start | bytes 8912896 | tf_op jit(solution)/shard_map/reduce_scatter | solution.py:94
  300.2 5.6 %copy-start.3 = (bf16[128,128,128]{1,2,0:T(8,128)(2,1)S(1)}, bf16[128,128,128]{1,2,0:T(8,128)(2,1)}, u32[]{:S(2)}) copy-start(bf16[128,128,128]{1,2,0:T(8,128)(2,1)} %get-tuple-element.396) | copy-start | bytes 12582916 | tf_op jit(solution)/shard_map/while
  339.4 5.6 %copy-start.3 = (bf16[128,128,128]{1,2,0:T(8,128)(2,1)S(1)}, bf16[128,128,128]{1,2,0:T(8,128)(2,1)}, u32[]{:S(2)}) copy-start(bf16[128,128,128]{1,2,0:T(8,128)(2,1)} %get-tuple-element.396) | copy-start | bytes 12582916 | tf_op jit(solution)/shard_map/while
  402.3 139.9 %copy-start.1 = (bf16[256,256]{1,0:T(8,128)(2,1)S(1)}, bf16[256,256]{1,0:T(8,128)(2,1)}, u32[]{:S(2)}) copy-start(bf16[256,256]{1,0:T(8,128)(2,1)} %param.12) | copy-start | bytes 393220
Sparse Core Ops, SparseCore 0:
  9.7 54.5 all-gather.2
  138.8 85.6 reduce-scatter.2
  228.2 70.4 all-gather.4
  304.6 139.7 all-reduce.1
  447.3 94.8 reduce-scatter.4
where the time goes:
time: 558 us; the launch traced here: 549 us
  waiting for transfers between devices  343 us (61%)
  matrix products  131 us (23%)
  local copies, waits for them, and re-layouts  33.5 us (6%)
  loops' own time  15.6 us (3%)
  between operations  14.9 us (3%)
  other arithmetic  10.7 us (2%)
    reduce_scatter x1, waiting for transfers between devices, body(): lax.psum_scatter(adjoint_part.astype(jnp.bfloat16), 'gr', scatter_dimensi...  96.1 us
    reduce_scatter x1, waiting for transfers between devices, body(): lax.psum_scatter(partial_value.astype(jnp.bfloat16), 'gc', scatter_dimens...  85.7 us
    all_gather x1, waiting for transfers between devices, body(): row_grads = lax.all_gather(grad_mixed, 'gc', axis=0, tiled=True)  62.9 us
    all_gather x1, waiting for transfers between devices, body(): column_feats = lax.all_gather(features, 'gr', axis=0, tiled=True)  55.7 us
    dot_general x4, matrix products, one_group(): jnp.einsum('go,gif->oif', target_hot, low_part, preferred_element_type=jn...  47.7 us
    psum x1, waiting for transfers between devices, body(): lax.psum(local_wgrad, ('gr', 'gc')) * (1.0 / math.sqrt(node_total))  42 us
    dot_general x4, matrix products, one_group(): jnp.einsum('go,gif->oif', target_hot, high_part, preferred_element_type=j...  33.7 us
    dot_general x4, matrix products, one_group(): jnp.einsum('gs,stf->gtf', source_hot, source_blocks, preferred_element_ty...  29.2 us
  transfers between devices with their start and end apart: 5, of which 5 were waited for; matrix products, arithmetic and copies ran while one was open for 20% of the time, Pallas kernels for 0%

commit v1 on v0

v1 whole, which is shorter than its diff:
```python
import functools
import math

import jax
import jax.numpy as jnp
from jax import lax
from jax.experimental import pallas as pl
from jax.experimental.pallas import tpu as pltpu
from jax.sharding import PartitionSpec as P

AXES = ("gr", "gc")
TILE = 128
CUTS = ((0, 5), (5, 11), (11, 16))
EXTRA = 2
GROUP = 8
LOAD = 8
PASS_VMEM = 40
F32 = jnp.float32
BF16 = jnp.bfloat16


def split_place(index):
    row, col = divmod(index, 8)
    y, rest = divmod(row, 4)
    xl, core = divmod(rest, 2)
    xh, z = divmod(col, 4)
    return y, xl, core, xh, z


def join_place(y, xl, core, xh, z):
    return ((y % 4) * 4 + (xl % 2) * 2 + core % 2) * 8 + (xh % 2) * 4 + z % 4


def move(value, y=0, xl=0, core=0, xh=0, z=0):
    masks = (y, xl, core, xh, z)
    pairs = []
    for index in range(128):
        at = split_place(index)
        pairs.append((index, join_place(*(a ^ b for a, b in zip(at, masks)))))
    return lax.ppermute(value, AXES, pairs)


def link_orders(ring, pair):
    near, far, other = (1, 0), (3, 0), (0, 1)
    orders = ((other, near, far), (near, far, other), (far, other, near))
    return [[({ring: r, pair: p}, r * 2 + p) for r, p in order] for order in orders]


def places(order):
    marks = [mark for _, mark in order]
    return [
        (marks[0] if p & 1 else 0) ^ (marks[1] if p & 2 else 0) ^ (marks[2] if p & 4 else 0)
        for p in range(8)
    ]


GR_LINKS = link_orders("y", "xl")
GC_LINKS = link_orders("z", "xh")


def after(value, *earlier):
    return lax.optimization_barrier((value,) + earlier)[0]


def spread(thirds, links, side=None, extra=0):
    held = [[third] for third in thirds]
    if extra:
        held[0], extra_sum = [thirds[0][:-extra]], thirds[0][-extra:]
    for step in range(3):
        sent = [parts[0] if len(parts) == 1 else jnp.concatenate(parts) for parts in held]
        if extra:
            sent[0] = jnp.concatenate(held[0] + [extra_sum]) if step else thirds[0]
        if side is not None:
            side(step, sent)
        got = [move(value, **order[step][0]) for value, order in zip(sent, links)]
        held = [parts + [value] for parts, value in zip(held, got)]
        if extra:
            held[0][-1] = got[0][:-extra]
            extra_sum = add_all(extra_sum, got[0][-extra:])
    return [array for pair in zip(sent, got) for array in pair]


def add_all(*terms):
    total = terms[0].astype(F32)
    for term in terms[1:]:
        total = total + term.astype(F32)
    return total.astype(BF16)


def collect(parts, links, extra=0):
    held = [[part] for part in parts[0::2]]
    sent = list(parts[1::2])
    extra_sum = sent[0][-extra:]
    for step in range(3):
        got = [move(value, **order[2 - step][0]) for value, order in zip(sent, links)]
        if extra:
            extra_sum = add_all(extra_sum, got[0][-extra:])
            got[0] = got[0][:-extra]
        held = [terms + [value] for terms, value in zip(held, got)]
        if step < 2:
            half = [terms[0].shape[0] // 2 for terms in held]
            sent = [add_all(*[t[h:] for t in terms]) for terms, h in zip(held, half)]
            held = [[t[:h] for t in terms] for terms, h in zip(held, half)]
            if extra:
                sent[0] = jnp.concatenate([sent[0], extra_sum])
    total = jnp.concatenate([add_all(*terms) for terms in held])
    return (total, extra_sum) if extra else total


def vmem_spec():
    return pl.BlockSpec(memory_space=pltpu.VMEM)


def smem_spec():
    return pl.BlockSpec(memory_space=pltpu.SMEM)


def any_spec():
    return pl.BlockSpec(memory_space=pl.ANY)


def hbm_spec():
    return pl.BlockSpec(memory_space=pltpu.HBM)


def cost(flops, moved):
    return pl.CostEstimate(flops=flops, bytes_accessed=moved, transcendentals=0)


def third_shapes(pieces=1, extra=0):
    counts = [pieces * (hi - lo) for lo, hi in CUTS]
    counts[0] += extra
    return [jax.ShapeDtypeStruct((count, TILE, TILE), BF16) for count in counts]


def third_of(tile):
    return next((at, tile - lo) for at, (lo, hi) in enumerate(CUTS) if lo <= tile < hi)


def turn_kernel(core_ref, own_ref, sib_ref, *out_refs):
    lanes = pl.ds(pl.multiple_of(core_ref[0] * TILE, TILE), TILE)
    for half, ref in enumerate((own_ref, sib_ref)):
        for tile in range(8):
            third, at = third_of(half * 8 + tile)
            out_refs[third][at] = ref[tile * TILE : (tile + 1) * TILE, lanes].T


def turn_in(core, own, sib):
    return pl.pallas_call(
        turn_kernel,
        out_shape=third_shapes(),
        in_specs=[smem_spec(), vmem_spec(), vmem_spec()],
        out_specs=[vmem_spec()] * 3,
        compiler_params=pltpu.CompilerParams(vmem_limit_bytes=8 << 20),
        cost_estimate=cost(0, 2 << 20),
        name="turn_in",
    )(core, own, sib)


def third_rows(links):
    rows = [[] for _ in range(6)]
    for third, (order, (lo, hi)) in enumerate(zip(links, CUTS)):
        for p, mark in enumerate(places(order)):
            rows[2 * third + p // 4].append(((p % 4) * (hi - lo), mark * 16 + lo, hi - lo))
    return rows


def array_place(ids):
    mark, tile = ids // 16, ids % 16
    turn, other = mark // 2, mark % 2
    near = ((turn == 1) | (turn == 2)).astype(jnp.int32)
    far = (turn >= 2).astype(jnp.int32)
    bits = ((other, near, far), (near, far, other), (far, other, near))
    array, row = jnp.zeros_like(ids), jnp.zeros_like(ids)
    for third, ((lo, hi), (a, b, c)) in enumerate(zip(CUTS, bits)):
        here = (tile >= lo) & (tile < hi)
        array = jnp.where(here, 2 * third + c, array)
        row = jnp.where(here, (a + 2 * b) * (hi - lo) + tile - lo, row)
    return array, row


def order_slots(array, row, target, dead):
    key = jnp.where(dead, 6, array).reshape(-1)
    count = key.shape[0]
    at = jnp.arange(count, dtype=jnp.int32)
    packed = (row + 32 * target).reshape(-1) + 4096 * at
    ahead = (key[None, :] < key[:, None]) | (
        (key[None, :] == key[:, None]) & (at[None, :] < at[:, None])
    )
    rank = jnp.sum(ahead.astype(jnp.int32), axis=1)
    listed = jnp.sum(jnp.where(rank[None, :] == at[:, None], packed[None, :], 0), axis=1)
    bounds = jnp.sum((key[None, :] < jnp.arange(7, dtype=jnp.int32)[:, None]).astype(jnp.int32), axis=1)
    return listed, bounds


def pass_kernel(adjoint, live_ref, list_ref, bound_ref, own_tiles, sib_tiles, *rest):
    sources, targets = rest[:6], rest[6:12]
    tile_buf, total, tile_sems = rest[12:]
    slots = own_tiles.shape[0]
    lists = (own_tiles, sib_tiles)
    groups = [lax.div(live_ref[side] + (LOAD - 1), LOAD) for side in range(2)]

    def tile_copy(side, group):
        first = pl.multiple_of(group * LOAD, LOAD)
        return pltpu.make_async_copy(
            lists[side].at[pl.ds(first, LOAD)],
            tile_buf.at[pl.ds(side * slots + first, LOAD)],
            tile_sems.at[side, group],
        )

    for side in range(2):
        pl.loop(0, groups[side])(lambda group, side=side: tile_copy(side, group).start())

    @pl.loop(0, total.shape[0] // 3)
    def _(at):
        total[pl.ds(at * 3, 3)] = jnp.zeros((3,) + total.shape[1:], F32)

    for side in range(2):
        pl.loop(0, groups[side])(lambda group, side=side: tile_copy(side, group).wait())

    dims = (((1,), (0,)), ((), ())) if adjoint else (((1,), (1,)), ((), ()))
    for array, source in enumerate(sources):
        first, last = bound_ref[array], bound_ref[array + 1]

        @pl.loop(0, lax.div(last - first + (GROUP - 1), GROUP))
        def _(group, source=source, first=first, last=last):
            products, places_to = [], []
            for step in range(GROUP):
                at = first + group * GROUP + step
                live = at < last
                entry = jnp.where(live, list_ref[jnp.minimum(at, 2 * slots - 1)], 0)
                places_to.append(jnp.where(live, (entry >> 5) & 127, 128))
                products.append(
                    lax.dot_general(
                        source[entry & 31],
                        tile_buf[entry >> 12],
                        dims,
                        preferred_element_type=F32,
                    )
                )
            for to, product in zip(places_to, products):
                total[to] = total[to] + product

    if adjoint:
        first, last = sources[0].shape[0] - EXTRA, sources[0].shape[0]
        extra = sources[0][first:last].astype(F32) + sources[1][first:last].astype(F32)
        targets[1][first:last] = extra.astype(BF16)
    for target, rows in zip(targets, third_rows(GR_LINKS if adjoint else GC_LINKS)):
        for first, at, count in rows:
            for step in range(count):
                target[first + step] = total[at + step].astype(BF16)


def block_pass(adjoint, live, listed, bounds, own_tiles, sib_tiles, sources):
    slots = own_tiles.shape[0]
    out_shape = [shape for shape in third_shapes(4) for _ in range(2)]
    if adjoint:
        out_shape[1] = third_shapes(4, EXTRA)[0]
    return pl.pallas_call(
        functools.partial(pass_kernel, adjoint),
        out_shape=out_shape,
        in_specs=[smem_spec()] * 3 + [any_spec()] * 2 + [vmem_spec()] * 6,
        out_specs=[vmem_spec()] * 6,
        scratch_shapes=[
            pltpu.VMEM((2 * slots, TILE, TILE), BF16),
            pltpu.VMEM((129, TILE, TILE), F32),
            pltpu.SemaphoreType.DMA((2, slots // LOAD)),
        ],
        compiler_params=pltpu.CompilerParams(vmem_limit_bytes=PASS_VMEM << 20),
        cost_estimate=cost(2 * 256 * TILE * TILE * TILE, 24 << 20),
        name="block_adjoint" if adjoint else "block_pass",
    )(live, listed, bounds, own_tiles, sib_tiles, *sources)


def dense_kernel(core_ref, weight_ref, own_cot, sib_cot, own_sums, sib_sums, *rest):
    act_ref, *mixed_refs, mixed_buf, wgrad_ref = rest
    core = core_ref[0]
    own_weight = weight_ref[pl.ds(pl.multiple_of(core * TILE, TILE), TILE), :]
    sib_weight = weight_ref[pl.ds(pl.multiple_of((1 - core) * TILE, TILE), TILE), :]
    wgrad_ref[...] = jnp.zeros(wgrad_ref.shape, F32)
    for half, cot_ref in enumerate((own_cot, sib_cot)):

        @pl.loop(0, 4)
        def _(pair, half=half, cot_ref=cot_ref):
            for step in range(2):
                tile = pair * 2 + step
                rows = pl.ds(pl.multiple_of(tile * TILE, TILE), TILE)
                own = own_sums[half * 8 + tile]
                sib = sib_sums[(1 - half) * 8 + tile]
                pre = jnp.dot(own.T, own_weight, preferred_element_type=F32)
                pre = pre + jnp.dot(sib.T, sib_weight, preferred_element_type=F32)
                sigmoid = jax.nn.sigmoid(pre)
                if half == 0:
                    act_ref[rows, :] = (pre * sigmoid).astype(BF16)
                slope = sigmoid * (1.0 + pre * (1.0 - sigmoid))
                grad = (cot_ref[rows, :].astype(F32) * slope).astype(BF16)
                wgrad_ref[...] += jnp.dot(own, grad, preferred_element_type=F32)
                mixed_buf[half * 8 + tile] = lax.dot_general(
                    own_weight, grad, (((1,), (1,)), ((), ())), preferred_element_type=F32
                ).astype(BF16)

    for ref, (lo, hi) in zip(mixed_refs, CUTS):
        ref[: hi - lo] = mixed_buf[lo:hi]
    for part in range(EXTRA):
        extra = wgrad_ref[:, part * TILE : (part + 1) * TILE]
        mixed_refs[0][CUTS[0][1] + part] = extra.astype(BF16)


def dense(core, weight, own_cot, sib_cot, own_sums, sib_sums):
    outs = pl.pallas_call(
        dense_kernel,
        out_shape=[
            jax.ShapeDtypeStruct(own_cot.shape, BF16),
        ]
        + third_shapes(1, EXTRA),
        in_specs=[smem_spec()] + [vmem_spec()] * 5,
        out_specs=[vmem_spec()] * 4,
        scratch_shapes=[
            pltpu.VMEM((16, TILE, TILE), BF16),
            pltpu.VMEM((TILE, EXTRA * TILE), F32),
        ],
        compiler_params=pltpu.CompilerParams(vmem_limit_bytes=24 << 20),
        cost_estimate=cost(2 * 2048 * 256 * 512, 4 << 20),
        name="dense",
    )(core, weight, own_cot, sib_cot, own_sums, sib_sums)
    return outs[0], outs[1:]


def back_kernel(core_ref, own_ref, sib_ref, out_ref):
    core = core_ref[0]
    for ref, half in ((own_ref, core), (sib_ref, 1 - core)):
        lanes = pl.ds(pl.multiple_of(half * TILE, TILE), TILE)
        for tile in range(8):
            out_ref[tile * TILE : (tile + 1) * TILE, lanes] = ref[tile].T


def turn_back(core, own_part, sib_part):
    return pl.pallas_call(
        back_kernel,
        out_shape=jax.ShapeDtypeStruct((8 * TILE, 2 * TILE), BF16),
        in_specs=[smem_spec()] + [vmem_spec()] * 2,
        out_specs=vmem_spec(),
        compiler_params=pltpu.CompilerParams(vmem_limit_bytes=8 << 20),
        cost_estimate=cost(0, 1 << 20),
        name="turn_back",
    )(core, own_part, sib_part)


def body(features, weight, cotangent, blocks, block_row, block_col, counts):
    row_at, col_at = lax.axis_index("gr"), lax.axis_index("gc")
    y, xl, core = row_at // 4, (row_at // 2) % 2, row_at % 2
    xh, z = col_at // 4, col_at % 4
    core_arg = core.reshape(1).astype(jnp.int32)

    sib_feats = move(features, core=1)
    slices = turn_in(core_arg, features, sib_feats)

    own_tiles = blocks[0, 0]
    slots = own_tiles.shape[0]
    fetched = []

    def fetch(step, sent):
        if step == 1:
            sent = sent[:1]
            live = jnp.broadcast_to(after(counts[0, 0], *sent), (slots,))
            rows, cols = after(block_row[0, 0], *sent), after(block_col[0, 0], *sent)
            lists = jnp.stack([rows, cols, live])
            fetched.extend([lists, move(lists, core=1)])
        if step == 2:
            fetched.append(move(after(cotangent, *sent), core=1))

    gathered = spread(slices, GR_LINKS, fetch)
    own_lists, sib_lists, sib_cot = fetched
    sib_tiles = move(after(own_tiles, slices[0]), core=1)
    lists = jnp.stack([own_lists, sib_lists], axis=1)
    rows, cols, live = lists[0], lists[1], lists[2, :, 0]
    side = jnp.arange(2, dtype=jnp.int32)[:, None]
    part = rows // 8
    row_ids = (((part % 4) ^ z) * 2 + ((part // 4) ^ xh)) * 16 + side * 8 + rows % 8
    part = cols // 8
    col_ids = ((part // 4) ^ y) * 32 + (((part // 2) % 2) ^ xl) * 16
    col_ids = col_ids + ((part % 2) ^ core) * 8 + cols % 8
    dead = jnp.arange(slots, dtype=jnp.int32)[None, :] >= live[:, None]
    by_col = order_slots(*array_place(col_ids), row_ids, dead)
    by_col = (after(by_col[0], sib_cot), by_col[1])
    by_row = order_slots(*array_place(row_ids), col_ids, dead)

    parts = block_pass(False, live, *by_col, own_tiles, sib_tiles, gathered)
    own_sums = collect(parts, GC_LINKS)
    sib_sums = move(own_sums, core=1)

    activations, mixed = dense(core_arg, weight, cotangent, sib_cot, own_sums, sib_sums)

    gathered = spread(mixed, GC_LINKS, extra=EXTRA)
    parts = block_pass(True, live, *by_row, own_tiles, sib_tiles, gathered)
    grads, wgrad = collect(parts, GR_LINKS, EXTRA)
    last = move(jnp.concatenate([grads[8:], wgrad]), core=1)
    feature_grad = turn_back(core_arg, grads[:8], last)

    node_total = features.shape[0] * lax.axis_size("gr") * lax.axis_size("gc")
    halves = [jnp.concatenate([part[-2], part[-1]], axis=1).astype(F32) for part in (wgrad, last)]
    weight_grad = jnp.where(core == 0, jnp.concatenate(halves), jnp.concatenate(halves[::-1]))
    weight_grad = weight_grad * (1.0 / math.sqrt(node_total))
    return (activations, weight_grad, feature_grad)


def solution(mesh):
    return jax.shard_map(
        body,
        mesh=mesh,
        in_specs=(
            P(("gr", "gc"), None),
            P(),
            P(("gr", "gc"), None),
            P("gr", "gc", None, None, None),
            P("gr", "gc", None),
            P("gr", "gc", None),
            P("gr", "gc"),
        ),
        out_specs=(P(("gr", "gc"), None), P(), P(("gr", "gc"), None)),
        check_vma=False,
    )
```

time: 558 us -> 200 us (0.36); the launches traced: 549 us -> 201 us
  waiting for transfers between devices: 343 us -> 113 us
  matrix products: 131 us -> 0 us
  starting transfers between devices: 0.2 us -> 52.4 us
  local copies, waits for them, and re-layouts: 33.5 us -> 1.7 us
  Pallas kernels: 0 us -> 20.5 us
  loops' own time: 15.6 us -> 0 us
  between operations: 14.9 us -> 1.83 us
    reduce_scatter x2 -> x0, waiting for transfers between devices: 182 us -> none  [the longest x1 96.1 us: body(): lax.psum_scatter(adjoint_part.astype(jnp.bfloat16), 'gr', scatter_dimensi...]
    dot_general x19 -> x0, matrix products: 131 us -> none  [the longest x4 47.7 us: one_group(): jnp.einsum('go,gif->oif', target_hot, low_part, preferred_element_type=jn...]
    all_gather x2 -> x0, waiting for transfers between devices: 119 us -> none  [the longest x1 62.9 us: body(): row_grads = lax.all_gather(grad_mixed, 'gc', axis=0, tiled=True)]
    ppermute x0 -> x42, waiting for transfers between devices: none -> 113 us  [move(): return lax.ppermute(value, AXES, pairs)]
    ppermute x0 -> x42, starting transfers between devices: none -> 52.4 us  [move(): return lax.ppermute(value, AXES, pairs)]
    psum x1 -> x0, waiting for transfers between devices: 42 us -> none  [body(): lax.psum(local_wgrad, ('gr', 'gc')) * (1.0 / math.sqrt(node_total))]
    pallas_call x0 -> x5, Pallas kernels: none -> 20.5 us  [the longest x2 15 us: block_pass(): pl.pallas_call(functools.partial(pass_kernel, adjoint), out_shape=out_sha...]
    another operation x2 -> x0, loops' own time: 15.6 us -> none  [block_pass(): lax.scan(one_group, jnp.zeros((out_tiles, tile_stack.shape[-1], source_bl...]
  transfers between devices with their start and end apart: 5 -> 42, of which waited for: 5 -> 30; matrix products, arithmetic and copies ran while one was open for 20% -> 5% of each run, Pallas kernels for 0% -> 0%
where the time goes in v1:
time: 200 us; the launch traced here: 201 us
  waiting for transfers between devices  113 us (56%)
  starting transfers between devices  52.4 us (26%)
  Pallas kernels  20.5 us (10%)
  other arithmetic  11.3 us (6%)
    ppermute x42, waiting for transfers between devices, move(): return lax.ppermute(value, AXES, pairs)  113 us
    ppermute x42, starting transfers between devices, move(): return lax.ppermute(value, AXES, pairs)  52.4 us
    pallas_call x2, Pallas kernels, block_pass(): pl.pallas_call(functools.partial(pass_kernel, adjoint), out_shape=out_sha...  15 us
    convert_element_type x23, other arithmetic, add_all(): return total.astype(BF16)  8.17 us
    pallas_call x1, Pallas kernels, dense(): pl.pallas_call(dense_kernel, out_shape=[jax.ShapeDtypeStruct(own_cot.shap...  4.4 us
  transfers between devices with their start and end apart: 42, of which 30 were waited for; matrix products, arithmetic and copies ran while one was open for 5% of the time, Pallas kernels for 0%

profile of v1, /device:TPU:0, one launch (start us, length us, event | category | flops | bytes accessed | tf_op | source)
XLA Modules:
  0.0 200.9 jit_solution(14249460839809344293)
XLA Ops:
  0.7 2.1 %collective-permute-done.sib_ref = bf16[1024,256]{1,0:T(8,128)(2,1)S(1)} collective-permute-done((bf16[1024,256]{1,0:T(8,128)(2,1)}, bf16[1024,256]{1,0:T(8,128)(2,1)S(1)}, u32[]{:S(2)}, u32[]{:S(2)}) %collective-permute-start) | collective-permute-done | bytes 524320 | tf_op jit(solution)/shard_map/ppermute | solution.py:40
  2.8 1.0 copy-done.2
  5.0 1.7 collective-permute-start.1
  6.7 1.6 collective-permute-start.3
  8.3 2.3 %collective-permute-start.5 = (bf16[5,128,128]{2,1,0:T(8,128)(2,1)S(1)}, bf16[5,128,128]{2,1,0:T(8,128)(2,1)S(1)}, u32[]{:S(2)}, u32[]{:S(2)}) collective-permute-start(bf16[5,128,128]{2,1,0:T(8,128)(2,1)S(1)} %get-tuple-element.30), channel_id=1, source_target_pairs={{0,96},{1,97},{2,98},{3,99},{4,100},{5,101},{6,102},{7,103},{8,104... | collective-permute-start | bytes 491528 | tf_op jit(solution)/shard_map/ppermute | solution.py:40
  10.6 1.0 collective-permute-done.1
  11.7 1.7 collective-permute-start.2
  13.4 0.7 fusion.39
  14.1 1.3 collective-permute-done.5
  15.5 0.6 collective-permute-start.6
  16.4 2.3 %collective-permute-start.4 = (bf16[12,128,128]{2,1,0:T(8,128)(2,1)S(1)}, bf16[12,128,128]{2,1,0:T(8,128)(2,1)S(1)}, u32[]{:S(2)}, u32[]{:S(2)}) collective-permute-start(bf16[12,128,128]{2,1,0:T(8,128)(2,1)S(1)} %pad_maximum_fusion.2), channel_id=1, source_target_pairs={{0,96},{1,97},{2,98},{3,99},{4,100},{5,101},{6,102},{7,103},{8,104... | collective-permute-start | bytes 1179656 | tf_op jit(solution)/shard_map/ppermute | solution.py:40
  18.8 5.6 %collective-permute-done.6 = bf16[10,128,128]{2,1,0:T(8,128)(2,1)S(1)} collective-permute-done((bf16[10,128,128]{2,1,0:T(8,128)(2,1)S(1)}, bf16[10,128,128]{2,1,0:T(8,128)(2,1)S(1)}, u32[]{:S(2)}, u32[]{:S(2)}) %collective-permute-start.6) | collective-permute-done | bytes 327712 | tf_op jit(solution)/shard_map/ppermute | solution.py:40
  24.9 3.2 %collective-permute-start.10 = (bf16[20,128,128]{2,1,0:T(8,128)(2,1)S(1)}, bf16[20,128,128]{2,1,0:T(8,128)(2,1)S(1)}, u32[]{:S(2)}, u32[]{:S(2)}) collective-permute-start(bf16[20,128,128]{2,1,0:T(8,128)(2,1)S(1)} %constant_dynamic-update-slice_fusion.2.rest_0_), channel_id=1, source_target_pairs={{0,96},{1,97},{2,98},{3,99},{4,100},{5,101},{6,102},{7,103},{8,104... | collective-permute-start | bytes 1966088 | tf_op jit(solution)/shard_map/ppermute | solution.py:40
  28.1 0.6 collective-permute-done.4
  28.8 1.0 collective-permute-start.11
  30.4 1.4 collective-permute-done.7.sib_cot
  31.8 7.7 %collective-permute-done.12.rest_5_ = bf16[20,128,128]{2,1,0:T(8,128)(2,1)S(1)} collective-permute-done((bf16[20,128,128]{2,1,0:T(8,128)(2,1)S(1)}, bf16[20,128,128]{2,1,0:T(8,128)(2,1)S(1)}, u32[]{:S(2)}, u32[]{:S(2)}) %collective-permute-start.12) | collective-permute-done | bytes 655392 | tf_op jit(solution)/shard_map/ppermute | solution.py:40
  39.5 3.1 %collective-permute-done.10.rest_1_ = bf16[20,128,128]{2,1,0:T(8,128)(2,1)S(1)} collective-permute-done((bf16[20,128,128]{2,1,0:T(8,128)(2,1)S(1)}, bf16[20,128,128]{2,1,0:T(8,128)(2,1)S(1)}, u32[]{:S(2)}, u32[]{:S(2)}) %collective-permute-start.10) | collective-permute-done | bytes 655392 | tf_op jit(solution)/shard_map/ppermute | solution.py:40
  42.6 4.5 %collective-permute-done.11.rest_3_ = bf16[24,128,128]{2,1,0:T(8,128)(2,1)S(1)} collective-permute-done((bf16[24,128,128]{2,1,0:T(8,128)(2,1)S(1)}, bf16[24,128,128]{2,1,0:T(8,128)(2,1)S(1)}, u32[]{:S(2)}, u32[]{:S(2)}) %collective-permute-start.11) | collective-permute-done | bytes 786464 | tf_op jit(solution)/shard_map/ppermute | solution.py:40
  47.1 8.4 %block_pass.1 = (bf16[20,128,128]{2,1,0:T(8,128)(2,1)S(1)}, bf16[20,128,128]{2,1,0:T(8,128)(2,1)S(1)}, bf16[24,128,128]{2,1,0:T(8,128)(2,1)S(1)}, bf16[24,128,12...) custom-call(s32[2]{0:T(128)S(1)} %add_reduce_fusion.live_ref, ...), custom_call_target="tpu_custom_call" | custom-call | flops 1073741824 | bytes 25165824 | tf_op jit(solution)/shard_map/block_pass/pallas_call | solution.py:259
  55.5 3.4 %collective-permute-start.13 = (bf16[20,128,128]{2,1,0:T(8,128)(2,1)S(1)}, bf16[20,128,128]{2,1,0:T(8,128)(2,1)S(1)}, u32[]{:S(2)}, u32[]{:S(2)}) collective-permute-start(bf16[20,128,128]{2,1,0:T(8,128)(2,1)S(1)} %get-tuple-element.38), channel_id=1, source_target_pairs={{0,3},{1,2},{2,1},{3,0},{4,7},{5,6},{6,5},{7,4},{8,11},{9,10},{10,... | collective-permute-start | bytes 1966088 | tf_op jit(solution)/shard_map/ppermute | solution.py:40
  58.9 4.3 %collective-permute-start.16 = (bf16[24,128,128]{2,1,0:T(8,128)(2,1)S(1)}, bf16[24,128,128]{2,1,0:T(8,128)(2,1)S(1)}, u32[]{:S(2)}, u32[]{:S(2)}) collective-permute-start(bf16[24,128,128]{2,1,0:T(8,128)(2,1)S(1)} %get-tuple-element.40), channel_id=1, source_target_pairs={{0,4},{1,5},{2,6},{3,7},{4,0},{5,1},{6,2},{7,3},{8,12},{9,13},{10,... | collective-permute-start | bytes 2359304 | tf_op jit(solution)/shard_map/ppermute | solution.py:40
  63.2 8.3 %collective-permute-done.13 = bf16[20,128,128]{2,1,0:T(8,128)(2,1)S(1)} collective-permute-done((bf16[20,128,128]{2,1,0:T(8,128)(2,1)S(1)}, bf16[20,128,128]{2,1,0:T(8,128)(2,1)S(1)}, u32[]{:S(2)}, u32[]{:S(2)}) %collective-permute-start.13) | collective-permute-done | bytes 655392 | tf_op jit(solution)/shard_map/ppermute | solution.py:40
  71.6 2.8 %collective-permute-done.19 = bf16[20,128,128]{2,1,0:T(8,128)(2,1)S(1)} collective-permute-done((bf16[20,128,128]{2,1,0:T(8,128)(2,1)S(1)}, bf16[20,128,128]{2,1,0:T(8,128)(2,1)S(1)}, u32[]{:S(2)}, u32[]{:S(2)}) %collective-permute-start.19) | collective-permute-done | bytes 655392 | tf_op jit(solution)/shard_map/ppermute | solution.py:40
  74.6 1.6 collective-permute-start.20
  76.1 5.3 %collective-permute-done.16 = bf16[24,128,128]{2,1,0:T(8,128)(2,1)S(1)} collective-permute-done((bf16[24,128,128]{2,1,0:T(8,128)(2,1)S(1)}, bf16[24,128,128]{2,1,0:T(8,128)(2,1)S(1)}, u32[]{:S(2)}, u32[]{:S(2)}) %collective-permute-start.16) | collective-permute-done | bytes 786464 | tf_op jit(solution)/shard_map/ppermute | solution.py:40
  81.5 0.7 collective-permute-start.17
  82.3 3.3 %collective-permute-start.15 = (bf16[5,128,128]{2,1,0:T(8,128)(2,1)S(1)}, bf16[5,128,128]{2,1,0:T(8,128)(2,1)S(1)}, u32[]{:S(2)}, u32[]{:S(2)}) collective-permute-start(bf16[5,128,128]{2,1,0:T(8,128)(2,1)S(1)} %add_convert_fusion.17), channel_id=1, source_target_pairs={{0,4},{1,5},{2,6},{3,7},{4,0},{5,1},{6,2},{7,3},{8,12},{9,13},{10,... | collective-permute-start | bytes 491528 | tf_op jit(solution)/shard_map/ppermute | solution.py:40
  85.7 1.0 collective-permute-done.20
  86.8 2.1 %collective-permute-start.21 = (bf16[5,128,128]{2,1,0:T(8,128)(2,1)S(1)}, bf16[5,128,128]{2,1,0:T(8,128)(2,1)S(1)}, u32[]{:S(2)}, u32[]{:S(2)}) collective-permute-start(bf16[5,128,128]{2,1,0:T(8,128)(2,1)S(1)} %add_convert_fusion.15), channel_id=1, source_target_pairs={{0,3},{1,2},{2,1},{3,0},{4,7},{5,6},{6,5},{7,4},{8,11},{9,10},{10,... | collective-permute-start | bytes 491528 | tf_op jit(solution)/shard_map/ppermute | solution.py:40
  89.3 1.9 collective-permute-done.17
  91.7 1.6 collective-permute-done.21
  93.5 3.6 %collective-permute-done.18 = bf16[6,128,128]{2,1,0:T(8,128)(2,1)S(1)} collective-permute-done((bf16[6,128,128]{2,1,0:T(8,128)(2,1)S(1)}, bf16[6,128,128]{2,1,0:T(8,128)(2,1)S(1)}, u32[]{:S(2)}, u32[]{:S(2)}) %collective-permute-start.18) | collective-permute-done | bytes 196640 | tf_op jit(solution)/shard_map/ppermute | solution.py:40
  97.3 1.9 collective-permute-done.22.sib_sums
  99.2 4.4 %dense.1 = (bf16[1024,256]{1,0:T(8,128)(2,1)}, bf16[7,128,128]{2,1,0:T(8,128)(2,1)S(1)}, bf16[6,128,128]{2,1,0:T(8,128)(2,1)S(1)}, bf16[5,128,128]{2,1,0:T(8,128)(2,1)S(1)}) custom-call(s32[1]{0:T(128)} %bitcast.core_ref, bf16[256,256]{1,0:T(8,128)(2,1)S(1)} %copy-done.3, bf16[1024,256]{1,0:T(8,128)(2,1)S(1)} %copy-done.1, ...), custom_call_target="tpu_custom_call" | custom-call | flops 536870912 | bytes 4194304 | tf_op jit(solution)/shard_map/dense/pallas_call | solution.py:310
  103.6 3.1 %collective-permute-start.23 = (bf16[7,128,128]{2,1,0:T(8,128)(2,1)S(1)}, bf16[7,128,128]{2,1,0:T(8,128)(2,1)S(1)}, u32[]{:S(2)}, u32[]{:S(2)}) collective-permute-start(bf16[7,128,128]{2,1,0:T(8,128)(2,1)S(1)} %get-tuple-element.44), channel_id=1, source_target_pairs={{0,4},{1,5},{2,6},{3,7},{4,0},{5,1},{6,2},{7,3},{8,12},{9,13},{10,... | collective-permute-start | bytes 688136 | tf_op jit(solution)/shard_map/ppermute | solution.py:40
  106.7 1.8 collective-permute-start.29
  108.5 6.3 %collective-permute-done.26 = bf16[6,128,128]{2,1,0:T(8,128)(2,1)S(1)} collective-permute-done((bf16[6,128,128]{2,1,0:T(8,128)(2,1)S(1)}, bf16[6,128,128]{2,1,0:T(8,128)(2,1)S(1)}, u32[]{:S(2)}, u32[]{:S(2)}) %collective-permute-start.26) | collective-permute-done | bytes 196640 | tf_op jit(solution)/shard_map/ppermute | solution.py:40
  114.9 1.6 collective-permute-start.27
  117.4 8.5 %collective-permute-done.27 = bf16[12,128,128]{2,1,0:T(8,128)(2,1)S(1)} collective-permute-done((bf16[12,128,128]{2,1,0:T(8,128)(2,1)S(1)}, bf16[12,128,128]{2,1,0:T(8,128)(2,1)S(1)}, u32[]{:S(2)}, u32[]{:S(2)}) %collective-permute-start.27) | collective-permute-done | bytes 393248 | tf_op jit(solution)/shard_map/ppermute | solution.py:40
  126.5 1.8 collective-permute-start.25
  129.1 13.1 %collective-permute-done.31.rest_5_ = bf16[20,128,128]{2,1,0:T(8,128)(2,1)S(1)} collective-permute-done((bf16[20,128,128]{2,1,0:T(8,128)(2,1)S(1)}, bf16[20,128,128]{2,1,0:T(8,128)(2,1)S(1)}, u32[]{:S(2)}, u32[]{:S(2)}) %collective-permute-start.31) | collective-permute-done | bytes 655392 | tf_op jit(solution)/shard_map/ppermute | solution.py:40
  142.2 1.1 collective-permute-done.25.rest_1_
  143.3 1.4 collective-permute-done.28.rest_3_
  144.7 6.6 %block_adjoint.1 = (bf16[20,128,128]{2,1,0:T(8,128)(2,1)S(1)}, bf16[22,128,128]{2,1,0:T(8,128)(2,1)S(1)}, bf16[24,128,128]{2,1,0:T(8,128)(2,1)S(1)}, bf16[24,128...) custom-call(s32[2]{0:T(128)S(1)} %add_reduce_fusion.live_ref, ...), custom_call_target="tpu_custom_call" | custom-call | flops 1073741824 | bytes 25165824 | tf_op jit(solution)/shard_map/block_adjoint/pallas_call | solution.py:259
  151.3 2.5 %collective-permute-start.38 = (bf16[20,128,128]{2,1,0:T(8,128)(2,1)S(1)}, bf16[20,128,128]{2,1,0:T(8,128)(2,1)}, u32[]{:S(2)}, u32[]{:S(2)}) collective-permute-start(bf16[20,128,128]{2,1,0:T(8,128)(2,1)S(1)} %get-tuple-element.52), channel_id=1, source_target_pairs={{0,32},{1,33},{2,34},{3,35},{4,36},{5,37},{6,38},{7,39},{8,40},{9,... | collective-permute-start | bytes 1966088 | tf_op jit(solution)/shard_map/ppermute | solution.py:40
  153.8 5.3 %collective-permute-start.35 = (bf16[24,128,128]{2,1,0:T(8,128)(2,1)}, bf16[24,128,128]{2,1,0:T(8,128)(2,1)S(1)}, u32[]{:S(2)}, u32[]{:S(2)}) collective-permute-start(bf16[24,128,128]{2,1,0:T(8,128)(2,1)} %copy-done.4), channel_id=1, source_target_pairs={{0,16},{1,17},{2,18},{3,19},{4,20},{5,21},{6,22},{7,23},{8,24},{9,... | collective-permute-start | bytes 2359304 | tf_op jit(solution)/shard_map/ppermute | solution.py:40
  159.1 6.5 %collective-permute-done.38 = bf16[20,128,128]{2,1,0:T(8,128)(2,1)} collective-permute-done((bf16[20,128,128]{2,1,0:T(8,128)(2,1)S(1)}, bf16[20,128,128]{2,1,0:T(8,128)(2,1)}, u32[]{:S(2)}, u32[]{:S(2)}) %collective-permute-start.38) | collective-permute-done | bytes 655392 | tf_op jit(solution)/shard_map/ppermute | solution.py:40
  165.6 1.1 add_convert_fusion.2
  166.7 1.4 collective-permute-start.39
  168.1 1.6 collective-permute-done.32
  169.7 0.9 add_convert_fusion.20
  170.5 1.1 add_convert_fusion.3
  171.7 6.0 %collective-permute-done.35 = bf16[24,128,128]{2,1,0:T(8,128)(2,1)S(1)} collective-permute-done((bf16[24,128,128]{2,1,0:T(8,128)(2,1)}, bf16[24,128,128]{2,1,0:T(8,128)(2,1)S(1)}, u32[]{:S(2)}, u32[]{:S(2)}) %collective-permute-start.35) | collective-permute-done | bytes 786464 | tf_op jit(solution)/shard_map/ppermute | solution.py:40
  178.0 3.3 %collective-permute-done.39 = bf16[10,128,128]{2,1,0:T(8,128)(2,1)S(1)} collective-permute-done((bf16[10,128,128]{2,1,0:T(8,128)(2,1)S(1)}, bf16[10,128,128]{2,1,0:T(8,128)(2,1)S(1)}, u32[]{:S(2)}, u32[]{:S(2)}) %collective-permute-start.39) | collective-permute-done | bytes 327712 | tf_op jit(solution)/shard_map/ppermute | solution.py:40
  181.3 1.0 add_convert_fusion.12
  182.6 1.0 add_convert_fusion.13
  183.7 1.8 collective-permute-start.34
  185.5 5.0 %collective-permute-done.40 = bf16[5,128,128]{2,1,0:T(8,128)(2,1)S(1)} collective-permute-done((bf16[5,128,128]{2,1,0:T(8,128)(2,1)S(1)}, bf16[5,128,128]{2,1,0:T(8,128)(2,1)S(1)}, u32[]{:S(2)}, u32[]{:S(2)}) %collective-permute-start.40) | collective-permute-done | bytes 163872 | tf_op jit(solution)/shard_map/ppermute | solution.py:40
  190.5 1.0 add_convert_fusion.11
  191.7 5.6 %collective-permute-done.37 = bf16[6,128,128]{2,1,0:T(8,128)(2,1)S(1)} collective-permute-done((bf16[6,128,128]{2,1,0:T(8,128)(2,1)S(1)}, bf16[6,128,128]{2,1,0:T(8,128)(2,1)S(1)}, u32[]{:S(2)}, u32[]{:S(2)}) %collective-permute-start.37) | collective-permute-done | bytes 196640 | tf_op jit(solution)/shard_map/ppermute | solution.py:40
  197.6 1.0 add_convert_fusion.10
  199.2 0.7 fusion.1
  200.0 1.0 turn_back.1
  (105 shorter events, 8.2 us)
Async XLA Ops:
  0.6 29.2 %copy-start.1 = (bf16[1024,256]{1,0:T(8,128)(2,1)S(1)}, bf16[1024,256]{1,0:T(8,128)(2,1)}, u32[]{:S(2)}) copy-start(bf16[1024,256]{1,0:T(8,128)(2,1)} %own_cot.1) | copy-start | bytes 1572868
  0.6 2.2 %collective-permute-start = (bf16[1024,256]{1,0:T(8,128)(2,1)}, bf16[1024,256]{1,0:T(8,128)(2,1)S(1)}, u32[]{:S(2)}, u32[]{:S(2)}) collective-permute-start(bf16[1024,256]{1,0:T(8,128)(2,1)} %own_ref.1), channel_id=1, source_target_pairs={{0,8},{1,9},{2,10},{3,11},{4,12},{5,13},{6,14},{7,15},{8,0},{9,1},... | collective-permute-start | bytes 1572872 | tf_op jit(solution)/shard_map/ppermute | solution.py:40
  2.8 1.0 copy-start.2
  4.1 43.0 %collective-permute-start.9 = (bf16[128,128,128]{2,1,0:T(8,128)(2,1)}, bf16[128,128,128]{2,1,0:T(8,128)(2,1)}, u32[]{:S(2)}, u32[]{:S(2)}) collective-permute-start(bf16[128,128,128]{2,1,0:T(8,128)(2,1)} %bitcast.30), channel_id=1, source_target_pairs={{0,8},{1,9},{2,10},{3,11},{4,12},{5,13},{6,14},{7,15},{8,0},{9,1},... | collective-permute-start | bytes 12582920 | tf_op jit(solution)/shard_map/ppermute | solution.py:40
  5.0 42.1 %copy-start = (bf16[1,1,128,128,128]{4,3,2,1,0:T(8,128)(2,1)S(1)}, bf16[1,1,128,128,128]{4,3,2,1,0:T(8,128)(2,1)}, u32[]{:S(2)}) copy-start(bf16[1,1,128,128,128]{4,3,2,1,0:T(8,128)(2,1)} %param.10) | copy-start | bytes 12582916
  5.0 6.6 %collective-permute-start.1 = (bf16[5,128,128]{2,1,0:T(8,128)(2,1)S(1)}, bf16[5,128,128]{2,1,0:T(8,128)(2,1)S(1)}, u32[]{:S(2)}, u32[]{:S(2)}) collective-permute-start(bf16[5,128,128]{2,1,0:T(8,128)(2,1)S(1)} %get-tuple-element.28), channel_id=1, source_target_pairs={{0,16},{1,17},{2,18},{3,19},{4,20},{5,21},{6,22},{7,23},{8,24},{9,... | collective-permute-start | bytes 491528 | tf_op jit(solution)/shard_map/ppermute | solution.py:40
  6.7 9.6 %collective-permute-start.3 = (bf16[6,128,128]{2,1,0:T(8,128)(2,1)S(1)}, bf16[6,128,128]{2,1,0:T(8,128)(2,1)S(1)}, u32[]{:S(2)}, u32[]{:S(2)}) collective-permute-start(bf16[6,128,128]{2,1,0:T(8,128)(2,1)S(1)} %get-tuple-element.29), channel_id=1, source_target_pairs={{0,32},{1,33},{2,34},{3,35},{4,36},{5,37},{6,38},{7,39},{8,40},{9,... | collective-permute-start | bytes 589832 | tf_op jit(solution)/shard_map/ppermute | solution.py:40
  8.3 7.2 %collective-permute-start.5 = (bf16[5,128,128]{2,1,0:T(8,128)(2,1)S(1)}, bf16[5,128,128]{2,1,0:T(8,128)(2,1)S(1)}, u32[]{:S(2)}, u32[]{:S(2)}) collective-permute-start(bf16[5,128,128]{2,1,0:T(8,128)(2,1)S(1)} %get-tuple-element.30), channel_id=1, source_target_pairs={{0,96},{1,97},{2,98},{3,99},{4,100},{5,101},{6,102},{7,103},{8,104... | collective-permute-start | bytes 491528 | tf_op jit(solution)/shard_map/ppermute | solution.py:40
  11.7 13.2 %collective-permute-start.2 = (bf16[10,128,128]{2,1,0:T(8,128)(2,1)S(1)}, bf16[10,128,128]{2,1,0:T(8,128)(2,1)S(1)}, u32[]{:S(2)}, u32[]{:S(2)}) collective-permute-start(bf16[10,128,128]{2,1,0:T(8,128)(2,1)S(1)} %get-tuple-element.59), channel_id=1, source_target_pairs={{0,32},{1,33},{2,34},{3,35},{4,36},{5,37},{6,38},{7,39},{8,40},{9,... | collective-permute-start | bytes 983048 | tf_op jit(solution)/shard_map/ppermute | solution.py:40
  14.1 2.0 %collective-permute-start.8 = (s32[3,128]{1,0:T(4,128)S(1)}, s32[3,128]{1,0:T(4,128)S(1)}, u32[]{:S(2)}, u32[]{:S(2)}) collective-permute-start(s32[3,128]{1,0:T(4,128)S(1)} %get-tuple-element.68), channel_id=1, source_target_pairs={{0,8},{1,9},{2,10},{3,11},{4,12},{5,13},{6,14},{7,15},{8,0},{9,1},... | collective-permute-start | bytes 4616 | tf_op jit(solution)/shard_map/ppermute | solution.py:40
  15.5 8.9 %collective-permute-start.6 = (bf16[10,128,128]{2,1,0:T(8,128)(2,1)S(1)}, bf16[10,128,128]{2,1,0:T(8,128)(2,1)S(1)}, u32[]{:S(2)}, u32[]{:S(2)}) collective-permute-start(bf16[10,128,128]{2,1,0:T(8,128)(2,1)S(1)} %pad_maximum_fusion.7), channel_id=1, source_target_pairs={{0,16},{1,17},{2,18},{3,19},{4,20},{5,21},{6,22},{7,23},{8,24},{9,... | collective-permute-start | bytes 983048 | tf_op jit(solution)/shard_map/ppermute | solution.py:40
  16.4 12.4 %collective-permute-start.4 = (bf16[12,128,128]{2,1,0:T(8,128)(2,1)S(1)}, bf16[12,128,128]{2,1,0:T(8,128)(2,1)S(1)}, u32[]{:S(2)}, u32[]{:S(2)}) collective-permute-start(bf16[12,128,128]{2,1,0:T(8,128)(2,1)S(1)} %pad_maximum_fusion.2), channel_id=1, source_target_pairs={{0,96},{1,97},{2,98},{3,99},{4,100},{5,101},{6,102},{7,103},{8,104... | collective-permute-start | bytes 1179656 | tf_op jit(solution)/shard_map/ppermute | solution.py:40
  24.4 15.0 %collective-permute-start.12 = (bf16[20,128,128]{2,1,0:T(8,128)(2,1)S(1)}, bf16[20,128,128]{2,1,0:T(8,128)(2,1)S(1)}, u32[]{:S(2)}, u32[]{:S(2)}) collective-permute-start(bf16[20,128,128]{2,1,0:T(8,128)(2,1)S(1)} %constant_dynamic-update-slice_fusion.8.rest_4_), channel_id=1, source_target_pairs={{0,32},{1,33},{2,34},{3,35},{4,36},{5,37},{6,38},{7,39},{8,40},{9,... | collective-permute-start | bytes 1966088 | tf_op jit(solution)/shard_map/ppermute | solution.py:40
  24.9 17.6 %collective-permute-start.10 = (bf16[20,128,128]{2,1,0:T(8,128)(2,1)S(1)}, bf16[20,128,128]{2,1,0:T(8,128)(2,1)S(1)}, u32[]{:S(2)}, u32[]{:S(2)}) collective-permute-start(bf16[20,128,128]{2,1,0:T(8,128)(2,1)S(1)} %constant_dynamic-update-slice_fusion.2.rest_0_), channel_id=1, source_target_pairs={{0,96},{1,97},{2,98},{3,99},{4,100},{5,101},{6,102},{7,103},{8,104... | collective-permute-start | bytes 1966088 | tf_op jit(solution)/shard_map/ppermute | solution.py:40
  28.8 18.3 %collective-permute-start.11 = (bf16[24,128,128]{2,1,0:T(8,128)(2,1)S(1)}, bf16[24,128,128]{2,1,0:T(8,128)(2,1)S(1)}, u32[]{:S(2)}, u32[]{:S(2)}) collective-permute-start(bf16[24,128,128]{2,1,0:T(8,128)(2,1)S(1)} %constant_dynamic-update-slice_fusion.5.rest_2_), channel_id=1, source_target_pairs={{0,16},{1,17},{2,18},{3,19},{4,20},{5,21},{6,22},{7,23},{8,24},{9,... | collective-permute-start | bytes 2359304 | tf_op jit(solution)/shard_map/ppermute | solution.py:40
  29.8 2.0 collective-permute-start.7
  55.5 15.9 %collective-permute-start.13 = (bf16[20,128,128]{2,1,0:T(8,128)(2,1)S(1)}, bf16[20,128,128]{2,1,0:T(8,128)(2,1)S(1)}, u32[]{:S(2)}, u32[]{:S(2)}) collective-permute-start(bf16[20,128,128]{2,1,0:T(8,128)(2,1)S(1)} %get-tuple-element.38), channel_id=1, source_target_pairs={{0,3},{1,2},{2,1},{3,0},{4,7},{5,6},{6,5},{7,4},{8,11},{9,10},{10,... | collective-permute-start | bytes 1966088 | tf_op jit(solution)/shard_map/ppermute | solution.py:40
  58.9 15.6 %collective-permute-start.19 = (bf16[20,128,128]{2,1,0:T(8,128)(2,1)S(1)}, bf16[20,128,128]{2,1,0:T(8,128)(2,1)S(1)}, u32[]{:S(2)}, u32[]{:S(2)}) collective-permute-start(bf16[20,128,128]{2,1,0:T(8,128)(2,1)S(1)} %get-tuple-element.42), channel_id=1, source_target_pairs={{0,1},{1,0},{2,3},{3,2},{4,5},{5,4},{6,7},{7,6},{8,9},{9,8},{10,11... | collective-permute-start | bytes 1966088 | tf_op jit(solution)/shard_map/ppermute | solution.py:40
  58.9 22.5 %collective-permute-start.16 = (bf16[24,128,128]{2,1,0:T(8,128)(2,1)S(1)}, bf16[24,128,128]{2,1,0:T(8,128)(2,1)S(1)}, u32[]{:S(2)}, u32[]{:S(2)}) collective-permute-start(bf16[24,128,128]{2,1,0:T(8,128)(2,1)S(1)} %get-tuple-element.40), channel_id=1, source_target_pairs={{0,4},{1,5},{2,6},{3,7},{4,0},{5,1},{6,2},{7,3},{8,12},{9,13},{10,... | collective-permute-start | bytes 2359304 | tf_op jit(solution)/shard_map/ppermute | solution.py:40
  71.5 27.7 %copy-start.3 = (bf16[256,256]{1,0:T(8,128)(2,1)S(1)}, bf16[256,256]{1,0:T(8,128)(2,1)}, u32[]{:S(2)}) copy-start(bf16[256,256]{1,0:T(8,128)(2,1)} %weight_ref.1) | copy-start | bytes 393220
  71.5 10.7 %collective-permute-start.14 = (bf16[10,128,128]{2,1,0:T(8,128)(2,1)S(1)}, bf16[10,128,128]{2,1,0:T(8,128)(2,1)S(1)}, u32[]{:S(2)}, u32[]{:S(2)}) collective-permute-start(bf16[10,128,128]{2,1,0:T(8,128)(2,1)S(1)} %add_convert_fusion.5), channel_id=1, source_target_pairs={{0,1},{1,0},{2,3},{3,2},{4,5},{5,4},{6,7},{7,6},{8,9},{9,8},{10,11... | collective-permute-start | bytes 983048 | tf_op jit(solution)/shard_map/ppermute | solution.py:40
  74.6 12.1 %collective-permute-start.20 = (bf16[10,128,128]{2,1,0:T(8,128)(2,1)S(1)}, bf16[10,128,128]{2,1,0:T(8,128)(2,1)S(1)}, u32[]{:S(2)}, u32[]{:S(2)}) collective-permute-start(bf16[10,128,128]{2,1,0:T(8,128)(2,1)S(1)} %add_convert_fusion.4), channel_id=1, source_target_pairs={{0,4},{1,5},{2,6},{3,7},{4,0},{5,1},{6,2},{7,3},{8,12},{9,13},{10,... | collective-permute-start | bytes 983048 | tf_op jit(solution)/shard_map/ppermute | solution.py:40
  81.5 9.7 %collective-permute-start.17 = (bf16[12,128,128]{2,1,0:T(8,128)(2,1)S(1)}, bf16[12,128,128]{2,1,0:T(8,128)(2,1)S(1)}, u32[]{:S(2)}, u32[]{:S(2)}) collective-permute-start(bf16[12,128,128]{2,1,0:T(8,128)(2,1)S(1)} %add_convert_fusion.1), channel_id=1, source_target_pairs={{0,3},{1,2},{2,1},{3,0},{4,7},{5,6},{6,5},{7,4},{8,11},{9,10},{10,... | collective-permute-start | bytes 1179656 | tf_op jit(solution)/shard_map/ppermute | solution.py:40
  82.3 6.9 %collective-permute-start.15 = (bf16[5,128,128]{2,1,0:T(8,128)(2,1)S(1)}, bf16[5,128,128]{2,1,0:T(8,128)(2,1)S(1)}, u32[]{:S(2)}, u32[]{:S(2)}) collective-permute-start(bf16[5,128,128]{2,1,0:T(8,128)(2,1)S(1)} %add_convert_fusion.17), channel_id=1, source_target_pairs={{0,4},{1,5},{2,6},{3,7},{4,0},{5,1},{6,2},{7,3},{8,12},{9,13},{10,... | collective-permute-start | bytes 491528 | tf_op jit(solution)/shard_map/ppermute | solution.py:40
  86.8 6.6 %collective-permute-start.21 = (bf16[5,128,128]{2,1,0:T(8,128)(2,1)S(1)}, bf16[5,128,128]{2,1,0:T(8,128)(2,1)S(1)}, u32[]{:S(2)}, u32[]{:S(2)}) collective-permute-start(bf16[5,128,128]{2,1,0:T(8,128)(2,1)S(1)} %add_convert_fusion.15), channel_id=1, source_target_pairs={{0,3},{1,2},{2,1},{3,0},{4,7},{5,6},{6,5},{7,4},{8,11},{9,10},{10,... | collective-permute-start | bytes 491528 | tf_op jit(solution)/shard_map/ppermute | solution.py:40
  91.3 5.8 %collective-permute-start.18 = (bf16[6,128,128]{2,1,0:T(8,128)(2,1)S(1)}, bf16[6,128,128]{2,1,0:T(8,128)(2,1)S(1)}, u32[]{:S(2)}, u32[]{:S(2)}) collective-permute-start(bf16[6,128,128]{2,1,0:T(8,128)(2,1)S(1)} %add_convert_fusion.9), channel_id=1, source_target_pairs={{0,1},{1,0},{2,3},{3,2},{4,5},{5,4},{6,7},{7,6},{8,9},{9,8},{10,11... | collective-permute-start | bytes 589832 | tf_op jit(solution)/shard_map/ppermute | solution.py:40
  97.2 2.0 collective-permute-start.22
  103.6 12.9 %collective-permute-start.23 = (bf16[7,128,128]{2,1,0:T(8,128)(2,1)S(1)}, bf16[7,128,128]{2,1,0:T(8,128)(2,1)S(1)}, u32[]{:S(2)}, u32[]{:S(2)}) collective-permute-start(bf16[7,128,128]{2,1,0:T(8,128)(2,1)S(1)} %get-tuple-element.44), channel_id=1, source_target_pairs={{0,4},{1,5},{2,6},{3,7},{4,0},{5,1},{6,2},{7,3},{8,12},{9,13},{10,... | collective-permute-start | bytes 688136 | tf_op jit(solution)/shard_map/ppermute | solution.py:40
  106.7 10.0 %collective-permute-start.29 = (bf16[5,128,128]{2,1,0:T(8,128)(2,1)S(1)}, bf16[5,128,128]{2,1,0:T(8,128)(2,1)S(1)}, u32[]{:S(2)}, u32[]{:S(2)}) collective-permute-start(bf16[5,128,128]{2,1,0:T(8,128)(2,1)S(1)} %get-tuple-element.46), channel_id=1, source_target_pairs={{0,3},{1,2},{2,1},{3,0},{4,7},{5,6},{6,5},{7,4},{8,11},{9,10},{10,... | collective-permute-start | bytes 491528 | tf_op jit(solution)/shard_map/ppermute | solution.py:40
  108.5 6.4 %collective-permute-start.26 = (bf16[6,128,128]{2,1,0:T(8,128)(2,1)S(1)}, bf16[6,128,128]{2,1,0:T(8,128)(2,1)S(1)}, u32[]{:S(2)}, u32[]{:S(2)}) collective-permute-start(bf16[6,128,128]{2,1,0:T(8,128)(2,1)S(1)} %get-tuple-element.45), channel_id=1, source_target_pairs={{0,1},{1,0},{2,3},{3,2},{4,5},{5,4},{6,7},{7,6},{8,9},{9,8},{10,11... | collective-permute-start | bytes 589832 | tf_op jit(solution)/shard_map/ppermute | solution.py:40
  114.9 11.0 %collective-permute-start.27 = (bf16[12,128,128]{2,1,0:T(8,128)(2,1)S(1)}, bf16[12,128,128]{2,1,0:T(8,128)(2,1)S(1)}, u32[]{:S(2)}, u32[]{:S(2)}) collective-permute-start(bf16[12,128,128]{2,1,0:T(8,128)(2,1)S(1)} %pad_maximum_fusion.4), channel_id=1, source_target_pairs={{0,3},{1,2},{2,1},{3,0},{4,7},{5,6},{6,5},{7,4},{8,11},{9,10},{10,... | collective-permute-start | bytes 1179656 | tf_op jit(solution)/shard_map/ppermute | solution.py:40
  116.6 9.7 %collective-permute-start.24 = (bf16[12,128,128]{2,1,0:T(8,128)(2,1)S(1)}, bf16[12,128,128]{2,1,0:T(8,128)(2,1)S(1)}, u32[]{:S(2)}, u32[]{:S(2)}) collective-permute-start(bf16[12,128,128]{2,1,0:T(8,128)(2,1)S(1)} %pad_maximum_fusion.3), channel_id=1, source_target_pairs={{0,1},{1,0},{2,3},{3,2},{4,5},{5,4},{6,7},{7,6},{8,9},{9,8},{10,11... | collective-permute-start | bytes 1179656 | tf_op jit(solution)/shard_map/ppermute | solution.py:40
  116.8 11.5 %collective-permute-start.30 = (bf16[10,128,128]{2,1,0:T(8,128)(2,1)S(1)}, bf16[10,128,128]{2,1,0:T(8,128)(2,1)S(1)}, u32[]{:S(2)}, u32[]{:S(2)}) collective-permute-start(bf16[10,128,128]{2,1,0:T(8,128)(2,1)S(1)} %pad_maximum_fusion.8), channel_id=1, source_target_pairs={{0,4},{1,5},{2,6},{3,7},{4,0},{5,1},{6,2},{7,3},{8,12},{9,13},{10,... | collective-permute-start | bytes 983048 | tf_op jit(solution)/shard_map/ppermute | solution.py:40
  125.9 18.8 %collective-permute-start.28 = (bf16[24,128,128]{2,1,0:T(8,128)(2,1)S(1)}, bf16[24,128,128]{2,1,0:T(8,128)(2,1)S(1)}, u32[]{:S(2)}, u32[]{:S(2)}) collective-permute-start(bf16[24,128,128]{2,1,0:T(8,128)(2,1)S(1)} %constant_dynamic-update-slice_fusion.11.rest_2_), channel_id=1, source_target_pairs={{0,4},{1,5},{2,6},{3,7},{4,0},{5,1},{6,2},{7,3},{8,12},{9,13},{10,... | collective-permute-start | bytes 2359304 | tf_op jit(solution)/shard_map/ppermute | solution.py:40
  126.5 16.8 %collective-permute-start.25 = (bf16[22,128,128]{2,1,0:T(8,128)(2,1)S(1)}, bf16[22,128,128]{2,1,0:T(8,128)(2,1)S(1)}, u32[]{:S(2)}, u32[]{:S(2)}) collective-permute-start(bf16[22,128,128]{2,1,0:T(8,128)(2,1)S(1)} %pad_maximum_fusion.rest_0_), channel_id=1, source_target_pairs={{0,3},{1,2},{2,1},{3,0},{4,7},{5,6},{6,5},{7,4},{8,11},{9,10},{10,... | collective-permute-start | bytes 2162696 | tf_op jit(solution)/shard_map/ppermute | solution.py:40
  128.3 13.9 %collective-permute-start.31 = (bf16[20,128,128]{2,1,0:T(8,128)(2,1)S(1)}, bf16[20,128,128]{2,1,0:T(8,128)(2,1)S(1)}, u32[]{:S(2)}, u32[]{:S(2)}) collective-permute-start(bf16[20,128,128]{2,1,0:T(8,128)(2,1)S(1)} %constant_dynamic-update-slice_fusion.14.rest_4_), channel_id=1, source_target_pairs={{0,1},{1,0},{2,3},{3,2},{4,5},{5,4},{6,7},{7,6},{8,9},{9,8},{10,11... | collective-permute-start | bytes 1966088 | tf_op jit(solution)/shard_map/ppermute | solution.py:40
  151.3 2.5 %copy-start.4 = (bf16[24,128,128]{2,1,0:T(8,128)(2,1)}, bf16[24,128,128]{2,1,0:T(8,128)(2,1)S(1)}, u32[]{:S(2)}) copy-start(bf16[24,128,128]{2,1,0:T(8,128)(2,1)S(1)} %get-tuple-element.50) | copy-start | bytes 2359300
  151.3 14.3 %collective-permute-start.38 = (bf16[20,128,128]{2,1,0:T(8,128)(2,1)S(1)}, bf16[20,128,128]{2,1,0:T(8,128)(2,1)}, u32[]{:S(2)}, u32[]{:S(2)}) collective-permute-start(bf16[20,128,128]{2,1,0:T(8,128)(2,1)S(1)} %get-tuple-element.52), channel_id=1, source_target_pairs={{0,32},{1,33},{2,34},{3,35},{4,36},{5,37},{6,38},{7,39},{8,40},{9,... | collective-permute-start | bytes 1966088 | tf_op jit(solution)/shard_map/ppermute | solution.py:40
  153.8 15.9 %collective-permute-start.32 = (bf16[22,128,128]{2,1,0:T(8,128)(2,1)S(1)}, bf16[22,128,128]{2,1,0:T(8,128)(2,1)}, u32[]{:S(2)}, u32[]{:S(2)}) collective-permute-start(bf16[22,128,128]{2,1,0:T(8,128)(2,1)S(1)} %get-tuple-element.47), channel_id=1, source_target_pairs={{0,96},{1,97},{2,98},{3,99},{4,100},{5,101},{6,102},{7,103},{8,104... | collective-permute-start | bytes 2162696 | tf_op jit(solution)/shard_map/ppermute | solution.py:40
  153.8 24.0 %collective-permute-start.35 = (bf16[24,128,128]{2,1,0:T(8,128)(2,1)}, bf16[24,128,128]{2,1,0:T(8,128)(2,1)S(1)}, u32[]{:S(2)}, u32[]{:S(2)}) collective-permute-start(bf16[24,128,128]{2,1,0:T(8,128)(2,1)} %copy-done.4), channel_id=1, source_target_pairs={{0,16},{1,17},{2,18},{3,19},{4,20},{5,21},{6,22},{7,23},{8,24},{9,... | collective-permute-start | bytes 2359304 | tf_op jit(solution)/shard_map/ppermute | solution.py:40
  166.7 14.6 %collective-permute-start.39 = (bf16[10,128,128]{2,1,0:T(8,128)(2,1)S(1)}, bf16[10,128,128]{2,1,0:T(8,128)(2,1)S(1)}, u32[]{:S(2)}, u32[]{:S(2)}) collective-permute-start(bf16[10,128,128]{2,1,0:T(8,128)(2,1)S(1)} %add_convert_fusion.2), channel_id=1, source_target_pairs={{0,16},{1,17},{2,18},{3,19},{4,20},{5,21},{6,22},{7,23},{8,24},{9,... | collective-permute-start | bytes 983048 | tf_op jit(solution)/shard_map/ppermute | solution.py:40
  171.6 11.0 %collective-permute-start.33 = (bf16[12,128,128]{2,1,0:T(8,128)(2,1)S(1)}, bf16[12,128,128]{2,1,0:T(8,128)(2,1)S(1)}, u32[]{:S(2)}, u32[]{:S(2)}) collective-permute-start(bf16[12,128,128]{2,1,0:T(8,128)(2,1)S(1)} %pad_maximum_fusion.5), channel_id=1, source_target_pairs={{0,32},{1,33},{2,34},{3,35},{4,36},{5,37},{6,38},{7,39},{8,40},{9,... | collective-permute-start | bytes 1179656 | tf_op jit(solution)/shard_map/ppermute | solution.py:40
  177.9 13.6 %collective-permute-start.36 = (bf16[12,128,128]{2,1,0:T(8,128)(2,1)S(1)}, bf16[12,128,128]{2,1,0:T(8,128)(2,1)S(1)}, u32[]{:S(2)}, u32[]{:S(2)}) collective-permute-start(bf16[12,128,128]{2,1,0:T(8,128)(2,1)S(1)} %add_convert_fusion), channel_id=1, source_target_pairs={{0,96},{1,97},{2,98},{3,99},{4,100},{5,101},{6,102},{7,103},{8,104... | collective-permute-start | bytes 1179656 | tf_op jit(solution)/shard_map/ppermute | solution.py:40
  182.3 8.2 %collective-permute-start.40 = (bf16[5,128,128]{2,1,0:T(8,128)(2,1)S(1)}, bf16[5,128,128]{2,1,0:T(8,128)(2,1)S(1)}, u32[]{:S(2)}, u32[]{:S(2)}) collective-permute-start(bf16[5,128,128]{2,1,0:T(8,128)(2,1)S(1)} %add_convert_fusion.12), channel_id=1, source_target_pairs={{0,96},{1,97},{2,98},{3,99},{4,100},{5,101},{6,102},{7,103},{8,104... | collective-permute-start | bytes 491528 | tf_op jit(solution)/shard_map/ppermute | solution.py:40
  183.7 8.0 %collective-permute-start.34 = (bf16[7,128,128]{2,1,0:T(8,128)(2,1)S(1)}, bf16[7,128,128]{2,1,0:T(8,128)(2,1)S(1)}, u32[]{:S(2)}, u32[]{:S(2)}) collective-permute-start(bf16[7,128,128]{2,1,0:T(8,128)(2,1)S(1)} %pad_maximum_fusion.10), channel_id=1, source_target_pairs={{0,16},{1,17},{2,18},{3,19},{4,20},{5,21},{6,22},{7,23},{8,24},{9,... | collective-permute-start | bytes 688136 | tf_op jit(solution)/shard_map/ppermute | solution.py:40
  191.6 5.7 %collective-permute-start.37 = (bf16[6,128,128]{2,1,0:T(8,128)(2,1)S(1)}, bf16[6,128,128]{2,1,0:T(8,128)(2,1)S(1)}, u32[]{:S(2)}, u32[]{:S(2)}) collective-permute-start(bf16[6,128,128]{2,1,0:T(8,128)(2,1)S(1)} %add_convert_fusion.7), channel_id=1, source_target_pairs={{0,32},{1,33},{2,34},{3,35},{4,36},{5,37},{6,38},{7,39},{8,40},{9,... | collective-permute-start | bytes 589832 | tf_op jit(solution)/shard_map/ppermute | solution.py:40
  197.5 1.7 collective-permute-start.41

commit v2 on v1

--- a/solution.py
+++ b/solution.py
@@ -10,11 +10,12 @@
 
 AXES = ("gr", "gc")
 TILE = 128
-CUTS = ((0, 5), (5, 11), (11, 16))
+CUTS = ((0, 6), (6, 11), (11, 16))
+SIDE = 1
 EXTRA = 2
 GROUP = 8
 LOAD = 8
-PASS_VMEM = 40
+PASS_VMEM = 26
 F32 = jnp.float32
 BF16 = jnp.bfloat16
 
@@ -62,21 +63,21 @@
     return lax.optimization_barrier((value,) + earlier)[0]
 
 
-def spread(thirds, links, side=None, extra=0):
+def spread(thirds, links, hook=None, extra=0):
     held = [[third] for third in thirds]
     if extra:
-        held[0], extra_sum = [thirds[0][:-extra]], thirds[0][-extra:]
+        held[SIDE], extra_sum = [thirds[SIDE][:-extra]], thirds[SIDE][-extra:]
     for step in range(3):
         sent = [parts[0] if len(parts) == 1 else jnp.concatenate(parts) for parts in held]
         if extra:
-            sent[0] = jnp.concatenate(held[0] + [extra_sum]) if step else thirds[0]
-        if side is not None:
-            side(step, sent)
+            sent[SIDE] = jnp.concatenate(held[SIDE] + [extra_sum]) if step else thirds[SIDE]
+        if hook is not None:
+            hook(step, sent)
         got = [move(value, **order[step][0]) for value, order in zip(sent, links)]
         held = [parts + [value] for parts, value in zip(held, got)]
         if extra:
-            held[0][-1] = got[0][:-extra]
-            extra_sum = add_all(extra_sum, got[0][-extra:])
+            held[SIDE][-1] = got[SIDE][:-extra]
+            extra_sum = add_all(extra_sum, got[SIDE][-extra:])
     return [array for pair in zip(sent, got) for array in pair]
 
 
@@ -90,19 +91,20 @@
 def collect(parts, links, extra=0):
     held = [[part] for part in parts[0::2]]
     sent = list(parts[1::2])
-    extra_sum = sent[0][-extra:]
+    extra_sum = sent[SIDE][-extra:]
     for step in range(3):
         got = [move(value, **order[2 - step][0]) for value, order in zip(sent, links)]
+        added = list(got)
         if extra:
-            extra_sum = add_all(extra_sum, got[0][-extra:])
-            got[0] = got[0][:-extra]
-        held = [terms + [value] for terms, value in zip(held, got)]
+            extra_sum = add_all(extra_sum, got[SIDE][-extra:])
+            added[SIDE] = got[SIDE][:-extra]
+        held = [terms + [value] for terms, value in zip(held, added)]
         if step < 2:
             half = [terms[0].shape[0] // 2 for terms in held]
             sent = [add_all(*[t[h:] for t in terms]) for terms, h in zip(held, half)]
             held = [[t[:h] for t in terms] for terms, h in zip(held, half)]
             if extra:
-                sent[0] = jnp.concatenate([sent[0], extra_sum])
+                sent[SIDE] = jnp.concatenate([sent[SIDE], extra_sum])
     total = jnp.concatenate([add_all(*terms) for terms in held])
     return (total, extra_sum) if extra else total
 
@@ -129,7 +131,7 @@
 
 def third_shapes(pieces=1, extra=0):
     counts = [pieces * (hi - lo) for lo, hi in CUTS]
-    counts[0] += extra
+    counts[SIDE] += extra
     return [jax.ShapeDtypeStruct((count, TILE, TILE), BF16) for count in counts]
 
 
@@ -155,14 +157,6 @@
         cost_estimate=cost(0, 2 << 20),
         name="turn_in",
     )(core, own, sib)
-
-
-def third_rows(links):
-    rows = [[] for _ in range(6)]
-    for third, (order, (lo, hi)) in enumerate(zip(links, CUTS)):
-        for p, mark in enumerate(places(order)):
-            rows[2 * third + p // 4].append(((p % 4) * (hi - lo), mark * 16 + lo, hi - lo))
-    return rows
 
 
 def array_place(ids):
@@ -179,48 +173,34 @@
     return array, row
 
 
-def order_slots(array, row, target, dead):
-    key = jnp.where(dead, 6, array).reshape(-1)
-    count = key.shape[0]
-    at = jnp.arange(count, dtype=jnp.int32)
+def total_row(ids):
+    array, row = array_place(ids)
+    first = sum(jnp.where(array // 2 == third, 4 * lo, 0) for third, (lo, _) in enumerate(CUTS))
+    return first + row + 64 * (1 - array % 2)
+
+
+def order_slots(source_ids, target_ids, dead):
+    array, row = array_place(source_ids)
+    target = total_row(target_ids)
+    late = jnp.where(target < 64, 3, 6)
+    key = jnp.where(dead, 9, array // 2 + jnp.where(array % 2 == 1, late, 0)).reshape(-1)
+    at = jnp.arange(key.shape[0], dtype=jnp.int32)
     packed = (row + 32 * target).reshape(-1) + 4096 * at
     ahead = (key[None, :] < key[:, None]) | (
         (key[None, :] == key[:, None]) & (at[None, :] < at[:, None])
     )
     rank = jnp.sum(ahead.astype(jnp.int32), axis=1)
     listed = jnp.sum(jnp.where(rank[None, :] == at[:, None], packed[None, :], 0), axis=1)
-    bounds = jnp.sum((key[None, :] < jnp.arange(7, dtype=jnp.int32)[:, None]).astype(jnp.int32), axis=1)
+    marks = jnp.arange(10, dtype=jnp.int32)[:, None]
+    bounds = jnp.sum((key[None, :] < marks).astype(jnp.int32), axis=1)
     return listed, bounds
 
 
-def pass_kernel(adjoint, live_ref, list_ref, bound_ref, own_tiles, sib_tiles, *rest):
-    sources, targets = rest[:6], rest[6:12]
-    tile_buf, total, tile_sems = rest[12:]
-    slots = own_tiles.shape[0]
-    lists = (own_tiles, sib_tiles)
-    groups = [lax.div(live_ref[side] + (LOAD - 1), LOAD) for side in range(2)]
-
-    def tile_copy(side, group):
-        first = pl.multiple_of(group * LOAD, LOAD)
-        return pltpu.make_async_copy(
-            lists[side].at[pl.ds(first, LOAD)],
-            tile_buf.at[pl.ds(side * slots + first, LOAD)],
-            tile_sems.at[side, group],
-        )
-
-    for side in range(2):
-        pl.loop(0, groups[side])(lambda group, side=side: tile_copy(side, group).start())
-
-    @pl.loop(0, total.shape[0] // 3)
-    def _(at):
-        total[pl.ds(at * 3, 3)] = jnp.zeros((3,) + total.shape[1:], F32)
-
-    for side in range(2):
-        pl.loop(0, groups[side])(lambda group, side=side: tile_copy(side, group).wait())
-
+def add_products(adjoint, first_class, list_ref, bound_ref, sources, tiles, total, base=0):
     dims = (((1,), (0,)), ((), ())) if adjoint else (((1,), (1,)), ((), ()))
-    for array, source in enumerate(sources):
-        first, last = bound_ref[array], bound_ref[array + 1]
+    final, unused = tiles.shape[0] - 1, total.shape[0] - 1
+    for index, source in enumerate(sources):
+        first, last = bound_ref[first_class + index], bound_ref[first_class + index + 1]
 
         @pl.loop(0, lax.div(last - first + (GROUP - 1), GROUP))
         def _(group, source=source, first=first, last=last):
@@ -228,12 +208,12 @@
             for step in range(GROUP):
                 at = first + group * GROUP + step
                 live = at < last
-                entry = jnp.where(live, list_ref[jnp.minimum(at, 2 * slots - 1)], 0)
-                places_to.append(jnp.where(live, (entry >> 5) & 127, 128))
+                entry = jnp.where(live, list_ref[jnp.minimum(at, final)], 0)
+                places_to.append(jnp.where(live, ((entry >> 5) & 127) - base, unused))
                 products.append(
                     lax.dot_general(
                         source[entry & 31],
-                        tile_buf[entry >> 12],
+                        tiles[entry >> 12],
                         dims,
                         preferred_element_type=F32,
                     )
@@ -241,35 +221,125 @@
             for to, product in zip(places_to, products):
                 total[to] = total[to] + product
 
+
+def clear(total):
+    @pl.loop(0, total.shape[0] // 3)
+    def _(at):
+        total[pl.ds(at * 3, 3)] = jnp.zeros((3,) + total.shape[1:], F32)
+
+
+def give(total, result):
+    @pl.loop(0, 32)
+    def _(at):
+        result[pl.ds(at * 4, 4)] = total[pl.ds(at * 4, 4)].astype(BF16)
+
+
+def load_kernel(live_ref, list_ref, bound_ref, own_tiles, sib_tiles, *rest):
+    sources, (result, tiles, total, sems) = rest[:3], rest[3:]
+    slots = own_tiles.shape[0]
+    lists = (own_tiles, sib_tiles)
+    groups = [lax.div(live_ref[side] + (LOAD - 1), LOAD) for side in range(2)]
+
+    def tile_copy(side, group):
+        first = pl.multiple_of(group * LOAD, LOAD)
+        return pltpu.make_async_copy(
+            lists[side].at[pl.ds(first, LOAD)],
+            tiles.at[pl.ds(side * slots + first, LOAD)],
+            sems.at[side, group],
+        )
+
+    for side in range(2):
+        pl.loop(0, groups[side])(lambda group, side=side: tile_copy(side, group).start())
+    clear(total)
+    for side in range(2):
+        pl.loop(0, groups[side])(lambda group, side=side: tile_copy(side, group).wait())
+    add_products(False, 0, list_ref, bound_ref, sources, tiles, total)
+    give(total, result)
+
+
+def early_kernel(list_ref, bound_ref, tiles, *rest):
+    sources, (result, total) = rest[:3], rest[3:]
+    clear(total)
+    add_products(True, 0, list_ref, bound_ref, sources, tiles, total)
+    give(total, result)
+
+
+def late_kernel(adjoint, kept, list_ref, bound_ref, tiles, before, *rest):
+    sources, rest = rest[:3], rest[3:]
+    if adjoint and not kept:
+        extra_ref, *rest = rest
+        rows = extra_ref.shape[0] - EXTRA, extra_ref.shape[0]
+        extra = extra_ref[rows[0] : rows[1]].astype(F32) + sources[SIDE][rows[0] : rows[1]].astype(F32)
+        rest[SIDE][rows[0] : rows[1]] = extra.astype(BF16)
+    *targets, total = rest
+    base = 64 if kept else 0
+
+    @pl.loop(0, 16)
+    def _(at):
+        total[pl.ds(at * 4, 4)] = before[pl.ds(base + at * 4, 4)].astype(F32)
+
+    add_products(
+        adjoint, 6 if kept else 3, list_ref, bound_ref, sources, tiles, total, base
+    )
+    for target, (lo, hi) in zip(targets, CUTS):
+        for row in range(4 * (hi - lo)):
+            target[row] = total[4 * lo + row].astype(BF16)
+
+
+TOTAL = jax.ShapeDtypeStruct((128, TILE, TILE), BF16)
+SUMS = pltpu.VMEM((129, TILE, TILE), F32)
+
+
+def pass_params():
+    return pltpu.CompilerParams(vmem_limit_bytes=PASS_VMEM << 20)
+
+
+def early_pass(adjoint, live, listed, bounds, tiles, sources):
+    estimate = cost(128 * TILE * TILE * TILE, 16 << 20)
     if adjoint:
-        first, last = sources[0].shape[0] - EXTRA, sources[0].shape[0]
-        extra = sources[0][first:last].astype(F32) + sources[1][first:last].astype(F32)
-        targets[1][first:last] = extra.astype(BF16)
-    for target, rows in zip(targets, third_rows(GR_LINKS if adjoint else GC_LINKS)):
-        for first, at, count in rows:
-            for step in range(count):
-                target[first + step] = total[at + step].astype(BF16)
-
-
-def block_pass(adjoint, live, listed, bounds, own_tiles, sib_tiles, sources):
-    slots = own_tiles.shape[0]
-    out_shape = [shape for shape in third_shapes(4) for _ in range(2)]
-    if adjoint:
-        out_shape[1] = third_shapes(4, EXTRA)[0]
+        return tiles, pl.pallas_call(
+            early_kernel,
+            out_shape=TOTAL,
+            in_specs=[smem_spec()] * 2 + [vmem_spec()] * 4,
+            out_specs=vmem_spec(),
+            scratch_shapes=[SUMS],
+            compiler_params=pass_params(),
+            cost_estimate=estimate,
+            name="early_adjoint",
+        )(listed, bounds, tiles, *sources)
+    slots = tiles[0].shape[0]
+    total, tiles = pl.pallas_call(
+        load_kernel,
+        out_shape=[TOTAL, jax.ShapeDtypeStruct((2 * slots, TILE, TILE), BF16)],
+        in_specs=[smem_spec()] * 3 + [any_spec()] * 2 + [vmem_spec()] * 3,
+        out_specs=[vmem_spec()] * 2,
+        scratch_shapes=[SUMS, pltpu.SemaphoreType.DMA((2, slots // LOAD))],
+        compiler_params=pass_params(),
+        cost_estimate=estimate,
+        name="early_pass",
+    )(live, listed, bounds, *tiles, *sources)
+    return tiles, total
+
+
+def late_pass(adjoint, kept, listed, bounds, tiles, total, sources, extra=()):
     return pl.pallas_call(
-        functools.partial(pass_kernel, adjoint),
-        out_shape=out_shape,
-        in_specs=[smem_spec()] * 3 + [any_spec()] * 2 + [vmem_spec()] * 6,
-        out_specs=[vmem_spec()] * 6,
-        scratch_shapes=[
-            pltpu.VMEM((2 * slots, TILE, TILE), BF16),
-            pltpu.VMEM((129, TILE, TILE), F32),
-            pltpu.SemaphoreType.DMA((2, slots // LOAD)),
-        ],
-        compiler_params=pltpu.CompilerParams(vmem_limit_bytes=PASS_VMEM << 20),
-        cost_estimate=cost(2 * 256 * TILE * TILE * TILE, 24 << 20),
-        name="block_adjoint" if adjoint else "block_pass",
-    )(live, listed, bounds, own_tiles, sib_tiles, *sources)
+        functools.partial(late_kernel, adjoint, kept),
+        out_shape=third_shapes(4, EXTRA if extra else 0),
+        in_specs=[smem_spec()] * 2 + [vmem_spec()] * (5 + len(extra)),
+        out_specs=[vmem_spec()] * 3,
+        scratch_shapes=[pltpu.VMEM((65, TILE, TILE), F32)],
+        compiler_params=pass_params(),
+        cost_estimate=cost(64 * TILE * TILE * TILE, 8 << 20),
+        name=("kept" if kept else "sent") + ("_adjoint" if adjoint else "_pass"),
+    )(listed, bounds, tiles, total, *sources, *extra)
+
+
+def block_pass(adjoint, live, order, tiles, sources):
+    extra = sources[2 * SIDE : 2 * SIDE + 1] if adjoint else ()
+    tiles, total = early_pass(adjoint, live, *order, tiles, sources[0::2])
+    sent = late_pass(adjoint, False, *order, tiles, total, sources[1::2], extra)
+    held = late_pass(adjoint, True, *order, tiles, total, sources[1::2])
+    return [array for pair in zip(held, sent) for array in pair], tiles
 
 
 def dense_kernel(core_ref, weight_ref, own_cot, sib_cot, own_sums, sib_sums, *rest):
@@ -303,7 +373,7 @@
         ref[: hi - lo] = mixed_buf[lo:hi]
     for part in range(EXTRA):
         extra = wgrad_ref[:, part * TILE : (part + 1) * TILE]
-        mixed_refs[0][CUTS[0][1] + part] = extra.astype(BF16)
+        mixed_refs[SIDE][CUTS[SIDE][1] - CUTS[SIDE][0] + part] = extra.astype(BF16)
 
 
 def dense(core, weight, own_cot, sib_cot, own_sums, sib_sums):
@@ -360,14 +430,12 @@
     fetched = []
 
     def fetch(step, sent):
-        if step == 1:
-            sent = sent[:1]
-            live = jnp.broadcast_to(after(counts[0, 0], *sent), (slots,))
-            rows, cols = after(block_row[0, 0], *sent), after(block_col[0, 0], *sent)
+        if step == 2:
+            event = sent[2]
+            live = jnp.broadcast_to(after(counts[0, 0], event), (slots,))
+            rows, cols = after(block_row[0, 0], event), after(block_col[0, 0], event)
             lists = jnp.stack([rows, cols, live])
-            fetched.extend([lists, move(lists, core=1)])
-        if step == 2:
-            fetched.append(move(after(cotangent, *sent), core=1))
+            fetched.extend([lists, move(lists, core=1), move(after(cotangent, event), core=1)])
 
     gathered = spread(slices, GR_LINKS, fetch)
     own_lists, sib_lists, sib_cot = fetched
@@ -381,18 +449,18 @@
     col_ids = ((part // 4) ^ y) * 32 + (((part // 2) % 2) ^ xl) * 16
     col_ids = col_ids + ((part % 2) ^ core) * 8 + cols % 8
     dead = jnp.arange(slots, dtype=jnp.int32)[None, :] >= live[:, None]
-    by_col = order_slots(*array_place(col_ids), row_ids, dead)
+    by_col = order_slots(col_ids, row_ids, dead)
     by_col = (after(by_col[0], sib_cot), by_col[1])
-    by_row = order_slots(*array_place(row_ids), col_ids, dead)
-
-    parts = block_pass(False, live, *by_col, own_tiles, sib_tiles, gathered)
+    by_row = order_slots(row_ids, col_ids, dead)
+
+    parts, tiles = block_pass(False, live, by_col, (own_tiles, sib_tiles), gathered)
     own_sums = collect(parts, GC_LINKS)
     sib_sums = move(own_sums, core=1)
 
     activations, mixed = dense(core_arg, weight, cotangent, sib_cot, own_sums, sib_sums)
 
     gathered = spread(mixed, GC_LINKS, extra=EXTRA)
-    parts = block_pass(True, live, *by_row, own_tiles, sib_tiles, gathered)
+    parts, _ = block_pass(True, live, by_row, tiles, gathered)
     grads, wgrad = collect(parts, GR_LINKS, EXTRA)
     last = move(jnp.concatenate([grads[8:], wgrad]), core=1)
     feature_grad = turn_back(core_arg, grads[:8], last)

time: 200 us -> 187 us (0.935); the launches traced: 201 us -> 185 us
  waiting for transfers between devices: 113 us -> 83.8 us
  starting transfers between devices: 52.4 us -> 59.8 us
  local copies, waits for them, and re-layouts: 1.7 us -> 8.06 us
    ppermute x42, waiting for transfers between devices: 113 us -> 83.8 us  [move(): return lax.ppermute(value, AXES, pairs)]
    ppermute x42, starting transfers between devices: 52.4 us -> 59.8 us  [move(): return lax.ppermute(value, AXES, pairs)]
    unnamed x18 -> x31, local copies, waits for them, and re-layouts: 1.27 us -> 7.7 us
    pallas_call x2 -> x6, Pallas kernels: 15 us -> 15.3 us  [the longest x4 8.47 us: late_pass(): pl.pallas_call(functools.partial(late_kernel, adjoint, kept), out_shape=t...]
  transfers between devices with their start and end apart: 42 -> 42, of which waited for: 30 -> 28; matrix products, arithmetic and copies ran while one was open for 5% -> 6% of each run, Pallas kernels for 0% -> 6%
where the time goes in v2:
time: 187 us; the launch traced here: 185 us
  waiting for transfers between devices  83.8 us (45%)
  starting transfers between devices  59.8 us (32%)
  Pallas kernels  20.9 us (11%)
  other arithmetic  10.7 us (6%)
  local copies, waits for them, and re-layouts  8.06 us (4%)
  between operations  1.87 us (1%)
    ppermute x42, waiting for transfers between devices, move(): return lax.ppermute(value, AXES, pairs)  83.8 us
    ppermute x42, starting transfers between devices, move(): return lax.ppermute(value, AXES, pairs)  59.8 us
    pallas_call x4, Pallas kernels, late_pass(): pl.pallas_call(functools.partial(late_kernel, adjoint, kept), out_shape=t...  8.47 us
    convert_element_type x23, other arithmetic, add_all(): return total.astype(BF16)  8.15 us
    unnamed x31, local copies, waits for them, and re-layouts  7.7 us
    pallas_call x1, Pallas kernels, dense(): pl.pallas_call(dense_kernel, out_shape=[jax.ShapeDtypeStruct(own_cot.shap...  4.4 us
    pallas_call x1, Pallas kernels, early_pass(): pl.pallas_call(load_kernel, out_shape=[TOTAL, jax.ShapeDtypeStruct((2 * s...  4.19 us
  transfers between devices with their start and end apart: 42, of which 28 were waited for; matrix products, arithmetic and copies ran while one was open for 6% of the time, Pallas kernels for 6%

profile of v2, /device:TPU:0, one launch (start us, length us, event | category | flops | bytes accessed | tf_op | source)
XLA Modules:
  0.0 185.2 jit_solution(14293704208536695258)
XLA Ops:
  0.7 2.1 %collective-permute-done.sib_ref = bf16[1024,256]{1,0:T(8,128)(2,1)S(1)} collective-permute-done((bf16[1024,256]{1,0:T(8,128)(2,1)}, bf16[1024,256]{1,0:T(8,128)(2,1)S(1)}, u32[]{:S(2)}, u32[]{:S(2)}) %collective-permute-start) | collective-permute-done | bytes 524320 | tf_op jit(solution)/shard_map/ppermute | solution.py:41
  2.8 1.0 copy-done.6
  5.0 3.2 %collective-permute-start.1 = (bf16[5,128,128]{2,1,0:T(8,128)(2,1)S(1)}, bf16[5,128,128]{2,1,0:T(8,128)(2,1)S(1)}, u32[]{:S(2)}, u32[]{:S(2)}) collective-permute-start(bf16[5,128,128]{2,1,0:T(8,128)(2,1)S(1)} %get-tuple-element.30), channel_id=1, source_target_pairs={{0,96},{1,97},{2,98},{3,99},{4,100},{5,101},{6,102},{7,103},{8,104... | collective-permute-start | bytes 491528 | tf_op jit(solution)/shard_map/ppermute | solution.py:41
  8.5 1.6 collective-permute-start.6
  10.1 2.9 %collective-permute-done.1 = bf16[5,128,128]{2,1,0:T(8,128)(2,1)S(1)} collective-permute-done((bf16[5,128,128]{2,1,0:T(8,128)(2,1)S(1)}, bf16[5,128,128]{2,1,0:T(8,128)(2,1)S(1)}, u32[]{:S(2)}, u32[]{:S(2)}) %collective-permute-start.1) | collective-permute-done | bytes 163872 | tf_op jit(solution)/shard_map/ppermute | solution.py:41
  13.0 1.6 collective-permute-start.2
  14.6 3.0 %collective-permute-start.9 = (bf16[10,128,128]{2,1,0:T(8,128)(2,1)S(1)}, bf16[10,128,128]{2,1,0:T(8,128)(2,1)S(1)}, u32[]{:S(2)}, u32[]{:S(2)}) collective-permute-start(bf16[10,128,128]{2,1,0:T(8,128)(2,1)S(1)} %pad_maximum_fusion.8), channel_id=1, source_target_pairs={{0,96},{1,97},{2,98},{3,99},{4,100},{5,101},{6,102},{7,103},{8,104... | collective-permute-start | bytes 983048 | tf_op jit(solution)/shard_map/ppermute | solution.py:41
  18.4 4.0 %collective-permute-done.2 = bf16[10,128,128]{2,1,0:T(8,128)(2,1)S(1)} collective-permute-done((bf16[10,128,128]{2,1,0:T(8,128)(2,1)S(1)}, bf16[10,128,128]{2,1,0:T(8,128)(2,1)S(1)}, u32[]{:S(2)}, u32[]{:S(2)}) %collective-permute-start.2) | collective-permute-done | bytes 327712 | tf_op jit(solution)/shard_map/ppermute | solution.py:41
  22.5 1.8 collective-permute-start.12
  24.9 1.2 collective-permute-done.4
  26.1 1.5 collective-permute-start.11
  27.9 1.9 %collective-permute-done.7 = bf16[12,128,128]{2,1,0:T(8,128)(2,1)S(1)} collective-permute-done((bf16[12,128,128]{2,1,0:T(8,128)(2,1)S(1)}, bf16[12,128,128]{2,1,0:T(8,128)(2,1)S(1)}, u32[]{:S(2)}, u32[]{:S(2)}) %collective-permute-start.7) | collective-permute-done | bytes 393248 | tf_op jit(solution)/shard_map/ppermute | solution.py:41
  30.6 4.2 %early_pass.1 = (bf16[128,128,128]{2,1,0:T(8,128)(2,1)S(1)}, bf16[256,128,128]{2,1,0:T(8,128)(2,1)S(1)}) custom-call(s32[2]{0:T(128)S(1)} %add_reduce_fusion.live_ref, s32[256]{0:T(256)S(1)} %select_reduce_fusion.1.list_ref, s32[10]{0:T(128)S(1)} %convert_reduce_fusion.3.bound_ref, bf16[128,128,128]{2,1,0:T(8,128)(2,1)S(1)} %bitcast.31, ...), custom_call_target="tpu_custom_call" | custom-call | flops 268435456 | bytes 16777216 | tf_op jit(solution)/shard_map/early_pass/pallas_call | solution.py:311
  34.8 8.1 %collective-permute-done.11.rest_1_ = bf16[20,128,128]{2,1,0:T(8,128)(2,1)S(1)} collective-permute-done((bf16[20,128,128]{2,1,0:T(8,128)(2,1)S(1)}, bf16[20,128,128]{2,1,0:T(8,128)(2,1)S(1)}, u32[]{:S(2)}, u32[]{:S(2)}) %collective-permute-start.11) | collective-permute-done | bytes 655392 | tf_op jit(solution)/shard_map/ppermute | solution.py:41
  42.9 5.7 %collective-permute-done.10.rest_0_ = bf16[24,128,128]{2,1,0:T(8,128)(2,1)S(1)} collective-permute-done((bf16[24,128,128]{2,1,0:T(8,128)(2,1)S(1)}, bf16[24,128,128]{2,1,0:T(8,128)(2,1)S(1)}, u32[]{:S(2)}, u32[]{:S(2)}) %collective-permute-start.10) | collective-permute-done | bytes 786464 | tf_op jit(solution)/shard_map/ppermute | solution.py:41
  48.6 2.0 %sent_pass.1 = (bf16[24,128,128]{2,1,0:T(8,128)(2,1)S(1)}, bf16[20,128,128]{2,1,0:T(8,128)(2,1)S(1)}, bf16[20,128,128]{2,1,0:T(8,128)(2,1)S(1)}) custom-call(s32[256]{0:T(256)S(1)} %select_reduce_fusion.1.list_ref, s32[10]{0:T(128)S(1)} %convert_reduce_fusion.3.bound_ref, bf16[256,128,128]{2,1,0:T(8,128)(2,1)S(1)} %get-tuple-element.39.tiles, ...), custom_call_target="tpu_custom_call" | custom-call | flops 134217728 | bytes 8388608 | tf_op jit(solution)/shard_map/sent_pass/pallas_call | solution.py:325
  50.7 2.0 %collective-permute-start.19 = (bf16[20,128,128]{2,1,0:T(8,128)(2,1)S(1)}, bf16[20,128,128]{2,1,0:T(8,128)(2,1)S(1)}, u32[]{:S(2)}, u32[]{:S(2)}) collective-permute-start(bf16[20,128,128]{2,1,0:T(8,128)(2,1)S(1)} %get-tuple-element.46), channel_id=1, source_target_pairs={{0,1},{1,0},{2,3},{3,2},{4,5},{5,4},{6,7},{7,6},{8,9},{9,8},{10,11... | collective-permute-start | bytes 1966088 | tf_op jit(solution)/shard_map/ppermute | solution.py:41
  52.7 2.7 %collective-permute-start.16 = (bf16[20,128,128]{2,1,0:T(8,128)(2,1)S(1)}, bf16[20,128,128]{2,1,0:T(8,128)(2,1)S(1)}, u32[]{:S(2)}, u32[]{:S(2)}) collective-permute-start(bf16[20,128,128]{2,1,0:T(8,128)(2,1)S(1)} %get-tuple-element.44), channel_id=1, source_target_pairs={{0,4},{1,5},{2,6},{3,7},{4,0},{5,1},{6,2},{7,3},{8,12},{9,13},{10,... | collective-permute-start | bytes 1966088 | tf_op jit(solution)/shard_map/ppermute | solution.py:41
  55.4 3.5 %collective-permute-start.13 = (bf16[24,128,128]{2,1,0:T(8,128)(2,1)S(1)}, bf16[24,128,128]{2,1,0:T(8,128)(2,1)S(1)}, u32[]{:S(2)}, u32[]{:S(2)}) collective-permute-start(bf16[24,128,128]{2,1,0:T(8,128)(2,1)S(1)} %get-tuple-element.42), channel_id=1, source_target_pairs={{0,3},{1,2},{2,1},{3,0},{4,7},{5,6},{6,5},{7,4},{8,11},{9,10},{10,... | collective-permute-start | bytes 2359304 | tf_op jit(solution)/shard_map/ppermute | solution.py:41
  58.8 2.0 %kept_pass.1 = (bf16[24,128,128]{2,1,0:T(8,128)(2,1)S(1)}, bf16[20,128,128]{2,1,0:T(8,128)(2,1)S(1)}, bf16[20,128,128]{2,1,0:T(8,128)(2,1)S(1)}) custom-call(s32[256]{0:T(256)S(1)} %select_reduce_fusion.1.list_ref, s32[10]{0:T(128)S(1)} %convert_reduce_fusion.3.bound_ref, bf16[256,128,128]{2,1,0:T(8,128)(2,1)S(1)} %get-tuple-element.39.tiles, ...), custom_call_target="tpu_custom_call" | custom-call | flops 134217728 | bytes 8388608 | tf_op jit(solution)/shard_map/kept_pass/pallas_call | solution.py:325
  60.9 3.7 %collective-permute-done.19 = bf16[20,128,128]{2,1,0:T(8,128)(2,1)S(1)} collective-permute-done((bf16[20,128,128]{2,1,0:T(8,128)(2,1)S(1)}, bf16[20,128,128]{2,1,0:T(8,128)(2,1)S(1)}, u32[]{:S(2)}, u32[]{:S(2)}) %collective-permute-start.19) | collective-permute-done | bytes 655392 | tf_op jit(solution)/shard_map/ppermute | solution.py:41
  64.7 3.7 %collective-permute-start.20 = (bf16[10,128,128]{2,1,0:T(8,128)(2,1)S(1)}, bf16[10,128,128]{2,1,0:T(8,128)(2,1)S(1)}, u32[]{:S(2)}, u32[]{:S(2)}) collective-permute-start(bf16[10,128,128]{2,1,0:T(8,128)(2,1)S(1)} %add_convert_fusion.4), channel_id=1, source_target_pairs={{0,4},{1,5},{2,6},{3,7},{4,0},{5,1},{6,2},{7,3},{8,12},{9,13},{10,... | collective-permute-start | bytes 983048 | tf_op jit(solution)/shard_map/ppermute | solution.py:41
  68.4 1.5 collective-permute-done.16
  70.0 2.8 %collective-permute-start.17 = (bf16[10,128,128]{2,1,0:T(8,128)(2,1)S(1)}, bf16[10,128,128]{2,1,0:T(8,128)(2,1)S(1)}, u32[]{:S(2)}, u32[]{:S(2)}) collective-permute-start(bf16[10,128,128]{2,1,0:T(8,128)(2,1)S(1)} %add_convert_fusion.5), channel_id=1, source_target_pairs={{0,3},{1,2},{2,1},{3,0},{4,7},{5,6},{6,5},{7,4},{8,11},{9,10},{10,... | collective-permute-start | bytes 983048 | tf_op jit(solution)/shard_map/ppermute | solution.py:41
  72.8 4.5 %collective-permute-done.13 = bf16[24,128,128]{2,1,0:T(8,128)(2,1)S(1)} collective-permute-done((bf16[24,128,128]{2,1,0:T(8,128)(2,1)S(1)}, bf16[24,128,128]{2,1,0:T(8,128)(2,1)S(1)}, u32[]{:S(2)}, u32[]{:S(2)}) %collective-permute-start.13) | collective-permute-done | bytes 786464 | tf_op jit(solution)/shard_map/ppermute | solution.py:41
  78.1 2.9 %collective-permute-start.21 = (bf16[5,128,128]{2,1,0:T(8,128)(2,1)S(1)}, bf16[5,128,128]{2,1,0:T(8,128)(2,1)S(1)}, u32[]{:S(2)}, u32[]{:S(2)}) collective-permute-start(bf16[5,128,128]{2,1,0:T(8,128)(2,1)S(1)} %add_convert_fusion.15), channel_id=1, source_target_pairs={{0,3},{1,2},{2,1},{3,0},{4,7},{5,6},{6,5},{7,4},{8,11},{9,10},{10,... | collective-permute-start | bytes 491528 | tf_op jit(solution)/shard_map/ppermute | solution.py:41
  80.9 1.6 collective-permute-done.17
  83.1 1.6 collective-permute-done.21
  84.8 1.3 collective-permute-done.14
  86.3 1.8 collective-permute-done.18
  88.1 5.3 %collective-permute-done.15 = bf16[6,128,128]{2,1,0:T(8,128)(2,1)S(1)} collective-permute-done((bf16[6,128,128]{2,1,0:T(8,128)(2,1)S(1)}, bf16[6,128,128]{2,1,0:T(8,128)(2,1)S(1)}, u32[]{:S(2)}, u32[]{:S(2)}) %collective-permute-start.15) | collective-permute-done | bytes 196640 | tf_op jit(solution)/shard_map/ppermute | solution.py:41
  93.9 1.9 %collective-permute-done.22.sib_sums = bf16[16,128,128]{2,1,0:T(8,128)(2,1)S(1)} collective-permute-done((bf16[16,128,128]{2,1,0:T(8,128)(2,1)S(1)}, bf16[16,128,128]{2,1,0:T(8,128)(2,1)S(1)}, u32[]{:S(2)}, u32[]{:S(2)}) %collective-permute-start.22) | collective-permute-done | bytes 524320 | tf_op jit(solution)/shard_map/ppermute | solution.py:41
  95.8 4.4 %dense.1 = (bf16[1024,256]{1,0:T(8,128)(2,1)}, bf16[6,128,128]{2,1,0:T(8,128)(2,1)S(1)}, bf16[7,128,128]{2,1,0:T(8,128)(2,1)S(1)}, bf16[5,128,128]{2,1,0:T(8,128)(2,1)S(1)}) custom-call(s32[1]{0:T(128)} %bitcast.core_ref, bf16[256,256]{1,0:T(8,128)(2,1)S(1)} %copy-done.7, bf16[1024,256]{1,0:T(8,128)(2,1)S(1)} %copy-done.5, ...), custom_call_target="tpu_custom_call" | custom-call | flops 536870912 | bytes 4194304 | tf_op jit(solution)/shard_map/dense/pallas_call | solution.py:380
  100.6 2.8 %collective-permute-start.27 = (bf16[5,128,128]{2,1,0:T(8,128)(2,1)S(1)}, bf16[5,128,128]{2,1,0:T(8,128)(2,1)S(1)}, u32[]{:S(2)}, u32[]{:S(2)}) collective-permute-start(bf16[5,128,128]{2,1,0:T(8,128)(2,1)S(1)} %get-tuple-element.50), channel_id=1, source_target_pairs={{0,3},{1,2},{2,1},{3,0},{4,7},{5,6},{6,5},{7,4},{8,11},{9,10},{10,... | collective-permute-start | bytes 491528 | tf_op jit(solution)/shard_map/ppermute | solution.py:41
  103.4 5.4 %collective-permute-done.23 = bf16[6,128,128]{2,1,0:T(8,128)(2,1)S(1)} collective-permute-done((bf16[6,128,128]{2,1,0:T(8,128)(2,1)S(1)}, bf16[6,128,128]{2,1,0:T(8,128)(2,1)S(1)}, u32[]{:S(2)}, u32[]{:S(2)}) %collective-permute-start.23) | collective-permute-done | bytes 196640 | tf_op jit(solution)/shard_map/ppermute | solution.py:41
  108.8 1.8 collective-permute-start.24
  110.7 2.8 %collective-permute-start.26 = (bf16[12,128,128]{2,1,0:T(8,128)(2,1)S(1)}, bf16[12,128,128]{2,1,0:T(8,128)(2,1)S(1)}, u32[]{:S(2)}, u32[]{:S(2)}) collective-permute-start(bf16[12,128,128]{2,1,0:T(8,128)(2,1)S(1)} %pad_maximum_fusion.4), channel_id=1, source_target_pairs={{0,3},{1,2},{2,1},{3,0},{4,7},{5,6},{6,5},{7,4},{8,11},{9,10},{10,... | collective-permute-start | bytes 1179656 | tf_op jit(solution)/shard_map/ppermute | solution.py:41
  113.9 4.9 %collective-permute-done.24 = bf16[12,128,128]{2,1,0:T(8,128)(2,1)S(1)} collective-permute-done((bf16[12,128,128]{2,1,0:T(8,128)(2,1)S(1)}, bf16[12,128,128]{2,1,0:T(8,128)(2,1)S(1)}, u32[]{:S(2)}, u32[]{:S(2)}) %collective-permute-start.24) | collective-permute-done | bytes 393248 | tf_op jit(solution)/shard_map/ppermute | solution.py:41
  118.9 2.8 %collective-permute-start.29 = (bf16[24,128,128]{2,1,0:T(8,128)(2,1)S(1)}, bf16[24,128,128]{2,1,0:T(8,128)(2,1)S(1)}, u32[]{:S(2)}, u32[]{:S(2)}) collective-permute-start(bf16[24,128,128]{2,1,0:T(8,128)(2,1)S(1)} %constant_dynamic-update-slice_fusion.9.rest_0_), channel_id=1, source_target_pairs={{0,3},{1,2},{2,1},{3,0},{4,7},{5,6},{6,5},{7,4},{8,11},{9,10},{10,... | collective-permute-start | bytes 2359304 | tf_op jit(solution)/shard_map/ppermute | solution.py:41
  124.2 2.7 %early_adjoint.1.before = bf16[128,128,128]{2,1,0:T(8,128)(2,1)S(1)} custom-call(s32[256]{0:T(256)S(1)} %select_reduce_fusion.list_ref, s32[10]{0:T(128)S(1)} %convert_reduce_fusion.2.bound_ref, bf16[256,128,128]{2,1,0:T(8,128)(2,1)S(1)} %get-tuple-element.39.tiles, bf16[24,128,128]{2,1,0:T(8,128)(2,1)S(1)} %constant_dynamic-update-slice_fusion.9.rest_0_, ...), custom_call_target="tpu_custom_call" | custom-call | flops 268435456 | bytes 16777216 | tf_op jit(solution)/shard_map/early_adjoint/pallas_call | solution.py:300
  126.9 10.5 %collective-permute-done.31.rest_2_ = bf16[20,128,128]{2,1,0:T(8,128)(2,1)S(1)} collective-permute-done((bf16[20,128,128]{2,1,0:T(8,128)(2,1)S(1)}, bf16[20,128,128]{2,1,0:T(8,128)(2,1)S(1)}, u32[]{:S(2)}, u32[]{:S(2)}) %collective-permute-start.31) | collective-permute-done | bytes 655392 | tf_op jit(solution)/shard_map/ppermute | solution.py:41
  137.4 1.9 %collective-permute-done.30.rest_1_ = bf16[22,128,128]{2,1,0:T(8,128)(2,1)S(1)} collective-permute-done((bf16[22,128,128]{2,1,0:T(8,128)(2,1)S(1)}, bf16[22,128,128]{2,1,0:T(8,128)(2,1)S(1)}, u32[]{:S(2)}, u32[]{:S(2)}) %collective-permute-start.30) | collective-permute-done | bytes 720928 | tf_op jit(solution)/shard_map/ppermute | solution.py:41
  139.3 2.6 %sent_adjoint.1 = (bf16[24,128,128]{2,1,0:T(8,128)(2,1)S(1)}, bf16[22,128,128]{2,1,0:T(8,128)(2,1)S(1)}, bf16[20,128,128]{2,1,0:T(8,128)(2,1)}) custom-call(s32[256]{0:T(256)S(1)} %select_reduce_fusion.list_ref, s32[10]{0:T(128)S(1)} %convert_reduce_fusion.2.bound_ref, bf16[256,128,128]{2,1,0:T(8,128)(2,1)S(1)} %get-tuple-element.39.tiles, ...), custom_call_target="tpu_custom_call" | custom-call | flops 134217728 | bytes 8388608 | tf_op jit(solution)/shard_map/sent_adjoint/pallas_call | solution.py:325
  142.7 0.9 collective-permute-start.35
  144.0 3.2 %collective-permute-start.39 = (bf16[24,128,128]{2,1,0:T(8,128)(2,1)}, bf16[24,128,128]{2,1,0:T(8,128)(2,1)S(1)}, u32[]{:S(2)}, u32[]{:S(2)}) collective-permute-start(bf16[24,128,128]{2,1,0:T(8,128)(2,1)} %copy-done.8), channel_id=1, source_target_pairs={{0,96},{1,97},{2,98},{3,99},{4,100},{5,101},{6,102},{7,103},{8,104... | collective-permute-start | bytes 2359304 | tf_op jit(solution)/shard_map/ppermute | solution.py:41
  147.2 3.4 %copy-done.1 = bf16[256,128,128]{2,1,0:T(8,128)(2,1)S(1)} copy-done((bf16[256,128,128]{2,1,0:T(8,128)(2,1)S(1)}, bf16[256,128,128]{2,1,0:T(8,128)(2,1)}, u32[]{:S(2)}) %copy-start.1) | copy-done | bytes 8388632
  150.6 2.2 %copy-done.3 = bf16[128,128,128]{2,1,0:T(8,128)(2,1)S(1)} copy-done((bf16[128,128,128]{2,1,0:T(8,128)(2,1)S(1)}, bf16[128,128,128]{2,1,0:T(8,128)(2,1)}, u32[]{:S(2)}) %copy-start.3) | copy-done | bytes 4194328
  152.8 1.8 kept_adjoint.1
  154.6 2.4 %collective-permute-done.35 = bf16[20,128,128]{2,1,0:T(8,128)(2,1)} collective-permute-done((bf16[20,128,128]{2,1,0:T(8,128)(2,1)}, bf16[20,128,128]{2,1,0:T(8,128)(2,1)}, u32[]{:S(2)}, u32[]{:S(2)}) %collective-permute-start.35) | collective-permute-done | bytes 655392 | tf_op jit(solution)/shard_map/ppermute | solution.py:41
  156.9 1.1 add_convert_fusion.2
  158.0 1.1 collective-permute-start.36
  160.9 1.1 add_convert_fusion.3
  162.0 3.6 %collective-permute-start.33 = (bf16[12,128,128]{2,1,0:T(8,128)(2,1)S(1)}, bf16[12,128,128]{2,1,0:T(8,128)(2,1)S(1)}, u32[]{:S(2)}, u32[]{:S(2)}) collective-permute-start(bf16[12,128,128]{2,1,0:T(8,128)(2,1)S(1)} %pad_maximum_fusion.5), channel_id=1, source_target_pairs={{0,96},{1,97},{2,98},{3,99},{4,100},{5,101},{6,102},{7,103},{8,104... | collective-permute-start | bytes 1179656 | tf_op jit(solution)/shard_map/ppermute | solution.py:41
  165.7 2.4 %collective-permute-start.40 = (bf16[12,128,128]{2,1,0:T(8,128)(2,1)S(1)}, bf16[12,128,128]{2,1,0:T(8,128)(2,1)S(1)}, u32[]{:S(2)}, u32[]{:S(2)}) collective-permute-start(bf16[12,128,128]{2,1,0:T(8,128)(2,1)S(1)} %add_convert_fusion), channel_id=1, source_target_pairs={{0,32},{1,33},{2,34},{3,35},{4,36},{5,37},{6,38},{7,39},{8,40},{9,... | collective-permute-start | bytes 1179656 | tf_op jit(solution)/shard_map/ppermute | solution.py:41
  168.1 1.0 add_convert_fusion.11
  169.1 1.0 collective-permute-start.37
  170.1 3.0 %collective-permute-done.33 = bf16[12,128,128]{2,1,0:T(8,128)(2,1)S(1)} collective-permute-done((bf16[12,128,128]{2,1,0:T(8,128)(2,1)S(1)}, bf16[12,128,128]{2,1,0:T(8,128)(2,1)S(1)}, u32[]{:S(2)}, u32[]{:S(2)}) %collective-permute-start.33) | collective-permute-done | bytes 393248 | tf_op jit(solution)/shard_map/ppermute | solution.py:41
  173.1 1.0 add_convert_fusion.13
  174.1 2.2 %collective-permute-start.34 = (bf16[7,128,128]{2,1,0:T(8,128)(2,1)S(1)}, bf16[7,128,128]{2,1,0:T(8,128)(2,1)S(1)}, u32[]{:S(2)}, u32[]{:S(2)}) collective-permute-start(bf16[7,128,128]{2,1,0:T(8,128)(2,1)S(1)} %pad_maximum_fusion.11), channel_id=1, source_target_pairs={{0,32},{1,33},{2,34},{3,35},{4,36},{5,37},{6,38},{7,39},{8,40},{9,... | collective-permute-start | bytes 688136 | tf_op jit(solution)/shard_map/ppermute | solution.py:41
  176.4 1.0 add_convert_fusion.10
  177.9 2.5 %collective-permute-done.34 = bf16[7,128,128]{2,1,0:T(8,128)(2,1)S(1)} collective-permute-done((bf16[7,128,128]{2,1,0:T(8,128)(2,1)S(1)}, bf16[7,128,128]{2,1,0:T(8,128)(2,1)S(1)}, u32[]{:S(2)}, u32[]{:S(2)}) %collective-permute-start.34) | collective-permute-done | bytes 229408 | tf_op jit(solution)/shard_map/ppermute | solution.py:41
  180.4 1.0 add_convert_fusion.12
  181.6 1.6 collective-permute-done.41
  184.2 1.0 turn_back.1
  (124 shorter events, 13.8 us)
Async XLA Ops:
  0.6 23.6 %copy-start.5 = (bf16[1024,256]{1,0:T(8,128)(2,1)S(1)}, bf16[1024,256]{1,0:T(8,128)(2,1)}, u32[]{:S(2)}) copy-start(bf16[1024,256]{1,0:T(8,128)(2,1)} %own_cot.1) | copy-start | bytes 1572868
  0.6 2.2 %collective-permute-start = (bf16[1024,256]{1,0:T(8,128)(2,1)}, bf16[1024,256]{1,0:T(8,128)(2,1)S(1)}, u32[]{:S(2)}, u32[]{:S(2)}) collective-permute-start(bf16[1024,256]{1,0:T(8,128)(2,1)} %own_ref.1), channel_id=1, source_target_pairs={{0,8},{1,9},{2,10},{3,11},{4,12},{5,13},{6,14},{7,15},{8,0},{9,1},... | collective-permute-start | bytes 1572872 | tf_op jit(solution)/shard_map/ppermute | solution.py:41
  2.8 1.0 copy-start.6
  3.9 20.3 %copy-start.9 = (s32[1,1,128]{2,1,0:T(1,128)S(1)}, s32[1,1,128]{2,1,0:T(1,128)}, u32[]{:S(2)}) copy-start(s32[1,1,128]{2,1,0:T(1,128)} %param.12) | copy-start | bytes 1540
  3.9 20.3 %copy-start.10 = (s32[1,1,128]{2,1,0:T(1,128)S(1)}, s32[1,1,128]{2,1,0:T(1,128)}, u32[]{:S(2)}) copy-start(s32[1,1,128]{2,1,0:T(1,128)} %param.11) | copy-start | bytes 1540
  4.1 26.5 %collective-permute-start.5 = (bf16[128,128,128]{2,1,0:T(8,128)(2,1)}, bf16[128,128,128]{2,1,0:T(8,128)(2,1)}, u32[]{:S(2)}, u32[]{:S(2)}) collective-permute-start(bf16[128,128,128]{2,1,0:T(8,128)(2,1)} %bitcast.30), channel_id=1, source_target_pairs={{0,8},{1,9},{2,10},{3,11},{4,12},{5,13},{6,14},{7,15},{8,0},{9,1},... | collective-permute-start | bytes 12582920 | tf_op jit(solution)/shard_map/ppermute | solution.py:41
  5.0 25.5 %copy-start.4 = (bf16[1,1,128,128,128]{4,3,2,1,0:T(8,128)(2,1)S(1)}, bf16[1,1,128,128,128]{4,3,2,1,0:T(8,128)(2,1)}, u32[]{:S(2)}) copy-start(bf16[1,1,128,128,128]{4,3,2,1,0:T(8,128)(2,1)} %param.10) | copy-start | bytes 12582916
  5.0 7.9 %collective-permute-start.1 = (bf16[5,128,128]{2,1,0:T(8,128)(2,1)S(1)}, bf16[5,128,128]{2,1,0:T(8,128)(2,1)S(1)}, u32[]{:S(2)}, u32[]{:S(2)}) collective-permute-start(bf16[5,128,128]{2,1,0:T(8,128)(2,1)S(1)} %get-tuple-element.30), channel_id=1, source_target_pairs={{0,96},{1,97},{2,98},{3,99},{4,100},{5,101},{6,102},{7,103},{8,104... | collective-permute-start | bytes 491528 | tf_op jit(solution)/shard_map/ppermute | solution.py:41
  8.3 6.3 %collective-permute-start.8 = (bf16[5,128,128]{2,1,0:T(8,128)(2,1)S(1)}, bf16[5,128,128]{2,1,0:T(8,128)(2,1)S(1)}, u32[]{:S(2)}, u32[]{:S(2)}) collective-permute-start(bf16[5,128,128]{2,1,0:T(8,128)(2,1)S(1)} %get-tuple-element.38), channel_id=1, source_target_pairs={{0,32},{1,33},{2,34},{3,35},{4,36},{5,37},{6,38},{7,39},{8,40},{9,... | collective-permute-start | bytes 491528 | tf_op jit(solution)/shard_map/ppermute | solution.py:41
  8.5 9.2 %collective-permute-start.6 = (bf16[6,128,128]{2,1,0:T(8,128)(2,1)S(1)}, bf16[6,128,128]{2,1,0:T(8,128)(2,1)S(1)}, u32[]{:S(2)}, u32[]{:S(2)}) collective-permute-start(bf16[6,128,128]{2,1,0:T(8,128)(2,1)S(1)} %get-tuple-element.36), channel_id=1, source_target_pairs={{0,16},{1,17},{2,18},{3,19},{4,20},{5,21},{6,22},{7,23},{8,24},{9,... | collective-permute-start | bytes 589832 | tf_op jit(solution)/shard_map/ppermute | solution.py:41
  13.0 9.4 %collective-permute-start.2 = (bf16[10,128,128]{2,1,0:T(8,128)(2,1)S(1)}, bf16[10,128,128]{2,1,0:T(8,128)(2,1)S(1)}, u32[]{:S(2)}, u32[]{:S(2)}) collective-permute-start(bf16[10,128,128]{2,1,0:T(8,128)(2,1)S(1)} %pad_maximum_fusion.7), channel_id=1, source_target_pairs={{0,16},{1,17},{2,18},{3,19},{4,20},{5,21},{6,22},{7,23},{8,24},{9,... | collective-permute-start | bytes 983048 | tf_op jit(solution)/shard_map/ppermute | solution.py:41
  14.6 10.3 %collective-permute-start.9 = (bf16[10,128,128]{2,1,0:T(8,128)(2,1)S(1)}, bf16[10,128,128]{2,1,0:T(8,128)(2,1)S(1)}, u32[]{:S(2)}, u32[]{:S(2)}) collective-permute-start(bf16[10,128,128]{2,1,0:T(8,128)(2,1)S(1)} %pad_maximum_fusion.8), channel_id=1, source_target_pairs={{0,96},{1,97},{2,98},{3,99},{4,100},{5,101},{6,102},{7,103},{8,104... | collective-permute-start | bytes 983048 | tf_op jit(solution)/shard_map/ppermute | solution.py:41
  17.7 12.1 %collective-permute-start.7 = (bf16[12,128,128]{2,1,0:T(8,128)(2,1)S(1)}, bf16[12,128,128]{2,1,0:T(8,128)(2,1)S(1)}, u32[]{:S(2)}, u32[]{:S(2)}) collective-permute-start(bf16[12,128,128]{2,1,0:T(8,128)(2,1)S(1)} %pad_maximum_fusion.2), channel_id=1, source_target_pairs={{0,32},{1,33},{2,34},{3,35},{4,36},{5,37},{6,38},{7,39},{8,40},{9,... | collective-permute-start | bytes 1179656 | tf_op jit(solution)/shard_map/ppermute | solution.py:41
  22.5 20.5 %collective-permute-start.12 = (bf16[20,128,128]{2,1,0:T(8,128)(2,1)S(1)}, bf16[20,128,128]{2,1,0:T(8,128)(2,1)S(1)}, u32[]{:S(2)}, u32[]{:S(2)}) collective-permute-start(bf16[20,128,128]{2,1,0:T(8,128)(2,1)S(1)} %constant_dynamic-update-slice_fusion.rest_2_), channel_id=1, source_target_pairs={{0,32},{1,33},{2,34},{3,35},{4,36},{5,37},{6,38},{7,39},{8,40},{9,... | collective-permute-start | bytes 1966088 | tf_op jit(solution)/shard_map/ppermute | solution.py:41
  24.2 6.3 %collective-permute-start.3 = (bf16[1024,256]{1,0:T(8,128)(2,1)S(1)}, bf16[1024,256]{1,0:T(8,128)(2,1)S(1)}, u32[]{:S(2)}, u32[]{:S(2)}) collective-permute-start(bf16[1024,256]{1,0:T(8,128)(2,1)S(1)} %copy-done.5), channel_id=1, source_target_pairs={{0,8},{1,9},{2,10},{3,11},{4,12},{5,13},{6,14},{7,15},{8,0},{9,1},... | collective-permute-start | bytes 1572872 | tf_op jit(solution)/shard_map/ppermute | solution.py:41
  24.9 1.3 collective-permute-start.4
  26.1 16.8 %collective-permute-start.11 = (bf16[20,128,128]{2,1,0:T(8,128)(2,1)S(1)}, bf16[20,128,128]{2,1,0:T(8,128)(2,1)S(1)}, u32[]{:S(2)}, u32[]{:S(2)}) collective-permute-start(bf16[20,128,128]{2,1,0:T(8,128)(2,1)S(1)} %constant_dynamic-update-slice_fusion.6.rest_1_), channel_id=1, source_target_pairs={{0,16},{1,17},{2,18},{3,19},{4,20},{5,21},{6,22},{7,23},{8,24},{9,... | collective-permute-start | bytes 1966088 | tf_op jit(solution)/shard_map/ppermute | solution.py:41
  29.9 18.7 %collective-permute-start.10 = (bf16[24,128,128]{2,1,0:T(8,128)(2,1)S(1)}, bf16[24,128,128]{2,1,0:T(8,128)(2,1)S(1)}, u32[]{:S(2)}, u32[]{:S(2)}) collective-permute-start(bf16[24,128,128]{2,1,0:T(8,128)(2,1)S(1)} %constant_dynamic-update-slice_fusion.3.rest_0_), channel_id=1, source_target_pairs={{0,96},{1,97},{2,98},{3,99},{4,100},{5,101},{6,102},{7,103},{8,104... | collective-permute-start | bytes 2359304 | tf_op jit(solution)/shard_map/ppermute | solution.py:41
  34.8 104.5 %copy-start = (bf16[256,128,128]{2,1,0:T(8,128)(2,1)}, bf16[256,128,128]{2,1,0:T(8,128)(2,1)S(1)}, u32[]{:S(2)}) copy-start(bf16[256,128,128]{2,1,0:T(8,128)(2,1)S(1)} %get-tuple-element.39.tiles) | copy-start | bytes 25165828
  50.7 13.9 %collective-permute-start.19 = (bf16[20,128,128]{2,1,0:T(8,128)(2,1)S(1)}, bf16[20,128,128]{2,1,0:T(8,128)(2,1)S(1)}, u32[]{:S(2)}, u32[]{:S(2)}) collective-permute-start(bf16[20,128,128]{2,1,0:T(8,128)(2,1)S(1)} %get-tuple-element.46), channel_id=1, source_target_pairs={{0,1},{1,0},{2,3},{3,2},{4,5},{5,4},{6,7},{7,6},{8,9},{9,8},{10,11... | collective-permute-start | bytes 1966088 | tf_op jit(solution)/shard_map/ppermute | solution.py:41
  52.7 17.2 %collective-permute-start.16 = (bf16[20,128,128]{2,1,0:T(8,128)(2,1)S(1)}, bf16[20,128,128]{2,1,0:T(8,128)(2,1)S(1)}, u32[]{:S(2)}, u32[]{:S(2)}) collective-permute-start(bf16[20,128,128]{2,1,0:T(8,128)(2,1)S(1)} %get-tuple-element.44), channel_id=1, source_target_pairs={{0,4},{1,5},{2,6},{3,7},{4,0},{5,1},{6,2},{7,3},{8,12},{9,13},{10,... | collective-permute-start | bytes 1966088 | tf_op jit(solution)/shard_map/ppermute | solution.py:41
  55.4 21.9 %collective-permute-start.13 = (bf16[24,128,128]{2,1,0:T(8,128)(2,1)S(1)}, bf16[24,128,128]{2,1,0:T(8,128)(2,1)S(1)}, u32[]{:S(2)}, u32[]{:S(2)}) collective-permute-start(bf16[24,128,128]{2,1,0:T(8,128)(2,1)S(1)} %get-tuple-element.42), channel_id=1, source_target_pairs={{0,3},{1,2},{2,1},{3,0},{4,7},{5,6},{6,5},{7,4},{8,11},{9,10},{10,... | collective-permute-start | bytes 2359304 | tf_op jit(solution)/shard_map/ppermute | solution.py:41
  64.7 31.1 %copy-start.7 = (bf16[256,256]{1,0:T(8,128)(2,1)S(1)}, bf16[256,256]{1,0:T(8,128)(2,1)}, u32[]{:S(2)}) copy-start(bf16[256,256]{1,0:T(8,128)(2,1)} %weight_ref.1) | copy-start | bytes 393220
  64.7 13.3 %collective-permute-start.20 = (bf16[10,128,128]{2,1,0:T(8,128)(2,1)S(1)}, bf16[10,128,128]{2,1,0:T(8,128)(2,1)S(1)}, u32[]{:S(2)}, u32[]{:S(2)}) collective-permute-start(bf16[10,128,128]{2,1,0:T(8,128)(2,1)S(1)} %add_convert_fusion.4), channel_id=1, source_target_pairs={{0,4},{1,5},{2,6},{3,7},{4,0},{5,1},{6,2},{7,3},{8,12},{9,13},{10,... | collective-permute-start | bytes 983048 | tf_op jit(solution)/shard_map/ppermute | solution.py:41
  70.0 12.6 %collective-permute-start.17 = (bf16[10,128,128]{2,1,0:T(8,128)(2,1)S(1)}, bf16[10,128,128]{2,1,0:T(8,128)(2,1)S(1)}, u32[]{:S(2)}, u32[]{:S(2)}) collective-permute-start(bf16[10,128,128]{2,1,0:T(8,128)(2,1)S(1)} %add_convert_fusion.5), channel_id=1, source_target_pairs={{0,3},{1,2},{2,1},{3,0},{4,7},{5,6},{6,5},{7,4},{8,11},{9,10},{10,... | collective-permute-start | bytes 983048 | tf_op jit(solution)/shard_map/ppermute | solution.py:41
  77.4 8.7 %collective-permute-start.14 = (bf16[12,128,128]{2,1,0:T(8,128)(2,1)S(1)}, bf16[12,128,128]{2,1,0:T(8,128)(2,1)S(1)}, u32[]{:S(2)}, u32[]{:S(2)}) collective-permute-start(bf16[12,128,128]{2,1,0:T(8,128)(2,1)S(1)} %add_convert_fusion.1), channel_id=1, source_target_pairs={{0,1},{1,0},{2,3},{3,2},{4,5},{5,4},{6,7},{7,6},{8,9},{9,8},{10,11... | collective-permute-start | bytes 1179656 | tf_op jit(solution)/shard_map/ppermute | solution.py:41
  78.1 6.6 %collective-permute-start.21 = (bf16[5,128,128]{2,1,0:T(8,128)(2,1)S(1)}, bf16[5,128,128]{2,1,0:T(8,128)(2,1)S(1)}, u32[]{:S(2)}, u32[]{:S(2)}) collective-permute-start(bf16[5,128,128]{2,1,0:T(8,128)(2,1)S(1)} %add_convert_fusion.15), channel_id=1, source_target_pairs={{0,3},{1,2},{2,1},{3,0},{4,7},{5,6},{6,5},{7,4},{8,11},{9,10},{10,... | collective-permute-start | bytes 491528 | tf_op jit(solution)/shard_map/ppermute | solution.py:41
  82.6 5.4 %collective-permute-start.18 = (bf16[5,128,128]{2,1,0:T(8,128)(2,1)S(1)}, bf16[5,128,128]{2,1,0:T(8,128)(2,1)S(1)}, u32[]{:S(2)}, u32[]{:S(2)}) collective-permute-start(bf16[5,128,128]{2,1,0:T(8,128)(2,1)S(1)} %add_convert_fusion.17), channel_id=1, source_target_pairs={{0,1},{1,0},{2,3},{3,2},{4,5},{5,4},{6,7},{7,6},{8,9},{9,8},{10,11... | collective-permute-start | bytes 491528 | tf_op jit(solution)/shard_map/ppermute | solution.py:41
  86.2 7.3 %collective-permute-start.15 = (bf16[6,128,128]{2,1,0:T(8,128)(2,1)S(1)}, bf16[6,128,128]{2,1,0:T(8,128)(2,1)S(1)}, u32[]{:S(2)}, u32[]{:S(2)}) collective-permute-start(bf16[6,128,128]{2,1,0:T(8,128)(2,1)S(1)} %add_convert_fusion.9), channel_id=1, source_target_pairs={{0,4},{1,5},{2,6},{3,7},{4,0},{5,1},{6,2},{7,3},{8,12},{9,13},{10,... | collective-permute-start | bytes 589832 | tf_op jit(solution)/shard_map/ppermute | solution.py:41
  93.6 2.2 %collective-permute-start.22 = (bf16[16,128,128]{2,1,0:T(8,128)(2,1)S(1)}, bf16[16,128,128]{2,1,0:T(8,128)(2,1)S(1)}, u32[]{:S(2)}, u32[]{:S(2)}) collective-permute-start(bf16[16,128,128]{2,1,0:T(8,128)(2,1)S(1)} %pad_maximum_fusion.1.own_sums), channel_id=1, source_target_pairs={{0,8},{1,9},{2,10},{3,11},{4,12},{5,13},{6,14},{7,15},{8,0},{9,1},... | collective-permute-start | bytes 1572872 | tf_op jit(solution)/shard_map/ppermute | solution.py:41
  100.2 10.4 %collective-permute-start.25 = (bf16[7,128,128]{2,1,0:T(8,128)(2,1)S(1)}, bf16[7,128,128]{2,1,0:T(8,128)(2,1)S(1)}, u32[]{:S(2)}, u32[]{:S(2)}) collective-permute-start(bf16[7,128,128]{2,1,0:T(8,128)(2,1)S(1)} %get-tuple-element.49), channel_id=1, source_target_pairs={{0,1},{1,0},{2,3},{3,2},{4,5},{5,4},{6,7},{7,6},{8,9},{9,8},{10,11... | collective-permute-start | bytes 688136 | tf_op jit(solution)/shard_map/ppermute | solution.py:41
  100.5 8.2 %collective-permute-start.23 = (bf16[6,128,128]{2,1,0:T(8,128)(2,1)S(1)}, bf16[6,128,128]{2,1,0:T(8,128)(2,1)S(1)}, u32[]{:S(2)}, u32[]{:S(2)}) collective-permute-start(bf16[6,128,128]{2,1,0:T(8,128)(2,1)S(1)} %get-tuple-element.48), channel_id=1, source_target_pairs={{0,4},{1,5},{2,6},{3,7},{4,0},{5,1},{6,2},{7,3},{8,12},{9,13},{10,... | collective-permute-start | bytes 589832 | tf_op jit(solution)/shard_map/ppermute | solution.py:41
  100.6 12.9 %collective-permute-start.27 = (bf16[5,128,128]{2,1,0:T(8,128)(2,1)S(1)}, bf16[5,128,128]{2,1,0:T(8,128)(2,1)S(1)}, u32[]{:S(2)}, u32[]{:S(2)}) collective-permute-start(bf16[5,128,128]{2,1,0:T(8,128)(2,1)S(1)} %get-tuple-element.50), channel_id=1, source_target_pairs={{0,3},{1,2},{2,1},{3,0},{4,7},{5,6},{6,5},{7,4},{8,11},{9,10},{10,... | collective-permute-start | bytes 491528 | tf_op jit(solution)/shard_map/ppermute | solution.py:41
  108.8 10.1 %collective-permute-start.24 = (bf16[12,128,128]{2,1,0:T(8,128)(2,1)S(1)}, bf16[12,128,128]{2,1,0:T(8,128)(2,1)S(1)}, u32[]{:S(2)}, u32[]{:S(2)}) collective-permute-start(bf16[12,128,128]{2,1,0:T(8,128)(2,1)S(1)} %pad_maximum_fusion.3), channel_id=1, source_target_pairs={{0,1},{1,0},{2,3},{3,2},{4,5},{5,4},{6,7},{7,6},{8,9},{9,8},{10,11... | collective-permute-start | bytes 1179656 | tf_op jit(solution)/shard_map/ppermute | solution.py:41
  110.7 11.8 %collective-permute-start.26 = (bf16[12,128,128]{2,1,0:T(8,128)(2,1)S(1)}, bf16[12,128,128]{2,1,0:T(8,128)(2,1)S(1)}, u32[]{:S(2)}, u32[]{:S(2)}) collective-permute-start(bf16[12,128,128]{2,1,0:T(8,128)(2,1)S(1)} %pad_maximum_fusion.4), channel_id=1, source_target_pairs={{0,3},{1,2},{2,1},{3,0},{4,7},{5,6},{6,5},{7,4},{8,11},{9,10},{10,... | collective-permute-start | bytes 1179656 | tf_op jit(solution)/shard_map/ppermute | solution.py:41
  113.5 9.6 %collective-permute-start.28 = (bf16[10,128,128]{2,1,0:T(8,128)(2,1)S(1)}, bf16[10,128,128]{2,1,0:T(8,128)(2,1)S(1)}, u32[]{:S(2)}, u32[]{:S(2)}) collective-permute-start(bf16[10,128,128]{2,1,0:T(8,128)(2,1)S(1)} %pad_maximum_fusion.9), channel_id=1, source_target_pairs={{0,4},{1,5},{2,6},{3,7},{4,0},{5,1},{6,2},{7,3},{8,12},{9,13},{10,... | collective-permute-start | bytes 983048 | tf_op jit(solution)/shard_map/ppermute | solution.py:41
  118.9 20.4 %collective-permute-start.29 = (bf16[24,128,128]{2,1,0:T(8,128)(2,1)S(1)}, bf16[24,128,128]{2,1,0:T(8,128)(2,1)S(1)}, u32[]{:S(2)}, u32[]{:S(2)}) collective-permute-start(bf16[24,128,128]{2,1,0:T(8,128)(2,1)S(1)} %constant_dynamic-update-slice_fusion.9.rest_0_), channel_id=1, source_target_pairs={{0,3},{1,2},{2,1},{3,0},{4,7},{5,6},{6,5},{7,4},{8,11},{9,10},{10,... | collective-permute-start | bytes 2359304 | tf_op jit(solution)/shard_map/ppermute | solution.py:41
  122.6 16.6 %collective-permute-start.30 = (bf16[22,128,128]{2,1,0:T(8,128)(2,1)S(1)}, bf16[22,128,128]{2,1,0:T(8,128)(2,1)S(1)}, u32[]{:S(2)}, u32[]{:S(2)}) collective-permute-start(bf16[22,128,128]{2,1,0:T(8,128)(2,1)S(1)} %pad_maximum_fusion.rest_1_.rest_3_), channel_id=1, source_target_pairs={{0,4},{1,5},{2,6},{3,7},{4,0},{5,1},{6,2},{7,3},{8,12},{9,13},{10,... | collective-permute-start | bytes 2162696 | tf_op jit(solution)/shard_map/ppermute | solution.py:41
  123.2 14.2 %collective-permute-start.31 = (bf16[20,128,128]{2,1,0:T(8,128)(2,1)S(1)}, bf16[20,128,128]{2,1,0:T(8,128)(2,1)S(1)}, u32[]{:S(2)}, u32[]{:S(2)}) collective-permute-start(bf16[20,128,128]{2,1,0:T(8,128)(2,1)S(1)} %constant_dynamic-update-slice_fusion.12.rest_2_), channel_id=1, source_target_pairs={{0,1},{1,0},{2,3},{3,2},{4,5},{5,4},{6,7},{7,6},{8,9},{9,8},{10,11... | collective-permute-start | bytes 1966088 | tf_op jit(solution)/shard_map/ppermute | solution.py:41
  126.9 15.0 %copy-start.2 = (bf16[128,128,128]{2,1,0:T(8,128)(2,1)}, bf16[128,128,128]{2,1,0:T(8,128)(2,1)S(1)}, u32[]{:S(2)}) copy-start(bf16[128,128,128]{2,1,0:T(8,128)(2,1)S(1)} %early_adjoint.1.before) | copy-start | bytes 12582916
  141.8 0.9 copy-start.8
  142.7 14.2 %collective-permute-start.35 = (bf16[20,128,128]{2,1,0:T(8,128)(2,1)}, bf16[20,128,128]{2,1,0:T(8,128)(2,1)}, u32[]{:S(2)}, u32[]{:S(2)}) collective-permute-start(bf16[20,128,128]{2,1,0:T(8,128)(2,1)} %get-tuple-element.54), channel_id=1, source_target_pairs={{0,32},{1,33},{2,34},{3,35},{4,36},{5,37},{6,38},{7,39},{8,40},{9,... | collective-permute-start | bytes 1966088 | tf_op jit(solution)/shard_map/ppermute | solution.py:41
  143.6 16.4 %collective-permute-start.32 = (bf16[22,128,128]{2,1,0:T(8,128)(2,1)S(1)}, bf16[22,128,128]{2,1,0:T(8,128)(2,1)}, u32[]{:S(2)}, u32[]{:S(2)}) collective-permute-start(bf16[22,128,128]{2,1,0:T(8,128)(2,1)S(1)} %get-tuple-element.51), channel_id=1, source_target_pairs={{0,16},{1,17},{2,18},{3,19},{4,20},{5,21},{6,22},{7,23},{8,24},{9,... | collective-permute-start | bytes 2162696 | tf_op jit(solution)/shard_map/ppermute | solution.py:41
  144.0 21.6 %collective-permute-start.39 = (bf16[24,128,128]{2,1,0:T(8,128)(2,1)}, bf16[24,128,128]{2,1,0:T(8,128)(2,1)S(1)}, u32[]{:S(2)}, u32[]{:S(2)}) collective-permute-start(bf16[24,128,128]{2,1,0:T(8,128)(2,1)} %copy-done.8), channel_id=1, source_target_pairs={{0,96},{1,97},{2,98},{3,99},{4,100},{5,101},{6,102},{7,103},{8,104... | collective-permute-start | bytes 2359304 | tf_op jit(solution)/shard_map/ppermute | solution.py:41
  147.2 3.4 %copy-start.1 = (bf16[256,128,128]{2,1,0:T(8,128)(2,1)S(1)}, bf16[256,128,128]{2,1,0:T(8,128)(2,1)}, u32[]{:S(2)}) copy-start(bf16[256,128,128]{2,1,0:T(8,128)(2,1)} %copy-done) | copy-start | bytes 25165828
  150.6 2.2 %copy-start.3 = (bf16[128,128,128]{2,1,0:T(8,128)(2,1)S(1)}, bf16[128,128,128]{2,1,0:T(8,128)(2,1)}, u32[]{:S(2)}) copy-start(bf16[128,128,128]{2,1,0:T(8,128)(2,1)} %copy-done.2) | copy-start | bytes 12582916
  158.0 10.1 %collective-permute-start.36 = (bf16[10,128,128]{2,1,0:T(8,128)(2,1)S(1)}, bf16[10,128,128]{2,1,0:T(8,128)(2,1)S(1)}, u32[]{:S(2)}, u32[]{:S(2)}) collective-permute-start(bf16[10,128,128]{2,1,0:T(8,128)(2,1)S(1)} %add_convert_fusion.2), channel_id=1, source_target_pairs={{0,16},{1,17},{2,18},{3,19},{4,20},{5,21},{6,22},{7,23},{8,24},{9,... | collective-permute-start | bytes 983048 | tf_op jit(solution)/shard_map/ppermute | solution.py:41
  162.0 11.1 %collective-permute-start.33 = (bf16[12,128,128]{2,1,0:T(8,128)(2,1)S(1)}, bf16[12,128,128]{2,1,0:T(8,128)(2,1)S(1)}, u32[]{:S(2)}, u32[]{:S(2)}) collective-permute-start(bf16[12,128,128]{2,1,0:T(8,128)(2,1)S(1)} %pad_maximum_fusion.5), channel_id=1, source_target_pairs={{0,96},{1,97},{2,98},{3,99},{4,100},{5,101},{6,102},{7,103},{8,104... | collective-permute-start | bytes 1179656 | tf_op jit(solution)/shard_map/ppermute | solution.py:41
  165.7 11.7 %collective-permute-start.40 = (bf16[12,128,128]{2,1,0:T(8,128)(2,1)S(1)}, bf16[12,128,128]{2,1,0:T(8,128)(2,1)S(1)}, u32[]{:S(2)}, u32[]{:S(2)}) collective-permute-start(bf16[12,128,128]{2,1,0:T(8,128)(2,1)S(1)} %add_convert_fusion), channel_id=1, source_target_pairs={{0,32},{1,33},{2,34},{3,35},{4,36},{5,37},{6,38},{7,39},{8,40},{9,... | collective-permute-start | bytes 1179656 | tf_op jit(solution)/shard_map/ppermute | solution.py:41
  169.1 7.3 %collective-permute-start.37 = (bf16[5,128,128]{2,1,0:T(8,128)(2,1)S(1)}, bf16[5,128,128]{2,1,0:T(8,128)(2,1)S(1)}, u32[]{:S(2)}, u32[]{:S(2)}) collective-permute-start(bf16[5,128,128]{2,1,0:T(8,128)(2,1)S(1)} %add_convert_fusion.11), channel_id=1, source_target_pairs={{0,96},{1,97},{2,98},{3,99},{4,100},{5,101},{6,102},{7,103},{8,104... | collective-permute-start | bytes 491528 | tf_op jit(solution)/shard_map/ppermute | solution.py:41
  174.1 6.2 %collective-permute-start.34 = (bf16[7,128,128]{2,1,0:T(8,128)(2,1)S(1)}, bf16[7,128,128]{2,1,0:T(8,128)(2,1)S(1)}, u32[]{:S(2)}, u32[]{:S(2)}) collective-permute-start(bf16[7,128,128]{2,1,0:T(8,128)(2,1)S(1)} %pad_maximum_fusion.11), channel_id=1, source_target_pairs={{0,32},{1,33},{2,34},{3,35},{4,36},{5,37},{6,38},{7,39},{8,40},{9,... | collective-permute-start | bytes 688136 | tf_op jit(solution)/shard_map/ppermute | solution.py:41
  177.5 5.7 %collective-permute-start.41 = (bf16[6,128,128]{2,1,0:T(8,128)(2,1)S(1)}, bf16[6,128,128]{2,1,0:T(8,128)(2,1)S(1)}, u32[]{:S(2)}, u32[]{:S(2)}) collective-permute-start(bf16[6,128,128]{2,1,0:T(8,128)(2,1)S(1)} %add_convert_fusion.7), channel_id=1, source_target_pairs={{0,16},{1,17},{2,18},{3,19},{4,20},{5,21},{6,22},{7,23},{8,24},{9,... | collective-permute-start | bytes 589832 | tf_op jit(solution)/shard_map/ppermute | solution.py:41
  181.5 1.9 %collective-permute-start.38 = (bf16[10,128,128]{2,1,0:T(8,128)(2,1)S(1)}, bf16[10,128,128]{2,1,0:T(8,128)(2,1)S(1)}, u32[]{:S(2)}, u32[]{:S(2)}) collective-permute-start(bf16[10,128,128]{2,1,0:T(8,128)(2,1)S(1)} %fusion), channel_id=1, source_target_pairs={{0,8},{1,9},{2,10},{3,11},{4,12},{5,13},{6,14},{7,15},{8,0},{9,1},... | collective-permute-start | bytes 983048 | tf_op jit(solution)/shard_map/ppermute | solution.py:41

commit v3 on v2

--- a/solution.py
+++ b/solution.py
@@ -43,7 +43,7 @@
 
 def link_orders(ring, pair):
     near, far, other = (1, 0), (3, 0), (0, 1)
-    orders = ((other, near, far), (near, far, other), (far, other, near))
+    orders = ((near, far, other), (far, other, near), (other, near, far))
     return [[({ring: r, pair: p}, r * 2 + p) for r, p in order] for order in orders]
 
 
@@ -164,7 +164,7 @@
     turn, other = mark // 2, mark % 2
     near = ((turn == 1) | (turn == 2)).astype(jnp.int32)
     far = (turn >= 2).astype(jnp.int32)
-    bits = ((other, near, far), (near, far, other), (far, other, near))
+    bits = ((near, far, other), (far, other, near), (other, near, far))
     array, row = jnp.zeros_like(ids), jnp.zeros_like(ids)
     for third, ((lo, hi), (a, b, c)) in enumerate(zip(CUTS, bits)):
         here = (tile >= lo) & (tile < hi)
@@ -342,58 +342,57 @@
     return [array for pair in zip(held, sent) for array in pair], tiles
 
 
-def dense_kernel(core_ref, weight_ref, own_cot, sib_cot, own_sums, sib_sums, *rest):
-    act_ref, *mixed_refs, mixed_buf, wgrad_ref = rest
+def dense_pair(weights, half, tile, cot_ref, own_sums, sib_sums):
+    own = [own_sums[half * 8 + tile + step] for step in range(2)]
+    sib = [sib_sums[(1 - half) * 8 + tile + step] for step in range(2)]
+    nodes = [jnp.concatenate([a.T, b.T], axis=1) for a, b in zip(own, sib)]
+    pre = jnp.dot(jnp.concatenate(nodes), weights, preferred_element_type=F32)
+    sigmoid = 0.5 * jnp.tanh(0.5 * pre) + 0.5
+    slope = sigmoid * (1.0 + pre * (1.0 - sigmoid))
+    cot = cot_ref[tile * TILE : (tile + 2) * TILE, :]
+    grad = (cot.astype(F32) * slope).astype(BF16)
+    wgrad = jnp.dot(jnp.concatenate(own, axis=1), grad, preferred_element_type=F32)
+    mixed = lax.dot_general(
+        weights[:TILE], grad, (((1,), (1,)), ((), ())), preferred_element_type=F32
+    ).astype(BF16)
+    return (pre * sigmoid).astype(BF16), wgrad, (mixed[:, :TILE], mixed[:, TILE:])
+
+
+def ordered_weight(core_ref, weight_ref):
     core = core_ref[0]
-    own_weight = weight_ref[pl.ds(pl.multiple_of(core * TILE, TILE), TILE), :]
-    sib_weight = weight_ref[pl.ds(pl.multiple_of((1 - core) * TILE, TILE), TILE), :]
-    wgrad_ref[...] = jnp.zeros(wgrad_ref.shape, F32)
-    for half, cot_ref in enumerate((own_cot, sib_cot)):
-
-        @pl.loop(0, 4)
-        def _(pair, half=half, cot_ref=cot_ref):
-            for step in range(2):
-                tile = pair * 2 + step
-                rows = pl.ds(pl.multiple_of(tile * TILE, TILE), TILE)
-                own = own_sums[half * 8 + tile]
-                sib = sib_sums[(1 - half) * 8 + tile]
-                pre = jnp.dot(own.T, own_weight, preferred_element_type=F32)
-                pre = pre + jnp.dot(sib.T, sib_weight, preferred_element_type=F32)
-                sigmoid = jax.nn.sigmoid(pre)
-                if half == 0:
-                    act_ref[rows, :] = (pre * sigmoid).astype(BF16)
-                slope = sigmoid * (1.0 + pre * (1.0 - sigmoid))
-                grad = (cot_ref[rows, :].astype(F32) * slope).astype(BF16)
-                wgrad_ref[...] += jnp.dot(own, grad, preferred_element_type=F32)
-                mixed_buf[half * 8 + tile] = lax.dot_general(
-                    own_weight, grad, (((1,), (1,)), ((), ())), preferred_element_type=F32
-                ).astype(BF16)
-
-    for ref, (lo, hi) in zip(mixed_refs, CUTS):
-        ref[: hi - lo] = mixed_buf[lo:hi]
+    halves = [pl.ds(pl.multiple_of(at * TILE, TILE), TILE) for at in (core, 1 - core)]
+    return jnp.concatenate([weight_ref[half, :] for half in halves])
+
+
+def dense_kernel(core_ref, weight_ref, own_cot, sib_cot, own_sums, sib_sums, act_ref, *mixed_refs):
+    weights = ordered_weight(core_ref, weight_ref)
+    total = None
+    for at in range(0, 16, 2):
+        half, tile = divmod(at, 8)
+        cot = sib_cot if half else own_cot
+        act, wgrad, mixed = dense_pair(weights, half, tile, cot, own_sums, sib_sums)
+        if not half:
+            act_ref[tile * TILE : (tile + 2) * TILE, :] = act
+        total = wgrad if total is None else total + wgrad
+        for step, value in enumerate(mixed):
+            third, place = third_of(at + step)
+            mixed_refs[third][place] = value
     for part in range(EXTRA):
-        extra = wgrad_ref[:, part * TILE : (part + 1) * TILE]
+        extra = total[:, part * TILE : (part + 1) * TILE]
         mixed_refs[SIDE][CUTS[SIDE][1] - CUTS[SIDE][0] + part] = extra.astype(BF16)
 
 
 def dense(core, weight, own_cot, sib_cot, own_sums, sib_sums):
-    outs = pl.pallas_call(
+    act, *mixed = pl.pallas_call(
         dense_kernel,
-        out_shape=[
-            jax.ShapeDtypeStruct(own_cot.shape, BF16),
-        ]
-        + third_shapes(1, EXTRA),
+        out_shape=[jax.ShapeDtypeStruct(own_cot.shape, BF16)] + third_shapes(1, EXTRA),
         in_specs=[smem_spec()] + [vmem_spec()] * 5,
         out_specs=[vmem_spec()] * 4,
-        scratch_shapes=[
-            pltpu.VMEM((16, TILE, TILE), BF16),
-            pltpu.VMEM((TILE, EXTRA * TILE), F32),
-        ],
         compiler_params=pltpu.CompilerParams(vmem_limit_bytes=24 << 20),
         cost_estimate=cost(2 * 2048 * 256 * 512, 4 << 20),
         name="dense",
     )(core, weight, own_cot, sib_cot, own_sums, sib_sums)
-    return outs[0], outs[1:]
+    return act, mixed
 
 
 def back_kernel(core_ref, own_ref, sib_ref, out_ref):

time: 187 us -> 184 us (0.984)
  Pallas kernels: 20.9 us -> 18.4 us
    pallas_call x1, Pallas kernels: 4.4 us -> 2.23 us  [dense(): pl.pallas_call(dense_kernel, out_shape=[jax.ShapeDtypeStruct(own_cot.shap...]
where the time goes in v3:
time: 184 us; the launch traced here: 182 us
  waiting for transfers between devices  83 us (45%)
  starting transfers between devices  59.9 us (33%)
  Pallas kernels  18.4 us (10%)
  other arithmetic  10.7 us (6%)
  local copies, waits for them, and re-layouts  8.07 us (4%)
  between operations  1.86 us (1%)
    ppermute x42, waiting for transfers between devices, move(): return lax.ppermute(value, AXES, pairs)  83 us
    ppermute x42, starting transfers between devices, move(): return lax.ppermute(value, AXES, pairs)  59.9 us
    pallas_call x4, Pallas kernels, late_pass(): pl.pallas_call(functools.partial(late_kernel, adjoint, kept), out_shape=t...  8.46 us
    convert_element_type x23, other arithmetic, add_all(): return total.astype(BF16)  8.15 us
    unnamed x31, local copies, waits for them, and re-layouts  7.7 us
    pallas_call x1, Pallas kernels, early_pass(): pl.pallas_call(load_kernel, out_shape=[TOTAL, jax.ShapeDtypeStruct((2 * s...  3.85 us
  transfers between devices with their start and end apart: 42, of which 28 were waited for; matrix products, arithmetic and copies ran while one was open for 6% of the time, Pallas kernels for 6%

profile of v3, /device:TPU:0, one launch (start us, length us, event | category | flops | bytes accessed | tf_op | source)
XLA Modules:
  0.0 181.9 jit_solution(10828836004373828629)
XLA Ops:
  0.7 2.1 %collective-permute-done.sib_ref = bf16[1024,256]{1,0:T(8,128)(2,1)S(1)} collective-permute-done((bf16[1024,256]{1,0:T(8,128)(2,1)}, bf16[1024,256]{1,0:T(8,128)(2,1)S(1)}, u32[]{:S(2)}, u32[]{:S(2)}) %collective-permute-start) | collective-permute-done | bytes 524320 | tf_op jit(solution)/shard_map/ppermute | solution.py:41
  2.8 1.0 copy-done.6
  5.0 1.7 collective-permute-start.1
  6.7 3.1 %collective-permute-start.8 = (bf16[5,128,128]{2,1,0:T(8,128)(2,1)S(1)}, bf16[5,128,128]{2,1,0:T(8,128)(2,1)S(1)}, u32[]{:S(2)}, u32[]{:S(2)}) collective-permute-start(bf16[5,128,128]{2,1,0:T(8,128)(2,1)S(1)} %get-tuple-element.38), channel_id=1, source_target_pairs={{0,96},{1,97},{2,98},{3,99},{4,100},{5,101},{6,102},{7,103},{8,104... | collective-permute-start | bytes 491528 | tf_op jit(solution)/shard_map/ppermute | solution.py:41
  10.1 1.5 collective-permute-done.1
  11.6 1.7 collective-permute-start.2
  13.4 0.9 collective-permute-done.8
  15.0 2.7 %collective-permute-done.6 = bf16[6,128,128]{2,1,0:T(8,128)(2,1)S(1)} collective-permute-done((bf16[6,128,128]{2,1,0:T(8,128)(2,1)S(1)}, bf16[6,128,128]{2,1,0:T(8,128)(2,1)S(1)}, u32[]{:S(2)}, u32[]{:S(2)}) %collective-permute-start.6) | collective-permute-done | bytes 196640 | tf_op jit(solution)/shard_map/ppermute | solution.py:41
  18.1 5.5 %collective-permute-done.2 = bf16[10,128,128]{2,1,0:T(8,128)(2,1)S(1)} collective-permute-done((bf16[10,128,128]{2,1,0:T(8,128)(2,1)S(1)}, bf16[10,128,128]{2,1,0:T(8,128)(2,1)S(1)}, u32[]{:S(2)}, u32[]{:S(2)}) %collective-permute-start.2) | collective-permute-done | bytes 327712 | tf_op jit(solution)/shard_map/ppermute | solution.py:41
  24.8 1.2 collective-permute-done.4
  26.5 2.6 %collective-permute-done.7 = bf16[12,128,128]{2,1,0:T(8,128)(2,1)S(1)} collective-permute-done((bf16[12,128,128]{2,1,0:T(8,128)(2,1)S(1)}, bf16[12,128,128]{2,1,0:T(8,128)(2,1)S(1)}, u32[]{:S(2)}, u32[]{:S(2)}) %collective-permute-start.7) | collective-permute-done | bytes 393248 | tf_op jit(solution)/shard_map/ppermute | solution.py:41
  30.3 3.8 %early_pass.1 = (bf16[128,128,128]{2,1,0:T(8,128)(2,1)S(1)}, bf16[256,128,128]{2,1,0:T(8,128)(2,1)S(1)}) custom-call(s32[2]{0:T(128)S(1)} %add_reduce_fusion.live_ref, s32[256]{0:T(256)S(1)} %select_reduce_fusion.1.list_ref, s32[10]{0:T(128)S(1)} %convert_reduce_fusion.3.bound_ref, bf16[128,128,128]{2,1,0:T(8,128)(2,1)S(1)} %bitcast.31, ...), custom_call_target="tpu_custom_call" | custom-call | flops 268435456 | bytes 16777216 | tf_op jit(solution)/shard_map/early_pass/pallas_call | solution.py:311
  34.2 8.6 %collective-permute-done.11.rest_1_ = bf16[20,128,128]{2,1,0:T(8,128)(2,1)S(1)} collective-permute-done((bf16[20,128,128]{2,1,0:T(8,128)(2,1)S(1)}, bf16[20,128,128]{2,1,0:T(8,128)(2,1)S(1)}, u32[]{:S(2)}, u32[]{:S(2)}) %collective-permute-start.11) | collective-permute-done | bytes 655392 | tf_op jit(solution)/shard_map/ppermute | solution.py:41
  42.8 3.3 %collective-permute-done.10.rest_0_ = bf16[24,128,128]{2,1,0:T(8,128)(2,1)S(1)} collective-permute-done((bf16[24,128,128]{2,1,0:T(8,128)(2,1)S(1)}, bf16[24,128,128]{2,1,0:T(8,128)(2,1)S(1)}, u32[]{:S(2)}, u32[]{:S(2)}) %collective-permute-start.10) | collective-permute-done | bytes 786464 | tf_op jit(solution)/shard_map/ppermute | solution.py:41
  46.1 2.0 %sent_pass.1 = (bf16[24,128,128]{2,1,0:T(8,128)(2,1)S(1)}, bf16[20,128,128]{2,1,0:T(8,128)(2,1)S(1)}, bf16[20,128,128]{2,1,0:T(8,128)(2,1)S(1)}) custom-call(s32[256]{0:T(256)S(1)} %select_reduce_fusion.1.list_ref, s32[10]{0:T(128)S(1)} %convert_reduce_fusion.3.bound_ref, bf16[256,128,128]{2,1,0:T(8,128)(2,1)S(1)} %get-tuple-element.39.tiles, ...), custom_call_target="tpu_custom_call" | custom-call | flops 134217728 | bytes 8388608 | tf_op jit(solution)/shard_map/sent_pass/pallas_call | solution.py:325
  48.1 4.4 %collective-permute-start.19 = (bf16[20,128,128]{2,1,0:T(8,128)(2,1)S(1)}, bf16[20,128,128]{2,1,0:T(8,128)(2,1)S(1)}, u32[]{:S(2)}, u32[]{:S(2)}) collective-permute-start(bf16[20,128,128]{2,1,0:T(8,128)(2,1)S(1)} %get-tuple-element.46), channel_id=1, source_target_pairs={{0,3},{1,2},{2,1},{3,0},{4,7},{5,6},{6,5},{7,4},{8,11},{9,10},{10,... | collective-permute-start | bytes 1966088 | tf_op jit(solution)/shard_map/ppermute | solution.py:41
  52.7 3.5 %collective-permute-start.13 = (bf16[24,128,128]{2,1,0:T(8,128)(2,1)S(1)}, bf16[24,128,128]{2,1,0:T(8,128)(2,1)S(1)}, u32[]{:S(2)}, u32[]{:S(2)}) collective-permute-start(bf16[24,128,128]{2,1,0:T(8,128)(2,1)S(1)} %get-tuple-element.42), channel_id=1, source_target_pairs={{0,4},{1,5},{2,6},{3,7},{4,0},{5,1},{6,2},{7,3},{8,12},{9,13},{10,... | collective-permute-start | bytes 2359304 | tf_op jit(solution)/shard_map/ppermute | solution.py:41
  56.2 2.0 %kept_pass.1 = (bf16[24,128,128]{2,1,0:T(8,128)(2,1)S(1)}, bf16[20,128,128]{2,1,0:T(8,128)(2,1)S(1)}, bf16[20,128,128]{2,1,0:T(8,128)(2,1)S(1)}) custom-call(s32[256]{0:T(256)S(1)} %select_reduce_fusion.1.list_ref, s32[10]{0:T(128)S(1)} %convert_reduce_fusion.3.bound_ref, bf16[256,128,128]{2,1,0:T(8,128)(2,1)S(1)} %get-tuple-element.39.tiles, ...), custom_call_target="tpu_custom_call" | custom-call | flops 134217728 | bytes 8388608 | tf_op jit(solution)/shard_map/kept_pass/pallas_call | solution.py:325
  58.3 6.0 %collective-permute-done.19 = bf16[20,128,128]{2,1,0:T(8,128)(2,1)S(1)} collective-permute-done((bf16[20,128,128]{2,1,0:T(8,128)(2,1)S(1)}, bf16[20,128,128]{2,1,0:T(8,128)(2,1)S(1)}, u32[]{:S(2)}, u32[]{:S(2)}) %collective-permute-start.19) | collective-permute-done | bytes 655392 | tf_op jit(solution)/shard_map/ppermute | solution.py:41
  64.5 3.6 %collective-permute-done.16 = bf16[20,128,128]{2,1,0:T(8,128)(2,1)S(1)} collective-permute-done((bf16[20,128,128]{2,1,0:T(8,128)(2,1)S(1)}, bf16[20,128,128]{2,1,0:T(8,128)(2,1)S(1)}, u32[]{:S(2)}, u32[]{:S(2)}) %collective-permute-start.16) | collective-permute-done | bytes 655392 | tf_op jit(solution)/shard_map/ppermute | solution.py:41
  68.3 3.7 %collective-permute-start.17 = (bf16[10,128,128]{2,1,0:T(8,128)(2,1)S(1)}, bf16[10,128,128]{2,1,0:T(8,128)(2,1)S(1)}, u32[]{:S(2)}, u32[]{:S(2)}) collective-permute-start(bf16[10,128,128]{2,1,0:T(8,128)(2,1)S(1)} %add_convert_fusion.5), channel_id=1, source_target_pairs={{0,4},{1,5},{2,6},{3,7},{4,0},{5,1},{6,2},{7,3},{8,12},{9,13},{10,... | collective-permute-start | bytes 983048 | tf_op jit(solution)/shard_map/ppermute | solution.py:41
  72.0 1.9 %collective-permute-done.13 = bf16[24,128,128]{2,1,0:T(8,128)(2,1)S(1)} collective-permute-done((bf16[24,128,128]{2,1,0:T(8,128)(2,1)S(1)}, bf16[24,128,128]{2,1,0:T(8,128)(2,1)S(1)}, u32[]{:S(2)}, u32[]{:S(2)}) %collective-permute-start.13) | collective-permute-done | bytes 786464 | tf_op jit(solution)/shard_map/ppermute | solution.py:41
  74.2 3.3 %collective-permute-start.21 = (bf16[5,128,128]{2,1,0:T(8,128)(2,1)S(1)}, bf16[5,128,128]{2,1,0:T(8,128)(2,1)S(1)}, u32[]{:S(2)}, u32[]{:S(2)}) collective-permute-start(bf16[5,128,128]{2,1,0:T(8,128)(2,1)S(1)} %add_convert_fusion.15), channel_id=1, source_target_pairs={{0,4},{1,5},{2,6},{3,7},{4,0},{5,1},{6,2},{7,3},{8,12},{9,13},{10,... | collective-permute-start | bytes 491528 | tf_op jit(solution)/shard_map/ppermute | solution.py:41
  77.5 1.6 collective-permute-done.17
  79.2 1.7 collective-permute-start.18
  81.2 2.5 %collective-permute-done.14 = bf16[12,128,128]{2,1,0:T(8,128)(2,1)S(1)} collective-permute-done((bf16[12,128,128]{2,1,0:T(8,128)(2,1)S(1)}, bf16[12,128,128]{2,1,0:T(8,128)(2,1)S(1)}, u32[]{:S(2)}, u32[]{:S(2)}) %collective-permute-start.14) | collective-permute-done | bytes 393248 | tf_op jit(solution)/shard_map/ppermute | solution.py:41
  84.1 1.7 collective-permute-done.18
  85.9 3.6 %collective-permute-done.15 = bf16[6,128,128]{2,1,0:T(8,128)(2,1)S(1)} collective-permute-done((bf16[6,128,128]{2,1,0:T(8,128)(2,1)S(1)}, bf16[6,128,128]{2,1,0:T(8,128)(2,1)S(1)}, u32[]{:S(2)}, u32[]{:S(2)}) %collective-permute-start.15) | collective-permute-done | bytes 196640 | tf_op jit(solution)/shard_map/ppermute | solution.py:41
  90.0 1.9 %collective-permute-done.22.sib_sums = bf16[16,128,128]{2,1,0:T(8,128)(2,1)S(1)} collective-permute-done((bf16[16,128,128]{2,1,0:T(8,128)(2,1)S(1)}, bf16[16,128,128]{2,1,0:T(8,128)(2,1)S(1)}, u32[]{:S(2)}, u32[]{:S(2)}) %collective-permute-start.22) | collective-permute-done | bytes 524320 | tf_op jit(solution)/shard_map/ppermute | solution.py:41
  91.9 2.2 %dense.1 = (bf16[1024,256]{1,0:T(8,128)(2,1)}, bf16[6,128,128]{2,1,0:T(8,128)(2,1)S(1)}, bf16[7,128,128]{2,1,0:T(8,128)(2,1)S(1)}, bf16[5,128,128]{2,1,0:T(8,128)(2,1)S(1)}) custom-call(s32[1]{0:T(128)} %bitcast.core_ref, bf16[256,256]{1,0:T(8,128)(2,1)S(1)} %copy-done.7, bf16[1024,256]{1,0:T(8,128)(2,1)S(1)} %copy-done.5, ...), custom_call_target="tpu_custom_call" | custom-call | flops 536870912 | bytes 4194304 | tf_op jit(solution)/shard_map/dense/pallas_call | solution.py:386
  94.2 1.2 collective-permute-start.25
  95.9 3.3 %collective-permute-start.27 = (bf16[5,128,128]{2,1,0:T(8,128)(2,1)S(1)}, bf16[5,128,128]{2,1,0:T(8,128)(2,1)S(1)}, u32[]{:S(2)}, u32[]{:S(2)}) collective-permute-start(bf16[5,128,128]{2,1,0:T(8,128)(2,1)S(1)} %get-tuple-element.50), channel_id=1, source_target_pairs={{0,4},{1,5},{2,6},{3,7},{4,0},{5,1},{6,2},{7,3},{8,12},{9,13},{10,... | collective-permute-start | bytes 491528 | tf_op jit(solution)/shard_map/ppermute | solution.py:41
  99.2 2.9 %collective-permute-done.23 = bf16[6,128,128]{2,1,0:T(8,128)(2,1)S(1)} collective-permute-done((bf16[6,128,128]{2,1,0:T(8,128)(2,1)S(1)}, bf16[6,128,128]{2,1,0:T(8,128)(2,1)S(1)}, u32[]{:S(2)}, u32[]{:S(2)}) %collective-permute-start.23) | collective-permute-done | bytes 196640 | tf_op jit(solution)/shard_map/ppermute | solution.py:41
  102.1 2.2 %collective-permute-start.24 = (bf16[12,128,128]{2,1,0:T(8,128)(2,1)S(1)}, bf16[12,128,128]{2,1,0:T(8,128)(2,1)S(1)}, u32[]{:S(2)}, u32[]{:S(2)}) collective-permute-start(bf16[12,128,128]{2,1,0:T(8,128)(2,1)S(1)} %pad_maximum_fusion.3), channel_id=1, source_target_pairs={{0,3},{1,2},{2,1},{3,0},{4,7},{5,6},{6,5},{7,4},{8,11},{9,10},{10,... | collective-permute-start | bytes 1179656 | tf_op jit(solution)/shard_map/ppermute | solution.py:41
  104.5 2.7 %collective-permute-start.26 = (bf16[12,128,128]{2,1,0:T(8,128)(2,1)S(1)}, bf16[12,128,128]{2,1,0:T(8,128)(2,1)S(1)}, u32[]{:S(2)}, u32[]{:S(2)}) collective-permute-start(bf16[12,128,128]{2,1,0:T(8,128)(2,1)S(1)} %pad_maximum_fusion.4), channel_id=1, source_target_pairs={{0,4},{1,5},{2,6},{3,7},{4,0},{5,1},{6,2},{7,3},{8,12},{9,13},{10,... | collective-permute-start | bytes 1179656 | tf_op jit(solution)/shard_map/ppermute | solution.py:41
  107.3 6.1 %collective-permute-done.24 = bf16[12,128,128]{2,1,0:T(8,128)(2,1)S(1)} collective-permute-done((bf16[12,128,128]{2,1,0:T(8,128)(2,1)S(1)}, bf16[12,128,128]{2,1,0:T(8,128)(2,1)S(1)}, u32[]{:S(2)}, u32[]{:S(2)}) %collective-permute-start.24) | collective-permute-done | bytes 393248 | tf_op jit(solution)/shard_map/ppermute | solution.py:41
  113.5 3.3 %collective-permute-start.29 = (bf16[24,128,128]{2,1,0:T(8,128)(2,1)S(1)}, bf16[24,128,128]{2,1,0:T(8,128)(2,1)S(1)}, u32[]{:S(2)}, u32[]{:S(2)}) collective-permute-start(bf16[24,128,128]{2,1,0:T(8,128)(2,1)S(1)} %constant_dynamic-update-slice_fusion.9.rest_0_), channel_id=1, source_target_pairs={{0,4},{1,5},{2,6},{3,7},{4,0},{5,1},{6,2},{7,3},{8,12},{9,13},{10,... | collective-permute-start | bytes 2359304 | tf_op jit(solution)/shard_map/ppermute | solution.py:41
  117.1 1.6 collective-permute-start.31
  119.1 2.7 %early_adjoint.1.before = bf16[128,128,128]{2,1,0:T(8,128)(2,1)S(1)} custom-call(s32[256]{0:T(256)S(1)} %select_reduce_fusion.list_ref, s32[10]{0:T(128)S(1)} %convert_reduce_fusion.2.bound_ref, bf16[256,128,128]{2,1,0:T(8,128)(2,1)S(1)} %get-tuple-element.39.tiles, bf16[24,128,128]{2,1,0:T(8,128)(2,1)S(1)} %constant_dynamic-update-slice_fusion.9.rest_0_, ...), custom_call_target="tpu_custom_call" | custom-call | flops 268435456 | bytes 16777216 | tf_op jit(solution)/shard_map/early_adjoint/pallas_call | solution.py:300
  121.8 11.0 %collective-permute-done.31.rest_2_ = bf16[20,128,128]{2,1,0:T(8,128)(2,1)S(1)} collective-permute-done((bf16[20,128,128]{2,1,0:T(8,128)(2,1)S(1)}, bf16[20,128,128]{2,1,0:T(8,128)(2,1)S(1)}, u32[]{:S(2)}, u32[]{:S(2)}) %collective-permute-start.31) | collective-permute-done | bytes 655392 | tf_op jit(solution)/shard_map/ppermute | solution.py:41
  132.9 2.6 %sent_adjoint.1 = (bf16[24,128,128]{2,1,0:T(8,128)(2,1)S(1)}, bf16[22,128,128]{2,1,0:T(8,128)(2,1)S(1)}, bf16[20,128,128]{2,1,0:T(8,128)(2,1)}) custom-call(s32[256]{0:T(256)S(1)} %select_reduce_fusion.list_ref, s32[10]{0:T(128)S(1)} %convert_reduce_fusion.2.bound_ref, bf16[256,128,128]{2,1,0:T(8,128)(2,1)S(1)} %get-tuple-element.39.tiles, ...), custom_call_target="tpu_custom_call" | custom-call | flops 134217728 | bytes 8388608 | tf_op jit(solution)/shard_map/sent_adjoint/pallas_call | solution.py:325
  136.3 2.8 %collective-permute-start.35 = (bf16[20,128,128]{2,1,0:T(8,128)(2,1)}, bf16[20,128,128]{2,1,0:T(8,128)(2,1)}, u32[]{:S(2)}, u32[]{:S(2)}) collective-permute-start(bf16[20,128,128]{2,1,0:T(8,128)(2,1)} %get-tuple-element.54), channel_id=1, source_target_pairs={{0,96},{1,97},{2,98},{3,99},{4,100},{5,101},{6,102},{7,103},{8,104... | collective-permute-start | bytes 1966088 | tf_op jit(solution)/shard_map/ppermute | solution.py:41
  139.2 2.2 %collective-permute-start.32 = (bf16[22,128,128]{2,1,0:T(8,128)(2,1)S(1)}, bf16[22,128,128]{2,1,0:T(8,128)(2,1)}, u32[]{:S(2)}, u32[]{:S(2)}) collective-permute-start(bf16[22,128,128]{2,1,0:T(8,128)(2,1)S(1)} %get-tuple-element.51), channel_id=1, source_target_pairs={{0,32},{1,33},{2,34},{3,35},{4,36},{5,37},{6,38},{7,39},{8,40},{9,... | collective-permute-start | bytes 2162696 | tf_op jit(solution)/shard_map/ppermute | solution.py:41
  141.3 2.5 %collective-permute-start.39 = (bf16[24,128,128]{2,1,0:T(8,128)(2,1)}, bf16[24,128,128]{2,1,0:T(8,128)(2,1)S(1)}, u32[]{:S(2)}, u32[]{:S(2)}) collective-permute-start(bf16[24,128,128]{2,1,0:T(8,128)(2,1)} %copy-done.8), channel_id=1, source_target_pairs={{0,16},{1,17},{2,18},{3,19},{4,20},{5,21},{6,22},{7,23},{8,24},{9,... | collective-permute-start | bytes 2359304 | tf_op jit(solution)/shard_map/ppermute | solution.py:41
  143.8 3.4 %copy-done.1 = bf16[256,128,128]{2,1,0:T(8,128)(2,1)S(1)} copy-done((bf16[256,128,128]{2,1,0:T(8,128)(2,1)S(1)}, bf16[256,128,128]{2,1,0:T(8,128)(2,1)}, u32[]{:S(2)}) %copy-start.1) | copy-done | bytes 8388632
  147.2 2.2 %copy-done.3 = bf16[128,128,128]{2,1,0:T(8,128)(2,1)S(1)} copy-done((bf16[128,128,128]{2,1,0:T(8,128)(2,1)S(1)}, bf16[128,128,128]{2,1,0:T(8,128)(2,1)}, u32[]{:S(2)}) %copy-start.3) | copy-done | bytes 4194328
  149.4 1.8 kept_adjoint.1
  151.5 1.1 add_convert_fusion.2
  152.6 2.8 %collective-permute-start.36 = (bf16[10,128,128]{2,1,0:T(8,128)(2,1)S(1)}, bf16[10,128,128]{2,1,0:T(8,128)(2,1)S(1)}, u32[]{:S(2)}, u32[]{:S(2)}) collective-permute-start(bf16[10,128,128]{2,1,0:T(8,128)(2,1)S(1)} %add_convert_fusion.2), channel_id=1, source_target_pairs={{0,32},{1,33},{2,34},{3,35},{4,36},{5,37},{6,38},{7,39},{8,40},{9,... | collective-permute-start | bytes 983048 | tf_op jit(solution)/shard_map/ppermute | solution.py:41
  155.4 1.5 collective-permute-done.32
  157.7 1.1 add_convert_fusion.3
  158.8 2.6 %collective-permute-start.33 = (bf16[12,128,128]{2,1,0:T(8,128)(2,1)S(1)}, bf16[12,128,128]{2,1,0:T(8,128)(2,1)S(1)}, u32[]{:S(2)}, u32[]{:S(2)}) collective-permute-start(bf16[12,128,128]{2,1,0:T(8,128)(2,1)S(1)} %pad_maximum_fusion.5), channel_id=1, source_target_pairs={{0,16},{1,17},{2,18},{3,19},{4,20},{5,21},{6,22},{7,23},{8,24},{9,... | collective-permute-start | bytes 1179656 | tf_op jit(solution)/shard_map/ppermute | solution.py:41
  161.5 0.9 collective-permute-start.40
  162.4 1.0 add_convert_fusion.11
  163.4 2.1 %collective-permute-start.37 = (bf16[5,128,128]{2,1,0:T(8,128)(2,1)S(1)}, bf16[5,128,128]{2,1,0:T(8,128)(2,1)S(1)}, u32[]{:S(2)}, u32[]{:S(2)}) collective-permute-start(bf16[5,128,128]{2,1,0:T(8,128)(2,1)S(1)} %add_convert_fusion.11), channel_id=1, source_target_pairs={{0,16},{1,17},{2,18},{3,19},{4,20},{5,21},{6,22},{7,23},{8,24},{9,... | collective-permute-start | bytes 491528 | tf_op jit(solution)/shard_map/ppermute | solution.py:41
  165.6 3.4 %collective-permute-done.33 = bf16[12,128,128]{2,1,0:T(8,128)(2,1)S(1)} collective-permute-done((bf16[12,128,128]{2,1,0:T(8,128)(2,1)S(1)}, bf16[12,128,128]{2,1,0:T(8,128)(2,1)S(1)}, u32[]{:S(2)}, u32[]{:S(2)}) %collective-permute-start.33) | collective-permute-done | bytes 393248 | tf_op jit(solution)/shard_map/ppermute | solution.py:41
  169.0 1.0 add_convert_fusion.13
  170.1 1.0 collective-permute-start.34
  171.0 1.0 add_convert_fusion.10
  172.0 0.9 collective-permute-done.40
  173.7 3.7 %collective-permute-done.34 = bf16[7,128,128]{2,1,0:T(8,128)(2,1)S(1)} collective-permute-done((bf16[7,128,128]{2,1,0:T(8,128)(2,1)S(1)}, bf16[7,128,128]{2,1,0:T(8,128)(2,1)S(1)}, u32[]{:S(2)}, u32[]{:S(2)}) %collective-permute-start.34) | collective-permute-done | bytes 229408 | tf_op jit(solution)/shard_map/ppermute | solution.py:41
  177.4 1.0 add_convert_fusion.12
  178.9 1.3 collective-permute-done.38.sib_ref
  180.9 1.0 turn_back.1
  (124 shorter events, 12.7 us)
Async XLA Ops:
  0.6 23.5 %copy-start.5 = (bf16[1024,256]{1,0:T(8,128)(2,1)S(1)}, bf16[1024,256]{1,0:T(8,128)(2,1)}, u32[]{:S(2)}) copy-start(bf16[1024,256]{1,0:T(8,128)(2,1)} %own_cot.1) | copy-start | bytes 1572868
  0.6 2.2 %collective-permute-start = (bf16[1024,256]{1,0:T(8,128)(2,1)}, bf16[1024,256]{1,0:T(8,128)(2,1)S(1)}, u32[]{:S(2)}, u32[]{:S(2)}) collective-permute-start(bf16[1024,256]{1,0:T(8,128)(2,1)} %own_ref.1), channel_id=1, source_target_pairs={{0,8},{1,9},{2,10},{3,11},{4,12},{5,13},{6,14},{7,15},{8,0},{9,1},... | collective-permute-start | bytes 1572872 | tf_op jit(solution)/shard_map/ppermute | solution.py:41
  2.8 1.0 copy-start.6
  3.9 20.2 %copy-start.9 = (s32[1,1,128]{2,1,0:T(1,128)S(1)}, s32[1,1,128]{2,1,0:T(1,128)}, u32[]{:S(2)}) copy-start(s32[1,1,128]{2,1,0:T(1,128)} %param.12) | copy-start | bytes 1540
  3.9 20.2 %copy-start.10 = (s32[1,1,128]{2,1,0:T(1,128)S(1)}, s32[1,1,128]{2,1,0:T(1,128)}, u32[]{:S(2)}) copy-start(s32[1,1,128]{2,1,0:T(1,128)} %param.11) | copy-start | bytes 1540
  4.1 26.2 %collective-permute-start.5 = (bf16[128,128,128]{2,1,0:T(8,128)(2,1)}, bf16[128,128,128]{2,1,0:T(8,128)(2,1)}, u32[]{:S(2)}, u32[]{:S(2)}) collective-permute-start(bf16[128,128,128]{2,1,0:T(8,128)(2,1)} %bitcast.30), channel_id=1, source_target_pairs={{0,8},{1,9},{2,10},{3,11},{4,12},{5,13},{6,14},{7,15},{8,0},{9,1},... | collective-permute-start | bytes 12582920 | tf_op jit(solution)/shard_map/ppermute | solution.py:41
  5.0 25.3 %copy-start.4 = (bf16[1,1,128,128,128]{4,3,2,1,0:T(8,128)(2,1)S(1)}, bf16[1,1,128,128,128]{4,3,2,1,0:T(8,128)(2,1)}, u32[]{:S(2)}) copy-start(bf16[1,1,128,128,128]{4,3,2,1,0:T(8,128)(2,1)} %param.10) | copy-start | bytes 12582916
  5.0 6.6 %collective-permute-start.1 = (bf16[5,128,128]{2,1,0:T(8,128)(2,1)S(1)}, bf16[5,128,128]{2,1,0:T(8,128)(2,1)S(1)}, u32[]{:S(2)}, u32[]{:S(2)}) collective-permute-start(bf16[5,128,128]{2,1,0:T(8,128)(2,1)S(1)} %get-tuple-element.30), channel_id=1, source_target_pairs={{0,16},{1,17},{2,18},{3,19},{4,20},{5,21},{6,22},{7,23},{8,24},{9,... | collective-permute-start | bytes 491528 | tf_op jit(solution)/shard_map/ppermute | solution.py:41
  6.7 7.5 %collective-permute-start.8 = (bf16[5,128,128]{2,1,0:T(8,128)(2,1)S(1)}, bf16[5,128,128]{2,1,0:T(8,128)(2,1)S(1)}, u32[]{:S(2)}, u32[]{:S(2)}) collective-permute-start(bf16[5,128,128]{2,1,0:T(8,128)(2,1)S(1)} %get-tuple-element.38), channel_id=1, source_target_pairs={{0,96},{1,97},{2,98},{3,99},{4,100},{5,101},{6,102},{7,103},{8,104... | collective-permute-start | bytes 491528 | tf_op jit(solution)/shard_map/ppermute | solution.py:41
  9.8 7.9 %collective-permute-start.6 = (bf16[6,128,128]{2,1,0:T(8,128)(2,1)S(1)}, bf16[6,128,128]{2,1,0:T(8,128)(2,1)S(1)}, u32[]{:S(2)}, u32[]{:S(2)}) collective-permute-start(bf16[6,128,128]{2,1,0:T(8,128)(2,1)S(1)} %get-tuple-element.36), channel_id=1, source_target_pairs={{0,32},{1,33},{2,34},{3,35},{4,36},{5,37},{6,38},{7,39},{8,40},{9,... | collective-permute-start | bytes 589832 | tf_op jit(solution)/shard_map/ppermute | solution.py:41
  11.6 11.9 %collective-permute-start.2 = (bf16[10,128,128]{2,1,0:T(8,128)(2,1)S(1)}, bf16[10,128,128]{2,1,0:T(8,128)(2,1)S(1)}, u32[]{:S(2)}, u32[]{:S(2)}) collective-permute-start(bf16[10,128,128]{2,1,0:T(8,128)(2,1)S(1)} %pad_maximum_fusion.7), channel_id=1, source_target_pairs={{0,32},{1,33},{2,34},{3,35},{4,36},{5,37},{6,38},{7,39},{8,40},{9,... | collective-permute-start | bytes 983048 | tf_op jit(solution)/shard_map/ppermute | solution.py:41
  14.3 9.9 %collective-permute-start.9 = (bf16[10,128,128]{2,1,0:T(8,128)(2,1)S(1)}, bf16[10,128,128]{2,1,0:T(8,128)(2,1)S(1)}, u32[]{:S(2)}, u32[]{:S(2)}) collective-permute-start(bf16[10,128,128]{2,1,0:T(8,128)(2,1)S(1)} %pad_maximum_fusion.8), channel_id=1, source_target_pairs={{0,16},{1,17},{2,18},{3,19},{4,20},{5,21},{6,22},{7,23},{8,24},{9,... | collective-permute-start | bytes 983048 | tf_op jit(solution)/shard_map/ppermute | solution.py:41
  17.8 11.4 %collective-permute-start.7 = (bf16[12,128,128]{2,1,0:T(8,128)(2,1)S(1)}, bf16[12,128,128]{2,1,0:T(8,128)(2,1)S(1)}, u32[]{:S(2)}, u32[]{:S(2)}) collective-permute-start(bf16[12,128,128]{2,1,0:T(8,128)(2,1)S(1)} %pad_maximum_fusion.2), channel_id=1, source_target_pairs={{0,96},{1,97},{2,98},{3,99},{4,100},{5,101},{6,102},{7,103},{8,104... | collective-permute-start | bytes 1179656 | tf_op jit(solution)/shard_map/ppermute | solution.py:41
  23.6 19.2 %collective-permute-start.12 = (bf16[20,128,128]{2,1,0:T(8,128)(2,1)S(1)}, bf16[20,128,128]{2,1,0:T(8,128)(2,1)S(1)}, u32[]{:S(2)}, u32[]{:S(2)}) collective-permute-start(bf16[20,128,128]{2,1,0:T(8,128)(2,1)S(1)} %constant_dynamic-update-slice_fusion.rest_2_), channel_id=1, source_target_pairs={{0,96},{1,97},{2,98},{3,99},{4,100},{5,101},{6,102},{7,103},{8,104... | collective-permute-start | bytes 1966088 | tf_op jit(solution)/shard_map/ppermute | solution.py:41
  24.1 6.2 %collective-permute-start.3 = (bf16[1024,256]{1,0:T(8,128)(2,1)S(1)}, bf16[1024,256]{1,0:T(8,128)(2,1)S(1)}, u32[]{:S(2)}, u32[]{:S(2)}) collective-permute-start(bf16[1024,256]{1,0:T(8,128)(2,1)S(1)} %copy-done.5), channel_id=1, source_target_pairs={{0,8},{1,9},{2,10},{3,11},{4,12},{5,13},{6,14},{7,15},{8,0},{9,1},... | collective-permute-start | bytes 1572872 | tf_op jit(solution)/shard_map/ppermute | solution.py:41
  24.2 1.8 collective-permute-start.4
  26.0 16.8 %collective-permute-start.11 = (bf16[20,128,128]{2,1,0:T(8,128)(2,1)S(1)}, bf16[20,128,128]{2,1,0:T(8,128)(2,1)S(1)}, u32[]{:S(2)}, u32[]{:S(2)}) collective-permute-start(bf16[20,128,128]{2,1,0:T(8,128)(2,1)S(1)} %constant_dynamic-update-slice_fusion.6.rest_1_), channel_id=1, source_target_pairs={{0,32},{1,33},{2,34},{3,35},{4,36},{5,37},{6,38},{7,39},{8,40},{9,... | collective-permute-start | bytes 1966088 | tf_op jit(solution)/shard_map/ppermute | solution.py:41
  29.2 16.9 %collective-permute-start.10 = (bf16[24,128,128]{2,1,0:T(8,128)(2,1)S(1)}, bf16[24,128,128]{2,1,0:T(8,128)(2,1)S(1)}, u32[]{:S(2)}, u32[]{:S(2)}) collective-permute-start(bf16[24,128,128]{2,1,0:T(8,128)(2,1)S(1)} %constant_dynamic-update-slice_fusion.3.rest_0_), channel_id=1, source_target_pairs={{0,16},{1,17},{2,18},{3,19},{4,20},{5,21},{6,22},{7,23},{8,24},{9,... | collective-permute-start | bytes 2359304 | tf_op jit(solution)/shard_map/ppermute | solution.py:41
  34.2 98.7 %copy-start = (bf16[256,128,128]{2,1,0:T(8,128)(2,1)}, bf16[256,128,128]{2,1,0:T(8,128)(2,1)S(1)}, u32[]{:S(2)}) copy-start(bf16[256,128,128]{2,1,0:T(8,128)(2,1)S(1)} %get-tuple-element.39.tiles) | copy-start | bytes 25165828
  48.1 16.1 %collective-permute-start.19 = (bf16[20,128,128]{2,1,0:T(8,128)(2,1)S(1)}, bf16[20,128,128]{2,1,0:T(8,128)(2,1)S(1)}, u32[]{:S(2)}, u32[]{:S(2)}) collective-permute-start(bf16[20,128,128]{2,1,0:T(8,128)(2,1)S(1)} %get-tuple-element.46), channel_id=1, source_target_pairs={{0,3},{1,2},{2,1},{3,0},{4,7},{5,6},{6,5},{7,4},{8,11},{9,10},{10,... | collective-permute-start | bytes 1966088 | tf_op jit(solution)/shard_map/ppermute | solution.py:41
  52.6 15.6 %collective-permute-start.16 = (bf16[20,128,128]{2,1,0:T(8,128)(2,1)S(1)}, bf16[20,128,128]{2,1,0:T(8,128)(2,1)S(1)}, u32[]{:S(2)}, u32[]{:S(2)}) collective-permute-start(bf16[20,128,128]{2,1,0:T(8,128)(2,1)S(1)} %get-tuple-element.44), channel_id=1, source_target_pairs={{0,1},{1,0},{2,3},{3,2},{4,5},{5,4},{6,7},{7,6},{8,9},{9,8},{10,11... | collective-permute-start | bytes 1966088 | tf_op jit(solution)/shard_map/ppermute | solution.py:41
  52.7 21.2 %collective-permute-start.13 = (bf16[24,128,128]{2,1,0:T(8,128)(2,1)S(1)}, bf16[24,128,128]{2,1,0:T(8,128)(2,1)S(1)}, u32[]{:S(2)}, u32[]{:S(2)}) collective-permute-start(bf16[24,128,128]{2,1,0:T(8,128)(2,1)S(1)} %get-tuple-element.42), channel_id=1, source_target_pairs={{0,4},{1,5},{2,6},{3,7},{4,0},{5,1},{6,2},{7,3},{8,12},{9,13},{10,... | collective-permute-start | bytes 2359304 | tf_op jit(solution)/shard_map/ppermute | solution.py:41
  64.3 27.6 %copy-start.7 = (bf16[256,256]{1,0:T(8,128)(2,1)S(1)}, bf16[256,256]{1,0:T(8,128)(2,1)}, u32[]{:S(2)}) copy-start(bf16[256,256]{1,0:T(8,128)(2,1)} %weight_ref.1) | copy-start | bytes 393220
  64.3 9.8 %collective-permute-start.20 = (bf16[10,128,128]{2,1,0:T(8,128)(2,1)S(1)}, bf16[10,128,128]{2,1,0:T(8,128)(2,1)S(1)}, u32[]{:S(2)}, u32[]{:S(2)}) collective-permute-start(bf16[10,128,128]{2,1,0:T(8,128)(2,1)S(1)} %add_convert_fusion.4), channel_id=1, source_target_pairs={{0,1},{1,0},{2,3},{3,2},{4,5},{5,4},{6,7},{7,6},{8,9},{9,8},{10,11... | collective-permute-start | bytes 983048 | tf_op jit(solution)/shard_map/ppermute | solution.py:41
  68.3 10.9 %collective-permute-start.17 = (bf16[10,128,128]{2,1,0:T(8,128)(2,1)S(1)}, bf16[10,128,128]{2,1,0:T(8,128)(2,1)S(1)}, u32[]{:S(2)}, u32[]{:S(2)}) collective-permute-start(bf16[10,128,128]{2,1,0:T(8,128)(2,1)S(1)} %add_convert_fusion.5), channel_id=1, source_target_pairs={{0,4},{1,5},{2,6},{3,7},{4,0},{5,1},{6,2},{7,3},{8,12},{9,13},{10,... | collective-permute-start | bytes 983048 | tf_op jit(solution)/shard_map/ppermute | solution.py:41
  74.0 9.7 %collective-permute-start.14 = (bf16[12,128,128]{2,1,0:T(8,128)(2,1)S(1)}, bf16[12,128,128]{2,1,0:T(8,128)(2,1)S(1)}, u32[]{:S(2)}, u32[]{:S(2)}) collective-permute-start(bf16[12,128,128]{2,1,0:T(8,128)(2,1)S(1)} %add_convert_fusion.1), channel_id=1, source_target_pairs={{0,3},{1,2},{2,1},{3,0},{4,7},{5,6},{6,5},{7,4},{8,11},{9,10},{10,... | collective-permute-start | bytes 1179656 | tf_op jit(solution)/shard_map/ppermute | solution.py:41
  74.2 6.9 %collective-permute-start.21 = (bf16[5,128,128]{2,1,0:T(8,128)(2,1)S(1)}, bf16[5,128,128]{2,1,0:T(8,128)(2,1)S(1)}, u32[]{:S(2)}, u32[]{:S(2)}) collective-permute-start(bf16[5,128,128]{2,1,0:T(8,128)(2,1)S(1)} %add_convert_fusion.15), channel_id=1, source_target_pairs={{0,4},{1,5},{2,6},{3,7},{4,0},{5,1},{6,2},{7,3},{8,12},{9,13},{10,... | collective-permute-start | bytes 491528 | tf_op jit(solution)/shard_map/ppermute | solution.py:41
  79.2 6.6 %collective-permute-start.18 = (bf16[5,128,128]{2,1,0:T(8,128)(2,1)S(1)}, bf16[5,128,128]{2,1,0:T(8,128)(2,1)S(1)}, u32[]{:S(2)}, u32[]{:S(2)}) collective-permute-start(bf16[5,128,128]{2,1,0:T(8,128)(2,1)S(1)} %add_convert_fusion.17), channel_id=1, source_target_pairs={{0,3},{1,2},{2,1},{3,0},{4,7},{5,6},{6,5},{7,4},{8,11},{9,10},{10,... | collective-permute-start | bytes 491528 | tf_op jit(solution)/shard_map/ppermute | solution.py:41
  83.8 5.8 %collective-permute-start.15 = (bf16[6,128,128]{2,1,0:T(8,128)(2,1)S(1)}, bf16[6,128,128]{2,1,0:T(8,128)(2,1)S(1)}, u32[]{:S(2)}, u32[]{:S(2)}) collective-permute-start(bf16[6,128,128]{2,1,0:T(8,128)(2,1)S(1)} %add_convert_fusion.9), channel_id=1, source_target_pairs={{0,1},{1,0},{2,3},{3,2},{4,5},{5,4},{6,7},{7,6},{8,9},{9,8},{10,11... | collective-permute-start | bytes 589832 | tf_op jit(solution)/shard_map/ppermute | solution.py:41
  89.8 2.2 %collective-permute-start.22 = (bf16[16,128,128]{2,1,0:T(8,128)(2,1)S(1)}, bf16[16,128,128]{2,1,0:T(8,128)(2,1)S(1)}, u32[]{:S(2)}, u32[]{:S(2)}) collective-permute-start(bf16[16,128,128]{2,1,0:T(8,128)(2,1)S(1)} %pad_maximum_fusion.1.own_sums), channel_id=1, source_target_pairs={{0,8},{1,9},{2,10},{3,11},{4,12},{5,13},{6,14},{7,15},{8,0},{9,1},... | collective-permute-start | bytes 1572872 | tf_op jit(solution)/shard_map/ppermute | solution.py:41
  94.2 10.2 %collective-permute-start.25 = (bf16[7,128,128]{2,1,0:T(8,128)(2,1)S(1)}, bf16[7,128,128]{2,1,0:T(8,128)(2,1)S(1)}, u32[]{:S(2)}, u32[]{:S(2)}) collective-permute-start(bf16[7,128,128]{2,1,0:T(8,128)(2,1)S(1)} %get-tuple-element.49), channel_id=1, source_target_pairs={{0,3},{1,2},{2,1},{3,0},{4,7},{5,6},{6,5},{7,4},{8,11},{9,10},{10,... | collective-permute-start | bytes 688136 | tf_op jit(solution)/shard_map/ppermute | solution.py:41
  95.4 6.7 %collective-permute-start.23 = (bf16[6,128,128]{2,1,0:T(8,128)(2,1)S(1)}, bf16[6,128,128]{2,1,0:T(8,128)(2,1)S(1)}, u32[]{:S(2)}, u32[]{:S(2)}) collective-permute-start(bf16[6,128,128]{2,1,0:T(8,128)(2,1)S(1)} %get-tuple-element.48), channel_id=1, source_target_pairs={{0,1},{1,0},{2,3},{3,2},{4,5},{5,4},{6,7},{7,6},{8,9},{9,8},{10,11... | collective-permute-start | bytes 589832 | tf_op jit(solution)/shard_map/ppermute | solution.py:41
  95.9 11.2 %collective-permute-start.27 = (bf16[5,128,128]{2,1,0:T(8,128)(2,1)S(1)}, bf16[5,128,128]{2,1,0:T(8,128)(2,1)S(1)}, u32[]{:S(2)}, u32[]{:S(2)}) collective-permute-start(bf16[5,128,128]{2,1,0:T(8,128)(2,1)S(1)} %get-tuple-element.50), channel_id=1, source_target_pairs={{0,4},{1,5},{2,6},{3,7},{4,0},{5,1},{6,2},{7,3},{8,12},{9,13},{10,... | collective-permute-start | bytes 491528 | tf_op jit(solution)/shard_map/ppermute | solution.py:41
  102.1 11.3 %collective-permute-start.24 = (bf16[12,128,128]{2,1,0:T(8,128)(2,1)S(1)}, bf16[12,128,128]{2,1,0:T(8,128)(2,1)S(1)}, u32[]{:S(2)}, u32[]{:S(2)}) collective-permute-start(bf16[12,128,128]{2,1,0:T(8,128)(2,1)S(1)} %pad_maximum_fusion.3), channel_id=1, source_target_pairs={{0,3},{1,2},{2,1},{3,0},{4,7},{5,6},{6,5},{7,4},{8,11},{9,10},{10,... | collective-permute-start | bytes 1179656 | tf_op jit(solution)/shard_map/ppermute | solution.py:41
  104.5 12.4 %collective-permute-start.26 = (bf16[12,128,128]{2,1,0:T(8,128)(2,1)S(1)}, bf16[12,128,128]{2,1,0:T(8,128)(2,1)S(1)}, u32[]{:S(2)}, u32[]{:S(2)}) collective-permute-start(bf16[12,128,128]{2,1,0:T(8,128)(2,1)S(1)} %pad_maximum_fusion.4), channel_id=1, source_target_pairs={{0,4},{1,5},{2,6},{3,7},{4,0},{5,1},{6,2},{7,3},{8,12},{9,13},{10,... | collective-permute-start | bytes 1179656 | tf_op jit(solution)/shard_map/ppermute | solution.py:41
  107.2 9.9 %collective-permute-start.28 = (bf16[10,128,128]{2,1,0:T(8,128)(2,1)S(1)}, bf16[10,128,128]{2,1,0:T(8,128)(2,1)S(1)}, u32[]{:S(2)}, u32[]{:S(2)}) collective-permute-start(bf16[10,128,128]{2,1,0:T(8,128)(2,1)S(1)} %pad_maximum_fusion.9), channel_id=1, source_target_pairs={{0,1},{1,0},{2,3},{3,2},{4,5},{5,4},{6,7},{7,6},{8,9},{9,8},{10,11... | collective-permute-start | bytes 983048 | tf_op jit(solution)/shard_map/ppermute | solution.py:41
  113.5 19.4 %collective-permute-start.29 = (bf16[24,128,128]{2,1,0:T(8,128)(2,1)S(1)}, bf16[24,128,128]{2,1,0:T(8,128)(2,1)S(1)}, u32[]{:S(2)}, u32[]{:S(2)}) collective-permute-start(bf16[24,128,128]{2,1,0:T(8,128)(2,1)S(1)} %constant_dynamic-update-slice_fusion.9.rest_0_), channel_id=1, source_target_pairs={{0,4},{1,5},{2,6},{3,7},{4,0},{5,1},{6,2},{7,3},{8,12},{9,13},{10,... | collective-permute-start | bytes 2359304 | tf_op jit(solution)/shard_map/ppermute | solution.py:41
  117.0 15.9 %collective-permute-start.30 = (bf16[22,128,128]{2,1,0:T(8,128)(2,1)S(1)}, bf16[22,128,128]{2,1,0:T(8,128)(2,1)S(1)}, u32[]{:S(2)}, u32[]{:S(2)}) collective-permute-start(bf16[22,128,128]{2,1,0:T(8,128)(2,1)S(1)} %pad_maximum_fusion.rest_1_.rest_3_), channel_id=1, source_target_pairs={{0,1},{1,0},{2,3},{3,2},{4,5},{5,4},{6,7},{7,6},{8,9},{9,8},{10,11... | collective-permute-start | bytes 2162696 | tf_op jit(solution)/shard_map/ppermute | solution.py:41
  117.1 15.7 %collective-permute-start.31 = (bf16[20,128,128]{2,1,0:T(8,128)(2,1)S(1)}, bf16[20,128,128]{2,1,0:T(8,128)(2,1)S(1)}, u32[]{:S(2)}, u32[]{:S(2)}) collective-permute-start(bf16[20,128,128]{2,1,0:T(8,128)(2,1)S(1)} %constant_dynamic-update-slice_fusion.12.rest_2_), channel_id=1, source_target_pairs={{0,3},{1,2},{2,1},{3,0},{4,7},{5,6},{6,5},{7,4},{8,11},{9,10},{10,... | collective-permute-start | bytes 1966088 | tf_op jit(solution)/shard_map/ppermute | solution.py:41
  121.8 13.7 %copy-start.2 = (bf16[128,128,128]{2,1,0:T(8,128)(2,1)}, bf16[128,128,128]{2,1,0:T(8,128)(2,1)S(1)}, u32[]{:S(2)}) copy-start(bf16[128,128,128]{2,1,0:T(8,128)(2,1)S(1)} %early_adjoint.1.before) | copy-start | bytes 12582916
  135.5 0.9 copy-start.8
  136.3 15.2 %collective-permute-start.35 = (bf16[20,128,128]{2,1,0:T(8,128)(2,1)}, bf16[20,128,128]{2,1,0:T(8,128)(2,1)}, u32[]{:S(2)}, u32[]{:S(2)}) collective-permute-start(bf16[20,128,128]{2,1,0:T(8,128)(2,1)} %get-tuple-element.54), channel_id=1, source_target_pairs={{0,96},{1,97},{2,98},{3,99},{4,100},{5,101},{6,102},{7,103},{8,104... | collective-permute-start | bytes 1966088 | tf_op jit(solution)/shard_map/ppermute | solution.py:41
  139.2 17.7 %collective-permute-start.32 = (bf16[22,128,128]{2,1,0:T(8,128)(2,1)S(1)}, bf16[22,128,128]{2,1,0:T(8,128)(2,1)}, u32[]{:S(2)}, u32[]{:S(2)}) collective-permute-start(bf16[22,128,128]{2,1,0:T(8,128)(2,1)S(1)} %get-tuple-element.51), channel_id=1, source_target_pairs={{0,32},{1,33},{2,34},{3,35},{4,36},{5,37},{6,38},{7,39},{8,40},{9,... | collective-permute-start | bytes 2162696 | tf_op jit(solution)/shard_map/ppermute | solution.py:41
  141.3 20.1 %collective-permute-start.39 = (bf16[24,128,128]{2,1,0:T(8,128)(2,1)}, bf16[24,128,128]{2,1,0:T(8,128)(2,1)S(1)}, u32[]{:S(2)}, u32[]{:S(2)}) collective-permute-start(bf16[24,128,128]{2,1,0:T(8,128)(2,1)} %copy-done.8), channel_id=1, source_target_pairs={{0,16},{1,17},{2,18},{3,19},{4,20},{5,21},{6,22},{7,23},{8,24},{9,... | collective-permute-start | bytes 2359304 | tf_op jit(solution)/shard_map/ppermute | solution.py:41
  143.8 3.4 %copy-start.1 = (bf16[256,128,128]{2,1,0:T(8,128)(2,1)S(1)}, bf16[256,128,128]{2,1,0:T(8,128)(2,1)}, u32[]{:S(2)}) copy-start(bf16[256,128,128]{2,1,0:T(8,128)(2,1)} %copy-done) | copy-start | bytes 25165828
  147.2 2.2 %copy-start.3 = (bf16[128,128,128]{2,1,0:T(8,128)(2,1)S(1)}, bf16[128,128,128]{2,1,0:T(8,128)(2,1)}, u32[]{:S(2)}) copy-start(bf16[128,128,128]{2,1,0:T(8,128)(2,1)} %copy-done.2) | copy-start | bytes 12582916
  152.6 9.8 %collective-permute-start.36 = (bf16[10,128,128]{2,1,0:T(8,128)(2,1)S(1)}, bf16[10,128,128]{2,1,0:T(8,128)(2,1)S(1)}, u32[]{:S(2)}, u32[]{:S(2)}) collective-permute-start(bf16[10,128,128]{2,1,0:T(8,128)(2,1)S(1)} %add_convert_fusion.2), channel_id=1, source_target_pairs={{0,32},{1,33},{2,34},{3,35},{4,36},{5,37},{6,38},{7,39},{8,40},{9,... | collective-permute-start | bytes 983048 | tf_op jit(solution)/shard_map/ppermute | solution.py:41
  158.8 10.2 %collective-permute-start.33 = (bf16[12,128,128]{2,1,0:T(8,128)(2,1)S(1)}, bf16[12,128,128]{2,1,0:T(8,128)(2,1)S(1)}, u32[]{:S(2)}, u32[]{:S(2)}) collective-permute-start(bf16[12,128,128]{2,1,0:T(8,128)(2,1)S(1)} %pad_maximum_fusion.5), channel_id=1, source_target_pairs={{0,16},{1,17},{2,18},{3,19},{4,20},{5,21},{6,22},{7,23},{8,24},{9,... | collective-permute-start | bytes 1179656 | tf_op jit(solution)/shard_map/ppermute | solution.py:41
  161.5 11.4 %collective-permute-start.40 = (bf16[12,128,128]{2,1,0:T(8,128)(2,1)S(1)}, bf16[12,128,128]{2,1,0:T(8,128)(2,1)S(1)}, u32[]{:S(2)}, u32[]{:S(2)}) collective-permute-start(bf16[12,128,128]{2,1,0:T(8,128)(2,1)S(1)} %add_convert_fusion), channel_id=1, source_target_pairs={{0,96},{1,97},{2,98},{3,99},{4,100},{5,101},{6,102},{7,103},{8,104... | collective-permute-start | bytes 1179656 | tf_op jit(solution)/shard_map/ppermute | solution.py:41
  163.4 7.6 %collective-permute-start.37 = (bf16[5,128,128]{2,1,0:T(8,128)(2,1)S(1)}, bf16[5,128,128]{2,1,0:T(8,128)(2,1)S(1)}, u32[]{:S(2)}, u32[]{:S(2)}) collective-permute-start(bf16[5,128,128]{2,1,0:T(8,128)(2,1)S(1)} %add_convert_fusion.11), channel_id=1, source_target_pairs={{0,16},{1,17},{2,18},{3,19},{4,20},{5,21},{6,22},{7,23},{8,24},{9,... | collective-permute-start | bytes 491528 | tf_op jit(solution)/shard_map/ppermute | solution.py:41
  170.1 7.3 %collective-permute-start.34 = (bf16[7,128,128]{2,1,0:T(8,128)(2,1)S(1)}, bf16[7,128,128]{2,1,0:T(8,128)(2,1)S(1)}, u32[]{:S(2)}, u32[]{:S(2)}) collective-permute-start(bf16[7,128,128]{2,1,0:T(8,128)(2,1)S(1)} %pad_maximum_fusion.11), channel_id=1, source_target_pairs={{0,96},{1,97},{2,98},{3,99},{4,100},{5,101},{6,102},{7,103},{8,104... | collective-permute-start | bytes 688136 | tf_op jit(solution)/shard_map/ppermute | solution.py:41
  173.0 5.7 %collective-permute-start.41 = (bf16[6,128,128]{2,1,0:T(8,128)(2,1)S(1)}, bf16[6,128,128]{2,1,0:T(8,128)(2,1)S(1)}, u32[]{:S(2)}, u32[]{:S(2)}) collective-permute-start(bf16[6,128,128]{2,1,0:T(8,128)(2,1)S(1)} %add_convert_fusion.7), channel_id=1, source_target_pairs={{0,32},{1,33},{2,34},{3,35},{4,36},{5,37},{6,38},{7,39},{8,40},{9,... | collective-permute-start | bytes 589832 | tf_op jit(solution)/shard_map/ppermute | solution.py:41
  178.5 1.7 collective-permute-start.38

commit v4 on v3

--- a/solution.py
+++ b/solution.py
@@ -13,6 +13,7 @@
 CUTS = ((0, 6), (6, 11), (11, 16))
 SIDE = 1
 EXTRA = 2
+NODES = 131072
 GROUP = 8
 LOAD = 8
 PASS_VMEM = 26
@@ -395,24 +396,34 @@
     return act, mixed
 
 
-def back_kernel(core_ref, own_ref, sib_ref, out_ref):
+def back_kernel(core_ref, own_ref, sib_ref, wgrad_ref, out_ref, weight_ref):
     core = core_ref[0]
+    scale = 1.0 / math.sqrt(NODES)
+    extra = sib_ref.shape[0] - EXTRA
     for ref, half in ((own_ref, core), (sib_ref, 1 - core)):
         lanes = pl.ds(pl.multiple_of(half * TILE, TILE), TILE)
         for tile in range(8):
             out_ref[tile * TILE : (tile + 1) * TILE, lanes] = ref[tile].T
-
-
-def turn_back(core, own_part, sib_part):
+    for ref, first, half in ((wgrad_ref, 0, core), (sib_ref, extra, 1 - core)):
+        rows = pl.ds(pl.multiple_of(half * TILE, TILE), TILE)
+        for part in range(EXTRA):
+            lanes = slice(part * TILE, (part + 1) * TILE)
+            weight_ref[rows, lanes] = ref[first + part].astype(F32) * scale
+
+
+def turn_back(core, own_part, sib_part, wgrad):
     return pl.pallas_call(
         back_kernel,
-        out_shape=jax.ShapeDtypeStruct((8 * TILE, 2 * TILE), BF16),
-        in_specs=[smem_spec()] + [vmem_spec()] * 2,
-        out_specs=vmem_spec(),
+        out_shape=[
+            jax.ShapeDtypeStruct((8 * TILE, 2 * TILE), BF16),
+            jax.ShapeDtypeStruct((2 * TILE, 2 * TILE), F32),
+        ],
+        in_specs=[smem_spec()] + [vmem_spec()] * 3,
+        out_specs=[vmem_spec()] * 2,
         compiler_params=pltpu.CompilerParams(vmem_limit_bytes=8 << 20),
         cost_estimate=cost(0, 1 << 20),
         name="turn_back",
-    )(core, own_part, sib_part)
+    )(core, own_part, sib_part, wgrad)
 
 
 def body(features, weight, cotangent, blocks, block_row, block_col, counts):
@@ -462,12 +473,7 @@
     parts, _ = block_pass(True, live, by_row, tiles, gathered)
     grads, wgrad = collect(parts, GR_LINKS, EXTRA)
     last = move(jnp.concatenate([grads[8:], wgrad]), core=1)
-    feature_grad = turn_back(core_arg, grads[:8], last)
-
-    node_total = features.shape[0] * lax.axis_size("gr") * lax.axis_size("gc")
-    halves = [jnp.concatenate([part[-2], part[-1]], axis=1).astype(F32) for part in (wgrad, last)]
-    weight_grad = jnp.where(core == 0, jnp.concatenate(halves), jnp.concatenate(halves[::-1]))
-    weight_grad = weight_grad * (1.0 / math.sqrt(node_total))
+    feature_grad, weight_grad = turn_back(core_arg, grads[:8], last, wgrad)
     return (activations, weight_grad, feature_grad)
 
 

time: 184 us -> 179 us (0.973); the launches traced: 182 us -> 179 us
  waiting for transfers between devices: 83 us -> 96.9 us
  other arithmetic: 10.7 us -> 3.5 us
  local copies, waits for them, and re-layouts: 8.07 us -> 1.6 us
  starting transfers between devices: 59.9 us -> 57.4 us
    ppermute x42, waiting for transfers between devices: 83 us -> 96.9 us  [move(): return lax.ppermute(value, AXES, pairs)]
    unnamed x31 -> x21, local copies, waits for them, and re-layouts: 7.7 us -> 1.25 us
    convert_element_type x23, other arithmetic: 8.15 us -> 1.7 us  [add_all(): return total.astype(BF16)]
    ppermute x42, starting transfers between devices: 59.9 us -> 57.4 us  [move(): return lax.ppermute(value, AXES, pairs)]
  transfers between devices with their start and end apart: 42 -> 42, of which waited for: 28 -> 30; matrix products, arithmetic and copies ran while one was open for 6% -> 2% of each run, Pallas kernels for 6% -> 6%
where the time goes in v4:
time: 179 us
  waiting for transfers between devices  96.9 us (54%)
  starting transfers between devices  57.4 us (32%)
  Pallas kernels  18 us (10%)
  other arithmetic  3.5 us (2%)
  between operations  1.85 us (1%)
    ppermute x42, waiting for transfers between devices, move(): return lax.ppermute(value, AXES, pairs)  96.9 us
    ppermute x42, starting transfers between devices, move(): return lax.ppermute(value, AXES, pairs)  57.4 us
    pallas_call x4, Pallas kernels, late_pass(): pl.pallas_call(functools.partial(late_kernel, adjoint, kept), out_shape=t...  7.72 us
    pallas_call x1, Pallas kernels, early_pass(): pl.pallas_call(load_kernel, out_shape=[TOTAL, jax.ShapeDtypeStruct((2 * s...  3.9 us
  transfers between devices with their start and end apart: 42, of which 30 were waited for; matrix products, arithmetic and copies ran while one was open for 2% of the time, Pallas kernels for 6%

profile of v4, /device:TPU:0, one launch (start us, length us, event | category | flops | bytes accessed | tf_op | source)
XLA Modules:
  0.0 179.3 jit_solution(2198478703342035716)
XLA Ops:
  0.7 2.1 %collective-permute-done.sib_ref = bf16[1024,256]{1,0:T(8,128)(2,1)S(1)} collective-permute-done((bf16[1024,256]{1,0:T(8,128)(2,1)}, bf16[1024,256]{1,0:T(8,128)(2,1)S(1)}, u32[]{:S(2)}, u32[]{:S(2)}) %collective-permute-start) | collective-permute-done | bytes 524320 | tf_op jit(solution)/shard_map/ppermute | solution.py:42
  2.8 1.0 copy-done.2
  5.0 1.7 collective-permute-start.1
  6.7 3.1 %collective-permute-start.8 = (bf16[5,128,128]{2,1,0:T(8,128)(2,1)S(1)}, bf16[5,128,128]{2,1,0:T(8,128)(2,1)S(1)}, u32[]{:S(2)}, u32[]{:S(2)}) collective-permute-start(bf16[5,128,128]{2,1,0:T(8,128)(2,1)S(1)} %get-tuple-element.40), channel_id=1, source_target_pairs={{0,96},{1,97},{2,98},{3,99},{4,100},{5,101},{6,102},{7,103},{8,104... | collective-permute-start | bytes 491528 | tf_op jit(solution)/shard_map/ppermute | solution.py:42
  10.1 1.5 collective-permute-done.1
  11.6 1.7 collective-permute-start.2
  13.4 0.9 collective-permute-done.8
  14.3 0.7 collective-permute-start.9
  15.0 2.7 %collective-permute-done.6 = bf16[6,128,128]{2,1,0:T(8,128)(2,1)S(1)} collective-permute-done((bf16[6,128,128]{2,1,0:T(8,128)(2,1)S(1)}, bf16[6,128,128]{2,1,0:T(8,128)(2,1)S(1)}, u32[]{:S(2)}, u32[]{:S(2)}) %collective-permute-start.6) | collective-permute-done | bytes 196640 | tf_op jit(solution)/shard_map/ppermute | solution.py:42
  18.1 5.5 %collective-permute-done.2 = bf16[10,128,128]{2,1,0:T(8,128)(2,1)S(1)} collective-permute-done((bf16[10,128,128]{2,1,0:T(8,128)(2,1)S(1)}, bf16[10,128,128]{2,1,0:T(8,128)(2,1)S(1)}, u32[]{:S(2)}, u32[]{:S(2)}) %collective-permute-start.2) | collective-permute-done | bytes 327712 | tf_op jit(solution)/shard_map/ppermute | solution.py:42
  24.8 1.2 collective-permute-done.4
  26.5 2.6 %collective-permute-done.7 = bf16[12,128,128]{2,1,0:T(8,128)(2,1)S(1)} collective-permute-done((bf16[12,128,128]{2,1,0:T(8,128)(2,1)S(1)}, bf16[12,128,128]{2,1,0:T(8,128)(2,1)S(1)}, u32[]{:S(2)}, u32[]{:S(2)}) %collective-permute-start.7) | collective-permute-done | bytes 393248 | tf_op jit(solution)/shard_map/ppermute | solution.py:42
  29.2 0.6 collective-permute-start.10
  30.3 3.9 %early_pass.1 = (bf16[128,128,128]{2,1,0:T(8,128)(2,1)S(1)}, bf16[256,128,128]{2,1,0:T(8,128)(2,1)S(1)}) custom-call(s32[2]{0:T(128)S(1)} %add_reduce_fusion.live_ref, s32[256]{0:T(256)S(1)} %select_reduce_fusion.1.list_ref, s32[10]{0:T(128)S(1)} %convert_reduce_fusion.3.bound_ref, bf16[128,128,128]{2,1,0:T(8,128)(2,1)S(1)} %bitcast.23, ...), custom_call_target="tpu_custom_call" | custom-call | flops 268435456 | bytes 16777216 | tf_op jit(solution)/shard_map/early_pass/pallas_call | solution.py:312
  34.2 8.6 %collective-permute-done.11.rest_1_ = bf16[20,128,128]{2,1,0:T(8,128)(2,1)S(1)} collective-permute-done((bf16[20,128,128]{2,1,0:T(8,128)(2,1)S(1)}, bf16[20,128,128]{2,1,0:T(8,128)(2,1)S(1)}, u32[]{:S(2)}, u32[]{:S(2)}) %collective-permute-start.11) | collective-permute-done | bytes 655392 | tf_op jit(solution)/shard_map/ppermute | solution.py:42
  42.8 3.3 %collective-permute-done.10.rest_0_ = bf16[24,128,128]{2,1,0:T(8,128)(2,1)S(1)} collective-permute-done((bf16[24,128,128]{2,1,0:T(8,128)(2,1)S(1)}, bf16[24,128,128]{2,1,0:T(8,128)(2,1)S(1)}, u32[]{:S(2)}, u32[]{:S(2)}) %collective-permute-start.10) | collective-permute-done | bytes 786464 | tf_op jit(solution)/shard_map/ppermute | solution.py:42
  46.1 2.0 %sent_pass.1 = (bf16[24,128,128]{2,1,0:T(8,128)(2,1)S(1)}, bf16[20,128,128]{2,1,0:T(8,128)(2,1)S(1)}, bf16[20,128,128]{2,1,0:T(8,128)(2,1)S(1)}) custom-call(s32[256]{0:T(256)S(1)} %select_reduce_fusion.1.list_ref, s32[10]{0:T(128)S(1)} %convert_reduce_fusion.3.bound_ref, bf16[256,128,128]{2,1,0:T(8,128)(2,1)S(1)} %get-tuple-element.41.tiles, ...), custom_call_target="tpu_custom_call" | custom-call | flops 134217728 | bytes 8388608 | tf_op jit(solution)/shard_map/sent_pass/pallas_call | solution.py:326
  48.1 4.1 %collective-permute-start.19 = (bf16[20,128,128]{2,1,0:T(8,128)(2,1)S(1)}, bf16[20,128,128]{2,1,0:T(8,128)(2,1)S(1)}, u32[]{:S(2)}, u32[]{:S(2)}) collective-permute-start(bf16[20,128,128]{2,1,0:T(8,128)(2,1)S(1)} %get-tuple-element.48), channel_id=1, source_target_pairs={{0,3},{1,2},{2,1},{3,0},{4,7},{5,6},{6,5},{7,4},{8,11},{9,10},{10,... | collective-permute-start | bytes 1966088 | tf_op jit(solution)/shard_map/ppermute | solution.py:42
  52.2 0.7 collective-permute-start.16
  53.0 2.3 %collective-permute-start.13 = (bf16[24,128,128]{2,1,0:T(8,128)(2,1)S(1)}, bf16[24,128,128]{2,1,0:T(8,128)(2,1)S(1)}, u32[]{:S(2)}, u32[]{:S(2)}) collective-permute-start(bf16[24,128,128]{2,1,0:T(8,128)(2,1)S(1)} %get-tuple-element.44), channel_id=1, source_target_pairs={{0,4},{1,5},{2,6},{3,7},{4,0},{5,1},{6,2},{7,3},{8,12},{9,13},{10,... | collective-permute-start | bytes 2359304 | tf_op jit(solution)/shard_map/ppermute | solution.py:42
  55.3 2.0 %kept_pass.1 = (bf16[24,128,128]{2,1,0:T(8,128)(2,1)S(1)}, bf16[20,128,128]{2,1,0:T(8,128)(2,1)S(1)}, bf16[20,128,128]{2,1,0:T(8,128)(2,1)S(1)}) custom-call(s32[256]{0:T(256)S(1)} %select_reduce_fusion.1.list_ref, s32[10]{0:T(128)S(1)} %convert_reduce_fusion.3.bound_ref, bf16[256,128,128]{2,1,0:T(8,128)(2,1)S(1)} %get-tuple-element.41.tiles, ...), custom_call_target="tpu_custom_call" | custom-call | flops 134217728 | bytes 8388608 | tf_op jit(solution)/shard_map/kept_pass/pallas_call | solution.py:326
  57.3 6.6 %collective-permute-done.19 = bf16[20,128,128]{2,1,0:T(8,128)(2,1)S(1)} collective-permute-done((bf16[20,128,128]{2,1,0:T(8,128)(2,1)S(1)}, bf16[20,128,128]{2,1,0:T(8,128)(2,1)S(1)}, u32[]{:S(2)}, u32[]{:S(2)}) %collective-permute-start.19) | collective-permute-done | bytes 655392 | tf_op jit(solution)/shard_map/ppermute | solution.py:42
  64.5 3.3 %collective-permute-done.16 = bf16[20,128,128]{2,1,0:T(8,128)(2,1)S(1)} collective-permute-done((bf16[20,128,128]{2,1,0:T(8,128)(2,1)S(1)}, bf16[20,128,128]{2,1,0:T(8,128)(2,1)S(1)}, u32[]{:S(2)}, u32[]{:S(2)}) %collective-permute-start.16) | collective-permute-done | bytes 655392 | tf_op jit(solution)/shard_map/ppermute | solution.py:42
  68.0 3.1 %collective-permute-start.17 = (bf16[10,128,128]{2,1,0:T(8,128)(2,1)S(1)}, bf16[10,128,128]{2,1,0:T(8,128)(2,1)S(1)}, u32[]{:S(2)}, u32[]{:S(2)}) collective-permute-start(bf16[10,128,128]{2,1,0:T(8,128)(2,1)S(1)} %add_convert_fusion.5), channel_id=1, source_target_pairs={{0,4},{1,5},{2,6},{3,7},{4,0},{5,1},{6,2},{7,3},{8,12},{9,13},{10,... | collective-permute-start | bytes 983048 | tf_op jit(solution)/shard_map/ppermute | solution.py:42
  71.1 2.3 %collective-permute-done.13 = bf16[24,128,128]{2,1,0:T(8,128)(2,1)S(1)} collective-permute-done((bf16[24,128,128]{2,1,0:T(8,128)(2,1)S(1)}, bf16[24,128,128]{2,1,0:T(8,128)(2,1)S(1)}, u32[]{:S(2)}, u32[]{:S(2)}) %collective-permute-start.13) | collective-permute-done | bytes 786464 | tf_op jit(solution)/shard_map/ppermute | solution.py:42
  73.4 0.7 collective-permute-start.14
  74.2 2.7 %collective-permute-start.21 = (bf16[5,128,128]{2,1,0:T(8,128)(2,1)S(1)}, bf16[5,128,128]{2,1,0:T(8,128)(2,1)S(1)}, u32[]{:S(2)}, u32[]{:S(2)}) collective-permute-start(bf16[5,128,128]{2,1,0:T(8,128)(2,1)S(1)} %add_convert_fusion.15), channel_id=1, source_target_pairs={{0,4},{1,5},{2,6},{3,7},{4,0},{5,1},{6,2},{7,3},{8,12},{9,13},{10,... | collective-permute-start | bytes 491528 | tf_op jit(solution)/shard_map/ppermute | solution.py:42
  76.9 1.7 collective-permute-done.17
  78.7 1.6 collective-permute-start.18
  80.3 0.9 collective-permute-done.21
  81.2 2.0 %collective-permute-done.14 = bf16[12,128,128]{2,1,0:T(8,128)(2,1)S(1)} collective-permute-done((bf16[12,128,128]{2,1,0:T(8,128)(2,1)S(1)}, bf16[12,128,128]{2,1,0:T(8,128)(2,1)S(1)}, u32[]{:S(2)}, u32[]{:S(2)}) %collective-permute-start.14) | collective-permute-done | bytes 393248 | tf_op jit(solution)/shard_map/ppermute | solution.py:42
  83.4 1.8 %collective-permute-done.18 = bf16[5,128,128]{2,1,0:T(8,128)(2,1)S(1)} collective-permute-done((bf16[5,128,128]{2,1,0:T(8,128)(2,1)S(1)}, bf16[5,128,128]{2,1,0:T(8,128)(2,1)S(1)}, u32[]{:S(2)}, u32[]{:S(2)}) %collective-permute-start.18) | collective-permute-done | bytes 163872 | tf_op jit(solution)/shard_map/ppermute | solution.py:42
  85.4 3.7 %collective-permute-done.15 = bf16[6,128,128]{2,1,0:T(8,128)(2,1)S(1)} collective-permute-done((bf16[6,128,128]{2,1,0:T(8,128)(2,1)S(1)}, bf16[6,128,128]{2,1,0:T(8,128)(2,1)S(1)}, u32[]{:S(2)}, u32[]{:S(2)}) %collective-permute-start.15) | collective-permute-done | bytes 196640 | tf_op jit(solution)/shard_map/ppermute | solution.py:42
  89.6 1.9 %collective-permute-done.22.sib_sums = bf16[16,128,128]{2,1,0:T(8,128)(2,1)S(1)} collective-permute-done((bf16[16,128,128]{2,1,0:T(8,128)(2,1)S(1)}, bf16[16,128,128]{2,1,0:T(8,128)(2,1)S(1)}, u32[]{:S(2)}, u32[]{:S(2)}) %collective-permute-start.22) | collective-permute-done | bytes 524320 | tf_op jit(solution)/shard_map/ppermute | solution.py:42
  91.5 2.2 %dense.1 = (bf16[1024,256]{1,0:T(8,128)(2,1)}, bf16[6,128,128]{2,1,0:T(8,128)(2,1)S(1)}, bf16[7,128,128]{2,1,0:T(8,128)(2,1)S(1)}, bf16[5,128,128]{2,1,0:T(8,128)(2,1)S(1)}) custom-call(s32[1]{0:T(128)} %bitcast.core_ref, bf16[256,256]{1,0:T(8,128)(2,1)S(1)} %copy-done.3, bf16[1024,256]{1,0:T(8,128)(2,1)S(1)} %copy-done.1, ...), custom_call_target="tpu_custom_call" | custom-call | flops 536870912 | bytes 4194304 | tf_op jit(solution)/shard_map/dense/pallas_call | solution.py:387
  93.7 1.5 collective-permute-start.25
  95.3 3.1 %collective-permute-start.27 = (bf16[5,128,128]{2,1,0:T(8,128)(2,1)S(1)}, bf16[5,128,128]{2,1,0:T(8,128)(2,1)S(1)}, u32[]{:S(2)}, u32[]{:S(2)}) collective-permute-start(bf16[5,128,128]{2,1,0:T(8,128)(2,1)S(1)} %get-tuple-element.52), channel_id=1, source_target_pairs={{0,4},{1,5},{2,6},{3,7},{4,0},{5,1},{6,2},{7,3},{8,12},{9,13},{10,... | collective-permute-start | bytes 491528 | tf_op jit(solution)/shard_map/ppermute | solution.py:42
  98.5 3.5 %collective-permute-done.23 = bf16[6,128,128]{2,1,0:T(8,128)(2,1)S(1)} collective-permute-done((bf16[6,128,128]{2,1,0:T(8,128)(2,1)S(1)}, bf16[6,128,128]{2,1,0:T(8,128)(2,1)S(1)}, u32[]{:S(2)}, u32[]{:S(2)}) %collective-permute-start.23) | collective-permute-done | bytes 196640 | tf_op jit(solution)/shard_map/ppermute | solution.py:42
  102.0 1.9 %collective-permute-start.24 = (bf16[12,128,128]{2,1,0:T(8,128)(2,1)S(1)}, bf16[12,128,128]{2,1,0:T(8,128)(2,1)S(1)}, u32[]{:S(2)}, u32[]{:S(2)}) collective-permute-start(bf16[12,128,128]{2,1,0:T(8,128)(2,1)S(1)} %pad_maximum_fusion.3), channel_id=1, source_target_pairs={{0,3},{1,2},{2,1},{3,0},{4,7},{5,6},{6,5},{7,4},{8,11},{9,10},{10,... | collective-permute-start | bytes 1179656 | tf_op jit(solution)/shard_map/ppermute | solution.py:42
  104.0 2.8 %collective-permute-start.26 = (bf16[12,128,128]{2,1,0:T(8,128)(2,1)S(1)}, bf16[12,128,128]{2,1,0:T(8,128)(2,1)S(1)}, u32[]{:S(2)}, u32[]{:S(2)}) collective-permute-start(bf16[12,128,128]{2,1,0:T(8,128)(2,1)S(1)} %pad_maximum_fusion.4), channel_id=1, source_target_pairs={{0,4},{1,5},{2,6},{3,7},{4,0},{5,1},{6,2},{7,3},{8,12},{9,13},{10,... | collective-permute-start | bytes 1179656 | tf_op jit(solution)/shard_map/ppermute | solution.py:42
  107.0 6.3 %collective-permute-done.24 = bf16[12,128,128]{2,1,0:T(8,128)(2,1)S(1)} collective-permute-done((bf16[12,128,128]{2,1,0:T(8,128)(2,1)S(1)}, bf16[12,128,128]{2,1,0:T(8,128)(2,1)S(1)}, u32[]{:S(2)}, u32[]{:S(2)}) %collective-permute-start.24) | collective-permute-done | bytes 393248 | tf_op jit(solution)/shard_map/ppermute | solution.py:42
  113.3 2.9 %collective-permute-start.29 = (bf16[24,128,128]{2,1,0:T(8,128)(2,1)S(1)}, bf16[24,128,128]{2,1,0:T(8,128)(2,1)S(1)}, u32[]{:S(2)}, u32[]{:S(2)}) collective-permute-start(bf16[24,128,128]{2,1,0:T(8,128)(2,1)S(1)} %constant_dynamic-update-slice_fusion.9.rest_0_), channel_id=1, source_target_pairs={{0,4},{1,5},{2,6},{3,7},{4,0},{5,1},{6,2},{7,3},{8,12},{9,13},{10,... | collective-permute-start | bytes 2359304 | tf_op jit(solution)/shard_map/ppermute | solution.py:42
  116.5 1.8 collective-permute-start.31
  118.8 2.9 %early_adjoint.1.before = bf16[128,128,128]{2,1,0:T(8,128)(2,1)S(1)} custom-call(s32[256]{0:T(256)S(1)} %select_reduce_fusion.list_ref, s32[10]{0:T(128)S(1)} %convert_reduce_fusion.2.bound_ref, bf16[256,128,128]{2,1,0:T(8,128)(2,1)S(1)} %get-tuple-element.41.tiles, bf16[24,128,128]{2,1,0:T(8,128)(2,1)S(1)} %constant_dynamic-update-slice_fusion.9.rest_0_, ...), custom_call_target="tpu_custom_call" | custom-call | flops 268435456 | bytes 16777216 | tf_op jit(solution)/shard_map/early_adjoint/pallas_call | solution.py:301
  121.7 10.6 %collective-permute-done.31.rest_2_ = bf16[20,128,128]{2,1,0:T(8,128)(2,1)S(1)} collective-permute-done((bf16[20,128,128]{2,1,0:T(8,128)(2,1)S(1)}, bf16[20,128,128]{2,1,0:T(8,128)(2,1)S(1)}, u32[]{:S(2)}, u32[]{:S(2)}) %collective-permute-start.31) | collective-permute-done | bytes 655392 | tf_op jit(solution)/shard_map/ppermute | solution.py:42
  132.4 1.8 %sent_adjoint.1 = (bf16[24,128,128]{2,1,0:T(8,128)(2,1)S(1)}, bf16[22,128,128]{2,1,0:T(8,128)(2,1)S(1)}, bf16[20,128,128]{2,1,0:T(8,128)(2,1)S(1)}) custom-call(s32[256]{0:T(256)S(1)} %select_reduce_fusion.list_ref, s32[10]{0:T(128)S(1)} %convert_reduce_fusion.2.bound_ref, bf16[256,128,128]{2,1,0:T(8,128)(2,1)S(1)} %get-tuple-element.41.tiles, ...), custom_call_target="tpu_custom_call" | custom-call | flops 134217728 | bytes 8388608 | tf_op jit(solution)/shard_map/sent_adjoint/pallas_call | solution.py:326
  134.3 2.7 %collective-permute-start.38 = (bf16[20,128,128]{2,1,0:T(8,128)(2,1)S(1)}, bf16[20,128,128]{2,1,0:T(8,128)(2,1)S(1)}, u32[]{:S(2)}, u32[]{:S(2)}) collective-permute-start(bf16[20,128,128]{2,1,0:T(8,128)(2,1)S(1)} %get-tuple-element.58), channel_id=1, source_target_pairs={{0,96},{1,97},{2,98},{3,99},{4,100},{5,101},{6,102},{7,103},{8,104... | collective-permute-start | bytes 1966088 | tf_op jit(solution)/shard_map/ppermute | solution.py:42
  137.0 3.9 %collective-permute-start.35 = (bf16[22,128,128]{2,1,0:T(8,128)(2,1)S(1)}, bf16[22,128,128]{2,1,0:T(8,128)(2,1)S(1)}, u32[]{:S(2)}, u32[]{:S(2)}) collective-permute-start(bf16[22,128,128]{2,1,0:T(8,128)(2,1)S(1)} %get-tuple-element.56), channel_id=1, source_target_pairs={{0,32},{1,33},{2,34},{3,35},{4,36},{5,37},{6,38},{7,39},{8,40},{9,... | collective-permute-start | bytes 2162696 | tf_op jit(solution)/shard_map/ppermute | solution.py:42
  140.8 1.5 collective-permute-start.32
  142.4 1.8 %kept_adjoint.1 = (bf16[24,128,128]{2,1,0:T(8,128)(2,1)S(1)}, bf16[20,128,128]{2,1,0:T(8,128)(2,1)S(1)}, bf16[20,128,128]{2,1,0:T(8,128)(2,1)S(1)}) custom-call(s32[256]{0:T(256)S(1)} %select_reduce_fusion.list_ref, s32[10]{0:T(128)S(1)} %convert_reduce_fusion.2.bound_ref, bf16[256,128,128]{2,1,0:T(8,128)(2,1)S(1)} %get-tuple-element.41.tiles, ...), custom_call_target="tpu_custom_call" | custom-call | flops 134217728 | bytes 8388608 | tf_op jit(solution)/shard_map/kept_adjoint/pallas_call | solution.py:326
  144.2 5.1 %collective-permute-done.38 = bf16[20,128,128]{2,1,0:T(8,128)(2,1)S(1)} collective-permute-done((bf16[20,128,128]{2,1,0:T(8,128)(2,1)S(1)}, bf16[20,128,128]{2,1,0:T(8,128)(2,1)S(1)}, u32[]{:S(2)}, u32[]{:S(2)}) %collective-permute-start.38) | collective-permute-done | bytes 655392 | tf_op jit(solution)/shard_map/ppermute | solution.py:42
  149.4 4.1 %collective-permute-start.39 = (bf16[10,128,128]{2,1,0:T(8,128)(2,1)S(1)}, bf16[10,128,128]{2,1,0:T(8,128)(2,1)S(1)}, u32[]{:S(2)}, u32[]{:S(2)}) collective-permute-start(bf16[10,128,128]{2,1,0:T(8,128)(2,1)S(1)} %add_convert_fusion.2), channel_id=1, source_target_pairs={{0,32},{1,33},{2,34},{3,35},{4,36},{5,37},{6,38},{7,39},{8,40},{9,... | collective-permute-start | bytes 983048 | tf_op jit(solution)/shard_map/ppermute | solution.py:42
  153.6 4.1 %collective-permute-done.35 = bf16[22,128,128]{2,1,0:T(8,128)(2,1)S(1)} collective-permute-done((bf16[22,128,128]{2,1,0:T(8,128)(2,1)S(1)}, bf16[22,128,128]{2,1,0:T(8,128)(2,1)S(1)}, u32[]{:S(2)}, u32[]{:S(2)}) %collective-permute-start.35) | collective-permute-done | bytes 720928 | tf_op jit(solution)/shard_map/ppermute | solution.py:42
  157.9 1.5 collective-permute-start.36
  159.3 1.3 collective-permute-done.32
  160.7 0.9 collective-permute-start.33
  161.6 1.5 collective-permute-start.40
  163.2 4.4 %collective-permute-done.36 = bf16[12,128,128]{2,1,0:T(8,128)(2,1)S(1)} collective-permute-done((bf16[12,128,128]{2,1,0:T(8,128)(2,1)S(1)}, bf16[12,128,128]{2,1,0:T(8,128)(2,1)S(1)}, u32[]{:S(2)}, u32[]{:S(2)}) %collective-permute-start.36) | collective-permute-done | bytes 393248 | tf_op jit(solution)/shard_map/ppermute | solution.py:42
  167.7 1.1 collective-permute-start.37
  168.8 0.6 collective-permute-done.40
  169.4 2.8 %collective-permute-done.33 = bf16[12,128,128]{2,1,0:T(8,128)(2,1)S(1)} collective-permute-done((bf16[12,128,128]{2,1,0:T(8,128)(2,1)S(1)}, bf16[12,128,128]{2,1,0:T(8,128)(2,1)S(1)}, u32[]{:S(2)}, u32[]{:S(2)}) %collective-permute-start.33) | collective-permute-done | bytes 393248 | tf_op jit(solution)/shard_map/ppermute | solution.py:42
  172.4 2.6 %collective-permute-done.37 = bf16[7,128,128]{2,1,0:T(8,128)(2,1)S(1)} collective-permute-done((bf16[7,128,128]{2,1,0:T(8,128)(2,1)S(1)}, bf16[7,128,128]{2,1,0:T(8,128)(2,1)S(1)}, u32[]{:S(2)}, u32[]{:S(2)}) %collective-permute-start.37) | collective-permute-done | bytes 229408 | tf_op jit(solution)/shard_map/ppermute | solution.py:42
  175.3 2.8 %collective-permute-done.34 = bf16[6,128,128]{2,1,0:T(8,128)(2,1)S(1)} collective-permute-done((bf16[6,128,128]{2,1,0:T(8,128)(2,1)S(1)}, bf16[6,128,128]{2,1,0:T(8,128)(2,1)S(1)}, u32[]{:S(2)}, u32[]{:S(2)}) %collective-permute-start.34) | collective-permute-done | bytes 196640 | tf_op jit(solution)/shard_map/ppermute | solution.py:42
  178.2 1.0 turn_back.1
  (109 shorter events, 7.7 us)
Async XLA Ops:
  0.6 23.5 %copy-start.1 = (bf16[1024,256]{1,0:T(8,128)(2,1)S(1)}, bf16[1024,256]{1,0:T(8,128)(2,1)}, u32[]{:S(2)}) copy-start(bf16[1024,256]{1,0:T(8,128)(2,1)} %own_cot.1) | copy-start | bytes 1572868
  0.6 2.2 %collective-permute-start = (bf16[1024,256]{1,0:T(8,128)(2,1)}, bf16[1024,256]{1,0:T(8,128)(2,1)S(1)}, u32[]{:S(2)}, u32[]{:S(2)}) collective-permute-start(bf16[1024,256]{1,0:T(8,128)(2,1)} %own_ref.1), channel_id=1, source_target_pairs={{0,8},{1,9},{2,10},{3,11},{4,12},{5,13},{6,14},{7,15},{8,0},{9,1},... | collective-permute-start | bytes 1572872 | tf_op jit(solution)/shard_map/ppermute | solution.py:42
  2.8 1.0 copy-start.2
  3.9 20.2 %copy-start.4 = (s32[1,1,128]{2,1,0:T(1,128)S(1)}, s32[1,1,128]{2,1,0:T(1,128)}, u32[]{:S(2)}) copy-start(s32[1,1,128]{2,1,0:T(1,128)} %param.12) | copy-start | bytes 1540
  3.9 20.2 %copy-start.5 = (s32[1,1,128]{2,1,0:T(1,128)S(1)}, s32[1,1,128]{2,1,0:T(1,128)}, u32[]{:S(2)}) copy-start(s32[1,1,128]{2,1,0:T(1,128)} %param.11) | copy-start | bytes 1540
  4.1 26.2 %collective-permute-start.5 = (bf16[128,128,128]{2,1,0:T(8,128)(2,1)}, bf16[128,128,128]{2,1,0:T(8,128)(2,1)}, u32[]{:S(2)}, u32[]{:S(2)}) collective-permute-start(bf16[128,128,128]{2,1,0:T(8,128)(2,1)} %bitcast.22), channel_id=1, source_target_pairs={{0,8},{1,9},{2,10},{3,11},{4,12},{5,13},{6,14},{7,15},{8,0},{9,1},... | collective-permute-start | bytes 12582920 | tf_op jit(solution)/shard_map/ppermute | solution.py:42
  5.0 25.3 %copy-start = (bf16[1,1,128,128,128]{4,3,2,1,0:T(8,128)(2,1)S(1)}, bf16[1,1,128,128,128]{4,3,2,1,0:T(8,128)(2,1)}, u32[]{:S(2)}) copy-start(bf16[1,1,128,128,128]{4,3,2,1,0:T(8,128)(2,1)} %param.10) | copy-start | bytes 12582916
  5.0 6.6 %collective-permute-start.1 = (bf16[5,128,128]{2,1,0:T(8,128)(2,1)S(1)}, bf16[5,128,128]{2,1,0:T(8,128)(2,1)S(1)}, u32[]{:S(2)}, u32[]{:S(2)}) collective-permute-start(bf16[5,128,128]{2,1,0:T(8,128)(2,1)S(1)} %get-tuple-element.32), channel_id=1, source_target_pairs={{0,16},{1,17},{2,18},{3,19},{4,20},{5,21},{6,22},{7,23},{8,24},{9,... | collective-permute-start | bytes 491528 | tf_op jit(solution)/shard_map/ppermute | solution.py:42
  6.7 7.5 %collective-permute-start.8 = (bf16[5,128,128]{2,1,0:T(8,128)(2,1)S(1)}, bf16[5,128,128]{2,1,0:T(8,128)(2,1)S(1)}, u32[]{:S(2)}, u32[]{:S(2)}) collective-permute-start(bf16[5,128,128]{2,1,0:T(8,128)(2,1)S(1)} %get-tuple-element.40), channel_id=1, source_target_pairs={{0,96},{1,97},{2,98},{3,99},{4,100},{5,101},{6,102},{7,103},{8,104... | collective-permute-start | bytes 491528 | tf_op jit(solution)/shard_map/ppermute | solution.py:42
  9.8 7.9 %collective-permute-start.6 = (bf16[6,128,128]{2,1,0:T(8,128)(2,1)S(1)}, bf16[6,128,128]{2,1,0:T(8,128)(2,1)S(1)}, u32[]{:S(2)}, u32[]{:S(2)}) collective-permute-start(bf16[6,128,128]{2,1,0:T(8,128)(2,1)S(1)} %get-tuple-element.38), channel_id=1, source_target_pairs={{0,32},{1,33},{2,34},{3,35},{4,36},{5,37},{6,38},{7,39},{8,40},{9,... | collective-permute-start | bytes 589832 | tf_op jit(solution)/shard_map/ppermute | solution.py:42
  11.6 11.9 %collective-permute-start.2 = (bf16[10,128,128]{2,1,0:T(8,128)(2,1)S(1)}, bf16[10,128,128]{2,1,0:T(8,128)(2,1)S(1)}, u32[]{:S(2)}, u32[]{:S(2)}) collective-permute-start(bf16[10,128,128]{2,1,0:T(8,128)(2,1)S(1)} %pad_maximum_fusion.7), channel_id=1, source_target_pairs={{0,32},{1,33},{2,34},{3,35},{4,36},{5,37},{6,38},{7,39},{8,40},{9,... | collective-permute-start | bytes 983048 | tf_op jit(solution)/shard_map/ppermute | solution.py:42
  14.3 9.9 %collective-permute-start.9 = (bf16[10,128,128]{2,1,0:T(8,128)(2,1)S(1)}, bf16[10,128,128]{2,1,0:T(8,128)(2,1)S(1)}, u32[]{:S(2)}, u32[]{:S(2)}) collective-permute-start(bf16[10,128,128]{2,1,0:T(8,128)(2,1)S(1)} %pad_maximum_fusion.8), channel_id=1, source_target_pairs={{0,16},{1,17},{2,18},{3,19},{4,20},{5,21},{6,22},{7,23},{8,24},{9,... | collective-permute-start | bytes 983048 | tf_op jit(solution)/shard_map/ppermute | solution.py:42
  17.8 11.4 %collective-permute-start.7 = (bf16[12,128,128]{2,1,0:T(8,128)(2,1)S(1)}, bf16[12,128,128]{2,1,0:T(8,128)(2,1)S(1)}, u32[]{:S(2)}, u32[]{:S(2)}) collective-permute-start(bf16[12,128,128]{2,1,0:T(8,128)(2,1)S(1)} %pad_maximum_fusion.2), channel_id=1, source_target_pairs={{0,96},{1,97},{2,98},{3,99},{4,100},{5,101},{6,102},{7,103},{8,104... | collective-permute-start | bytes 1179656 | tf_op jit(solution)/shard_map/ppermute | solution.py:42
  23.6 19.2 %collective-permute-start.12 = (bf16[20,128,128]{2,1,0:T(8,128)(2,1)S(1)}, bf16[20,128,128]{2,1,0:T(8,128)(2,1)S(1)}, u32[]{:S(2)}, u32[]{:S(2)}) collective-permute-start(bf16[20,128,128]{2,1,0:T(8,128)(2,1)S(1)} %constant_dynamic-update-slice_fusion.rest_2_), channel_id=1, source_target_pairs={{0,96},{1,97},{2,98},{3,99},{4,100},{5,101},{6,102},{7,103},{8,104... | collective-permute-start | bytes 1966088 | tf_op jit(solution)/shard_map/ppermute | solution.py:42
  24.1 6.2 %collective-permute-start.3 = (bf16[1024,256]{1,0:T(8,128)(2,1)S(1)}, bf16[1024,256]{1,0:T(8,128)(2,1)S(1)}, u32[]{:S(2)}, u32[]{:S(2)}) collective-permute-start(bf16[1024,256]{1,0:T(8,128)(2,1)S(1)} %copy-done.1), channel_id=1, source_target_pairs={{0,8},{1,9},{2,10},{3,11},{4,12},{5,13},{6,14},{7,15},{8,0},{9,1},... | collective-permute-start | bytes 1572872 | tf_op jit(solution)/shard_map/ppermute | solution.py:42
  24.2 1.8 %collective-permute-start.4 = (s32[3,128]{1,0:T(4,128)S(1)}, s32[3,128]{1,0:T(4,128)S(1)}, u32[]{:S(2)}, u32[]{:S(2)}) collective-permute-start(s32[3,128]{1,0:T(4,128)S(1)} %get-tuple-element.81), channel_id=1, source_target_pairs={{0,8},{1,9},{2,10},{3,11},{4,12},{5,13},{6,14},{7,15},{8,0},{9,1},... | collective-permute-start | bytes 4616 | tf_op jit(solution)/shard_map/ppermute | solution.py:42
  26.0 16.8 %collective-permute-start.11 = (bf16[20,128,128]{2,1,0:T(8,128)(2,1)S(1)}, bf16[20,128,128]{2,1,0:T(8,128)(2,1)S(1)}, u32[]{:S(2)}, u32[]{:S(2)}) collective-permute-start(bf16[20,128,128]{2,1,0:T(8,128)(2,1)S(1)} %constant_dynamic-update-slice_fusion.6.rest_1_), channel_id=1, source_target_pairs={{0,32},{1,33},{2,34},{3,35},{4,36},{5,37},{6,38},{7,39},{8,40},{9,... | collective-permute-start | bytes 1966088 | tf_op jit(solution)/shard_map/ppermute | solution.py:42
  29.2 16.9 %collective-permute-start.10 = (bf16[24,128,128]{2,1,0:T(8,128)(2,1)S(1)}, bf16[24,128,128]{2,1,0:T(8,128)(2,1)S(1)}, u32[]{:S(2)}, u32[]{:S(2)}) collective-permute-start(bf16[24,128,128]{2,1,0:T(8,128)(2,1)S(1)} %constant_dynamic-update-slice_fusion.3.rest_0_), channel_id=1, source_target_pairs={{0,16},{1,17},{2,18},{3,19},{4,20},{5,21},{6,22},{7,23},{8,24},{9,... | collective-permute-start | bytes 2359304 | tf_op jit(solution)/shard_map/ppermute | solution.py:42
  48.1 15.8 %collective-permute-start.19 = (bf16[20,128,128]{2,1,0:T(8,128)(2,1)S(1)}, bf16[20,128,128]{2,1,0:T(8,128)(2,1)S(1)}, u32[]{:S(2)}, u32[]{:S(2)}) collective-permute-start(bf16[20,128,128]{2,1,0:T(8,128)(2,1)S(1)} %get-tuple-element.48), channel_id=1, source_target_pairs={{0,3},{1,2},{2,1},{3,0},{4,7},{5,6},{6,5},{7,4},{8,11},{9,10},{10,... | collective-permute-start | bytes 1966088 | tf_op jit(solution)/shard_map/ppermute | solution.py:42
  52.2 15.6 %collective-permute-start.16 = (bf16[20,128,128]{2,1,0:T(8,128)(2,1)S(1)}, bf16[20,128,128]{2,1,0:T(8,128)(2,1)S(1)}, u32[]{:S(2)}, u32[]{:S(2)}) collective-permute-start(bf16[20,128,128]{2,1,0:T(8,128)(2,1)S(1)} %get-tuple-element.46), channel_id=1, source_target_pairs={{0,1},{1,0},{2,3},{3,2},{4,5},{5,4},{6,7},{7,6},{8,9},{9,8},{10,11... | collective-permute-start | bytes 1966088 | tf_op jit(solution)/shard_map/ppermute | solution.py:42
  53.0 20.3 %collective-permute-start.13 = (bf16[24,128,128]{2,1,0:T(8,128)(2,1)S(1)}, bf16[24,128,128]{2,1,0:T(8,128)(2,1)S(1)}, u32[]{:S(2)}, u32[]{:S(2)}) collective-permute-start(bf16[24,128,128]{2,1,0:T(8,128)(2,1)S(1)} %get-tuple-element.44), channel_id=1, source_target_pairs={{0,4},{1,5},{2,6},{3,7},{4,0},{5,1},{6,2},{7,3},{8,12},{9,13},{10,... | collective-permute-start | bytes 2359304 | tf_op jit(solution)/shard_map/ppermute | solution.py:42
  64.0 27.5 %copy-start.3 = (bf16[256,256]{1,0:T(8,128)(2,1)S(1)}, bf16[256,256]{1,0:T(8,128)(2,1)}, u32[]{:S(2)}) copy-start(bf16[256,256]{1,0:T(8,128)(2,1)} %weight_ref.1) | copy-start | bytes 393220
  64.0 10.2 %collective-permute-start.20 = (bf16[10,128,128]{2,1,0:T(8,128)(2,1)S(1)}, bf16[10,128,128]{2,1,0:T(8,128)(2,1)S(1)}, u32[]{:S(2)}, u32[]{:S(2)}) collective-permute-start(bf16[10,128,128]{2,1,0:T(8,128)(2,1)S(1)} %add_convert_fusion.4), channel_id=1, source_target_pairs={{0,1},{1,0},{2,3},{3,2},{4,5},{5,4},{6,7},{7,6},{8,9},{9,8},{10,11... | collective-permute-start | bytes 983048 | tf_op jit(solution)/shard_map/ppermute | solution.py:42
  68.0 10.6 %collective-permute-start.17 = (bf16[10,128,128]{2,1,0:T(8,128)(2,1)S(1)}, bf16[10,128,128]{2,1,0:T(8,128)(2,1)S(1)}, u32[]{:S(2)}, u32[]{:S(2)}) collective-permute-start(bf16[10,128,128]{2,1,0:T(8,128)(2,1)S(1)} %add_convert_fusion.5), channel_id=1, source_target_pairs={{0,4},{1,5},{2,6},{3,7},{4,0},{5,1},{6,2},{7,3},{8,12},{9,13},{10,... | collective-permute-start | bytes 983048 | tf_op jit(solution)/shard_map/ppermute | solution.py:42
  73.4 9.8 %collective-permute-start.14 = (bf16[12,128,128]{2,1,0:T(8,128)(2,1)S(1)}, bf16[12,128,128]{2,1,0:T(8,128)(2,1)S(1)}, u32[]{:S(2)}, u32[]{:S(2)}) collective-permute-start(bf16[12,128,128]{2,1,0:T(8,128)(2,1)S(1)} %add_convert_fusion.1), channel_id=1, source_target_pairs={{0,3},{1,2},{2,1},{3,0},{4,7},{5,6},{6,5},{7,4},{8,11},{9,10},{10,... | collective-permute-start | bytes 1179656 | tf_op jit(solution)/shard_map/ppermute | solution.py:42
  74.2 6.9 %collective-permute-start.21 = (bf16[5,128,128]{2,1,0:T(8,128)(2,1)S(1)}, bf16[5,128,128]{2,1,0:T(8,128)(2,1)S(1)}, u32[]{:S(2)}, u32[]{:S(2)}) collective-permute-start(bf16[5,128,128]{2,1,0:T(8,128)(2,1)S(1)} %add_convert_fusion.15), channel_id=1, source_target_pairs={{0,4},{1,5},{2,6},{3,7},{4,0},{5,1},{6,2},{7,3},{8,12},{9,13},{10,... | collective-permute-start | bytes 491528 | tf_op jit(solution)/shard_map/ppermute | solution.py:42
  78.7 6.6 %collective-permute-start.18 = (bf16[5,128,128]{2,1,0:T(8,128)(2,1)S(1)}, bf16[5,128,128]{2,1,0:T(8,128)(2,1)S(1)}, u32[]{:S(2)}, u32[]{:S(2)}) collective-permute-start(bf16[5,128,128]{2,1,0:T(8,128)(2,1)S(1)} %add_convert_fusion.17), channel_id=1, source_target_pairs={{0,3},{1,2},{2,1},{3,0},{4,7},{5,6},{6,5},{7,4},{8,11},{9,10},{10,... | collective-permute-start | bytes 491528 | tf_op jit(solution)/shard_map/ppermute | solution.py:42
  83.4 5.8 %collective-permute-start.15 = (bf16[6,128,128]{2,1,0:T(8,128)(2,1)S(1)}, bf16[6,128,128]{2,1,0:T(8,128)(2,1)S(1)}, u32[]{:S(2)}, u32[]{:S(2)}) collective-permute-start(bf16[6,128,128]{2,1,0:T(8,128)(2,1)S(1)} %add_convert_fusion.9), channel_id=1, source_target_pairs={{0,1},{1,0},{2,3},{3,2},{4,5},{5,4},{6,7},{7,6},{8,9},{9,8},{10,11... | collective-permute-start | bytes 589832 | tf_op jit(solution)/shard_map/ppermute | solution.py:42
  89.3 2.2 %collective-permute-start.22 = (bf16[16,128,128]{2,1,0:T(8,128)(2,1)S(1)}, bf16[16,128,128]{2,1,0:T(8,128)(2,1)S(1)}, u32[]{:S(2)}, u32[]{:S(2)}) collective-permute-start(bf16[16,128,128]{2,1,0:T(8,128)(2,1)S(1)} %pad_maximum_fusion.1.own_sums), channel_id=1, source_target_pairs={{0,8},{1,9},{2,10},{3,11},{4,12},{5,13},{6,14},{7,15},{8,0},{9,1},... | collective-permute-start | bytes 1572872 | tf_op jit(solution)/shard_map/ppermute | solution.py:42
  93.7 10.2 %collective-permute-start.25 = (bf16[7,128,128]{2,1,0:T(8,128)(2,1)S(1)}, bf16[7,128,128]{2,1,0:T(8,128)(2,1)S(1)}, u32[]{:S(2)}, u32[]{:S(2)}) collective-permute-start(bf16[7,128,128]{2,1,0:T(8,128)(2,1)S(1)} %get-tuple-element.51), channel_id=1, source_target_pairs={{0,3},{1,2},{2,1},{3,0},{4,7},{5,6},{6,5},{7,4},{8,11},{9,10},{10,... | collective-permute-start | bytes 688136 | tf_op jit(solution)/shard_map/ppermute | solution.py:42
  95.2 6.7 %collective-permute-start.23 = (bf16[6,128,128]{2,1,0:T(8,128)(2,1)S(1)}, bf16[6,128,128]{2,1,0:T(8,128)(2,1)S(1)}, u32[]{:S(2)}, u32[]{:S(2)}) collective-permute-start(bf16[6,128,128]{2,1,0:T(8,128)(2,1)S(1)} %get-tuple-element.50), channel_id=1, source_target_pairs={{0,1},{1,0},{2,3},{3,2},{4,5},{5,4},{6,7},{7,6},{8,9},{9,8},{10,11... | collective-permute-start | bytes 589832 | tf_op jit(solution)/shard_map/ppermute | solution.py:42
  95.3 11.5 %collective-permute-start.27 = (bf16[5,128,128]{2,1,0:T(8,128)(2,1)S(1)}, bf16[5,128,128]{2,1,0:T(8,128)(2,1)S(1)}, u32[]{:S(2)}, u32[]{:S(2)}) collective-permute-start(bf16[5,128,128]{2,1,0:T(8,128)(2,1)S(1)} %get-tuple-element.52), channel_id=1, source_target_pairs={{0,4},{1,5},{2,6},{3,7},{4,0},{5,1},{6,2},{7,3},{8,12},{9,13},{10,... | collective-permute-start | bytes 491528 | tf_op jit(solution)/shard_map/ppermute | solution.py:42
  102.0 11.3 %collective-permute-start.24 = (bf16[12,128,128]{2,1,0:T(8,128)(2,1)S(1)}, bf16[12,128,128]{2,1,0:T(8,128)(2,1)S(1)}, u32[]{:S(2)}, u32[]{:S(2)}) collective-permute-start(bf16[12,128,128]{2,1,0:T(8,128)(2,1)S(1)} %pad_maximum_fusion.3), channel_id=1, source_target_pairs={{0,3},{1,2},{2,1},{3,0},{4,7},{5,6},{6,5},{7,4},{8,11},{9,10},{10,... | collective-permute-start | bytes 1179656 | tf_op jit(solution)/shard_map/ppermute | solution.py:42
  104.0 12.2 %collective-permute-start.26 = (bf16[12,128,128]{2,1,0:T(8,128)(2,1)S(1)}, bf16[12,128,128]{2,1,0:T(8,128)(2,1)S(1)}, u32[]{:S(2)}, u32[]{:S(2)}) collective-permute-start(bf16[12,128,128]{2,1,0:T(8,128)(2,1)S(1)} %pad_maximum_fusion.4), channel_id=1, source_target_pairs={{0,4},{1,5},{2,6},{3,7},{4,0},{5,1},{6,2},{7,3},{8,12},{9,13},{10,... | collective-permute-start | bytes 1179656 | tf_op jit(solution)/shard_map/ppermute | solution.py:42
  106.8 9.7 %collective-permute-start.28 = (bf16[10,128,128]{2,1,0:T(8,128)(2,1)S(1)}, bf16[10,128,128]{2,1,0:T(8,128)(2,1)S(1)}, u32[]{:S(2)}, u32[]{:S(2)}) collective-permute-start(bf16[10,128,128]{2,1,0:T(8,128)(2,1)S(1)} %pad_maximum_fusion.9), channel_id=1, source_target_pairs={{0,1},{1,0},{2,3},{3,2},{4,5},{5,4},{6,7},{7,6},{8,9},{9,8},{10,11... | collective-permute-start | bytes 983048 | tf_op jit(solution)/shard_map/ppermute | solution.py:42
  113.3 19.1 %collective-permute-start.29 = (bf16[24,128,128]{2,1,0:T(8,128)(2,1)S(1)}, bf16[24,128,128]{2,1,0:T(8,128)(2,1)S(1)}, u32[]{:S(2)}, u32[]{:S(2)}) collective-permute-start(bf16[24,128,128]{2,1,0:T(8,128)(2,1)S(1)} %constant_dynamic-update-slice_fusion.9.rest_0_), channel_id=1, source_target_pairs={{0,4},{1,5},{2,6},{3,7},{4,0},{5,1},{6,2},{7,3},{8,12},{9,13},{10,... | collective-permute-start | bytes 2359304 | tf_op jit(solution)/shard_map/ppermute | solution.py:42
  116.4 15.9 %collective-permute-start.30 = (bf16[22,128,128]{2,1,0:T(8,128)(2,1)S(1)}, bf16[22,128,128]{2,1,0:T(8,128)(2,1)S(1)}, u32[]{:S(2)}, u32[]{:S(2)}) collective-permute-start(bf16[22,128,128]{2,1,0:T(8,128)(2,1)S(1)} %pad_maximum_fusion.rest_1_.rest_3_), channel_id=1, source_target_pairs={{0,1},{1,0},{2,3},{3,2},{4,5},{5,4},{6,7},{7,6},{8,9},{9,8},{10,11... | collective-permute-start | bytes 2162696 | tf_op jit(solution)/shard_map/ppermute | solution.py:42
  116.5 15.7 %collective-permute-start.31 = (bf16[20,128,128]{2,1,0:T(8,128)(2,1)S(1)}, bf16[20,128,128]{2,1,0:T(8,128)(2,1)S(1)}, u32[]{:S(2)}, u32[]{:S(2)}) collective-permute-start(bf16[20,128,128]{2,1,0:T(8,128)(2,1)S(1)} %constant_dynamic-update-slice_fusion.12.rest_2_), channel_id=1, source_target_pairs={{0,3},{1,2},{2,1},{3,0},{4,7},{5,6},{6,5},{7,4},{8,11},{9,10},{10,... | collective-permute-start | bytes 1966088 | tf_op jit(solution)/shard_map/ppermute | solution.py:42
  134.3 15.1 %collective-permute-start.38 = (bf16[20,128,128]{2,1,0:T(8,128)(2,1)S(1)}, bf16[20,128,128]{2,1,0:T(8,128)(2,1)S(1)}, u32[]{:S(2)}, u32[]{:S(2)}) collective-permute-start(bf16[20,128,128]{2,1,0:T(8,128)(2,1)S(1)} %get-tuple-element.58), channel_id=1, source_target_pairs={{0,96},{1,97},{2,98},{3,99},{4,100},{5,101},{6,102},{7,103},{8,104... | collective-permute-start | bytes 1966088 | tf_op jit(solution)/shard_map/ppermute | solution.py:42
  137.0 20.7 %collective-permute-start.35 = (bf16[22,128,128]{2,1,0:T(8,128)(2,1)S(1)}, bf16[22,128,128]{2,1,0:T(8,128)(2,1)S(1)}, u32[]{:S(2)}, u32[]{:S(2)}) collective-permute-start(bf16[22,128,128]{2,1,0:T(8,128)(2,1)S(1)} %get-tuple-element.56), channel_id=1, source_target_pairs={{0,32},{1,33},{2,34},{3,35},{4,36},{5,37},{6,38},{7,39},{8,40},{9,... | collective-permute-start | bytes 2162696 | tf_op jit(solution)/shard_map/ppermute | solution.py:42
  140.8 19.8 %collective-permute-start.32 = (bf16[24,128,128]{2,1,0:T(8,128)(2,1)S(1)}, bf16[24,128,128]{2,1,0:T(8,128)(2,1)S(1)}, u32[]{:S(2)}, u32[]{:S(2)}) collective-permute-start(bf16[24,128,128]{2,1,0:T(8,128)(2,1)S(1)} %get-tuple-element.54), channel_id=1, source_target_pairs={{0,16},{1,17},{2,18},{3,19},{4,20},{5,21},{6,22},{7,23},{8,24},{9,... | collective-permute-start | bytes 2359304 | tf_op jit(solution)/shard_map/ppermute | solution.py:42
  149.4 12.1 %collective-permute-start.39 = (bf16[10,128,128]{2,1,0:T(8,128)(2,1)S(1)}, bf16[10,128,128]{2,1,0:T(8,128)(2,1)S(1)}, u32[]{:S(2)}, u32[]{:S(2)}) collective-permute-start(bf16[10,128,128]{2,1,0:T(8,128)(2,1)S(1)} %add_convert_fusion.2), channel_id=1, source_target_pairs={{0,32},{1,33},{2,34},{3,35},{4,36},{5,37},{6,38},{7,39},{8,40},{9,... | collective-permute-start | bytes 983048 | tf_op jit(solution)/shard_map/ppermute | solution.py:42
  157.9 9.7 %collective-permute-start.36 = (bf16[12,128,128]{2,1,0:T(8,128)(2,1)S(1)}, bf16[12,128,128]{2,1,0:T(8,128)(2,1)S(1)}, u32[]{:S(2)}, u32[]{:S(2)}) collective-permute-start(bf16[12,128,128]{2,1,0:T(8,128)(2,1)S(1)} %pad_maximum_fusion.5), channel_id=1, source_target_pairs={{0,16},{1,17},{2,18},{3,19},{4,20},{5,21},{6,22},{7,23},{8,24},{9,... | collective-permute-start | bytes 1179656 | tf_op jit(solution)/shard_map/ppermute | solution.py:42
  160.7 11.5 %collective-permute-start.33 = (bf16[12,128,128]{2,1,0:T(8,128)(2,1)S(1)}, bf16[12,128,128]{2,1,0:T(8,128)(2,1)S(1)}, u32[]{:S(2)}, u32[]{:S(2)}) collective-permute-start(bf16[12,128,128]{2,1,0:T(8,128)(2,1)S(1)} %add_convert_fusion), channel_id=1, source_target_pairs={{0,96},{1,97},{2,98},{3,99},{4,100},{5,101},{6,102},{7,103},{8,104... | collective-permute-start | bytes 1179656 | tf_op jit(solution)/shard_map/ppermute | solution.py:42
  161.6 7.7 %collective-permute-start.40 = (bf16[5,128,128]{2,1,0:T(8,128)(2,1)S(1)}, bf16[5,128,128]{2,1,0:T(8,128)(2,1)S(1)}, u32[]{:S(2)}, u32[]{:S(2)}) collective-permute-start(bf16[5,128,128]{2,1,0:T(8,128)(2,1)S(1)} %add_convert_fusion.11), channel_id=1, source_target_pairs={{0,16},{1,17},{2,18},{3,19},{4,20},{5,21},{6,22},{7,23},{8,24},{9,... | collective-permute-start | bytes 491528 | tf_op jit(solution)/shard_map/ppermute | solution.py:42
  167.7 7.3 %collective-permute-start.37 = (bf16[7,128,128]{2,1,0:T(8,128)(2,1)S(1)}, bf16[7,128,128]{2,1,0:T(8,128)(2,1)S(1)}, u32[]{:S(2)}, u32[]{:S(2)}) collective-permute-start(bf16[7,128,128]{2,1,0:T(8,128)(2,1)S(1)} %pad_maximum_fusion.11), channel_id=1, source_target_pairs={{0,96},{1,97},{2,98},{3,99},{4,100},{5,101},{6,102},{7,103},{8,104... | collective-permute-start | bytes 688136 | tf_op jit(solution)/shard_map/ppermute | solution.py:42
  172.3 5.7 %collective-permute-start.34 = (bf16[6,128,128]{2,1,0:T(8,128)(2,1)S(1)}, bf16[6,128,128]{2,1,0:T(8,128)(2,1)S(1)}, u32[]{:S(2)}, u32[]{:S(2)}) collective-permute-start(bf16[6,128,128]{2,1,0:T(8,128)(2,1)S(1)} %add_convert_fusion.7), channel_id=1, source_target_pairs={{0,32},{1,33},{2,34},{3,35},{4,36},{5,37},{6,38},{7,39},{8,40},{9,... | collective-permute-start | bytes 589832 | tf_op jit(solution)/shard_map/ppermute | solution.py:42
  175.2 3.0 %collective-permute-start.41 = (bf16[10,128,128]{2,1,0:T(8,128)(2,1)S(1)}, bf16[10,128,128]{2,1,0:T(8,128)(2,1)S(1)}, u32[]{:S(2)}, u32[]{:S(2)}) collective-permute-start(bf16[10,128,128]{2,1,0:T(8,128)(2,1)S(1)} %fusion), channel_id=1, source_target_pairs={{0,8},{1,9},{2,10},{3,11},{4,12},{5,13},{6,14},{7,15},{8,0},{9,1},... | collective-permute-start | bytes 983048 | tf_op jit(solution)/shard_map/ppermute | solution.py:42

commit v5 on v4

--- a/solution.py
+++ b/solution.py
@@ -140,7 +140,11 @@
     return next((at, tile - lo) for at, (lo, hi) in enumerate(CUTS) if lo <= tile < hi)
 
 
-def turn_kernel(core_ref, own_ref, sib_ref, *out_refs):
+def turn_kernel(core_ref, own_any, sib_ref, *rest):
+    out_refs, (own_ref, sem) = rest[:3], rest[3:]
+    load = pltpu.make_async_copy(own_any, own_ref, sem)
+    load.start()
+    load.wait()
     lanes = pl.ds(pl.multiple_of(core_ref[0] * TILE, TILE), TILE)
     for half, ref in enumerate((own_ref, sib_ref)):
         for tile in range(8):
@@ -152,8 +156,9 @@
     return pl.pallas_call(
         turn_kernel,
         out_shape=third_shapes(),
-        in_specs=[smem_spec(), vmem_spec(), vmem_spec()],
+        in_specs=[smem_spec(), any_spec(), vmem_spec()],
         out_specs=[vmem_spec()] * 3,
+        scratch_shapes=[pltpu.VMEM(own.shape, BF16), pltpu.SemaphoreType.DMA],
         compiler_params=pltpu.CompilerParams(vmem_limit_bytes=8 << 20),
         cost_estimate=cost(0, 2 << 20),
         name="turn_in",

time: 179 us -> 180 us (level)
  Pallas kernels: 18 us -> 22.5 us
  waiting for transfers between devices: 96.9 us -> 92.8 us
    ppermute x42, waiting for transfers between devices: 96.9 us -> 92.8 us  [move(): return lax.ppermute(value, AXES, pairs)]
    pallas_call x1, Pallas kernels: 3.9 us -> 6.09 us  [early_pass(): pl.pallas_call(load_kernel, out_shape=[TOTAL, jax.ShapeDtypeStruct((2 * s...]
  transfers between devices with their start and end apart: 42 -> 42, of which waited for: 30 -> 29; matrix products, arithmetic and copies ran while one was open for 2% -> 2% of each run, Pallas kernels for 6% -> 8%
where the time goes in v5:
time: 180 us; the launch traced here: 179 us
  waiting for transfers between devices  92.8 us (52%)
  starting transfers between devices  56.7 us (32%)
  Pallas kernels  22.5 us (12%)
  other arithmetic  3.5 us (2%)
  between operations  1.84 us (1%)
    ppermute x42, waiting for transfers between devices, move(): return lax.ppermute(value, AXES, pairs)  92.8 us
    ppermute x42, starting transfers between devices, move(): return lax.ppermute(value, AXES, pairs)  56.7 us
    pallas_call x4, Pallas kernels, late_pass(): pl.pallas_call(functools.partial(late_kernel, adjoint, kept), out_shape=t...  9.05 us
    pallas_call x1, Pallas kernels, early_pass(): pl.pallas_call(load_kernel, out_shape=[TOTAL, jax.ShapeDtypeStruct((2 * s...  6.09 us
    pallas_call x1, Pallas kernels, early_pass(): pl.pallas_call(early_kernel, out_shape=TOTAL, in_specs=[smem_spec()] * 2...  3.84 us
  transfers between devices with their start and end apart: 42, of which 29 were waited for; matrix products, arithmetic and copies ran while one was open for 2% of the time, Pallas kernels for 8%

profile of v5, /device:TPU:0, one launch (start us, length us, event | category | flops | bytes accessed | tf_op | source)
XLA Modules:
  0.0 178.9 jit_solution(17236441017643907244)
XLA Ops:
  0.7 2.1 %collective-permute-done.sib_ref = bf16[1024,256]{1,0:T(8,128)(2,1)S(1)} collective-permute-done((bf16[1024,256]{1,0:T(8,128)(2,1)}, bf16[1024,256]{1,0:T(8,128)(2,1)S(1)}, u32[]{:S(2)}, u32[]{:S(2)}) %collective-permute-start) | collective-permute-done | bytes 524320 | tf_op jit(solution)/shard_map/ppermute | solution.py:42
  2.8 1.0 copy-done.2
  5.1 1.7 collective-permute-start.1
  6.8 3.1 %collective-permute-start.8 = (bf16[5,128,128]{2,1,0:T(8,128)(2,1)S(1)}, bf16[5,128,128]{2,1,0:T(8,128)(2,1)S(1)}, u32[]{:S(2)}, u32[]{:S(2)}) collective-permute-start(bf16[5,128,128]{2,1,0:T(8,128)(2,1)S(1)} %get-tuple-element.40), channel_id=1, source_target_pairs={{0,96},{1,97},{2,98},{3,99},{4,100},{5,101},{6,102},{7,103},{8,104... | collective-permute-start | bytes 491528 | tf_op jit(solution)/shard_map/ppermute | solution.py:42
  10.1 1.5 collective-permute-done.1
  11.7 1.7 collective-permute-start.2
  13.4 0.9 collective-permute-done.8
  14.4 0.7 collective-permute-start.9
  15.1 2.7 %collective-permute-done.6 = bf16[6,128,128]{2,1,0:T(8,128)(2,1)S(1)} collective-permute-done((bf16[6,128,128]{2,1,0:T(8,128)(2,1)S(1)}, bf16[6,128,128]{2,1,0:T(8,128)(2,1)S(1)}, u32[]{:S(2)}, u32[]{:S(2)}) %collective-permute-start.6) | collective-permute-done | bytes 196640 | tf_op jit(solution)/shard_map/ppermute | solution.py:42
  18.1 5.5 %collective-permute-done.2 = bf16[10,128,128]{2,1,0:T(8,128)(2,1)S(1)} collective-permute-done((bf16[10,128,128]{2,1,0:T(8,128)(2,1)S(1)}, bf16[10,128,128]{2,1,0:T(8,128)(2,1)S(1)}, u32[]{:S(2)}, u32[]{:S(2)}) %collective-permute-start.2) | collective-permute-done | bytes 327712 | tf_op jit(solution)/shard_map/ppermute | solution.py:42
  24.8 1.2 collective-permute-done.4
  26.5 2.6 %collective-permute-done.7 = bf16[12,128,128]{2,1,0:T(8,128)(2,1)S(1)} collective-permute-done((bf16[12,128,128]{2,1,0:T(8,128)(2,1)S(1)}, bf16[12,128,128]{2,1,0:T(8,128)(2,1)S(1)}, u32[]{:S(2)}, u32[]{:S(2)}) %collective-permute-start.7) | collective-permute-done | bytes 393248 | tf_op jit(solution)/shard_map/ppermute | solution.py:42
  29.2 0.6 collective-permute-start.10
  30.4 6.1 %early_pass.1 = (bf16[128,128,128]{2,1,0:T(8,128)(2,1)S(1)}, bf16[256,128,128]{2,1,0:T(8,128)(2,1)S(1)}) custom-call(s32[2]{0:T(128)S(1)} %add_reduce_fusion.live_ref, s32[256]{0:T(256)S(1)} %select_reduce_fusion.1.list_ref, s32[10]{0:T(128)S(1)} %convert_reduce_fusion.3.bound_ref, bf16[128,128,128]{2,1,0:T(8,128)(2,1)S(1)} %bitcast.23, ...), custom_call_target="tpu_custom_call" | custom-call | flops 268435456 | bytes 16777216 | tf_op jit(solution)/shard_map/early_pass/pallas_call | solution.py:317
  36.5 6.4 %collective-permute-done.11.rest_1_ = bf16[20,128,128]{2,1,0:T(8,128)(2,1)S(1)} collective-permute-done((bf16[20,128,128]{2,1,0:T(8,128)(2,1)S(1)}, bf16[20,128,128]{2,1,0:T(8,128)(2,1)S(1)}, u32[]{:S(2)}, u32[]{:S(2)}) %collective-permute-start.11) | collective-permute-done | bytes 655392 | tf_op jit(solution)/shard_map/ppermute | solution.py:42
  42.9 3.3 %collective-permute-done.10.rest_0_ = bf16[24,128,128]{2,1,0:T(8,128)(2,1)S(1)} collective-permute-done((bf16[24,128,128]{2,1,0:T(8,128)(2,1)S(1)}, bf16[24,128,128]{2,1,0:T(8,128)(2,1)S(1)}, u32[]{:S(2)}, u32[]{:S(2)}) %collective-permute-start.10) | collective-permute-done | bytes 786464 | tf_op jit(solution)/shard_map/ppermute | solution.py:42
  46.1 2.0 %sent_pass.1 = (bf16[24,128,128]{2,1,0:T(8,128)(2,1)S(1)}, bf16[20,128,128]{2,1,0:T(8,128)(2,1)S(1)}, bf16[20,128,128]{2,1,0:T(8,128)(2,1)S(1)}) custom-call(s32[256]{0:T(256)S(1)} %select_reduce_fusion.1.list_ref, s32[10]{0:T(128)S(1)} %convert_reduce_fusion.3.bound_ref, bf16[256,128,128]{2,1,0:T(8,128)(2,1)S(1)} %get-tuple-element.41.tiles, ...), custom_call_target="tpu_custom_call" | custom-call | flops 134217728 | bytes 8388608 | tf_op jit(solution)/shard_map/sent_pass/pallas_call | solution.py:331
  48.2 4.1 %collective-permute-start.19 = (bf16[20,128,128]{2,1,0:T(8,128)(2,1)S(1)}, bf16[20,128,128]{2,1,0:T(8,128)(2,1)S(1)}, u32[]{:S(2)}, u32[]{:S(2)}) collective-permute-start(bf16[20,128,128]{2,1,0:T(8,128)(2,1)S(1)} %get-tuple-element.48), channel_id=1, source_target_pairs={{0,3},{1,2},{2,1},{3,0},{4,7},{5,6},{6,5},{7,4},{8,11},{9,10},{10,... | collective-permute-start | bytes 1966088 | tf_op jit(solution)/shard_map/ppermute | solution.py:42
  52.4 3.3 %collective-permute-start.13 = (bf16[24,128,128]{2,1,0:T(8,128)(2,1)S(1)}, bf16[24,128,128]{2,1,0:T(8,128)(2,1)S(1)}, u32[]{:S(2)}, u32[]{:S(2)}) collective-permute-start(bf16[24,128,128]{2,1,0:T(8,128)(2,1)S(1)} %get-tuple-element.44), channel_id=1, source_target_pairs={{0,4},{1,5},{2,6},{3,7},{4,0},{5,1},{6,2},{7,3},{8,12},{9,13},{10,... | collective-permute-start | bytes 2359304 | tf_op jit(solution)/shard_map/ppermute | solution.py:42
  55.8 2.7 %kept_pass.1 = (bf16[24,128,128]{2,1,0:T(8,128)(2,1)S(1)}, bf16[20,128,128]{2,1,0:T(8,128)(2,1)S(1)}, bf16[20,128,128]{2,1,0:T(8,128)(2,1)S(1)}) custom-call(s32[256]{0:T(256)S(1)} %select_reduce_fusion.1.list_ref, s32[10]{0:T(128)S(1)} %convert_reduce_fusion.3.bound_ref, bf16[256,128,128]{2,1,0:T(8,128)(2,1)S(1)} %get-tuple-element.41.tiles, ...), custom_call_target="tpu_custom_call" | custom-call | flops 134217728 | bytes 8388608 | tf_op jit(solution)/shard_map/kept_pass/pallas_call | solution.py:331
  58.4 5.5 %collective-permute-done.19 = bf16[20,128,128]{2,1,0:T(8,128)(2,1)S(1)} collective-permute-done((bf16[20,128,128]{2,1,0:T(8,128)(2,1)S(1)}, bf16[20,128,128]{2,1,0:T(8,128)(2,1)S(1)}, u32[]{:S(2)}, u32[]{:S(2)}) %collective-permute-start.19) | collective-permute-done | bytes 655392 | tf_op jit(solution)/shard_map/ppermute | solution.py:42
  64.2 3.7 %collective-permute-done.16 = bf16[20,128,128]{2,1,0:T(8,128)(2,1)S(1)} collective-permute-done((bf16[20,128,128]{2,1,0:T(8,128)(2,1)S(1)}, bf16[20,128,128]{2,1,0:T(8,128)(2,1)S(1)}, u32[]{:S(2)}, u32[]{:S(2)}) %collective-permute-start.16) | collective-permute-done | bytes 655392 | tf_op jit(solution)/shard_map/ppermute | solution.py:42
  68.0 3.1 %collective-permute-start.17 = (bf16[10,128,128]{2,1,0:T(8,128)(2,1)S(1)}, bf16[10,128,128]{2,1,0:T(8,128)(2,1)S(1)}, u32[]{:S(2)}, u32[]{:S(2)}) collective-permute-start(bf16[10,128,128]{2,1,0:T(8,128)(2,1)S(1)} %add_convert_fusion.5), channel_id=1, source_target_pairs={{0,4},{1,5},{2,6},{3,7},{4,0},{5,1},{6,2},{7,3},{8,12},{9,13},{10,... | collective-permute-start | bytes 983048 | tf_op jit(solution)/shard_map/ppermute | solution.py:42
  71.1 2.1 %collective-permute-done.13 = bf16[24,128,128]{2,1,0:T(8,128)(2,1)S(1)} collective-permute-done((bf16[24,128,128]{2,1,0:T(8,128)(2,1)S(1)}, bf16[24,128,128]{2,1,0:T(8,128)(2,1)S(1)}, u32[]{:S(2)}, u32[]{:S(2)}) %collective-permute-start.13) | collective-permute-done | bytes 786464 | tf_op jit(solution)/shard_map/ppermute | solution.py:42
  73.4 0.8 collective-permute-start.14
  74.2 3.6 %collective-permute-start.21 = (bf16[5,128,128]{2,1,0:T(8,128)(2,1)S(1)}, bf16[5,128,128]{2,1,0:T(8,128)(2,1)S(1)}, u32[]{:S(2)}, u32[]{:S(2)}) collective-permute-start(bf16[5,128,128]{2,1,0:T(8,128)(2,1)S(1)} %add_convert_fusion.15), channel_id=1, source_target_pairs={{0,4},{1,5},{2,6},{3,7},{4,0},{5,1},{6,2},{7,3},{8,12},{9,13},{10,... | collective-permute-start | bytes 491528 | tf_op jit(solution)/shard_map/ppermute | solution.py:42
  77.8 0.7 collective-permute-done.17
  78.6 1.6 collective-permute-start.18
  80.1 1.0 collective-permute-done.21
  81.2 1.7 collective-permute-done.14
  82.9 0.5 collective-permute-start.15
  83.5 1.7 collective-permute-done.18
  85.3 3.4 %collective-permute-done.15 = bf16[6,128,128]{2,1,0:T(8,128)(2,1)S(1)} collective-permute-done((bf16[6,128,128]{2,1,0:T(8,128)(2,1)S(1)}, bf16[6,128,128]{2,1,0:T(8,128)(2,1)S(1)}, u32[]{:S(2)}, u32[]{:S(2)}) %collective-permute-start.15) | collective-permute-done | bytes 196640 | tf_op jit(solution)/shard_map/ppermute | solution.py:42
  89.1 1.9 %collective-permute-done.22.sib_sums = bf16[16,128,128]{2,1,0:T(8,128)(2,1)S(1)} collective-permute-done((bf16[16,128,128]{2,1,0:T(8,128)(2,1)S(1)}, bf16[16,128,128]{2,1,0:T(8,128)(2,1)S(1)}, u32[]{:S(2)}, u32[]{:S(2)}) %collective-permute-start.22) | collective-permute-done | bytes 524320 | tf_op jit(solution)/shard_map/ppermute | solution.py:42
  91.0 2.2 %dense.1 = (bf16[1024,256]{1,0:T(8,128)(2,1)}, bf16[6,128,128]{2,1,0:T(8,128)(2,1)S(1)}, bf16[7,128,128]{2,1,0:T(8,128)(2,1)S(1)}, bf16[5,128,128]{2,1,0:T(8,128)(2,1)S(1)}) custom-call(s32[1]{0:T(128)} %bitcast.core_ref, bf16[256,256]{1,0:T(8,128)(2,1)S(1)} %copy-done.3, bf16[1024,256]{1,0:T(8,128)(2,1)S(1)} %copy-done.1, ...), custom_call_target="tpu_custom_call" | custom-call | flops 536870912 | bytes 4194304 | tf_op jit(solution)/shard_map/dense/pallas_call | solution.py:392
  93.3 1.6 collective-permute-start.25
  95.3 2.9 %collective-permute-start.27 = (bf16[5,128,128]{2,1,0:T(8,128)(2,1)S(1)}, bf16[5,128,128]{2,1,0:T(8,128)(2,1)S(1)}, u32[]{:S(2)}, u32[]{:S(2)}) collective-permute-start(bf16[5,128,128]{2,1,0:T(8,128)(2,1)S(1)} %get-tuple-element.52), channel_id=1, source_target_pairs={{0,4},{1,5},{2,6},{3,7},{4,0},{5,1},{6,2},{7,3},{8,12},{9,13},{10,... | collective-permute-start | bytes 491528 | tf_op jit(solution)/shard_map/ppermute | solution.py:42
  98.2 3.5 %collective-permute-done.23 = bf16[6,128,128]{2,1,0:T(8,128)(2,1)S(1)} collective-permute-done((bf16[6,128,128]{2,1,0:T(8,128)(2,1)S(1)}, bf16[6,128,128]{2,1,0:T(8,128)(2,1)S(1)}, u32[]{:S(2)}, u32[]{:S(2)}) %collective-permute-start.23) | collective-permute-done | bytes 196640 | tf_op jit(solution)/shard_map/ppermute | solution.py:42
  101.7 1.8 %collective-permute-start.24 = (bf16[12,128,128]{2,1,0:T(8,128)(2,1)S(1)}, bf16[12,128,128]{2,1,0:T(8,128)(2,1)S(1)}, u32[]{:S(2)}, u32[]{:S(2)}) collective-permute-start(bf16[12,128,128]{2,1,0:T(8,128)(2,1)S(1)} %pad_maximum_fusion.3), channel_id=1, source_target_pairs={{0,3},{1,2},{2,1},{3,0},{4,7},{5,6},{6,5},{7,4},{8,11},{9,10},{10,... | collective-permute-start | bytes 1179656 | tf_op jit(solution)/shard_map/ppermute | solution.py:42
  103.6 2.8 %collective-permute-start.26 = (bf16[12,128,128]{2,1,0:T(8,128)(2,1)S(1)}, bf16[12,128,128]{2,1,0:T(8,128)(2,1)S(1)}, u32[]{:S(2)}, u32[]{:S(2)}) collective-permute-start(bf16[12,128,128]{2,1,0:T(8,128)(2,1)S(1)} %pad_maximum_fusion.4), channel_id=1, source_target_pairs={{0,4},{1,5},{2,6},{3,7},{4,0},{5,1},{6,2},{7,3},{8,12},{9,13},{10,... | collective-permute-start | bytes 1179656 | tf_op jit(solution)/shard_map/ppermute | solution.py:42
  106.6 6.4 %collective-permute-done.24 = bf16[12,128,128]{2,1,0:T(8,128)(2,1)S(1)} collective-permute-done((bf16[12,128,128]{2,1,0:T(8,128)(2,1)S(1)}, bf16[12,128,128]{2,1,0:T(8,128)(2,1)S(1)}, u32[]{:S(2)}, u32[]{:S(2)}) %collective-permute-start.24) | collective-permute-done | bytes 393248 | tf_op jit(solution)/shard_map/ppermute | solution.py:42
  113.0 3.1 %collective-permute-start.29 = (bf16[24,128,128]{2,1,0:T(8,128)(2,1)S(1)}, bf16[24,128,128]{2,1,0:T(8,128)(2,1)S(1)}, u32[]{:S(2)}, u32[]{:S(2)}) collective-permute-start(bf16[24,128,128]{2,1,0:T(8,128)(2,1)S(1)} %constant_dynamic-update-slice_fusion.9.rest_0_), channel_id=1, source_target_pairs={{0,4},{1,5},{2,6},{3,7},{4,0},{5,1},{6,2},{7,3},{8,12},{9,13},{10,... | collective-permute-start | bytes 2359304 | tf_op jit(solution)/shard_map/ppermute | solution.py:42
  116.4 1.5 collective-permute-start.31
  118.4 3.8 %early_adjoint.1.before = bf16[128,128,128]{2,1,0:T(8,128)(2,1)S(1)} custom-call(s32[256]{0:T(256)S(1)} %select_reduce_fusion.list_ref, s32[10]{0:T(128)S(1)} %convert_reduce_fusion.2.bound_ref, bf16[256,128,128]{2,1,0:T(8,128)(2,1)S(1)} %get-tuple-element.41.tiles, bf16[24,128,128]{2,1,0:T(8,128)(2,1)S(1)} %constant_dynamic-update-slice_fusion.9.rest_0_, ...), custom_call_target="tpu_custom_call" | custom-call | flops 268435456 | bytes 16777216 | tf_op jit(solution)/shard_map/early_adjoint/pallas_call | solution.py:306
  122.2 9.9 %collective-permute-done.31.rest_2_ = bf16[20,128,128]{2,1,0:T(8,128)(2,1)S(1)} collective-permute-done((bf16[20,128,128]{2,1,0:T(8,128)(2,1)S(1)}, bf16[20,128,128]{2,1,0:T(8,128)(2,1)S(1)}, u32[]{:S(2)}, u32[]{:S(2)}) %collective-permute-start.31) | collective-permute-done | bytes 655392 | tf_op jit(solution)/shard_map/ppermute | solution.py:42
  132.2 1.8 %sent_adjoint.1 = (bf16[24,128,128]{2,1,0:T(8,128)(2,1)S(1)}, bf16[22,128,128]{2,1,0:T(8,128)(2,1)S(1)}, bf16[20,128,128]{2,1,0:T(8,128)(2,1)S(1)}) custom-call(s32[256]{0:T(256)S(1)} %select_reduce_fusion.list_ref, s32[10]{0:T(128)S(1)} %convert_reduce_fusion.2.bound_ref, bf16[256,128,128]{2,1,0:T(8,128)(2,1)S(1)} %get-tuple-element.41.tiles, ...), custom_call_target="tpu_custom_call" | custom-call | flops 134217728 | bytes 8388608 | tf_op jit(solution)/shard_map/sent_adjoint/pallas_call | solution.py:331
  134.0 3.5 %collective-permute-start.38 = (bf16[20,128,128]{2,1,0:T(8,128)(2,1)S(1)}, bf16[20,128,128]{2,1,0:T(8,128)(2,1)S(1)}, u32[]{:S(2)}, u32[]{:S(2)}) collective-permute-start(bf16[20,128,128]{2,1,0:T(8,128)(2,1)S(1)} %get-tuple-element.58), channel_id=1, source_target_pairs={{0,96},{1,97},{2,98},{3,99},{4,100},{5,101},{6,102},{7,103},{8,104... | collective-permute-start | bytes 1966088 | tf_op jit(solution)/shard_map/ppermute | solution.py:42
  137.5 3.0 %collective-permute-start.35 = (bf16[22,128,128]{2,1,0:T(8,128)(2,1)S(1)}, bf16[22,128,128]{2,1,0:T(8,128)(2,1)S(1)}, u32[]{:S(2)}, u32[]{:S(2)}) collective-permute-start(bf16[22,128,128]{2,1,0:T(8,128)(2,1)S(1)} %get-tuple-element.56), channel_id=1, source_target_pairs={{0,32},{1,33},{2,34},{3,35},{4,36},{5,37},{6,38},{7,39},{8,40},{9,... | collective-permute-start | bytes 2162696 | tf_op jit(solution)/shard_map/ppermute | solution.py:42
  140.4 1.0 collective-permute-start.32
  141.4 2.5 %kept_adjoint.1 = (bf16[24,128,128]{2,1,0:T(8,128)(2,1)S(1)}, bf16[20,128,128]{2,1,0:T(8,128)(2,1)S(1)}, bf16[20,128,128]{2,1,0:T(8,128)(2,1)S(1)}) custom-call(s32[256]{0:T(256)S(1)} %select_reduce_fusion.list_ref, s32[10]{0:T(128)S(1)} %convert_reduce_fusion.2.bound_ref, bf16[256,128,128]{2,1,0:T(8,128)(2,1)S(1)} %get-tuple-element.41.tiles, ...), custom_call_target="tpu_custom_call" | custom-call | flops 134217728 | bytes 8388608 | tf_op jit(solution)/shard_map/kept_adjoint/pallas_call | solution.py:331
  143.9 5.6 %collective-permute-done.38 = bf16[20,128,128]{2,1,0:T(8,128)(2,1)S(1)} collective-permute-done((bf16[20,128,128]{2,1,0:T(8,128)(2,1)S(1)}, bf16[20,128,128]{2,1,0:T(8,128)(2,1)S(1)}, u32[]{:S(2)}, u32[]{:S(2)}) %collective-permute-start.38) | collective-permute-done | bytes 655392 | tf_op jit(solution)/shard_map/ppermute | solution.py:42
  149.6 3.6 %collective-permute-start.39 = (bf16[10,128,128]{2,1,0:T(8,128)(2,1)S(1)}, bf16[10,128,128]{2,1,0:T(8,128)(2,1)S(1)}, u32[]{:S(2)}, u32[]{:S(2)}) collective-permute-start(bf16[10,128,128]{2,1,0:T(8,128)(2,1)S(1)} %add_convert_fusion.2), channel_id=1, source_target_pairs={{0,32},{1,33},{2,34},{3,35},{4,36},{5,37},{6,38},{7,39},{8,40},{9,... | collective-permute-start | bytes 983048 | tf_op jit(solution)/shard_map/ppermute | solution.py:42
  153.2 4.0 %collective-permute-done.35 = bf16[22,128,128]{2,1,0:T(8,128)(2,1)S(1)} collective-permute-done((bf16[22,128,128]{2,1,0:T(8,128)(2,1)S(1)}, bf16[22,128,128]{2,1,0:T(8,128)(2,1)S(1)}, u32[]{:S(2)}, u32[]{:S(2)}) %collective-permute-start.35) | collective-permute-done | bytes 720928 | tf_op jit(solution)/shard_map/ppermute | solution.py:42
  157.3 1.1 collective-permute-start.36
  158.3 1.9 %collective-permute-done.32 = bf16[24,128,128]{2,1,0:T(8,128)(2,1)S(1)} collective-permute-done((bf16[24,128,128]{2,1,0:T(8,128)(2,1)S(1)}, bf16[24,128,128]{2,1,0:T(8,128)(2,1)S(1)}, u32[]{:S(2)}, u32[]{:S(2)}) %collective-permute-start.32) | collective-permute-done | bytes 786464 | tf_op jit(solution)/shard_map/ppermute | solution.py:42
  160.3 0.8 collective-permute-start.33
  161.2 1.2 collective-permute-start.40
  162.4 4.8 %collective-permute-done.36 = bf16[12,128,128]{2,1,0:T(8,128)(2,1)S(1)} collective-permute-done((bf16[12,128,128]{2,1,0:T(8,128)(2,1)S(1)}, bf16[12,128,128]{2,1,0:T(8,128)(2,1)S(1)}, u32[]{:S(2)}, u32[]{:S(2)}) %collective-permute-start.36) | collective-permute-done | bytes 393248 | tf_op jit(solution)/shard_map/ppermute | solution.py:42
  167.3 1.1 collective-permute-start.37
  168.4 0.6 collective-permute-done.40
  169.0 2.8 %collective-permute-done.33 = bf16[12,128,128]{2,1,0:T(8,128)(2,1)S(1)} collective-permute-done((bf16[12,128,128]{2,1,0:T(8,128)(2,1)S(1)}, bf16[12,128,128]{2,1,0:T(8,128)(2,1)S(1)}, u32[]{:S(2)}, u32[]{:S(2)}) %collective-permute-start.33) | collective-permute-done | bytes 393248 | tf_op jit(solution)/shard_map/ppermute | solution.py:42
  172.0 2.6 %collective-permute-done.37 = bf16[7,128,128]{2,1,0:T(8,128)(2,1)S(1)} collective-permute-done((bf16[7,128,128]{2,1,0:T(8,128)(2,1)S(1)}, bf16[7,128,128]{2,1,0:T(8,128)(2,1)S(1)}, u32[]{:S(2)}, u32[]{:S(2)}) %collective-permute-start.37) | collective-permute-done | bytes 229408 | tf_op jit(solution)/shard_map/ppermute | solution.py:42
  174.9 2.8 %collective-permute-done.34 = bf16[6,128,128]{2,1,0:T(8,128)(2,1)S(1)} collective-permute-done((bf16[6,128,128]{2,1,0:T(8,128)(2,1)S(1)}, bf16[6,128,128]{2,1,0:T(8,128)(2,1)S(1)}, u32[]{:S(2)}, u32[]{:S(2)}) %collective-permute-start.34) | collective-permute-done | bytes 196640 | tf_op jit(solution)/shard_map/ppermute | solution.py:42
  177.8 1.0 turn_back.1
  (109 shorter events, 7.6 us)
Async XLA Ops:
  0.6 23.5 %copy-start.1 = (bf16[1024,256]{1,0:T(8,128)(2,1)S(1)}, bf16[1024,256]{1,0:T(8,128)(2,1)}, u32[]{:S(2)}) copy-start(bf16[1024,256]{1,0:T(8,128)(2,1)} %own_cot.1) | copy-start | bytes 1572868
  0.6 2.2 %collective-permute-start = (bf16[1024,256]{1,0:T(8,128)(2,1)}, bf16[1024,256]{1,0:T(8,128)(2,1)S(1)}, u32[]{:S(2)}, u32[]{:S(2)}) collective-permute-start(bf16[1024,256]{1,0:T(8,128)(2,1)} %own_any.1), channel_id=1, source_target_pairs={{0,8},{1,9},{2,10},{3,11},{4,12},{5,13},{6,14},{7,15},{8,0},{9,1},... | collective-permute-start | bytes 1572872 | tf_op jit(solution)/shard_map/ppermute | solution.py:42
  2.8 1.0 copy-start.2
  3.9 20.3 %copy-start.4 = (s32[1,1,128]{2,1,0:T(1,128)S(1)}, s32[1,1,128]{2,1,0:T(1,128)}, u32[]{:S(2)}) copy-start(s32[1,1,128]{2,1,0:T(1,128)} %param.12) | copy-start | bytes 1540
  3.9 20.3 %copy-start.5 = (s32[1,1,128]{2,1,0:T(1,128)S(1)}, s32[1,1,128]{2,1,0:T(1,128)}, u32[]{:S(2)}) copy-start(s32[1,1,128]{2,1,0:T(1,128)} %param.11) | copy-start | bytes 1540
  4.1 26.2 %collective-permute-start.5 = (bf16[128,128,128]{2,1,0:T(8,128)(2,1)}, bf16[128,128,128]{2,1,0:T(8,128)(2,1)}, u32[]{:S(2)}, u32[]{:S(2)}) collective-permute-start(bf16[128,128,128]{2,1,0:T(8,128)(2,1)} %bitcast.22), channel_id=1, source_target_pairs={{0,8},{1,9},{2,10},{3,11},{4,12},{5,13},{6,14},{7,15},{8,0},{9,1},... | collective-permute-start | bytes 12582920 | tf_op jit(solution)/shard_map/ppermute | solution.py:42
  5.1 25.3 %copy-start = (bf16[1,1,128,128,128]{4,3,2,1,0:T(8,128)(2,1)S(1)}, bf16[1,1,128,128,128]{4,3,2,1,0:T(8,128)(2,1)}, u32[]{:S(2)}) copy-start(bf16[1,1,128,128,128]{4,3,2,1,0:T(8,128)(2,1)} %param.10) | copy-start | bytes 12582916
  5.1 6.6 %collective-permute-start.1 = (bf16[5,128,128]{2,1,0:T(8,128)(2,1)S(1)}, bf16[5,128,128]{2,1,0:T(8,128)(2,1)S(1)}, u32[]{:S(2)}, u32[]{:S(2)}) collective-permute-start(bf16[5,128,128]{2,1,0:T(8,128)(2,1)S(1)} %get-tuple-element.32), channel_id=1, source_target_pairs={{0,16},{1,17},{2,18},{3,19},{4,20},{5,21},{6,22},{7,23},{8,24},{9,... | collective-permute-start | bytes 491528 | tf_op jit(solution)/shard_map/ppermute | solution.py:42
  6.8 7.5 %collective-permute-start.8 = (bf16[5,128,128]{2,1,0:T(8,128)(2,1)S(1)}, bf16[5,128,128]{2,1,0:T(8,128)(2,1)S(1)}, u32[]{:S(2)}, u32[]{:S(2)}) collective-permute-start(bf16[5,128,128]{2,1,0:T(8,128)(2,1)S(1)} %get-tuple-element.40), channel_id=1, source_target_pairs={{0,96},{1,97},{2,98},{3,99},{4,100},{5,101},{6,102},{7,103},{8,104... | collective-permute-start | bytes 491528 | tf_op jit(solution)/shard_map/ppermute | solution.py:42
  9.9 7.9 %collective-permute-start.6 = (bf16[6,128,128]{2,1,0:T(8,128)(2,1)S(1)}, bf16[6,128,128]{2,1,0:T(8,128)(2,1)S(1)}, u32[]{:S(2)}, u32[]{:S(2)}) collective-permute-start(bf16[6,128,128]{2,1,0:T(8,128)(2,1)S(1)} %get-tuple-element.38), channel_id=1, source_target_pairs={{0,32},{1,33},{2,34},{3,35},{4,36},{5,37},{6,38},{7,39},{8,40},{9,... | collective-permute-start | bytes 589832 | tf_op jit(solution)/shard_map/ppermute | solution.py:42
  11.7 11.9 %collective-permute-start.2 = (bf16[10,128,128]{2,1,0:T(8,128)(2,1)S(1)}, bf16[10,128,128]{2,1,0:T(8,128)(2,1)S(1)}, u32[]{:S(2)}, u32[]{:S(2)}) collective-permute-start(bf16[10,128,128]{2,1,0:T(8,128)(2,1)S(1)} %pad_maximum_fusion.7), channel_id=1, source_target_pairs={{0,32},{1,33},{2,34},{3,35},{4,36},{5,37},{6,38},{7,39},{8,40},{9,... | collective-permute-start | bytes 983048 | tf_op jit(solution)/shard_map/ppermute | solution.py:42
  14.4 9.9 %collective-permute-start.9 = (bf16[10,128,128]{2,1,0:T(8,128)(2,1)S(1)}, bf16[10,128,128]{2,1,0:T(8,128)(2,1)S(1)}, u32[]{:S(2)}, u32[]{:S(2)}) collective-permute-start(bf16[10,128,128]{2,1,0:T(8,128)(2,1)S(1)} %pad_maximum_fusion.8), channel_id=1, source_target_pairs={{0,16},{1,17},{2,18},{3,19},{4,20},{5,21},{6,22},{7,23},{8,24},{9,... | collective-permute-start | bytes 983048 | tf_op jit(solution)/shard_map/ppermute | solution.py:42
  17.8 11.4 %collective-permute-start.7 = (bf16[12,128,128]{2,1,0:T(8,128)(2,1)S(1)}, bf16[12,128,128]{2,1,0:T(8,128)(2,1)S(1)}, u32[]{:S(2)}, u32[]{:S(2)}) collective-permute-start(bf16[12,128,128]{2,1,0:T(8,128)(2,1)S(1)} %pad_maximum_fusion.2), channel_id=1, source_target_pairs={{0,96},{1,97},{2,98},{3,99},{4,100},{5,101},{6,102},{7,103},{8,104... | collective-permute-start | bytes 1179656 | tf_op jit(solution)/shard_map/ppermute | solution.py:42
  23.6 19.2 %collective-permute-start.12 = (bf16[20,128,128]{2,1,0:T(8,128)(2,1)S(1)}, bf16[20,128,128]{2,1,0:T(8,128)(2,1)S(1)}, u32[]{:S(2)}, u32[]{:S(2)}) collective-permute-start(bf16[20,128,128]{2,1,0:T(8,128)(2,1)S(1)} %constant_dynamic-update-slice_fusion.rest_2_), channel_id=1, source_target_pairs={{0,96},{1,97},{2,98},{3,99},{4,100},{5,101},{6,102},{7,103},{8,104... | collective-permute-start | bytes 1966088 | tf_op jit(solution)/shard_map/ppermute | solution.py:42
  24.2 6.2 %collective-permute-start.3 = (bf16[1024,256]{1,0:T(8,128)(2,1)S(1)}, bf16[1024,256]{1,0:T(8,128)(2,1)S(1)}, u32[]{:S(2)}, u32[]{:S(2)}) collective-permute-start(bf16[1024,256]{1,0:T(8,128)(2,1)S(1)} %copy-done.1), channel_id=1, source_target_pairs={{0,8},{1,9},{2,10},{3,11},{4,12},{5,13},{6,14},{7,15},{8,0},{9,1},... | collective-permute-start | bytes 1572872 | tf_op jit(solution)/shard_map/ppermute | solution.py:42
  24.3 1.8 %collective-permute-start.4 = (s32[3,128]{1,0:T(4,128)S(1)}, s32[3,128]{1,0:T(4,128)S(1)}, u32[]{:S(2)}, u32[]{:S(2)}) collective-permute-start(s32[3,128]{1,0:T(4,128)S(1)} %get-tuple-element.81), channel_id=1, source_target_pairs={{0,8},{1,9},{2,10},{3,11},{4,12},{5,13},{6,14},{7,15},{8,0},{9,1},... | collective-permute-start | bytes 4616 | tf_op jit(solution)/shard_map/ppermute | solution.py:42
  26.1 16.8 %collective-permute-start.11 = (bf16[20,128,128]{2,1,0:T(8,128)(2,1)S(1)}, bf16[20,128,128]{2,1,0:T(8,128)(2,1)S(1)}, u32[]{:S(2)}, u32[]{:S(2)}) collective-permute-start(bf16[20,128,128]{2,1,0:T(8,128)(2,1)S(1)} %constant_dynamic-update-slice_fusion.6.rest_1_), channel_id=1, source_target_pairs={{0,32},{1,33},{2,34},{3,35},{4,36},{5,37},{6,38},{7,39},{8,40},{9,... | collective-permute-start | bytes 1966088 | tf_op jit(solution)/shard_map/ppermute | solution.py:42
  29.2 16.9 %collective-permute-start.10 = (bf16[24,128,128]{2,1,0:T(8,128)(2,1)S(1)}, bf16[24,128,128]{2,1,0:T(8,128)(2,1)S(1)}, u32[]{:S(2)}, u32[]{:S(2)}) collective-permute-start(bf16[24,128,128]{2,1,0:T(8,128)(2,1)S(1)} %constant_dynamic-update-slice_fusion.3.rest_0_), channel_id=1, source_target_pairs={{0,16},{1,17},{2,18},{3,19},{4,20},{5,21},{6,22},{7,23},{8,24},{9,... | collective-permute-start | bytes 2359304 | tf_op jit(solution)/shard_map/ppermute | solution.py:42
  48.2 15.8 %collective-permute-start.19 = (bf16[20,128,128]{2,1,0:T(8,128)(2,1)S(1)}, bf16[20,128,128]{2,1,0:T(8,128)(2,1)S(1)}, u32[]{:S(2)}, u32[]{:S(2)}) collective-permute-start(bf16[20,128,128]{2,1,0:T(8,128)(2,1)S(1)} %get-tuple-element.48), channel_id=1, source_target_pairs={{0,3},{1,2},{2,1},{3,0},{4,7},{5,6},{6,5},{7,4},{8,11},{9,10},{10,... | collective-permute-start | bytes 1966088 | tf_op jit(solution)/shard_map/ppermute | solution.py:42
  52.3 15.6 %collective-permute-start.16 = (bf16[20,128,128]{2,1,0:T(8,128)(2,1)S(1)}, bf16[20,128,128]{2,1,0:T(8,128)(2,1)S(1)}, u32[]{:S(2)}, u32[]{:S(2)}) collective-permute-start(bf16[20,128,128]{2,1,0:T(8,128)(2,1)S(1)} %get-tuple-element.46), channel_id=1, source_target_pairs={{0,1},{1,0},{2,3},{3,2},{4,5},{5,4},{6,7},{7,6},{8,9},{9,8},{10,11... | collective-permute-start | bytes 1966088 | tf_op jit(solution)/shard_map/ppermute | solution.py:42
  52.4 20.8 %collective-permute-start.13 = (bf16[24,128,128]{2,1,0:T(8,128)(2,1)S(1)}, bf16[24,128,128]{2,1,0:T(8,128)(2,1)S(1)}, u32[]{:S(2)}, u32[]{:S(2)}) collective-permute-start(bf16[24,128,128]{2,1,0:T(8,128)(2,1)S(1)} %get-tuple-element.44), channel_id=1, source_target_pairs={{0,4},{1,5},{2,6},{3,7},{4,0},{5,1},{6,2},{7,3},{8,12},{9,13},{10,... | collective-permute-start | bytes 2359304 | tf_op jit(solution)/shard_map/ppermute | solution.py:42
  64.1 27.0 %copy-start.3 = (bf16[256,256]{1,0:T(8,128)(2,1)S(1)}, bf16[256,256]{1,0:T(8,128)(2,1)}, u32[]{:S(2)}) copy-start(bf16[256,256]{1,0:T(8,128)(2,1)} %weight_ref.1) | copy-start | bytes 393220
  64.1 10.1 %collective-permute-start.20 = (bf16[10,128,128]{2,1,0:T(8,128)(2,1)S(1)}, bf16[10,128,128]{2,1,0:T(8,128)(2,1)S(1)}, u32[]{:S(2)}, u32[]{:S(2)}) collective-permute-start(bf16[10,128,128]{2,1,0:T(8,128)(2,1)S(1)} %add_convert_fusion.4), channel_id=1, source_target_pairs={{0,1},{1,0},{2,3},{3,2},{4,5},{5,4},{6,7},{7,6},{8,9},{9,8},{10,11... | collective-permute-start | bytes 983048 | tf_op jit(solution)/shard_map/ppermute | solution.py:42
  68.0 10.5 %collective-permute-start.17 = (bf16[10,128,128]{2,1,0:T(8,128)(2,1)S(1)}, bf16[10,128,128]{2,1,0:T(8,128)(2,1)S(1)}, u32[]{:S(2)}, u32[]{:S(2)}) collective-permute-start(bf16[10,128,128]{2,1,0:T(8,128)(2,1)S(1)} %add_convert_fusion.5), channel_id=1, source_target_pairs={{0,4},{1,5},{2,6},{3,7},{4,0},{5,1},{6,2},{7,3},{8,12},{9,13},{10,... | collective-permute-start | bytes 983048 | tf_op jit(solution)/shard_map/ppermute | solution.py:42
  73.4 9.5 %collective-permute-start.14 = (bf16[12,128,128]{2,1,0:T(8,128)(2,1)S(1)}, bf16[12,128,128]{2,1,0:T(8,128)(2,1)S(1)}, u32[]{:S(2)}, u32[]{:S(2)}) collective-permute-start(bf16[12,128,128]{2,1,0:T(8,128)(2,1)S(1)} %add_convert_fusion.1), channel_id=1, source_target_pairs={{0,3},{1,2},{2,1},{3,0},{4,7},{5,6},{6,5},{7,4},{8,11},{9,10},{10,... | collective-permute-start | bytes 1179656 | tf_op jit(solution)/shard_map/ppermute | solution.py:42
  74.2 6.9 %collective-permute-start.21 = (bf16[5,128,128]{2,1,0:T(8,128)(2,1)S(1)}, bf16[5,128,128]{2,1,0:T(8,128)(2,1)S(1)}, u32[]{:S(2)}, u32[]{:S(2)}) collective-permute-start(bf16[5,128,128]{2,1,0:T(8,128)(2,1)S(1)} %add_convert_fusion.15), channel_id=1, source_target_pairs={{0,4},{1,5},{2,6},{3,7},{4,0},{5,1},{6,2},{7,3},{8,12},{9,13},{10,... | collective-permute-start | bytes 491528 | tf_op jit(solution)/shard_map/ppermute | solution.py:42
  78.6 6.6 %collective-permute-start.18 = (bf16[5,128,128]{2,1,0:T(8,128)(2,1)S(1)}, bf16[5,128,128]{2,1,0:T(8,128)(2,1)S(1)}, u32[]{:S(2)}, u32[]{:S(2)}) collective-permute-start(bf16[5,128,128]{2,1,0:T(8,128)(2,1)S(1)} %add_convert_fusion.17), channel_id=1, source_target_pairs={{0,3},{1,2},{2,1},{3,0},{4,7},{5,6},{6,5},{7,4},{8,11},{9,10},{10,... | collective-permute-start | bytes 491528 | tf_op jit(solution)/shard_map/ppermute | solution.py:42
  82.9 5.8 %collective-permute-start.15 = (bf16[6,128,128]{2,1,0:T(8,128)(2,1)S(1)}, bf16[6,128,128]{2,1,0:T(8,128)(2,1)S(1)}, u32[]{:S(2)}, u32[]{:S(2)}) collective-permute-start(bf16[6,128,128]{2,1,0:T(8,128)(2,1)S(1)} %add_convert_fusion.9), channel_id=1, source_target_pairs={{0,1},{1,0},{2,3},{3,2},{4,5},{5,4},{6,7},{7,6},{8,9},{9,8},{10,11... | collective-permute-start | bytes 589832 | tf_op jit(solution)/shard_map/ppermute | solution.py:42
  88.9 2.2 %collective-permute-start.22 = (bf16[16,128,128]{2,1,0:T(8,128)(2,1)S(1)}, bf16[16,128,128]{2,1,0:T(8,128)(2,1)S(1)}, u32[]{:S(2)}, u32[]{:S(2)}) collective-permute-start(bf16[16,128,128]{2,1,0:T(8,128)(2,1)S(1)} %pad_maximum_fusion.1.own_sums), channel_id=1, source_target_pairs={{0,8},{1,9},{2,10},{3,11},{4,12},{5,13},{6,14},{7,15},{8,0},{9,1},... | collective-permute-start | bytes 1572872 | tf_op jit(solution)/shard_map/ppermute | solution.py:42
  93.3 10.2 %collective-permute-start.25 = (bf16[7,128,128]{2,1,0:T(8,128)(2,1)S(1)}, bf16[7,128,128]{2,1,0:T(8,128)(2,1)S(1)}, u32[]{:S(2)}, u32[]{:S(2)}) collective-permute-start(bf16[7,128,128]{2,1,0:T(8,128)(2,1)S(1)} %get-tuple-element.51), channel_id=1, source_target_pairs={{0,3},{1,2},{2,1},{3,0},{4,7},{5,6},{6,5},{7,4},{8,11},{9,10},{10,... | collective-permute-start | bytes 688136 | tf_op jit(solution)/shard_map/ppermute | solution.py:42
  94.9 6.7 %collective-permute-start.23 = (bf16[6,128,128]{2,1,0:T(8,128)(2,1)S(1)}, bf16[6,128,128]{2,1,0:T(8,128)(2,1)S(1)}, u32[]{:S(2)}, u32[]{:S(2)}) collective-permute-start(bf16[6,128,128]{2,1,0:T(8,128)(2,1)S(1)} %get-tuple-element.50), channel_id=1, source_target_pairs={{0,1},{1,0},{2,3},{3,2},{4,5},{5,4},{6,7},{7,6},{8,9},{9,8},{10,11... | collective-permute-start | bytes 589832 | tf_op jit(solution)/shard_map/ppermute | solution.py:42
  95.3 11.2 %collective-permute-start.27 = (bf16[5,128,128]{2,1,0:T(8,128)(2,1)S(1)}, bf16[5,128,128]{2,1,0:T(8,128)(2,1)S(1)}, u32[]{:S(2)}, u32[]{:S(2)}) collective-permute-start(bf16[5,128,128]{2,1,0:T(8,128)(2,1)S(1)} %get-tuple-element.52), channel_id=1, source_target_pairs={{0,4},{1,5},{2,6},{3,7},{4,0},{5,1},{6,2},{7,3},{8,12},{9,13},{10,... | collective-permute-start | bytes 491528 | tf_op jit(solution)/shard_map/ppermute | solution.py:42
  101.7 11.3 %collective-permute-start.24 = (bf16[12,128,128]{2,1,0:T(8,128)(2,1)S(1)}, bf16[12,128,128]{2,1,0:T(8,128)(2,1)S(1)}, u32[]{:S(2)}, u32[]{:S(2)}) collective-permute-start(bf16[12,128,128]{2,1,0:T(8,128)(2,1)S(1)} %pad_maximum_fusion.3), channel_id=1, source_target_pairs={{0,3},{1,2},{2,1},{3,0},{4,7},{5,6},{6,5},{7,4},{8,11},{9,10},{10,... | collective-permute-start | bytes 1179656 | tf_op jit(solution)/shard_map/ppermute | solution.py:42
  103.6 12.5 %collective-permute-start.26 = (bf16[12,128,128]{2,1,0:T(8,128)(2,1)S(1)}, bf16[12,128,128]{2,1,0:T(8,128)(2,1)S(1)}, u32[]{:S(2)}, u32[]{:S(2)}) collective-permute-start(bf16[12,128,128]{2,1,0:T(8,128)(2,1)S(1)} %pad_maximum_fusion.4), channel_id=1, source_target_pairs={{0,4},{1,5},{2,6},{3,7},{4,0},{5,1},{6,2},{7,3},{8,12},{9,13},{10,... | collective-permute-start | bytes 1179656 | tf_op jit(solution)/shard_map/ppermute | solution.py:42
  106.4 9.9 %collective-permute-start.28 = (bf16[10,128,128]{2,1,0:T(8,128)(2,1)S(1)}, bf16[10,128,128]{2,1,0:T(8,128)(2,1)S(1)}, u32[]{:S(2)}, u32[]{:S(2)}) collective-permute-start(bf16[10,128,128]{2,1,0:T(8,128)(2,1)S(1)} %pad_maximum_fusion.9), channel_id=1, source_target_pairs={{0,1},{1,0},{2,3},{3,2},{4,5},{5,4},{6,7},{7,6},{8,9},{9,8},{10,11... | collective-permute-start | bytes 983048 | tf_op jit(solution)/shard_map/ppermute | solution.py:42
  113.0 19.1 %collective-permute-start.29 = (bf16[24,128,128]{2,1,0:T(8,128)(2,1)S(1)}, bf16[24,128,128]{2,1,0:T(8,128)(2,1)S(1)}, u32[]{:S(2)}, u32[]{:S(2)}) collective-permute-start(bf16[24,128,128]{2,1,0:T(8,128)(2,1)S(1)} %constant_dynamic-update-slice_fusion.9.rest_0_), channel_id=1, source_target_pairs={{0,4},{1,5},{2,6},{3,7},{4,0},{5,1},{6,2},{7,3},{8,12},{9,13},{10,... | collective-permute-start | bytes 2359304 | tf_op jit(solution)/shard_map/ppermute | solution.py:42
  116.3 15.9 %collective-permute-start.30 = (bf16[22,128,128]{2,1,0:T(8,128)(2,1)S(1)}, bf16[22,128,128]{2,1,0:T(8,128)(2,1)S(1)}, u32[]{:S(2)}, u32[]{:S(2)}) collective-permute-start(bf16[22,128,128]{2,1,0:T(8,128)(2,1)S(1)} %pad_maximum_fusion.rest_1_.rest_3_), channel_id=1, source_target_pairs={{0,1},{1,0},{2,3},{3,2},{4,5},{5,4},{6,7},{7,6},{8,9},{9,8},{10,11... | collective-permute-start | bytes 2162696 | tf_op jit(solution)/shard_map/ppermute | solution.py:42
  116.4 15.7 %collective-permute-start.31 = (bf16[20,128,128]{2,1,0:T(8,128)(2,1)S(1)}, bf16[20,128,128]{2,1,0:T(8,128)(2,1)S(1)}, u32[]{:S(2)}, u32[]{:S(2)}) collective-permute-start(bf16[20,128,128]{2,1,0:T(8,128)(2,1)S(1)} %constant_dynamic-update-slice_fusion.12.rest_2_), channel_id=1, source_target_pairs={{0,3},{1,2},{2,1},{3,0},{4,7},{5,6},{6,5},{7,4},{8,11},{9,10},{10,... | collective-permute-start | bytes 1966088 | tf_op jit(solution)/shard_map/ppermute | solution.py:42
  134.0 15.5 %collective-permute-start.38 = (bf16[20,128,128]{2,1,0:T(8,128)(2,1)S(1)}, bf16[20,128,128]{2,1,0:T(8,128)(2,1)S(1)}, u32[]{:S(2)}, u32[]{:S(2)}) collective-permute-start(bf16[20,128,128]{2,1,0:T(8,128)(2,1)S(1)} %get-tuple-element.58), channel_id=1, source_target_pairs={{0,96},{1,97},{2,98},{3,99},{4,100},{5,101},{6,102},{7,103},{8,104... | collective-permute-start | bytes 1966088 | tf_op jit(solution)/shard_map/ppermute | solution.py:42
  137.5 19.7 %collective-permute-start.35 = (bf16[22,128,128]{2,1,0:T(8,128)(2,1)S(1)}, bf16[22,128,128]{2,1,0:T(8,128)(2,1)S(1)}, u32[]{:S(2)}, u32[]{:S(2)}) collective-permute-start(bf16[22,128,128]{2,1,0:T(8,128)(2,1)S(1)} %get-tuple-element.56), channel_id=1, source_target_pairs={{0,32},{1,33},{2,34},{3,35},{4,36},{5,37},{6,38},{7,39},{8,40},{9,... | collective-permute-start | bytes 2162696 | tf_op jit(solution)/shard_map/ppermute | solution.py:42
  140.4 19.8 %collective-permute-start.32 = (bf16[24,128,128]{2,1,0:T(8,128)(2,1)S(1)}, bf16[24,128,128]{2,1,0:T(8,128)(2,1)S(1)}, u32[]{:S(2)}, u32[]{:S(2)}) collective-permute-start(bf16[24,128,128]{2,1,0:T(8,128)(2,1)S(1)} %get-tuple-element.54), channel_id=1, source_target_pairs={{0,16},{1,17},{2,18},{3,19},{4,20},{5,21},{6,22},{7,23},{8,24},{9,... | collective-permute-start | bytes 2359304 | tf_op jit(solution)/shard_map/ppermute | solution.py:42
  149.6 11.5 %collective-permute-start.39 = (bf16[10,128,128]{2,1,0:T(8,128)(2,1)S(1)}, bf16[10,128,128]{2,1,0:T(8,128)(2,1)S(1)}, u32[]{:S(2)}, u32[]{:S(2)}) collective-permute-start(bf16[10,128,128]{2,1,0:T(8,128)(2,1)S(1)} %add_convert_fusion.2), channel_id=1, source_target_pairs={{0,32},{1,33},{2,34},{3,35},{4,36},{5,37},{6,38},{7,39},{8,40},{9,... | collective-permute-start | bytes 983048 | tf_op jit(solution)/shard_map/ppermute | solution.py:42
  157.3 9.9 %collective-permute-start.36 = (bf16[12,128,128]{2,1,0:T(8,128)(2,1)S(1)}, bf16[12,128,128]{2,1,0:T(8,128)(2,1)S(1)}, u32[]{:S(2)}, u32[]{:S(2)}) collective-permute-start(bf16[12,128,128]{2,1,0:T(8,128)(2,1)S(1)} %pad_maximum_fusion.5), channel_id=1, source_target_pairs={{0,16},{1,17},{2,18},{3,19},{4,20},{5,21},{6,22},{7,23},{8,24},{9,... | collective-permute-start | bytes 1179656 | tf_op jit(solution)/shard_map/ppermute | solution.py:42
  160.3 11.5 %collective-permute-start.33 = (bf16[12,128,128]{2,1,0:T(8,128)(2,1)S(1)}, bf16[12,128,128]{2,1,0:T(8,128)(2,1)S(1)}, u32[]{:S(2)}, u32[]{:S(2)}) collective-permute-start(bf16[12,128,128]{2,1,0:T(8,128)(2,1)S(1)} %add_convert_fusion), channel_id=1, source_target_pairs={{0,96},{1,97},{2,98},{3,99},{4,100},{5,101},{6,102},{7,103},{8,104... | collective-permute-start | bytes 1179656 | tf_op jit(solution)/shard_map/ppermute | solution.py:42
  161.2 7.7 %collective-permute-start.40 = (bf16[5,128,128]{2,1,0:T(8,128)(2,1)S(1)}, bf16[5,128,128]{2,1,0:T(8,128)(2,1)S(1)}, u32[]{:S(2)}, u32[]{:S(2)}) collective-permute-start(bf16[5,128,128]{2,1,0:T(8,128)(2,1)S(1)} %add_convert_fusion.11), channel_id=1, source_target_pairs={{0,16},{1,17},{2,18},{3,19},{4,20},{5,21},{6,22},{7,23},{8,24},{9,... | collective-permute-start | bytes 491528 | tf_op jit(solution)/shard_map/ppermute | solution.py:42
  167.3 7.3 %collective-permute-start.37 = (bf16[7,128,128]{2,1,0:T(8,128)(2,1)S(1)}, bf16[7,128,128]{2,1,0:T(8,128)(2,1)S(1)}, u32[]{:S(2)}, u32[]{:S(2)}) collective-permute-start(bf16[7,128,128]{2,1,0:T(8,128)(2,1)S(1)} %pad_maximum_fusion.11), channel_id=1, source_target_pairs={{0,96},{1,97},{2,98},{3,99},{4,100},{5,101},{6,102},{7,103},{8,104... | collective-permute-start | bytes 688136 | tf_op jit(solution)/shard_map/ppermute | solution.py:42
  171.9 5.7 %collective-permute-start.34 = (bf16[6,128,128]{2,1,0:T(8,128)(2,1)S(1)}, bf16[6,128,128]{2,1,0:T(8,128)(2,1)S(1)}, u32[]{:S(2)}, u32[]{:S(2)}) collective-permute-start(bf16[6,128,128]{2,1,0:T(8,128)(2,1)S(1)} %add_convert_fusion.7), channel_id=1, source_target_pairs={{0,32},{1,33},{2,34},{3,35},{4,36},{5,37},{6,38},{7,39},{8,40},{9,... | collective-permute-start | bytes 589832 | tf_op jit(solution)/shard_map/ppermute | solution.py:42
  174.8 3.0 %collective-permute-start.41 = (bf16[10,128,128]{2,1,0:T(8,128)(2,1)S(1)}, bf16[10,128,128]{2,1,0:T(8,128)(2,1)S(1)}, u32[]{:S(2)}, u32[]{:S(2)}) collective-permute-start(bf16[10,128,128]{2,1,0:T(8,128)(2,1)S(1)} %fusion), channel_id=1, source_target_pairs={{0,8},{1,9},{2,10},{3,11},{4,12},{5,13},{6,14},{7,15},{8,0},{9,1},... | collective-permute-start | bytes 983048 | tf_op jit(solution)/shard_map/ppermute | solution.py:42

commit v6 on v4

--- a/solution.py
+++ b/solution.py
@@ -44,7 +44,7 @@
 
 def link_orders(ring, pair):
     near, far, other = (1, 0), (3, 0), (0, 1)
-    orders = ((near, far, other), (far, other, near), (other, near, far))
+    orders = ((far, other, near), (other, near, far), (near, far, other))
     return [[({ring: r, pair: p}, r * 2 + p) for r, p in order] for order in orders]
 
 
@@ -165,7 +165,7 @@
     turn, other = mark // 2, mark % 2
     near = ((turn == 1) | (turn == 2)).astype(jnp.int32)
     far = (turn >= 2).astype(jnp.int32)
-    bits = ((near, far, other), (far, other, near), (other, near, far))
+    bits = ((far, other, near), (other, near, far), (near, far, other))
     array, row = jnp.zeros_like(ids), jnp.zeros_like(ids)
     for third, ((lo, hi), (a, b, c)) in enumerate(zip(CUTS, bits)):
         here = (tile >= lo) & (tile < hi)

time: 179 us -> 181 us (1.011)
  starting transfers between devices: 57.4 us -> 42.6 us
  waiting for transfers between devices: 96.9 us -> 111 us
  Pallas kernels: 18 us -> 21.1 us
    ppermute x42, starting transfers between devices: 57.4 us -> 42.6 us  [move(): return lax.ppermute(value, AXES, pairs)]
    ppermute x42, waiting for transfers between devices: 96.9 us -> 111 us  [move(): return lax.ppermute(value, AXES, pairs)]
  transfers between devices with their start and end apart: 42 -> 42, of which waited for: 30 -> 29; matrix products, arithmetic and copies ran while one was open for 2% -> 2% of each run, Pallas kernels for 6% -> 7%
where the time goes in v6:
time: 181 us
  waiting for transfers between devices  111 us (61%)
  starting transfers between devices  42.6 us (24%)
  Pallas kernels  21.1 us (12%)
  other arithmetic  3.51 us (2%)
  between operations  1.89 us (1%)
    ppermute x42, waiting for transfers between devices, move(): return lax.ppermute(value, AXES, pairs)  111 us
    ppermute x42, starting transfers between devices, move(): return lax.ppermute(value, AXES, pairs)  42.6 us
    pallas_call x4, Pallas kernels, late_pass(): pl.pallas_call(functools.partial(late_kernel, adjoint, kept), out_shape=t...  9.29 us
    pallas_call x1, Pallas kernels, early_pass(): pl.pallas_call(load_kernel, out_shape=[TOTAL, jax.ShapeDtypeStruct((2 * s...  5.16 us
  transfers between devices with their start and end apart: 42, of which 29 were waited for; matrix products, arithmetic and copies ran while one was open for 2% of the time, Pallas kernels for 7%

profile of v6, /device:TPU:0, one launch (start us, length us, event | category | flops | bytes accessed | tf_op | source)
XLA Modules:
  0.0 181.3 jit_solution(3110486873296126548)
XLA Ops:
  0.7 2.1 %collective-permute-done.sib_ref = bf16[1024,256]{1,0:T(8,128)(2,1)S(1)} collective-permute-done((bf16[1024,256]{1,0:T(8,128)(2,1)}, bf16[1024,256]{1,0:T(8,128)(2,1)S(1)}, u32[]{:S(2)}, u32[]{:S(2)}) %collective-permute-start) | collective-permute-done | bytes 524320 | tf_op jit(solution)/shard_map/ppermute | solution.py:42
  2.8 1.0 copy-done.2
  4.1 0.2 collective-permute-start.5
  5.0 1.8 collective-permute-start.1
  6.8 1.6 collective-permute-start.8
  8.4 2.3 %collective-permute-start.6 = (bf16[6,128,128]{2,1,0:T(8,128)(2,1)S(1)}, bf16[6,128,128]{2,1,0:T(8,128)(2,1)S(1)}, u32[]{:S(2)}, u32[]{:S(2)}) collective-permute-start(bf16[6,128,128]{2,1,0:T(8,128)(2,1)S(1)} %get-tuple-element.38), channel_id=1, source_target_pairs={{0,96},{1,97},{2,98},{3,99},{4,100},{5,101},{6,102},{7,103},{8,104... | collective-permute-start | bytes 589832 | tf_op jit(solution)/shard_map/ppermute | solution.py:42
  10.7 0.9 collective-permute-done.1
  11.6 3.2 %collective-permute-start.2 = (bf16[10,128,128]{2,1,0:T(8,128)(2,1)S(1)}, bf16[10,128,128]{2,1,0:T(8,128)(2,1)S(1)}, u32[]{:S(2)}, u32[]{:S(2)}) collective-permute-start(bf16[10,128,128]{2,1,0:T(8,128)(2,1)S(1)} %pad_maximum_fusion.7), channel_id=1, source_target_pairs={{0,96},{1,97},{2,98},{3,99},{4,100},{5,101},{6,102},{7,103},{8,104... | collective-permute-start | bytes 983048 | tf_op jit(solution)/shard_map/ppermute | solution.py:42
  14.8 0.2 collective-permute-start.9
  15.1 2.2 %collective-permute-done.6 = bf16[6,128,128]{2,1,0:T(8,128)(2,1)S(1)} collective-permute-done((bf16[6,128,128]{2,1,0:T(8,128)(2,1)S(1)}, bf16[6,128,128]{2,1,0:T(8,128)(2,1)S(1)}, u32[]{:S(2)}, u32[]{:S(2)}) %collective-permute-start.6) | collective-permute-done | bytes 196640 | tf_op jit(solution)/shard_map/ppermute | solution.py:42
  17.5 5.8 %collective-permute-done.2 = bf16[10,128,128]{2,1,0:T(8,128)(2,1)S(1)} collective-permute-done((bf16[10,128,128]{2,1,0:T(8,128)(2,1)S(1)}, bf16[10,128,128]{2,1,0:T(8,128)(2,1)S(1)}, u32[]{:S(2)}, u32[]{:S(2)}) %collective-permute-start.2) | collective-permute-done | bytes 327712 | tf_op jit(solution)/shard_map/ppermute | solution.py:42
  23.4 0.6 collective-permute-start.12
  24.1 0.5 collective-permute-start.4
  24.7 1.2 collective-permute-done.4
  25.9 2.8 %collective-permute-start.11 = (bf16[20,128,128]{2,1,0:T(8,128)(2,1)S(1)}, bf16[20,128,128]{2,1,0:T(8,128)(2,1)S(1)}, u32[]{:S(2)}, u32[]{:S(2)}) collective-permute-start(bf16[20,128,128]{2,1,0:T(8,128)(2,1)S(1)} %constant_dynamic-update-slice_fusion.6.rest_1_), channel_id=1, source_target_pairs={{0,96},{1,97},{2,98},{3,99},{4,100},{5,101},{6,102},{7,103},{8,104... | collective-permute-start | bytes 1966088 | tf_op jit(solution)/shard_map/ppermute | solution.py:42
  29.7 5.2 %early_pass.1 = (bf16[128,128,128]{2,1,0:T(8,128)(2,1)S(1)}, bf16[256,128,128]{2,1,0:T(8,128)(2,1)S(1)}) custom-call(s32[2]{0:T(128)S(1)} %add_reduce_fusion.live_ref, s32[256]{0:T(256)S(1)} %select_reduce_fusion.1.list_ref, s32[10]{0:T(128)S(1)} %convert_reduce_fusion.3.bound_ref, bf16[128,128,128]{2,1,0:T(8,128)(2,1)S(1)} %bitcast.23, ...), custom_call_target="tpu_custom_call" | custom-call | flops 268435456 | bytes 16777216 | tf_op jit(solution)/shard_map/early_pass/pallas_call | solution.py:312
  34.9 9.0 %collective-permute-done.11.rest_1_ = bf16[20,128,128]{2,1,0:T(8,128)(2,1)S(1)} collective-permute-done((bf16[20,128,128]{2,1,0:T(8,128)(2,1)S(1)}, bf16[20,128,128]{2,1,0:T(8,128)(2,1)S(1)}, u32[]{:S(2)}, u32[]{:S(2)}) %collective-permute-start.11) | collective-permute-done | bytes 655392 | tf_op jit(solution)/shard_map/ppermute | solution.py:42
  43.9 4.6 %collective-permute-done.10.rest_0_ = bf16[24,128,128]{2,1,0:T(8,128)(2,1)S(1)} collective-permute-done((bf16[24,128,128]{2,1,0:T(8,128)(2,1)S(1)}, bf16[24,128,128]{2,1,0:T(8,128)(2,1)S(1)}, u32[]{:S(2)}, u32[]{:S(2)}) %collective-permute-start.10) | collective-permute-done | bytes 786464 | tf_op jit(solution)/shard_map/ppermute | solution.py:42
  48.5 2.7 %sent_pass.1 = (bf16[24,128,128]{2,1,0:T(8,128)(2,1)S(1)}, bf16[20,128,128]{2,1,0:T(8,128)(2,1)S(1)}, bf16[20,128,128]{2,1,0:T(8,128)(2,1)S(1)}) custom-call(s32[256]{0:T(256)S(1)} %select_reduce_fusion.1.list_ref, s32[10]{0:T(128)S(1)} %convert_reduce_fusion.3.bound_ref, bf16[256,128,128]{2,1,0:T(8,128)(2,1)S(1)} %get-tuple-element.41.tiles, ...), custom_call_target="tpu_custom_call" | custom-call | flops 134217728 | bytes 8388608 | tf_op jit(solution)/shard_map/sent_pass/pallas_call | solution.py:326
  51.2 2.8 %collective-permute-start.19 = (bf16[20,128,128]{2,1,0:T(8,128)(2,1)S(1)}, bf16[20,128,128]{2,1,0:T(8,128)(2,1)S(1)}, u32[]{:S(2)}, u32[]{:S(2)}) collective-permute-start(bf16[20,128,128]{2,1,0:T(8,128)(2,1)S(1)} %get-tuple-element.48), channel_id=1, source_target_pairs={{0,4},{1,5},{2,6},{3,7},{4,0},{5,1},{6,2},{7,3},{8,12},{9,13},{10,... | collective-permute-start | bytes 1966088 | tf_op jit(solution)/shard_map/ppermute | solution.py:42
  54.0 3.7 %collective-permute-start.16 = (bf16[20,128,128]{2,1,0:T(8,128)(2,1)S(1)}, bf16[20,128,128]{2,1,0:T(8,128)(2,1)S(1)}, u32[]{:S(2)}, u32[]{:S(2)}) collective-permute-start(bf16[20,128,128]{2,1,0:T(8,128)(2,1)S(1)} %get-tuple-element.46), channel_id=1, source_target_pairs={{0,3},{1,2},{2,1},{3,0},{4,7},{5,6},{6,5},{7,4},{8,11},{9,10},{10,... | collective-permute-start | bytes 1966088 | tf_op jit(solution)/shard_map/ppermute | solution.py:42
  57.7 0.4 collective-permute-start.13
  58.1 2.0 %kept_pass.1 = (bf16[24,128,128]{2,1,0:T(8,128)(2,1)S(1)}, bf16[20,128,128]{2,1,0:T(8,128)(2,1)S(1)}, bf16[20,128,128]{2,1,0:T(8,128)(2,1)S(1)}) custom-call(s32[256]{0:T(256)S(1)} %select_reduce_fusion.1.list_ref, s32[10]{0:T(128)S(1)} %convert_reduce_fusion.3.bound_ref, bf16[256,128,128]{2,1,0:T(8,128)(2,1)S(1)} %get-tuple-element.41.tiles, ...), custom_call_target="tpu_custom_call" | custom-call | flops 134217728 | bytes 8388608 | tf_op jit(solution)/shard_map/kept_pass/pallas_call | solution.py:326
  60.2 7.9 %collective-permute-done.19 = bf16[20,128,128]{2,1,0:T(8,128)(2,1)S(1)} collective-permute-done((bf16[20,128,128]{2,1,0:T(8,128)(2,1)S(1)}, bf16[20,128,128]{2,1,0:T(8,128)(2,1)S(1)}, u32[]{:S(2)}, u32[]{:S(2)}) %collective-permute-start.19) | collective-permute-done | bytes 655392 | tf_op jit(solution)/shard_map/ppermute | solution.py:42
  68.2 4.4 %collective-permute-start.20 = (bf16[10,128,128]{2,1,0:T(8,128)(2,1)S(1)}, bf16[10,128,128]{2,1,0:T(8,128)(2,1)S(1)}, u32[]{:S(2)}, u32[]{:S(2)}) collective-permute-start(bf16[10,128,128]{2,1,0:T(8,128)(2,1)S(1)} %add_convert_fusion.4), channel_id=1, source_target_pairs={{0,3},{1,2},{2,1},{3,0},{4,7},{5,6},{6,5},{7,4},{8,11},{9,10},{10,... | collective-permute-start | bytes 983048 | tf_op jit(solution)/shard_map/ppermute | solution.py:42
  72.8 4.5 %collective-permute-done.13 = bf16[24,128,128]{2,1,0:T(8,128)(2,1)S(1)} collective-permute-done((bf16[24,128,128]{2,1,0:T(8,128)(2,1)S(1)}, bf16[24,128,128]{2,1,0:T(8,128)(2,1)S(1)}, u32[]{:S(2)}, u32[]{:S(2)}) %collective-permute-start.13) | collective-permute-done | bytes 786464 | tf_op jit(solution)/shard_map/ppermute | solution.py:42
  77.4 1.1 collective-permute-start.14
  78.6 0.2 collective-permute-start.21
  78.9 5.2 %collective-permute-done.17 = bf16[10,128,128]{2,1,0:T(8,128)(2,1)S(1)} collective-permute-done((bf16[10,128,128]{2,1,0:T(8,128)(2,1)S(1)}, bf16[10,128,128]{2,1,0:T(8,128)(2,1)S(1)}, u32[]{:S(2)}, u32[]{:S(2)}) %collective-permute-start.17) | collective-permute-done | bytes 327712 | tf_op jit(solution)/shard_map/ppermute | solution.py:42
  84.1 1.5 collective-permute-start.18
  85.9 2.6 %collective-permute-done.14 = bf16[12,128,128]{2,1,0:T(8,128)(2,1)S(1)} collective-permute-done((bf16[12,128,128]{2,1,0:T(8,128)(2,1)S(1)}, bf16[12,128,128]{2,1,0:T(8,128)(2,1)S(1)}, u32[]{:S(2)}, u32[]{:S(2)}) %collective-permute-start.14) | collective-permute-done | bytes 393248 | tf_op jit(solution)/shard_map/ppermute | solution.py:42
  88.7 2.3 %collective-permute-done.18 = bf16[5,128,128]{2,1,0:T(8,128)(2,1)S(1)} collective-permute-done((bf16[5,128,128]{2,1,0:T(8,128)(2,1)S(1)}, bf16[5,128,128]{2,1,0:T(8,128)(2,1)S(1)}, u32[]{:S(2)}, u32[]{:S(2)}) %collective-permute-start.18) | collective-permute-done | bytes 163872 | tf_op jit(solution)/shard_map/ppermute | solution.py:42
  91.1 4.5 %collective-permute-done.15 = bf16[6,128,128]{2,1,0:T(8,128)(2,1)S(1)} collective-permute-done((bf16[6,128,128]{2,1,0:T(8,128)(2,1)S(1)}, bf16[6,128,128]{2,1,0:T(8,128)(2,1)S(1)}, u32[]{:S(2)}, u32[]{:S(2)}) %collective-permute-start.15) | collective-permute-done | bytes 196640 | tf_op jit(solution)/shard_map/ppermute | solution.py:42
  95.8 0.3 collective-permute-start.22
  96.0 1.9 %collective-permute-done.22.sib_sums = bf16[16,128,128]{2,1,0:T(8,128)(2,1)S(1)} collective-permute-done((bf16[16,128,128]{2,1,0:T(8,128)(2,1)S(1)}, bf16[16,128,128]{2,1,0:T(8,128)(2,1)S(1)}, u32[]{:S(2)}, u32[]{:S(2)}) %collective-permute-start.22) | collective-permute-done | bytes 524320 | tf_op jit(solution)/shard_map/ppermute | solution.py:42
  97.9 2.2 %dense.1 = (bf16[1024,256]{1,0:T(8,128)(2,1)}, bf16[6,128,128]{2,1,0:T(8,128)(2,1)S(1)}, bf16[7,128,128]{2,1,0:T(8,128)(2,1)S(1)}, bf16[5,128,128]{2,1,0:T(8,128)(2,1)S(1)}) custom-call(s32[1]{0:T(128)} %bitcast.core_ref, bf16[256,256]{1,0:T(8,128)(2,1)S(1)} %copy-done.3, bf16[1024,256]{1,0:T(8,128)(2,1)S(1)} %copy-done.1, ...), custom_call_target="tpu_custom_call" | custom-call | flops 536870912 | bytes 4194304 | tf_op jit(solution)/shard_map/dense/pallas_call | solution.py:387
  100.2 0.9 collective-permute-start.25
  101.3 7.7 %collective-permute-done.23 = bf16[6,128,128]{2,1,0:T(8,128)(2,1)S(1)} collective-permute-done((bf16[6,128,128]{2,1,0:T(8,128)(2,1)S(1)}, bf16[6,128,128]{2,1,0:T(8,128)(2,1)S(1)}, u32[]{:S(2)}, u32[]{:S(2)}) %collective-permute-start.23) | collective-permute-done | bytes 196640 | tf_op jit(solution)/shard_map/ppermute | solution.py:42
  109.1 2.8 %collective-permute-start.24 = (bf16[12,128,128]{2,1,0:T(8,128)(2,1)S(1)}, bf16[12,128,128]{2,1,0:T(8,128)(2,1)S(1)}, u32[]{:S(2)}, u32[]{:S(2)}) collective-permute-start(bf16[12,128,128]{2,1,0:T(8,128)(2,1)S(1)} %pad_maximum_fusion.3), channel_id=1, source_target_pairs={{0,4},{1,5},{2,6},{3,7},{4,0},{5,1},{6,2},{7,3},{8,12},{9,13},{10,... | collective-permute-start | bytes 1179656 | tf_op jit(solution)/shard_map/ppermute | solution.py:42
  112.1 0.4 collective-permute-start.28
  112.6 8.1 %collective-permute-done.24 = bf16[12,128,128]{2,1,0:T(8,128)(2,1)S(1)} collective-permute-done((bf16[12,128,128]{2,1,0:T(8,128)(2,1)S(1)}, bf16[12,128,128]{2,1,0:T(8,128)(2,1)S(1)}, u32[]{:S(2)}, u32[]{:S(2)}) %collective-permute-start.24) | collective-permute-done | bytes 393248 | tf_op jit(solution)/shard_map/ppermute | solution.py:42
  120.8 1.2 collective-permute-done.26
  122.2 0.4 collective-permute-start.30
  122.7 1.8 %collective-permute-start.31 = (bf16[20,128,128]{2,1,0:T(8,128)(2,1)S(1)}, bf16[20,128,128]{2,1,0:T(8,128)(2,1)S(1)}, u32[]{:S(2)}, u32[]{:S(2)}) collective-permute-start(bf16[20,128,128]{2,1,0:T(8,128)(2,1)S(1)} %constant_dynamic-update-slice_fusion.12.rest_2_), channel_id=1, source_target_pairs={{0,4},{1,5},{2,6},{3,7},{4,0},{5,1},{6,2},{7,3},{8,12},{9,13},{10,... | collective-permute-start | bytes 1966088 | tf_op jit(solution)/shard_map/ppermute | solution.py:42
  125.0 3.1 %early_adjoint.1.before = bf16[128,128,128]{2,1,0:T(8,128)(2,1)S(1)} custom-call(s32[256]{0:T(256)S(1)} %select_reduce_fusion.list_ref, s32[10]{0:T(128)S(1)} %convert_reduce_fusion.2.bound_ref, bf16[256,128,128]{2,1,0:T(8,128)(2,1)S(1)} %get-tuple-element.41.tiles, bf16[24,128,128]{2,1,0:T(8,128)(2,1)S(1)} %constant_dynamic-update-slice_fusion.9.rest_0_, ...), custom_call_target="tpu_custom_call" | custom-call | flops 268435456 | bytes 16777216 | tf_op jit(solution)/shard_map/early_adjoint/pallas_call | solution.py:301
  128.1 10.6 %collective-permute-done.31.rest_2_ = bf16[20,128,128]{2,1,0:T(8,128)(2,1)S(1)} collective-permute-done((bf16[20,128,128]{2,1,0:T(8,128)(2,1)S(1)}, bf16[20,128,128]{2,1,0:T(8,128)(2,1)S(1)}, u32[]{:S(2)}, u32[]{:S(2)}) %collective-permute-start.31) | collective-permute-done | bytes 655392 | tf_op jit(solution)/shard_map/ppermute | solution.py:42
  138.7 0.3 collective-permute-done.30.rest_1_
  139.1 2.3 %sent_adjoint.1 = (bf16[24,128,128]{2,1,0:T(8,128)(2,1)S(1)}, bf16[22,128,128]{2,1,0:T(8,128)(2,1)S(1)}, bf16[20,128,128]{2,1,0:T(8,128)(2,1)S(1)}) custom-call(s32[256]{0:T(256)S(1)} %select_reduce_fusion.list_ref, s32[10]{0:T(128)S(1)} %convert_reduce_fusion.2.bound_ref, bf16[256,128,128]{2,1,0:T(8,128)(2,1)S(1)} %get-tuple-element.41.tiles, ...), custom_call_target="tpu_custom_call" | custom-call | flops 134217728 | bytes 8388608 | tf_op jit(solution)/shard_map/sent_adjoint/pallas_call | solution.py:326
  141.4 1.4 collective-permute-start.38
  142.7 0.8 collective-permute-start.35
  143.6 2.3 %kept_adjoint.1 = (bf16[24,128,128]{2,1,0:T(8,128)(2,1)S(1)}, bf16[20,128,128]{2,1,0:T(8,128)(2,1)S(1)}, bf16[20,128,128]{2,1,0:T(8,128)(2,1)S(1)}) custom-call(s32[256]{0:T(256)S(1)} %select_reduce_fusion.list_ref, s32[10]{0:T(128)S(1)} %convert_reduce_fusion.2.bound_ref, bf16[256,128,128]{2,1,0:T(8,128)(2,1)S(1)} %get-tuple-element.41.tiles, ...), custom_call_target="tpu_custom_call" | custom-call | flops 134217728 | bytes 8388608 | tf_op jit(solution)/shard_map/kept_adjoint/pallas_call | solution.py:326
  145.9 9.3 %collective-permute-done.38 = bf16[20,128,128]{2,1,0:T(8,128)(2,1)S(1)} collective-permute-done((bf16[20,128,128]{2,1,0:T(8,128)(2,1)S(1)}, bf16[20,128,128]{2,1,0:T(8,128)(2,1)S(1)}, u32[]{:S(2)}, u32[]{:S(2)}) %collective-permute-start.38) | collective-permute-done | bytes 655392 | tf_op jit(solution)/shard_map/ppermute | solution.py:42
  155.2 1.7 collective-permute-start.39
  157.0 4.4 %collective-permute-done.35 = bf16[22,128,128]{2,1,0:T(8,128)(2,1)S(1)} collective-permute-done((bf16[22,128,128]{2,1,0:T(8,128)(2,1)S(1)}, bf16[22,128,128]{2,1,0:T(8,128)(2,1)S(1)}, u32[]{:S(2)}, u32[]{:S(2)}) %collective-permute-start.35) | collective-permute-done | bytes 720928 | tf_op jit(solution)/shard_map/ppermute | solution.py:42
  161.7 1.0 collective-permute-done.32
  162.8 1.3 collective-permute-start.33
  164.1 1.3 collective-permute-done.39
  165.7 5.5 %collective-permute-done.36 = bf16[12,128,128]{2,1,0:T(8,128)(2,1)S(1)} collective-permute-done((bf16[12,128,128]{2,1,0:T(8,128)(2,1)S(1)}, bf16[12,128,128]{2,1,0:T(8,128)(2,1)S(1)}, u32[]{:S(2)}, u32[]{:S(2)}) %collective-permute-start.36) | collective-permute-done | bytes 393248 | tf_op jit(solution)/shard_map/ppermute | solution.py:42
  171.3 0.6 collective-permute-start.37
  171.9 1.1 collective-permute-done.40
  173.2 1.7 collective-permute-start.34
  174.9 2.5 %collective-permute-done.37 = bf16[7,128,128]{2,1,0:T(8,128)(2,1)S(1)} collective-permute-done((bf16[7,128,128]{2,1,0:T(8,128)(2,1)S(1)}, bf16[7,128,128]{2,1,0:T(8,128)(2,1)S(1)}, u32[]{:S(2)}, u32[]{:S(2)}) %collective-permute-start.37) | collective-permute-done | bytes 229408 | tf_op jit(solution)/shard_map/ppermute | solution.py:42
  177.7 2.5 %collective-permute-done.34 = bf16[6,128,128]{2,1,0:T(8,128)(2,1)S(1)} collective-permute-done((bf16[6,128,128]{2,1,0:T(8,128)(2,1)S(1)}, bf16[6,128,128]{2,1,0:T(8,128)(2,1)S(1)}, u32[]{:S(2)}, u32[]{:S(2)}) %collective-permute-start.34) | collective-permute-done | bytes 196640 | tf_op jit(solution)/shard_map/ppermute | solution.py:42
  180.3 1.0 turn_back.1
  (109 shorter events, 5.7 us)
Async XLA Ops:
  0.6 23.4 %copy-start.1 = (bf16[1024,256]{1,0:T(8,128)(2,1)S(1)}, bf16[1024,256]{1,0:T(8,128)(2,1)}, u32[]{:S(2)}) copy-start(bf16[1024,256]{1,0:T(8,128)(2,1)} %own_cot.1) | copy-start | bytes 1572868
  0.6 2.2 %collective-permute-start = (bf16[1024,256]{1,0:T(8,128)(2,1)}, bf16[1024,256]{1,0:T(8,128)(2,1)S(1)}, u32[]{:S(2)}, u32[]{:S(2)}) collective-permute-start(bf16[1024,256]{1,0:T(8,128)(2,1)} %own_ref.1), channel_id=1, source_target_pairs={{0,8},{1,9},{2,10},{3,11},{4,12},{5,13},{6,14},{7,15},{8,0},{9,1},... | collective-permute-start | bytes 1572872 | tf_op jit(solution)/shard_map/ppermute | solution.py:42
  2.8 1.0 copy-start.2
  3.9 20.1 %copy-start.4 = (s32[1,1,128]{2,1,0:T(1,128)S(1)}, s32[1,1,128]{2,1,0:T(1,128)}, u32[]{:S(2)}) copy-start(s32[1,1,128]{2,1,0:T(1,128)} %param.12) | copy-start | bytes 1540
  3.9 20.1 %copy-start.5 = (s32[1,1,128]{2,1,0:T(1,128)S(1)}, s32[1,1,128]{2,1,0:T(1,128)}, u32[]{:S(2)}) copy-start(s32[1,1,128]{2,1,0:T(1,128)} %param.11) | copy-start | bytes 1540
  4.1 25.6 %collective-permute-start.5 = (bf16[128,128,128]{2,1,0:T(8,128)(2,1)}, bf16[128,128,128]{2,1,0:T(8,128)(2,1)}, u32[]{:S(2)}, u32[]{:S(2)}) collective-permute-start(bf16[128,128,128]{2,1,0:T(8,128)(2,1)} %bitcast.22), channel_id=1, source_target_pairs={{0,8},{1,9},{2,10},{3,11},{4,12},{5,13},{6,14},{7,15},{8,0},{9,1},... | collective-permute-start | bytes 12582920 | tf_op jit(solution)/shard_map/ppermute | solution.py:42
  5.0 24.7 %copy-start = (bf16[1,1,128,128,128]{4,3,2,1,0:T(8,128)(2,1)S(1)}, bf16[1,1,128,128,128]{4,3,2,1,0:T(8,128)(2,1)}, u32[]{:S(2)}) copy-start(bf16[1,1,128,128,128]{4,3,2,1,0:T(8,128)(2,1)} %param.10) | copy-start | bytes 12582916
  5.0 6.6 %collective-permute-start.1 = (bf16[5,128,128]{2,1,0:T(8,128)(2,1)S(1)}, bf16[5,128,128]{2,1,0:T(8,128)(2,1)S(1)}, u32[]{:S(2)}, u32[]{:S(2)}) collective-permute-start(bf16[5,128,128]{2,1,0:T(8,128)(2,1)S(1)} %get-tuple-element.32), channel_id=1, source_target_pairs={{0,32},{1,33},{2,34},{3,35},{4,36},{5,37},{6,38},{7,39},{8,40},{9,... | collective-permute-start | bytes 491528 | tf_op jit(solution)/shard_map/ppermute | solution.py:42
  6.8 8.0 %collective-permute-start.8 = (bf16[5,128,128]{2,1,0:T(8,128)(2,1)S(1)}, bf16[5,128,128]{2,1,0:T(8,128)(2,1)S(1)}, u32[]{:S(2)}, u32[]{:S(2)}) collective-permute-start(bf16[5,128,128]{2,1,0:T(8,128)(2,1)S(1)} %get-tuple-element.40), channel_id=1, source_target_pairs={{0,16},{1,17},{2,18},{3,19},{4,20},{5,21},{6,22},{7,23},{8,24},{9,... | collective-permute-start | bytes 491528 | tf_op jit(solution)/shard_map/ppermute | solution.py:42
  8.4 8.9 %collective-permute-start.6 = (bf16[6,128,128]{2,1,0:T(8,128)(2,1)S(1)}, bf16[6,128,128]{2,1,0:T(8,128)(2,1)S(1)}, u32[]{:S(2)}, u32[]{:S(2)}) collective-permute-start(bf16[6,128,128]{2,1,0:T(8,128)(2,1)S(1)} %get-tuple-element.38), channel_id=1, source_target_pairs={{0,96},{1,97},{2,98},{3,99},{4,100},{5,101},{6,102},{7,103},{8,104... | collective-permute-start | bytes 589832 | tf_op jit(solution)/shard_map/ppermute | solution.py:42
  11.6 11.7 %collective-permute-start.2 = (bf16[10,128,128]{2,1,0:T(8,128)(2,1)S(1)}, bf16[10,128,128]{2,1,0:T(8,128)(2,1)S(1)}, u32[]{:S(2)}, u32[]{:S(2)}) collective-permute-start(bf16[10,128,128]{2,1,0:T(8,128)(2,1)S(1)} %pad_maximum_fusion.7), channel_id=1, source_target_pairs={{0,96},{1,97},{2,98},{3,99},{4,100},{5,101},{6,102},{7,103},{8,104... | collective-permute-start | bytes 983048 | tf_op jit(solution)/shard_map/ppermute | solution.py:42
  14.8 9.2 %collective-permute-start.9 = (bf16[10,128,128]{2,1,0:T(8,128)(2,1)S(1)}, bf16[10,128,128]{2,1,0:T(8,128)(2,1)S(1)}, u32[]{:S(2)}, u32[]{:S(2)}) collective-permute-start(bf16[10,128,128]{2,1,0:T(8,128)(2,1)S(1)} %pad_maximum_fusion.8), channel_id=1, source_target_pairs={{0,32},{1,33},{2,34},{3,35},{4,36},{5,37},{6,38},{7,39},{8,40},{9,... | collective-permute-start | bytes 983048 | tf_op jit(solution)/shard_map/ppermute | solution.py:42
  17.4 11.7 %collective-permute-start.7 = (bf16[12,128,128]{2,1,0:T(8,128)(2,1)S(1)}, bf16[12,128,128]{2,1,0:T(8,128)(2,1)S(1)}, u32[]{:S(2)}, u32[]{:S(2)}) collective-permute-start(bf16[12,128,128]{2,1,0:T(8,128)(2,1)S(1)} %pad_maximum_fusion.2), channel_id=1, source_target_pairs={{0,16},{1,17},{2,18},{3,19},{4,20},{5,21},{6,22},{7,23},{8,24},{9,... | collective-permute-start | bytes 1179656 | tf_op jit(solution)/shard_map/ppermute | solution.py:42
  23.4 20.5 %collective-permute-start.12 = (bf16[20,128,128]{2,1,0:T(8,128)(2,1)S(1)}, bf16[20,128,128]{2,1,0:T(8,128)(2,1)S(1)}, u32[]{:S(2)}, u32[]{:S(2)}) collective-permute-start(bf16[20,128,128]{2,1,0:T(8,128)(2,1)S(1)} %constant_dynamic-update-slice_fusion.rest_2_), channel_id=1, source_target_pairs={{0,16},{1,17},{2,18},{3,19},{4,20},{5,21},{6,22},{7,23},{8,24},{9,... | collective-permute-start | bytes 1966088 | tf_op jit(solution)/shard_map/ppermute | solution.py:42
  24.0 5.7 %collective-permute-start.3 = (bf16[1024,256]{1,0:T(8,128)(2,1)S(1)}, bf16[1024,256]{1,0:T(8,128)(2,1)S(1)}, u32[]{:S(2)}, u32[]{:S(2)}) collective-permute-start(bf16[1024,256]{1,0:T(8,128)(2,1)S(1)} %copy-done.1), channel_id=1, source_target_pairs={{0,8},{1,9},{2,10},{3,11},{4,12},{5,13},{6,14},{7,15},{8,0},{9,1},... | collective-permute-start | bytes 1572872 | tf_op jit(solution)/shard_map/ppermute | solution.py:42
  24.1 1.8 %collective-permute-start.4 = (s32[3,128]{1,0:T(4,128)S(1)}, s32[3,128]{1,0:T(4,128)S(1)}, u32[]{:S(2)}, u32[]{:S(2)}) collective-permute-start(s32[3,128]{1,0:T(4,128)S(1)} %get-tuple-element.81), channel_id=1, source_target_pairs={{0,8},{1,9},{2,10},{3,11},{4,12},{5,13},{6,14},{7,15},{8,0},{9,1},... | collective-permute-start | bytes 4616 | tf_op jit(solution)/shard_map/ppermute | solution.py:42
  25.9 18.0 %collective-permute-start.11 = (bf16[20,128,128]{2,1,0:T(8,128)(2,1)S(1)}, bf16[20,128,128]{2,1,0:T(8,128)(2,1)S(1)}, u32[]{:S(2)}, u32[]{:S(2)}) collective-permute-start(bf16[20,128,128]{2,1,0:T(8,128)(2,1)S(1)} %constant_dynamic-update-slice_fusion.6.rest_1_), channel_id=1, source_target_pairs={{0,96},{1,97},{2,98},{3,99},{4,100},{5,101},{6,102},{7,103},{8,104... | collective-permute-start | bytes 1966088 | tf_op jit(solution)/shard_map/ppermute | solution.py:42
  29.1 19.4 %collective-permute-start.10 = (bf16[24,128,128]{2,1,0:T(8,128)(2,1)S(1)}, bf16[24,128,128]{2,1,0:T(8,128)(2,1)S(1)}, u32[]{:S(2)}, u32[]{:S(2)}) collective-permute-start(bf16[24,128,128]{2,1,0:T(8,128)(2,1)S(1)} %constant_dynamic-update-slice_fusion.3.rest_0_), channel_id=1, source_target_pairs={{0,32},{1,33},{2,34},{3,35},{4,36},{5,37},{6,38},{7,39},{8,40},{9,... | collective-permute-start | bytes 2359304 | tf_op jit(solution)/shard_map/ppermute | solution.py:42
  51.2 16.9 %collective-permute-start.19 = (bf16[20,128,128]{2,1,0:T(8,128)(2,1)S(1)}, bf16[20,128,128]{2,1,0:T(8,128)(2,1)S(1)}, u32[]{:S(2)}, u32[]{:S(2)}) collective-permute-start(bf16[20,128,128]{2,1,0:T(8,128)(2,1)S(1)} %get-tuple-element.48), channel_id=1, source_target_pairs={{0,4},{1,5},{2,6},{3,7},{4,0},{5,1},{6,2},{7,3},{8,12},{9,13},{10,... | collective-permute-start | bytes 1966088 | tf_op jit(solution)/shard_map/ppermute | solution.py:42
  54.0 18.6 %collective-permute-start.16 = (bf16[20,128,128]{2,1,0:T(8,128)(2,1)S(1)}, bf16[20,128,128]{2,1,0:T(8,128)(2,1)S(1)}, u32[]{:S(2)}, u32[]{:S(2)}) collective-permute-start(bf16[20,128,128]{2,1,0:T(8,128)(2,1)S(1)} %get-tuple-element.46), channel_id=1, source_target_pairs={{0,3},{1,2},{2,1},{3,0},{4,7},{5,6},{6,5},{7,4},{8,11},{9,10},{10,... | collective-permute-start | bytes 1966088 | tf_op jit(solution)/shard_map/ppermute | solution.py:42
  57.7 19.6 %collective-permute-start.13 = (bf16[24,128,128]{2,1,0:T(8,128)(2,1)S(1)}, bf16[24,128,128]{2,1,0:T(8,128)(2,1)S(1)}, u32[]{:S(2)}, u32[]{:S(2)}) collective-permute-start(bf16[24,128,128]{2,1,0:T(8,128)(2,1)S(1)} %get-tuple-element.44), channel_id=1, source_target_pairs={{0,1},{1,0},{2,3},{3,2},{4,5},{5,4},{6,7},{7,6},{8,9},{9,8},{10,11... | collective-permute-start | bytes 2359304 | tf_op jit(solution)/shard_map/ppermute | solution.py:42
  68.2 29.8 %copy-start.3 = (bf16[256,256]{1,0:T(8,128)(2,1)S(1)}, bf16[256,256]{1,0:T(8,128)(2,1)}, u32[]{:S(2)}) copy-start(bf16[256,256]{1,0:T(8,128)(2,1)} %weight_ref.1) | copy-start | bytes 393220
  68.2 10.4 %collective-permute-start.20 = (bf16[10,128,128]{2,1,0:T(8,128)(2,1)S(1)}, bf16[10,128,128]{2,1,0:T(8,128)(2,1)S(1)}, u32[]{:S(2)}, u32[]{:S(2)}) collective-permute-start(bf16[10,128,128]{2,1,0:T(8,128)(2,1)S(1)} %add_convert_fusion.4), channel_id=1, source_target_pairs={{0,3},{1,2},{2,1},{3,0},{4,7},{5,6},{6,5},{7,4},{8,11},{9,10},{10,... | collective-permute-start | bytes 983048 | tf_op jit(solution)/shard_map/ppermute | solution.py:42
  72.7 11.3 %collective-permute-start.17 = (bf16[10,128,128]{2,1,0:T(8,128)(2,1)S(1)}, bf16[10,128,128]{2,1,0:T(8,128)(2,1)S(1)}, u32[]{:S(2)}, u32[]{:S(2)}) collective-permute-start(bf16[10,128,128]{2,1,0:T(8,128)(2,1)S(1)} %add_convert_fusion.5), channel_id=1, source_target_pairs={{0,1},{1,0},{2,3},{3,2},{4,5},{5,4},{6,7},{7,6},{8,9},{9,8},{10,11... | collective-permute-start | bytes 983048 | tf_op jit(solution)/shard_map/ppermute | solution.py:42
  77.4 11.1 %collective-permute-start.14 = (bf16[12,128,128]{2,1,0:T(8,128)(2,1)S(1)}, bf16[12,128,128]{2,1,0:T(8,128)(2,1)S(1)}, u32[]{:S(2)}, u32[]{:S(2)}) collective-permute-start(bf16[12,128,128]{2,1,0:T(8,128)(2,1)S(1)} %add_convert_fusion.1), channel_id=1, source_target_pairs={{0,4},{1,5},{2,6},{3,7},{4,0},{5,1},{6,2},{7,3},{8,12},{9,13},{10,... | collective-permute-start | bytes 1179656 | tf_op jit(solution)/shard_map/ppermute | solution.py:42
  78.6 7.2 %collective-permute-start.21 = (bf16[5,128,128]{2,1,0:T(8,128)(2,1)S(1)}, bf16[5,128,128]{2,1,0:T(8,128)(2,1)S(1)}, u32[]{:S(2)}, u32[]{:S(2)}) collective-permute-start(bf16[5,128,128]{2,1,0:T(8,128)(2,1)S(1)} %add_convert_fusion.15), channel_id=1, source_target_pairs={{0,1},{1,0},{2,3},{3,2},{4,5},{5,4},{6,7},{7,6},{8,9},{9,8},{10,11... | collective-permute-start | bytes 491528 | tf_op jit(solution)/shard_map/ppermute | solution.py:42
  84.1 6.9 %collective-permute-start.18 = (bf16[5,128,128]{2,1,0:T(8,128)(2,1)S(1)}, bf16[5,128,128]{2,1,0:T(8,128)(2,1)S(1)}, u32[]{:S(2)}, u32[]{:S(2)}) collective-permute-start(bf16[5,128,128]{2,1,0:T(8,128)(2,1)S(1)} %add_convert_fusion.17), channel_id=1, source_target_pairs={{0,4},{1,5},{2,6},{3,7},{4,0},{5,1},{6,2},{7,3},{8,12},{9,13},{10,... | collective-permute-start | bytes 491528 | tf_op jit(solution)/shard_map/ppermute | solution.py:42
  88.6 7.0 %collective-permute-start.15 = (bf16[6,128,128]{2,1,0:T(8,128)(2,1)S(1)}, bf16[6,128,128]{2,1,0:T(8,128)(2,1)S(1)}, u32[]{:S(2)}, u32[]{:S(2)}) collective-permute-start(bf16[6,128,128]{2,1,0:T(8,128)(2,1)S(1)} %add_convert_fusion.9), channel_id=1, source_target_pairs={{0,3},{1,2},{2,1},{3,0},{4,7},{5,6},{6,5},{7,4},{8,11},{9,10},{10,... | collective-permute-start | bytes 589832 | tf_op jit(solution)/shard_map/ppermute | solution.py:42
  95.8 2.2 %collective-permute-start.22 = (bf16[16,128,128]{2,1,0:T(8,128)(2,1)S(1)}, bf16[16,128,128]{2,1,0:T(8,128)(2,1)S(1)}, u32[]{:S(2)}, u32[]{:S(2)}) collective-permute-start(bf16[16,128,128]{2,1,0:T(8,128)(2,1)S(1)} %pad_maximum_fusion.1.own_sums), channel_id=1, source_target_pairs={{0,8},{1,9},{2,10},{3,11},{4,12},{5,13},{6,14},{7,15},{8,0},{9,1},... | collective-permute-start | bytes 1572872 | tf_op jit(solution)/shard_map/ppermute | solution.py:42
  100.2 11.7 %collective-permute-start.25 = (bf16[7,128,128]{2,1,0:T(8,128)(2,1)S(1)}, bf16[7,128,128]{2,1,0:T(8,128)(2,1)S(1)}, u32[]{:S(2)}, u32[]{:S(2)}) collective-permute-start(bf16[7,128,128]{2,1,0:T(8,128)(2,1)S(1)} %get-tuple-element.51), channel_id=1, source_target_pairs={{0,4},{1,5},{2,6},{3,7},{4,0},{5,1},{6,2},{7,3},{8,12},{9,13},{10,... | collective-permute-start | bytes 688136 | tf_op jit(solution)/shard_map/ppermute | solution.py:42
  101.1 7.9 %collective-permute-start.23 = (bf16[6,128,128]{2,1,0:T(8,128)(2,1)S(1)}, bf16[6,128,128]{2,1,0:T(8,128)(2,1)S(1)}, u32[]{:S(2)}, u32[]{:S(2)}) collective-permute-start(bf16[6,128,128]{2,1,0:T(8,128)(2,1)S(1)} %get-tuple-element.50), channel_id=1, source_target_pairs={{0,3},{1,2},{2,1},{3,0},{4,7},{5,6},{6,5},{7,4},{8,11},{9,10},{10,... | collective-permute-start | bytes 589832 | tf_op jit(solution)/shard_map/ppermute | solution.py:42
  101.2 10.9 %collective-permute-start.27 = (bf16[5,128,128]{2,1,0:T(8,128)(2,1)S(1)}, bf16[5,128,128]{2,1,0:T(8,128)(2,1)S(1)}, u32[]{:S(2)}, u32[]{:S(2)}) collective-permute-start(bf16[5,128,128]{2,1,0:T(8,128)(2,1)S(1)} %get-tuple-element.52), channel_id=1, source_target_pairs={{0,1},{1,0},{2,3},{3,2},{4,5},{5,4},{6,7},{7,6},{8,9},{9,8},{10,11... | collective-permute-start | bytes 491528 | tf_op jit(solution)/shard_map/ppermute | solution.py:42
  109.1 11.6 %collective-permute-start.24 = (bf16[12,128,128]{2,1,0:T(8,128)(2,1)S(1)}, bf16[12,128,128]{2,1,0:T(8,128)(2,1)S(1)}, u32[]{:S(2)}, u32[]{:S(2)}) collective-permute-start(bf16[12,128,128]{2,1,0:T(8,128)(2,1)S(1)} %pad_maximum_fusion.3), channel_id=1, source_target_pairs={{0,4},{1,5},{2,6},{3,7},{4,0},{5,1},{6,2},{7,3},{8,12},{9,13},{10,... | collective-permute-start | bytes 1179656 | tf_op jit(solution)/shard_map/ppermute | solution.py:42
  112.0 10.1 %collective-permute-start.26 = (bf16[12,128,128]{2,1,0:T(8,128)(2,1)S(1)}, bf16[12,128,128]{2,1,0:T(8,128)(2,1)S(1)}, u32[]{:S(2)}, u32[]{:S(2)}) collective-permute-start(bf16[12,128,128]{2,1,0:T(8,128)(2,1)S(1)} %pad_maximum_fusion.4), channel_id=1, source_target_pairs={{0,1},{1,0},{2,3},{3,2},{4,5},{5,4},{6,7},{7,6},{8,9},{9,8},{10,11... | collective-permute-start | bytes 1179656 | tf_op jit(solution)/shard_map/ppermute | solution.py:42
  112.1 10.5 %collective-permute-start.28 = (bf16[10,128,128]{2,1,0:T(8,128)(2,1)S(1)}, bf16[10,128,128]{2,1,0:T(8,128)(2,1)S(1)}, u32[]{:S(2)}, u32[]{:S(2)}) collective-permute-start(bf16[10,128,128]{2,1,0:T(8,128)(2,1)S(1)} %pad_maximum_fusion.9), channel_id=1, source_target_pairs={{0,3},{1,2},{2,1},{3,0},{4,7},{5,6},{6,5},{7,4},{8,11},{9,10},{10,... | collective-permute-start | bytes 983048 | tf_op jit(solution)/shard_map/ppermute | solution.py:42
  120.7 18.3 %collective-permute-start.29 = (bf16[24,128,128]{2,1,0:T(8,128)(2,1)S(1)}, bf16[24,128,128]{2,1,0:T(8,128)(2,1)S(1)}, u32[]{:S(2)}, u32[]{:S(2)}) collective-permute-start(bf16[24,128,128]{2,1,0:T(8,128)(2,1)S(1)} %constant_dynamic-update-slice_fusion.9.rest_0_), channel_id=1, source_target_pairs={{0,1},{1,0},{2,3},{3,2},{4,5},{5,4},{6,7},{7,6},{8,9},{9,8},{10,11... | collective-permute-start | bytes 2359304 | tf_op jit(solution)/shard_map/ppermute | solution.py:42
  122.2 16.8 %collective-permute-start.30 = (bf16[22,128,128]{2,1,0:T(8,128)(2,1)S(1)}, bf16[22,128,128]{2,1,0:T(8,128)(2,1)S(1)}, u32[]{:S(2)}, u32[]{:S(2)}) collective-permute-start(bf16[22,128,128]{2,1,0:T(8,128)(2,1)S(1)} %pad_maximum_fusion.rest_1_.rest_3_), channel_id=1, source_target_pairs={{0,3},{1,2},{2,1},{3,0},{4,7},{5,6},{6,5},{7,4},{8,11},{9,10},{10,... | collective-permute-start | bytes 2162696 | tf_op jit(solution)/shard_map/ppermute | solution.py:42
  122.7 16.0 %collective-permute-start.31 = (bf16[20,128,128]{2,1,0:T(8,128)(2,1)S(1)}, bf16[20,128,128]{2,1,0:T(8,128)(2,1)S(1)}, u32[]{:S(2)}, u32[]{:S(2)}) collective-permute-start(bf16[20,128,128]{2,1,0:T(8,128)(2,1)S(1)} %constant_dynamic-update-slice_fusion.12.rest_2_), channel_id=1, source_target_pairs={{0,4},{1,5},{2,6},{3,7},{4,0},{5,1},{6,2},{7,3},{8,12},{9,13},{10,... | collective-permute-start | bytes 1966088 | tf_op jit(solution)/shard_map/ppermute | solution.py:42
  141.4 13.8 %collective-permute-start.38 = (bf16[20,128,128]{2,1,0:T(8,128)(2,1)S(1)}, bf16[20,128,128]{2,1,0:T(8,128)(2,1)S(1)}, u32[]{:S(2)}, u32[]{:S(2)}) collective-permute-start(bf16[20,128,128]{2,1,0:T(8,128)(2,1)S(1)} %get-tuple-element.58), channel_id=1, source_target_pairs={{0,16},{1,17},{2,18},{3,19},{4,20},{5,21},{6,22},{7,23},{8,24},{9,... | collective-permute-start | bytes 1966088 | tf_op jit(solution)/shard_map/ppermute | solution.py:42
  142.7 18.7 %collective-permute-start.35 = (bf16[22,128,128]{2,1,0:T(8,128)(2,1)S(1)}, bf16[22,128,128]{2,1,0:T(8,128)(2,1)S(1)}, u32[]{:S(2)}, u32[]{:S(2)}) collective-permute-start(bf16[22,128,128]{2,1,0:T(8,128)(2,1)S(1)} %get-tuple-element.56), channel_id=1, source_target_pairs={{0,96},{1,97},{2,98},{3,99},{4,100},{5,101},{6,102},{7,103},{8,104... | collective-permute-start | bytes 2162696 | tf_op jit(solution)/shard_map/ppermute | solution.py:42
  143.6 19.1 %collective-permute-start.32 = (bf16[24,128,128]{2,1,0:T(8,128)(2,1)S(1)}, bf16[24,128,128]{2,1,0:T(8,128)(2,1)S(1)}, u32[]{:S(2)}, u32[]{:S(2)}) collective-permute-start(bf16[24,128,128]{2,1,0:T(8,128)(2,1)S(1)} %get-tuple-element.54), channel_id=1, source_target_pairs={{0,32},{1,33},{2,34},{3,35},{4,36},{5,37},{6,38},{7,39},{8,40},{9,... | collective-permute-start | bytes 2359304 | tf_op jit(solution)/shard_map/ppermute | solution.py:42
  155.2 10.1 %collective-permute-start.39 = (bf16[10,128,128]{2,1,0:T(8,128)(2,1)S(1)}, bf16[10,128,128]{2,1,0:T(8,128)(2,1)S(1)}, u32[]{:S(2)}, u32[]{:S(2)}) collective-permute-start(bf16[10,128,128]{2,1,0:T(8,128)(2,1)S(1)} %add_convert_fusion.2), channel_id=1, source_target_pairs={{0,96},{1,97},{2,98},{3,99},{4,100},{5,101},{6,102},{7,103},{8,104... | collective-permute-start | bytes 983048 | tf_op jit(solution)/shard_map/ppermute | solution.py:42
  161.6 9.6 %collective-permute-start.36 = (bf16[12,128,128]{2,1,0:T(8,128)(2,1)S(1)}, bf16[12,128,128]{2,1,0:T(8,128)(2,1)S(1)}, u32[]{:S(2)}, u32[]{:S(2)}) collective-permute-start(bf16[12,128,128]{2,1,0:T(8,128)(2,1)S(1)} %pad_maximum_fusion.5), channel_id=1, source_target_pairs={{0,32},{1,33},{2,34},{3,35},{4,36},{5,37},{6,38},{7,39},{8,40},{9,... | collective-permute-start | bytes 1179656 | tf_op jit(solution)/shard_map/ppermute | solution.py:42
  162.8 10.3 %collective-permute-start.33 = (bf16[12,128,128]{2,1,0:T(8,128)(2,1)S(1)}, bf16[12,128,128]{2,1,0:T(8,128)(2,1)S(1)}, u32[]{:S(2)}, u32[]{:S(2)}) collective-permute-start(bf16[12,128,128]{2,1,0:T(8,128)(2,1)S(1)} %add_convert_fusion), channel_id=1, source_target_pairs={{0,16},{1,17},{2,18},{3,19},{4,20},{5,21},{6,22},{7,23},{8,24},{9,... | collective-permute-start | bytes 1179656 | tf_op jit(solution)/shard_map/ppermute | solution.py:42
  165.5 7.5 %collective-permute-start.40 = (bf16[5,128,128]{2,1,0:T(8,128)(2,1)S(1)}, bf16[5,128,128]{2,1,0:T(8,128)(2,1)S(1)}, u32[]{:S(2)}, u32[]{:S(2)}) collective-permute-start(bf16[5,128,128]{2,1,0:T(8,128)(2,1)S(1)} %add_convert_fusion.11), channel_id=1, source_target_pairs={{0,32},{1,33},{2,34},{3,35},{4,36},{5,37},{6,38},{7,39},{8,40},{9,... | collective-permute-start | bytes 491528 | tf_op jit(solution)/shard_map/ppermute | solution.py:42
  171.3 6.1 %collective-permute-start.37 = (bf16[7,128,128]{2,1,0:T(8,128)(2,1)S(1)}, bf16[7,128,128]{2,1,0:T(8,128)(2,1)S(1)}, u32[]{:S(2)}, u32[]{:S(2)}) collective-permute-start(bf16[7,128,128]{2,1,0:T(8,128)(2,1)S(1)} %pad_maximum_fusion.11), channel_id=1, source_target_pairs={{0,16},{1,17},{2,18},{3,19},{4,20},{5,21},{6,22},{7,23},{8,24},{9,... | collective-permute-start | bytes 688136 | tf_op jit(solution)/shard_map/ppermute | solution.py:42
  173.2 7.0 %collective-permute-start.34 = (bf16[6,128,128]{2,1,0:T(8,128)(2,1)S(1)}, bf16[6,128,128]{2,1,0:T(8,128)(2,1)S(1)}, u32[]{:S(2)}, u32[]{:S(2)}) collective-permute-start(bf16[6,128,128]{2,1,0:T(8,128)(2,1)S(1)} %add_convert_fusion.7), channel_id=1, source_target_pairs={{0,96},{1,97},{2,98},{3,99},{4,100},{5,101},{6,102},{7,103},{8,104... | collective-permute-start | bytes 589832 | tf_op jit(solution)/shard_map/ppermute | solution.py:42
  177.6 2.7 %collective-permute-start.41 = (bf16[10,128,128]{2,1,0:T(8,128)(2,1)S(1)}, bf16[10,128,128]{2,1,0:T(8,128)(2,1)S(1)}, u32[]{:S(2)}, u32[]{:S(2)}) collective-permute-start(bf16[10,128,128]{2,1,0:T(8,128)(2,1)S(1)} %fusion), channel_id=1, source_target_pairs={{0,8},{1,9},{2,10},{3,11},{4,12},{5,13},{6,14},{7,15},{8,0},{9,1},... | collective-permute-start | bytes 983048 | tf_op jit(solution)/shard_map/ppermute | solution.py:42

commit v7 on v4

--- a/solution.py
+++ b/solution.py
@@ -10,8 +10,8 @@
 
 AXES = ("gr", "gc")
 TILE = 128
-CUTS = ((0, 6), (6, 11), (11, 16))
-SIDE = 1
+CUTS = ((0, 5), (5, 11), (11, 16))
+SIDE = 0
 EXTRA = 2
 NODES = 131072
 GROUP = 8

time: 179 us -> 186 us (1.039)
  waiting for transfers between devices: 96.9 us -> 119 us
  starting transfers between devices: 57.4 us -> 40.9 us
    ppermute x42, waiting for transfers between devices: 96.9 us -> 119 us  [move(): return lax.ppermute(value, AXES, pairs)]
    ppermute x42, starting transfers between devices: 57.4 us -> 40.9 us  [move(): return lax.ppermute(value, AXES, pairs)]
  transfers between devices with their start and end apart: 42 -> 42, of which waited for: 30 -> 24; matrix products, arithmetic and copies ran while one was open for 2% -> 2% of each run, Pallas kernels for 6% -> 6%
where the time goes in v7:
time: 186 us
  waiting for transfers between devices  119 us (64%)
  starting transfers between devices  40.9 us (22%)
  Pallas kernels  18.5 us (10%)
  other arithmetic  3.51 us (2%)
  between operations  1.86 us (1%)
    ppermute x42, waiting for transfers between devices, move(): return lax.ppermute(value, AXES, pairs)  119 us
    ppermute x42, starting transfers between devices, move(): return lax.ppermute(value, AXES, pairs)  40.9 us
    pallas_call x4, Pallas kernels, late_pass(): pl.pallas_call(functools.partial(late_kernel, adjoint, kept), out_shape=t...  7.74 us
    pallas_call x1, Pallas kernels, early_pass(): pl.pallas_call(load_kernel, out_shape=[TOTAL, jax.ShapeDtypeStruct((2 * s...  4.35 us
  transfers between devices with their start and end apart: 42, of which 24 were waited for; matrix products, arithmetic and copies ran while one was open for 2% of the time, Pallas kernels for 6%

profile of v7, /device:TPU:0, one launch (start us, length us, event | category | flops | bytes accessed | tf_op | source)
XLA Modules:
  0.0 185.7 jit_solution(17346617142953374777)
XLA Ops:
  0.7 2.1 %collective-permute-done.sib_ref = bf16[1024,256]{1,0:T(8,128)(2,1)S(1)} collective-permute-done((bf16[1024,256]{1,0:T(8,128)(2,1)}, bf16[1024,256]{1,0:T(8,128)(2,1)S(1)}, u32[]{:S(2)}, u32[]{:S(2)}) %collective-permute-start) | collective-permute-done | bytes 524320 | tf_op jit(solution)/shard_map/ppermute | solution.py:42
  2.8 1.0 copy-done.2
  4.1 0.2 collective-permute-start.5
  5.0 1.7 collective-permute-start.1
  6.7 1.7 collective-permute-start.6
  8.4 2.3 %collective-permute-start.8 = (bf16[6,128,128]{2,1,0:T(8,128)(2,1)S(1)}, bf16[6,128,128]{2,1,0:T(8,128)(2,1)S(1)}, u32[]{:S(2)}, u32[]{:S(2)}) collective-permute-start(bf16[6,128,128]{2,1,0:T(8,128)(2,1)S(1)} %get-tuple-element.40), channel_id=1, source_target_pairs={{0,96},{1,97},{2,98},{3,99},{4,100},{5,101},{6,102},{7,103},{8,104... | collective-permute-start | bytes 589832 | tf_op jit(solution)/shard_map/ppermute | solution.py:42
  10.7 0.9 collective-permute-done.1
  11.6 1.7 collective-permute-start.2
  13.4 2.7 %collective-permute-start.7 = (bf16[10,128,128]{2,1,0:T(8,128)(2,1)S(1)}, bf16[10,128,128]{2,1,0:T(8,128)(2,1)S(1)}, u32[]{:S(2)}, u32[]{:S(2)}) collective-permute-start(bf16[10,128,128]{2,1,0:T(8,128)(2,1)S(1)} %pad_maximum_fusion.8), channel_id=1, source_target_pairs={{0,96},{1,97},{2,98},{3,99},{4,100},{5,101},{6,102},{7,103},{8,104... | collective-permute-start | bytes 983048 | tf_op jit(solution)/shard_map/ppermute | solution.py:42
  16.3 1.0 collective-permute-start.9
  17.4 3.5 %collective-permute-done.2 = bf16[10,128,128]{2,1,0:T(8,128)(2,1)S(1)} collective-permute-done((bf16[10,128,128]{2,1,0:T(8,128)(2,1)S(1)}, bf16[10,128,128]{2,1,0:T(8,128)(2,1)S(1)}, u32[]{:S(2)}, u32[]{:S(2)}) %collective-permute-start.2) | collective-permute-done | bytes 327712 | tf_op jit(solution)/shard_map/ppermute | solution.py:42
  20.9 3.2 %collective-permute-start.12 = (bf16[20,128,128]{2,1,0:T(8,128)(2,1)S(1)}, bf16[20,128,128]{2,1,0:T(8,128)(2,1)S(1)}, u32[]{:S(2)}, u32[]{:S(2)}) collective-permute-start(bf16[20,128,128]{2,1,0:T(8,128)(2,1)S(1)} %constant_dynamic-update-slice_fusion.rest_2_), channel_id=1, source_target_pairs={{0,96},{1,97},{2,98},{3,99},{4,100},{5,101},{6,102},{7,103},{8,104... | collective-permute-start | bytes 1966088 | tf_op jit(solution)/shard_map/ppermute | solution.py:42
  24.2 0.5 collective-permute-start.4
  24.8 1.2 collective-permute-done.4
  26.0 1.5 collective-permute-start.10
  27.9 0.2 collective-permute-start.11
  28.3 0.2 convert_reduce_fusion.1
  28.7 4.3 %early_pass.1 = (bf16[128,128,128]{2,1,0:T(8,128)(2,1)S(1)}, bf16[256,128,128]{2,1,0:T(8,128)(2,1)S(1)}) custom-call(s32[2]{0:T(128)S(1)} %add_reduce_fusion.live_ref, s32[256]{0:T(256)S(1)} %select_reduce_fusion.1.list_ref, s32[10]{0:T(128)S(1)} %convert_reduce_fusion.3.bound_ref, bf16[128,128,128]{2,1,0:T(8,128)(2,1)S(1)} %bitcast.23, ...), custom_call_target="tpu_custom_call" | custom-call | flops 268435456 | bytes 16777216 | tf_op jit(solution)/shard_map/early_pass/pallas_call | solution.py:312
  33.0 9.8 %collective-permute-done.10.rest_0_ = bf16[20,128,128]{2,1,0:T(8,128)(2,1)S(1)} collective-permute-done((bf16[20,128,128]{2,1,0:T(8,128)(2,1)S(1)}, bf16[20,128,128]{2,1,0:T(8,128)(2,1)S(1)}, u32[]{:S(2)}, u32[]{:S(2)}) %collective-permute-start.10) | collective-permute-done | bytes 655392 | tf_op jit(solution)/shard_map/ppermute | solution.py:42
  42.8 4.5 %collective-permute-done.11.rest_1_ = bf16[24,128,128]{2,1,0:T(8,128)(2,1)S(1)} collective-permute-done((bf16[24,128,128]{2,1,0:T(8,128)(2,1)S(1)}, bf16[24,128,128]{2,1,0:T(8,128)(2,1)S(1)}, u32[]{:S(2)}, u32[]{:S(2)}) %collective-permute-start.11) | collective-permute-done | bytes 786464 | tf_op jit(solution)/shard_map/ppermute | solution.py:42
  47.3 2.0 %sent_pass.1 = (bf16[20,128,128]{2,1,0:T(8,128)(2,1)S(1)}, bf16[24,128,128]{2,1,0:T(8,128)(2,1)S(1)}, bf16[20,128,128]{2,1,0:T(8,128)(2,1)S(1)}) custom-call(s32[256]{0:T(256)S(1)} %select_reduce_fusion.1.list_ref, s32[10]{0:T(128)S(1)} %convert_reduce_fusion.3.bound_ref, bf16[256,128,128]{2,1,0:T(8,128)(2,1)S(1)} %get-tuple-element.41.tiles, ...), custom_call_target="tpu_custom_call" | custom-call | flops 134217728 | bytes 8388608 | tf_op jit(solution)/shard_map/sent_pass/pallas_call | solution.py:326
  49.3 4.1 %collective-permute-start.19 = (bf16[20,128,128]{2,1,0:T(8,128)(2,1)S(1)}, bf16[20,128,128]{2,1,0:T(8,128)(2,1)S(1)}, u32[]{:S(2)}, u32[]{:S(2)}) collective-permute-start(bf16[20,128,128]{2,1,0:T(8,128)(2,1)S(1)} %get-tuple-element.48), channel_id=1, source_target_pairs={{0,3},{1,2},{2,1},{3,0},{4,7},{5,6},{6,5},{7,4},{8,11},{9,10},{10,... | collective-permute-start | bytes 1966088 | tf_op jit(solution)/shard_map/ppermute | solution.py:42
  53.5 3.4 %collective-permute-start.13 = (bf16[20,128,128]{2,1,0:T(8,128)(2,1)S(1)}, bf16[20,128,128]{2,1,0:T(8,128)(2,1)S(1)}, u32[]{:S(2)}, u32[]{:S(2)}) collective-permute-start(bf16[20,128,128]{2,1,0:T(8,128)(2,1)S(1)} %get-tuple-element.44), channel_id=1, source_target_pairs={{0,4},{1,5},{2,6},{3,7},{4,0},{5,1},{6,2},{7,3},{8,12},{9,13},{10,... | collective-permute-start | bytes 1966088 | tf_op jit(solution)/shard_map/ppermute | solution.py:42
  56.8 2.0 %kept_pass.1 = (bf16[20,128,128]{2,1,0:T(8,128)(2,1)S(1)}, bf16[24,128,128]{2,1,0:T(8,128)(2,1)S(1)}, bf16[20,128,128]{2,1,0:T(8,128)(2,1)S(1)}) custom-call(s32[256]{0:T(256)S(1)} %select_reduce_fusion.1.list_ref, s32[10]{0:T(128)S(1)} %convert_reduce_fusion.3.bound_ref, bf16[256,128,128]{2,1,0:T(8,128)(2,1)S(1)} %get-tuple-element.41.tiles, ...), custom_call_target="tpu_custom_call" | custom-call | flops 134217728 | bytes 8388608 | tf_op jit(solution)/shard_map/kept_pass/pallas_call | solution.py:326
  58.9 8.5 %collective-permute-done.19 = bf16[20,128,128]{2,1,0:T(8,128)(2,1)S(1)} collective-permute-done((bf16[20,128,128]{2,1,0:T(8,128)(2,1)S(1)}, bf16[20,128,128]{2,1,0:T(8,128)(2,1)S(1)}, u32[]{:S(2)}, u32[]{:S(2)}) %collective-permute-start.19) | collective-permute-done | bytes 655392 | tf_op jit(solution)/shard_map/ppermute | solution.py:42
  67.5 2.9 %collective-permute-done.13 = bf16[20,128,128]{2,1,0:T(8,128)(2,1)S(1)} collective-permute-done((bf16[20,128,128]{2,1,0:T(8,128)(2,1)S(1)}, bf16[20,128,128]{2,1,0:T(8,128)(2,1)S(1)}, u32[]{:S(2)}, u32[]{:S(2)}) %collective-permute-start.13) | collective-permute-done | bytes 655392 | tf_op jit(solution)/shard_map/ppermute | solution.py:42
  70.5 0.5 collective-permute-start.14
  71.0 6.3 %collective-permute-done.16 = bf16[24,128,128]{2,1,0:T(8,128)(2,1)S(1)} collective-permute-done((bf16[24,128,128]{2,1,0:T(8,128)(2,1)S(1)}, bf16[24,128,128]{2,1,0:T(8,128)(2,1)S(1)}, u32[]{:S(2)}, u32[]{:S(2)}) %collective-permute-start.16) | collective-permute-done | bytes 786464 | tf_op jit(solution)/shard_map/ppermute | solution.py:42
  77.4 0.3 collective-permute-start.17
  77.7 4.0 %collective-permute-done.20 = bf16[10,128,128]{2,1,0:T(8,128)(2,1)S(1)} collective-permute-done((bf16[10,128,128]{2,1,0:T(8,128)(2,1)S(1)}, bf16[10,128,128]{2,1,0:T(8,128)(2,1)S(1)}, u32[]{:S(2)}, u32[]{:S(2)}) %collective-permute-start.20) | collective-permute-done | bytes 327712 | tf_op jit(solution)/shard_map/ppermute | solution.py:42
  81.8 0.4 collective-permute-start.21
  82.2 0.4 collective-permute-start.15
  82.6 7.7 %collective-permute-done.21 = bf16[5,128,128]{2,1,0:T(8,128)(2,1)S(1)} collective-permute-done((bf16[5,128,128]{2,1,0:T(8,128)(2,1)S(1)}, bf16[5,128,128]{2,1,0:T(8,128)(2,1)S(1)}, u32[]{:S(2)}, u32[]{:S(2)}) %collective-permute-start.21) | collective-permute-done | bytes 163872 | tf_op jit(solution)/shard_map/ppermute | solution.py:42
  90.7 6.7 %collective-permute-done.18 = bf16[6,128,128]{2,1,0:T(8,128)(2,1)S(1)} collective-permute-done((bf16[6,128,128]{2,1,0:T(8,128)(2,1)S(1)}, bf16[6,128,128]{2,1,0:T(8,128)(2,1)S(1)}, u32[]{:S(2)}, u32[]{:S(2)}) %collective-permute-start.18) | collective-permute-done | bytes 196640 | tf_op jit(solution)/shard_map/ppermute | solution.py:42
  97.6 0.3 collective-permute-start.22
  97.9 1.9 %collective-permute-done.22.sib_sums = bf16[16,128,128]{2,1,0:T(8,128)(2,1)S(1)} collective-permute-done((bf16[16,128,128]{2,1,0:T(8,128)(2,1)S(1)}, bf16[16,128,128]{2,1,0:T(8,128)(2,1)S(1)}, u32[]{:S(2)}, u32[]{:S(2)}) %collective-permute-start.22) | collective-permute-done | bytes 524320 | tf_op jit(solution)/shard_map/ppermute | solution.py:42
  99.8 2.2 %dense.1 = (bf16[1024,256]{1,0:T(8,128)(2,1)}, bf16[7,128,128]{2,1,0:T(8,128)(2,1)S(1)}, bf16[6,128,128]{2,1,0:T(8,128)(2,1)S(1)}, bf16[5,128,128]{2,1,0:T(8,128)(2,1)S(1)}) custom-call(s32[1]{0:T(128)} %bitcast.core_ref, bf16[256,256]{1,0:T(8,128)(2,1)S(1)} %copy-done.3, bf16[1024,256]{1,0:T(8,128)(2,1)S(1)} %copy-done.1, ...), custom_call_target="tpu_custom_call" | custom-call | flops 536870912 | bytes 4194304 | tf_op jit(solution)/shard_map/dense/pallas_call | solution.py:387
  102.3 0.5 collective-permute-start.27
  102.8 7.6 %collective-permute-done.25 = bf16[6,128,128]{2,1,0:T(8,128)(2,1)S(1)} collective-permute-done((bf16[6,128,128]{2,1,0:T(8,128)(2,1)S(1)}, bf16[6,128,128]{2,1,0:T(8,128)(2,1)S(1)}, u32[]{:S(2)}, u32[]{:S(2)}) %collective-permute-start.25) | collective-permute-done | bytes 196640 | tf_op jit(solution)/shard_map/ppermute | solution.py:42
  110.4 0.3 collective-permute-start.26
  110.8 0.4 collective-permute-start.24
  111.3 0.6 collective-permute-start.28
  112.0 10.4 %collective-permute-done.26 = bf16[12,128,128]{2,1,0:T(8,128)(2,1)S(1)} collective-permute-done((bf16[12,128,128]{2,1,0:T(8,128)(2,1)S(1)}, bf16[12,128,128]{2,1,0:T(8,128)(2,1)S(1)}, u32[]{:S(2)}, u32[]{:S(2)}) %collective-permute-start.26) | collective-permute-done | bytes 393248 | tf_op jit(solution)/shard_map/ppermute | solution.py:42
  122.4 0.3 collective-permute-start.30
  122.8 2.9 %collective-permute-start.29 = (bf16[22,128,128]{2,1,0:T(8,128)(2,1)S(1)}, bf16[22,128,128]{2,1,0:T(8,128)(2,1)S(1)}, u32[]{:S(2)}, u32[]{:S(2)}) collective-permute-start(bf16[22,128,128]{2,1,0:T(8,128)(2,1)S(1)} %pad_maximum_fusion.rest_0_.rest_3_), channel_id=1, source_target_pairs={{0,4},{1,5},{2,6},{3,7},{4,0},{5,1},{6,2},{7,3},{8,12},{9,13},{10,... | collective-permute-start | bytes 2162696 | tf_op jit(solution)/shard_map/ppermute | solution.py:42
  125.8 0.6 collective-permute-start.31
  126.5 0.2 convert_reduce_fusion
  126.8 2.9 %early_adjoint.1.before = bf16[128,128,128]{2,1,0:T(8,128)(2,1)S(1)} custom-call(s32[256]{0:T(256)S(1)} %select_reduce_fusion.list_ref, s32[10]{0:T(128)S(1)} %convert_reduce_fusion.2.bound_ref, bf16[256,128,128]{2,1,0:T(8,128)(2,1)S(1)} %get-tuple-element.41.tiles, bf16[22,128,128]{2,1,0:T(8,128)(2,1)S(1)} %pad_maximum_fusion.rest_0_.rest_3_, ...), custom_call_target="tpu_custom_call" | custom-call | flops 268435456 | bytes 16777216 | tf_op jit(solution)/shard_map/early_adjoint/pallas_call | solution.py:301
  129.7 11.8 %collective-permute-done.31.rest_2_ = bf16[20,128,128]{2,1,0:T(8,128)(2,1)S(1)} collective-permute-done((bf16[20,128,128]{2,1,0:T(8,128)(2,1)S(1)}, bf16[20,128,128]{2,1,0:T(8,128)(2,1)S(1)}, u32[]{:S(2)}, u32[]{:S(2)}) %collective-permute-start.31) | collective-permute-done | bytes 655392 | tf_op jit(solution)/shard_map/ppermute | solution.py:42
  141.5 1.8 sent_adjoint.1
  143.4 1.5 collective-permute-start.38
  144.9 1.8 kept_adjoint.1
  146.7 11.5 %collective-permute-done.38 = bf16[20,128,128]{2,1,0:T(8,128)(2,1)S(1)} collective-permute-done((bf16[20,128,128]{2,1,0:T(8,128)(2,1)S(1)}, bf16[20,128,128]{2,1,0:T(8,128)(2,1)S(1)}, u32[]{:S(2)}, u32[]{:S(2)}) %collective-permute-start.38) | collective-permute-done | bytes 655392 | tf_op jit(solution)/shard_map/ppermute | solution.py:42
  158.4 1.9 %collective-permute-done.32 = bf16[22,128,128]{2,1,0:T(8,128)(2,1)S(1)} collective-permute-done((bf16[22,128,128]{2,1,0:T(8,128)(2,1)S(1)}, bf16[22,128,128]{2,1,0:T(8,128)(2,1)S(1)}, u32[]{:S(2)}, u32[]{:S(2)}) %collective-permute-start.32) | collective-permute-done | bytes 720928 | tf_op jit(solution)/shard_map/ppermute | solution.py:42
  160.5 1.2 collective-permute-start.33
  161.6 3.6 %collective-permute-done.35 = bf16[24,128,128]{2,1,0:T(8,128)(2,1)S(1)} collective-permute-done((bf16[24,128,128]{2,1,0:T(8,128)(2,1)S(1)}, bf16[24,128,128]{2,1,0:T(8,128)(2,1)S(1)}, u32[]{:S(2)}, u32[]{:S(2)}) %collective-permute-start.35) | collective-permute-done | bytes 786464 | tf_op jit(solution)/shard_map/ppermute | solution.py:42
  165.3 1.8 collective-permute-start.36
  167.1 1.6 collective-permute-done.39
  168.8 2.3 %collective-permute-start.40 = (bf16[5,128,128]{2,1,0:T(8,128)(2,1)S(1)}, bf16[5,128,128]{2,1,0:T(8,128)(2,1)S(1)}, u32[]{:S(2)}, u32[]{:S(2)}) collective-permute-start(bf16[5,128,128]{2,1,0:T(8,128)(2,1)S(1)} %add_convert_fusion.11), channel_id=1, source_target_pairs={{0,16},{1,17},{2,18},{3,19},{4,20},{5,21},{6,22},{7,23},{8,24},{9,... | collective-permute-start | bytes 491528 | tf_op jit(solution)/shard_map/ppermute | solution.py:42
  171.3 4.3 %collective-permute-done.40 = bf16[5,128,128]{2,1,0:T(8,128)(2,1)S(1)} collective-permute-done((bf16[5,128,128]{2,1,0:T(8,128)(2,1)S(1)}, bf16[5,128,128]{2,1,0:T(8,128)(2,1)S(1)}, u32[]{:S(2)}, u32[]{:S(2)}) %collective-permute-start.40) | collective-permute-done | bytes 163872 | tf_op jit(solution)/shard_map/ppermute | solution.py:42
  175.9 1.9 %collective-permute-start.37 = (bf16[6,128,128]{2,1,0:T(8,128)(2,1)S(1)}, bf16[6,128,128]{2,1,0:T(8,128)(2,1)S(1)}, u32[]{:S(2)}, u32[]{:S(2)}) collective-permute-start(bf16[6,128,128]{2,1,0:T(8,128)(2,1)S(1)} %add_convert_fusion.7), channel_id=1, source_target_pairs={{0,96},{1,97},{2,98},{3,99},{4,100},{5,101},{6,102},{7,103},{8,104... | collective-permute-start | bytes 589832 | tf_op jit(solution)/shard_map/ppermute | solution.py:42
  177.8 5.0 %collective-permute-done.37 = bf16[6,128,128]{2,1,0:T(8,128)(2,1)S(1)} collective-permute-done((bf16[6,128,128]{2,1,0:T(8,128)(2,1)S(1)}, bf16[6,128,128]{2,1,0:T(8,128)(2,1)S(1)}, u32[]{:S(2)}, u32[]{:S(2)}) %collective-permute-start.37) | collective-permute-done | bytes 196640 | tf_op jit(solution)/shard_map/ppermute | solution.py:42
  183.2 1.5 collective-permute-done.41.sib_ref
  184.7 1.0 turn_back.1
  (109 shorter events, 4.9 us)
Async XLA Ops:
  0.6 23.5 %copy-start.1 = (bf16[1024,256]{1,0:T(8,128)(2,1)S(1)}, bf16[1024,256]{1,0:T(8,128)(2,1)}, u32[]{:S(2)}) copy-start(bf16[1024,256]{1,0:T(8,128)(2,1)} %own_cot.1) | copy-start | bytes 1572868
  0.6 2.2 %collective-permute-start = (bf16[1024,256]{1,0:T(8,128)(2,1)}, bf16[1024,256]{1,0:T(8,128)(2,1)S(1)}, u32[]{:S(2)}, u32[]{:S(2)}) collective-permute-start(bf16[1024,256]{1,0:T(8,128)(2,1)} %own_ref.1), channel_id=1, source_target_pairs={{0,8},{1,9},{2,10},{3,11},{4,12},{5,13},{6,14},{7,15},{8,0},{9,1},... | collective-permute-start | bytes 1572872 | tf_op jit(solution)/shard_map/ppermute | solution.py:42
  2.8 1.0 copy-start.2
  3.9 20.2 %copy-start.4 = (s32[1,1,128]{2,1,0:T(1,128)S(1)}, s32[1,1,128]{2,1,0:T(1,128)}, u32[]{:S(2)}) copy-start(s32[1,1,128]{2,1,0:T(1,128)} %param.12) | copy-start | bytes 1540
  3.9 20.2 %copy-start.5 = (s32[1,1,128]{2,1,0:T(1,128)S(1)}, s32[1,1,128]{2,1,0:T(1,128)}, u32[]{:S(2)}) copy-start(s32[1,1,128]{2,1,0:T(1,128)} %param.11) | copy-start | bytes 1540
  4.1 24.6 %collective-permute-start.5 = (bf16[128,128,128]{2,1,0:T(8,128)(2,1)}, bf16[128,128,128]{2,1,0:T(8,128)(2,1)}, u32[]{:S(2)}, u32[]{:S(2)}) collective-permute-start(bf16[128,128,128]{2,1,0:T(8,128)(2,1)} %bitcast.22), channel_id=1, source_target_pairs={{0,8},{1,9},{2,10},{3,11},{4,12},{5,13},{6,14},{7,15},{8,0},{9,1},... | collective-permute-start | bytes 12582920 | tf_op jit(solution)/shard_map/ppermute | solution.py:42
  5.0 23.6 %copy-start = (bf16[1,1,128,128,128]{4,3,2,1,0:T(8,128)(2,1)S(1)}, bf16[1,1,128,128,128]{4,3,2,1,0:T(8,128)(2,1)}, u32[]{:S(2)}) copy-start(bf16[1,1,128,128,128]{4,3,2,1,0:T(8,128)(2,1)} %param.10) | copy-start | bytes 12582916
  5.0 6.6 %collective-permute-start.1 = (bf16[5,128,128]{2,1,0:T(8,128)(2,1)S(1)}, bf16[5,128,128]{2,1,0:T(8,128)(2,1)S(1)}, u32[]{:S(2)}, u32[]{:S(2)}) collective-permute-start(bf16[5,128,128]{2,1,0:T(8,128)(2,1)S(1)} %get-tuple-element.32), channel_id=1, source_target_pairs={{0,16},{1,17},{2,18},{3,19},{4,20},{5,21},{6,22},{7,23},{8,24},{9,... | collective-permute-start | bytes 491528 | tf_op jit(solution)/shard_map/ppermute | solution.py:42
  6.7 6.6 %collective-permute-start.6 = (bf16[5,128,128]{2,1,0:T(8,128)(2,1)S(1)}, bf16[5,128,128]{2,1,0:T(8,128)(2,1)S(1)}, u32[]{:S(2)}, u32[]{:S(2)}) collective-permute-start(bf16[5,128,128]{2,1,0:T(8,128)(2,1)S(1)} %get-tuple-element.38), channel_id=1, source_target_pairs={{0,32},{1,33},{2,34},{3,35},{4,36},{5,37},{6,38},{7,39},{8,40},{9,... | collective-permute-start | bytes 491528 | tf_op jit(solution)/shard_map/ppermute | solution.py:42
  8.4 7.9 %collective-permute-start.8 = (bf16[6,128,128]{2,1,0:T(8,128)(2,1)S(1)}, bf16[6,128,128]{2,1,0:T(8,128)(2,1)S(1)}, u32[]{:S(2)}, u32[]{:S(2)}) collective-permute-start(bf16[6,128,128]{2,1,0:T(8,128)(2,1)S(1)} %get-tuple-element.40), channel_id=1, source_target_pairs={{0,96},{1,97},{2,98},{3,99},{4,100},{5,101},{6,102},{7,103},{8,104... | collective-permute-start | bytes 589832 | tf_op jit(solution)/shard_map/ppermute | solution.py:42
  11.6 9.3 %collective-permute-start.2 = (bf16[10,128,128]{2,1,0:T(8,128)(2,1)S(1)}, bf16[10,128,128]{2,1,0:T(8,128)(2,1)S(1)}, u32[]{:S(2)}, u32[]{:S(2)}) collective-permute-start(bf16[10,128,128]{2,1,0:T(8,128)(2,1)S(1)} %pad_maximum_fusion.7), channel_id=1, source_target_pairs={{0,32},{1,33},{2,34},{3,35},{4,36},{5,37},{6,38},{7,39},{8,40},{9,... | collective-permute-start | bytes 983048 | tf_op jit(solution)/shard_map/ppermute | solution.py:42
  13.4 10.8 %collective-permute-start.7 = (bf16[10,128,128]{2,1,0:T(8,128)(2,1)S(1)}, bf16[10,128,128]{2,1,0:T(8,128)(2,1)S(1)}, u32[]{:S(2)}, u32[]{:S(2)}) collective-permute-start(bf16[10,128,128]{2,1,0:T(8,128)(2,1)S(1)} %pad_maximum_fusion.8), channel_id=1, source_target_pairs={{0,96},{1,97},{2,98},{3,99},{4,100},{5,101},{6,102},{7,103},{8,104... | collective-permute-start | bytes 983048 | tf_op jit(solution)/shard_map/ppermute | solution.py:42
  16.3 11.5 %collective-permute-start.9 = (bf16[12,128,128]{2,1,0:T(8,128)(2,1)S(1)}, bf16[12,128,128]{2,1,0:T(8,128)(2,1)S(1)}, u32[]{:S(2)}, u32[]{:S(2)}) collective-permute-start(bf16[12,128,128]{2,1,0:T(8,128)(2,1)S(1)} %pad_maximum_fusion.2), channel_id=1, source_target_pairs={{0,16},{1,17},{2,18},{3,19},{4,20},{5,21},{6,22},{7,23},{8,24},{9,... | collective-permute-start | bytes 1179656 | tf_op jit(solution)/shard_map/ppermute | solution.py:42
  20.9 21.9 %collective-permute-start.12 = (bf16[20,128,128]{2,1,0:T(8,128)(2,1)S(1)}, bf16[20,128,128]{2,1,0:T(8,128)(2,1)S(1)}, u32[]{:S(2)}, u32[]{:S(2)}) collective-permute-start(bf16[20,128,128]{2,1,0:T(8,128)(2,1)S(1)} %constant_dynamic-update-slice_fusion.rest_2_), channel_id=1, source_target_pairs={{0,96},{1,97},{2,98},{3,99},{4,100},{5,101},{6,102},{7,103},{8,104... | collective-permute-start | bytes 1966088 | tf_op jit(solution)/shard_map/ppermute | solution.py:42
  24.1 4.5 %collective-permute-start.3 = (bf16[1024,256]{1,0:T(8,128)(2,1)S(1)}, bf16[1024,256]{1,0:T(8,128)(2,1)S(1)}, u32[]{:S(2)}, u32[]{:S(2)}) collective-permute-start(bf16[1024,256]{1,0:T(8,128)(2,1)S(1)} %copy-done.1), channel_id=1, source_target_pairs={{0,8},{1,9},{2,10},{3,11},{4,12},{5,13},{6,14},{7,15},{8,0},{9,1},... | collective-permute-start | bytes 1572872 | tf_op jit(solution)/shard_map/ppermute | solution.py:42
  24.2 1.8 collective-permute-start.4
  26.0 16.8 %collective-permute-start.10 = (bf16[20,128,128]{2,1,0:T(8,128)(2,1)S(1)}, bf16[20,128,128]{2,1,0:T(8,128)(2,1)S(1)}, u32[]{:S(2)}, u32[]{:S(2)}) collective-permute-start(bf16[20,128,128]{2,1,0:T(8,128)(2,1)S(1)} %constant_dynamic-update-slice_fusion.3.rest_0_), channel_id=1, source_target_pairs={{0,16},{1,17},{2,18},{3,19},{4,20},{5,21},{6,22},{7,23},{8,24},{9,... | collective-permute-start | bytes 1966088 | tf_op jit(solution)/shard_map/ppermute | solution.py:42
  27.9 19.4 %collective-permute-start.11 = (bf16[24,128,128]{2,1,0:T(8,128)(2,1)S(1)}, bf16[24,128,128]{2,1,0:T(8,128)(2,1)S(1)}, u32[]{:S(2)}, u32[]{:S(2)}) collective-permute-start(bf16[24,128,128]{2,1,0:T(8,128)(2,1)S(1)} %constant_dynamic-update-slice_fusion.6.rest_1_), channel_id=1, source_target_pairs={{0,32},{1,33},{2,34},{3,35},{4,36},{5,37},{6,38},{7,39},{8,40},{9,... | collective-permute-start | bytes 2359304 | tf_op jit(solution)/shard_map/ppermute | solution.py:42
  49.3 18.0 %collective-permute-start.19 = (bf16[20,128,128]{2,1,0:T(8,128)(2,1)S(1)}, bf16[20,128,128]{2,1,0:T(8,128)(2,1)S(1)}, u32[]{:S(2)}, u32[]{:S(2)}) collective-permute-start(bf16[20,128,128]{2,1,0:T(8,128)(2,1)S(1)} %get-tuple-element.48), channel_id=1, source_target_pairs={{0,3},{1,2},{2,1},{3,0},{4,7},{5,6},{6,5},{7,4},{8,11},{9,10},{10,... | collective-permute-start | bytes 1966088 | tf_op jit(solution)/shard_map/ppermute | solution.py:42
  53.5 17.0 %collective-permute-start.13 = (bf16[20,128,128]{2,1,0:T(8,128)(2,1)S(1)}, bf16[20,128,128]{2,1,0:T(8,128)(2,1)S(1)}, u32[]{:S(2)}, u32[]{:S(2)}) collective-permute-start(bf16[20,128,128]{2,1,0:T(8,128)(2,1)S(1)} %get-tuple-element.44), channel_id=1, source_target_pairs={{0,4},{1,5},{2,6},{3,7},{4,0},{5,1},{6,2},{7,3},{8,12},{9,13},{10,... | collective-permute-start | bytes 1966088 | tf_op jit(solution)/shard_map/ppermute | solution.py:42
  56.8 20.5 %collective-permute-start.16 = (bf16[24,128,128]{2,1,0:T(8,128)(2,1)S(1)}, bf16[24,128,128]{2,1,0:T(8,128)(2,1)S(1)}, u32[]{:S(2)}, u32[]{:S(2)}) collective-permute-start(bf16[24,128,128]{2,1,0:T(8,128)(2,1)S(1)} %get-tuple-element.46), channel_id=1, source_target_pairs={{0,1},{1,0},{2,3},{3,2},{4,5},{5,4},{6,7},{7,6},{8,9},{9,8},{10,11... | collective-permute-start | bytes 2359304 | tf_op jit(solution)/shard_map/ppermute | solution.py:42
  67.4 32.3 %copy-start.3 = (bf16[256,256]{1,0:T(8,128)(2,1)S(1)}, bf16[256,256]{1,0:T(8,128)(2,1)}, u32[]{:S(2)}) copy-start(bf16[256,256]{1,0:T(8,128)(2,1)} %weight_ref.1) | copy-start | bytes 393220
  67.5 14.3 %collective-permute-start.20 = (bf16[10,128,128]{2,1,0:T(8,128)(2,1)S(1)}, bf16[10,128,128]{2,1,0:T(8,128)(2,1)S(1)}, u32[]{:S(2)}, u32[]{:S(2)}) collective-permute-start(bf16[10,128,128]{2,1,0:T(8,128)(2,1)S(1)} %add_convert_fusion.4), channel_id=1, source_target_pairs={{0,1},{1,0},{2,3},{3,2},{4,5},{5,4},{6,7},{7,6},{8,9},{9,8},{10,11... | collective-permute-start | bytes 983048 | tf_op jit(solution)/shard_map/ppermute | solution.py:42
  70.5 11.6 %collective-permute-start.14 = (bf16[10,128,128]{2,1,0:T(8,128)(2,1)S(1)}, bf16[10,128,128]{2,1,0:T(8,128)(2,1)S(1)}, u32[]{:S(2)}, u32[]{:S(2)}) collective-permute-start(bf16[10,128,128]{2,1,0:T(8,128)(2,1)S(1)} %add_convert_fusion.5), channel_id=1, source_target_pairs={{0,3},{1,2},{2,1},{3,0},{4,7},{5,6},{6,5},{7,4},{8,11},{9,10},{10,... | collective-permute-start | bytes 983048 | tf_op jit(solution)/shard_map/ppermute | solution.py:42
  77.4 13.0 %collective-permute-start.17 = (bf16[12,128,128]{2,1,0:T(8,128)(2,1)S(1)}, bf16[12,128,128]{2,1,0:T(8,128)(2,1)S(1)}, u32[]{:S(2)}, u32[]{:S(2)}) collective-permute-start(bf16[12,128,128]{2,1,0:T(8,128)(2,1)S(1)} %add_convert_fusion.1), channel_id=1, source_target_pairs={{0,4},{1,5},{2,6},{3,7},{4,0},{5,1},{6,2},{7,3},{8,12},{9,13},{10,... | collective-permute-start | bytes 1179656 | tf_op jit(solution)/shard_map/ppermute | solution.py:42
  81.8 8.5 %collective-permute-start.21 = (bf16[5,128,128]{2,1,0:T(8,128)(2,1)S(1)}, bf16[5,128,128]{2,1,0:T(8,128)(2,1)S(1)}, u32[]{:S(2)}, u32[]{:S(2)}) collective-permute-start(bf16[5,128,128]{2,1,0:T(8,128)(2,1)S(1)} %add_convert_fusion.15), channel_id=1, source_target_pairs={{0,4},{1,5},{2,6},{3,7},{4,0},{5,1},{6,2},{7,3},{8,12},{9,13},{10,... | collective-permute-start | bytes 491528 | tf_op jit(solution)/shard_map/ppermute | solution.py:42
  82.2 8.4 %collective-permute-start.15 = (bf16[5,128,128]{2,1,0:T(8,128)(2,1)S(1)}, bf16[5,128,128]{2,1,0:T(8,128)(2,1)S(1)}, u32[]{:S(2)}, u32[]{:S(2)}) collective-permute-start(bf16[5,128,128]{2,1,0:T(8,128)(2,1)S(1)} %add_convert_fusion.17), channel_id=1, source_target_pairs={{0,1},{1,0},{2,3},{3,2},{4,5},{5,4},{6,7},{7,6},{8,9},{9,8},{10,11... | collective-permute-start | bytes 491528 | tf_op jit(solution)/shard_map/ppermute | solution.py:42
  90.5 7.0 %collective-permute-start.18 = (bf16[6,128,128]{2,1,0:T(8,128)(2,1)S(1)}, bf16[6,128,128]{2,1,0:T(8,128)(2,1)S(1)}, u32[]{:S(2)}, u32[]{:S(2)}) collective-permute-start(bf16[6,128,128]{2,1,0:T(8,128)(2,1)S(1)} %add_convert_fusion.9), channel_id=1, source_target_pairs={{0,3},{1,2},{2,1},{3,0},{4,7},{5,6},{6,5},{7,4},{8,11},{9,10},{10,... | collective-permute-start | bytes 589832 | tf_op jit(solution)/shard_map/ppermute | solution.py:42
  97.6 2.2 %collective-permute-start.22 = (bf16[16,128,128]{2,1,0:T(8,128)(2,1)S(1)}, bf16[16,128,128]{2,1,0:T(8,128)(2,1)S(1)}, u32[]{:S(2)}, u32[]{:S(2)}) collective-permute-start(bf16[16,128,128]{2,1,0:T(8,128)(2,1)S(1)} %pad_maximum_fusion.1.own_sums), channel_id=1, source_target_pairs={{0,8},{1,9},{2,10},{3,11},{4,12},{5,13},{6,14},{7,15},{8,0},{9,1},... | collective-permute-start | bytes 1572872 | tf_op jit(solution)/shard_map/ppermute | solution.py:42
  102.0 8.6 %collective-permute-start.23 = (bf16[7,128,128]{2,1,0:T(8,128)(2,1)S(1)}, bf16[7,128,128]{2,1,0:T(8,128)(2,1)S(1)}, u32[]{:S(2)}, u32[]{:S(2)}) collective-permute-start(bf16[7,128,128]{2,1,0:T(8,128)(2,1)S(1)} %get-tuple-element.50), channel_id=1, source_target_pairs={{0,1},{1,0},{2,3},{3,2},{4,5},{5,4},{6,7},{7,6},{8,9},{9,8},{10,11... | collective-permute-start | bytes 688136 | tf_op jit(solution)/shard_map/ppermute | solution.py:42
  102.2 8.2 %collective-permute-start.25 = (bf16[6,128,128]{2,1,0:T(8,128)(2,1)S(1)}, bf16[6,128,128]{2,1,0:T(8,128)(2,1)S(1)}, u32[]{:S(2)}, u32[]{:S(2)}) collective-permute-start(bf16[6,128,128]{2,1,0:T(8,128)(2,1)S(1)} %get-tuple-element.51), channel_id=1, source_target_pairs={{0,3},{1,2},{2,1},{3,0},{4,7},{5,6},{6,5},{7,4},{8,11},{9,10},{10,... | collective-permute-start | bytes 589832 | tf_op jit(solution)/shard_map/ppermute | solution.py:42
  102.3 8.9 %collective-permute-start.27 = (bf16[5,128,128]{2,1,0:T(8,128)(2,1)S(1)}, bf16[5,128,128]{2,1,0:T(8,128)(2,1)S(1)}, u32[]{:S(2)}, u32[]{:S(2)}) collective-permute-start(bf16[5,128,128]{2,1,0:T(8,128)(2,1)S(1)} %get-tuple-element.52), channel_id=1, source_target_pairs={{0,4},{1,5},{2,6},{3,7},{4,0},{5,1},{6,2},{7,3},{8,12},{9,13},{10,... | collective-permute-start | bytes 491528 | tf_op jit(solution)/shard_map/ppermute | solution.py:42
  110.4 11.9 %collective-permute-start.26 = (bf16[12,128,128]{2,1,0:T(8,128)(2,1)S(1)}, bf16[12,128,128]{2,1,0:T(8,128)(2,1)S(1)}, u32[]{:S(2)}, u32[]{:S(2)}) collective-permute-start(bf16[12,128,128]{2,1,0:T(8,128)(2,1)S(1)} %pad_maximum_fusion.4), channel_id=1, source_target_pairs={{0,4},{1,5},{2,6},{3,7},{4,0},{5,1},{6,2},{7,3},{8,12},{9,13},{10,... | collective-permute-start | bytes 1179656 | tf_op jit(solution)/shard_map/ppermute | solution.py:42
  110.8 11.9 %collective-permute-start.24 = (bf16[12,128,128]{2,1,0:T(8,128)(2,1)S(1)}, bf16[12,128,128]{2,1,0:T(8,128)(2,1)S(1)}, u32[]{:S(2)}, u32[]{:S(2)}) collective-permute-start(bf16[12,128,128]{2,1,0:T(8,128)(2,1)S(1)} %pad_maximum_fusion.3), channel_id=1, source_target_pairs={{0,3},{1,2},{2,1},{3,0},{4,7},{5,6},{6,5},{7,4},{8,11},{9,10},{10,... | collective-permute-start | bytes 1179656 | tf_op jit(solution)/shard_map/ppermute | solution.py:42
  111.3 14.4 %collective-permute-start.28 = (bf16[10,128,128]{2,1,0:T(8,128)(2,1)S(1)}, bf16[10,128,128]{2,1,0:T(8,128)(2,1)S(1)}, u32[]{:S(2)}, u32[]{:S(2)}) collective-permute-start(bf16[10,128,128]{2,1,0:T(8,128)(2,1)S(1)} %pad_maximum_fusion.9), channel_id=1, source_target_pairs={{0,1},{1,0},{2,3},{3,2},{4,5},{5,4},{6,7},{7,6},{8,9},{9,8},{10,11... | collective-permute-start | bytes 983048 | tf_op jit(solution)/shard_map/ppermute | solution.py:42
  122.4 19.1 %collective-permute-start.30 = (bf16[24,128,128]{2,1,0:T(8,128)(2,1)S(1)}, bf16[24,128,128]{2,1,0:T(8,128)(2,1)S(1)}, u32[]{:S(2)}, u32[]{:S(2)}) collective-permute-start(bf16[24,128,128]{2,1,0:T(8,128)(2,1)S(1)} %constant_dynamic-update-slice_fusion.9.rest_1_), channel_id=1, source_target_pairs={{0,1},{1,0},{2,3},{3,2},{4,5},{5,4},{6,7},{7,6},{8,9},{9,8},{10,11... | collective-permute-start | bytes 2359304 | tf_op jit(solution)/shard_map/ppermute | solution.py:42
  122.8 18.7 %collective-permute-start.29 = (bf16[22,128,128]{2,1,0:T(8,128)(2,1)S(1)}, bf16[22,128,128]{2,1,0:T(8,128)(2,1)S(1)}, u32[]{:S(2)}, u32[]{:S(2)}) collective-permute-start(bf16[22,128,128]{2,1,0:T(8,128)(2,1)S(1)} %pad_maximum_fusion.rest_0_.rest_3_), channel_id=1, source_target_pairs={{0,4},{1,5},{2,6},{3,7},{4,0},{5,1},{6,2},{7,3},{8,12},{9,13},{10,... | collective-permute-start | bytes 2162696 | tf_op jit(solution)/shard_map/ppermute | solution.py:42
  125.8 15.8 %collective-permute-start.31 = (bf16[20,128,128]{2,1,0:T(8,128)(2,1)S(1)}, bf16[20,128,128]{2,1,0:T(8,128)(2,1)S(1)}, u32[]{:S(2)}, u32[]{:S(2)}) collective-permute-start(bf16[20,128,128]{2,1,0:T(8,128)(2,1)S(1)} %constant_dynamic-update-slice_fusion.12.rest_2_), channel_id=1, source_target_pairs={{0,3},{1,2},{2,1},{3,0},{4,7},{5,6},{6,5},{7,4},{8,11},{9,10},{10,... | collective-permute-start | bytes 1966088 | tf_op jit(solution)/shard_map/ppermute | solution.py:42
  143.4 14.8 %collective-permute-start.38 = (bf16[20,128,128]{2,1,0:T(8,128)(2,1)S(1)}, bf16[20,128,128]{2,1,0:T(8,128)(2,1)S(1)}, u32[]{:S(2)}, u32[]{:S(2)}) collective-permute-start(bf16[20,128,128]{2,1,0:T(8,128)(2,1)S(1)} %get-tuple-element.58), channel_id=1, source_target_pairs={{0,96},{1,97},{2,98},{3,99},{4,100},{5,101},{6,102},{7,103},{8,104... | collective-permute-start | bytes 1966088 | tf_op jit(solution)/shard_map/ppermute | solution.py:42
  144.8 15.4 %collective-permute-start.32 = (bf16[22,128,128]{2,1,0:T(8,128)(2,1)S(1)}, bf16[22,128,128]{2,1,0:T(8,128)(2,1)S(1)}, u32[]{:S(2)}, u32[]{:S(2)}) collective-permute-start(bf16[22,128,128]{2,1,0:T(8,128)(2,1)S(1)} %get-tuple-element.54), channel_id=1, source_target_pairs={{0,16},{1,17},{2,18},{3,19},{4,20},{5,21},{6,22},{7,23},{8,24},{9,... | collective-permute-start | bytes 2162696 | tf_op jit(solution)/shard_map/ppermute | solution.py:42
  144.9 20.4 %collective-permute-start.35 = (bf16[24,128,128]{2,1,0:T(8,128)(2,1)S(1)}, bf16[24,128,128]{2,1,0:T(8,128)(2,1)S(1)}, u32[]{:S(2)}, u32[]{:S(2)}) collective-permute-start(bf16[24,128,128]{2,1,0:T(8,128)(2,1)S(1)} %get-tuple-element.56), channel_id=1, source_target_pairs={{0,32},{1,33},{2,34},{3,35},{4,36},{5,37},{6,38},{7,39},{8,40},{9,... | collective-permute-start | bytes 2359304 | tf_op jit(solution)/shard_map/ppermute | solution.py:42
  158.3 10.4 %collective-permute-start.39 = (bf16[10,128,128]{2,1,0:T(8,128)(2,1)S(1)}, bf16[10,128,128]{2,1,0:T(8,128)(2,1)S(1)}, u32[]{:S(2)}, u32[]{:S(2)}) collective-permute-start(bf16[10,128,128]{2,1,0:T(8,128)(2,1)S(1)} %add_convert_fusion.2), channel_id=1, source_target_pairs={{0,32},{1,33},{2,34},{3,35},{4,36},{5,37},{6,38},{7,39},{8,40},{9,... | collective-permute-start | bytes 983048 | tf_op jit(solution)/shard_map/ppermute | solution.py:42
  160.5 10.6 %collective-permute-start.33 = (bf16[12,128,128]{2,1,0:T(8,128)(2,1)S(1)}, bf16[12,128,128]{2,1,0:T(8,128)(2,1)S(1)}, u32[]{:S(2)}, u32[]{:S(2)}) collective-permute-start(bf16[12,128,128]{2,1,0:T(8,128)(2,1)S(1)} %pad_maximum_fusion.5), channel_id=1, source_target_pairs={{0,96},{1,97},{2,98},{3,99},{4,100},{5,101},{6,102},{7,103},{8,104... | collective-permute-start | bytes 1179656 | tf_op jit(solution)/shard_map/ppermute | solution.py:42
  165.3 10.4 %collective-permute-start.36 = (bf16[12,128,128]{2,1,0:T(8,128)(2,1)S(1)}, bf16[12,128,128]{2,1,0:T(8,128)(2,1)S(1)}, u32[]{:S(2)}, u32[]{:S(2)}) collective-permute-start(bf16[12,128,128]{2,1,0:T(8,128)(2,1)S(1)} %add_convert_fusion), channel_id=1, source_target_pairs={{0,16},{1,17},{2,18},{3,19},{4,20},{5,21},{6,22},{7,23},{8,24},{9,... | collective-permute-start | bytes 1179656 | tf_op jit(solution)/shard_map/ppermute | solution.py:42
  168.8 6.9 %collective-permute-start.40 = (bf16[5,128,128]{2,1,0:T(8,128)(2,1)S(1)}, bf16[5,128,128]{2,1,0:T(8,128)(2,1)S(1)}, u32[]{:S(2)}, u32[]{:S(2)}) collective-permute-start(bf16[5,128,128]{2,1,0:T(8,128)(2,1)S(1)} %add_convert_fusion.11), channel_id=1, source_target_pairs={{0,16},{1,17},{2,18},{3,19},{4,20},{5,21},{6,22},{7,23},{8,24},{9,... | collective-permute-start | bytes 491528 | tf_op jit(solution)/shard_map/ppermute | solution.py:42
  171.2 6.5 %collective-permute-start.34 = (bf16[7,128,128]{2,1,0:T(8,128)(2,1)S(1)}, bf16[7,128,128]{2,1,0:T(8,128)(2,1)S(1)}, u32[]{:S(2)}, u32[]{:S(2)}) collective-permute-start(bf16[7,128,128]{2,1,0:T(8,128)(2,1)S(1)} %pad_maximum_fusion.11), channel_id=1, source_target_pairs={{0,32},{1,33},{2,34},{3,35},{4,36},{5,37},{6,38},{7,39},{8,40},{9,... | collective-permute-start | bytes 688136 | tf_op jit(solution)/shard_map/ppermute | solution.py:42
  175.9 7.0 %collective-permute-start.37 = (bf16[6,128,128]{2,1,0:T(8,128)(2,1)S(1)}, bf16[6,128,128]{2,1,0:T(8,128)(2,1)S(1)}, u32[]{:S(2)}, u32[]{:S(2)}) collective-permute-start(bf16[6,128,128]{2,1,0:T(8,128)(2,1)S(1)} %add_convert_fusion.7), channel_id=1, source_target_pairs={{0,96},{1,97},{2,98},{3,99},{4,100},{5,101},{6,102},{7,103},{8,104... | collective-permute-start | bytes 589832 | tf_op jit(solution)/shard_map/ppermute | solution.py:42
  183.0 1.7 collective-permute-start.41
